TPU v7x, 32 devices: a whole 2x2x4 slice. The times are simulated.
32 devices in a mesh: fsdp: 8 (over y, x, core), ctx: 4 (over z).
Axes of the slice: x: 2, y: 2, z: 4, core: 2. Of those that a mesh axis runs over, the one named last changes fastest.
Arguments:
- hidden_in: bfloat16 [8, 1024, 2048], P('fsdp', 'ctx'), may hold values from -6 to 6
- w_mix: bfloat16 [1, 2048, 8192], P(None, 'fsdp'), may hold values from -0.125 to 0.125
- w_dt: bfloat16 [1, 2048, 48], P(None, 'fsdp'), may hold values from -0.25 to 0.25
- w_attn_out: bfloat16 [1, 2048, 1024], P(None, 'fsdp'), may hold values from -1.5 to 1.5
- w_ssm_out: bfloat16 [1, 2048, 3072], P(None, 'fsdp'), may hold values from -0.109375 to 0.109375
- w_gate: bfloat16 [1, 2048, 4096], P(None, 'fsdp'), may hold values from -0.125 to 0.125
- w_up: bfloat16 [1, 2048, 4096], P(None, 'fsdp'), may hold values from -0.125 to 0.125
- w_down: bfloat16 [1, 2048, 4096], P(None, 'fsdp'), may hold values from -0.09375 to 0.09375
- norm_gains: float32 [1, 2, 2048], replicated, may hold values from 0.5 to 1.5
- dt_bias: float32 [1, 48], replicated, as said below
- a_log: float32 [1, 48], replicated, may hold values from -0.7 to 1.5
- skip_scale: float32 [1, 48], replicated, may hold values from 0.5 to 1.5
- cotangent: bfloat16 [8, 1024, 2048], P('fsdp', 'ctx'), may hold values from -6 to 6
Outputs:
- hidden_out: bfloat16 [8, 1024, 2048], P('fsdp', 'ctx')
- grad_hidden: float32 [8, 1024, 2048], P('fsdp', 'ctx')
- grad_w_mix: float32 [1, 2048, 8192], P(None, 'fsdp')
- grad_w_dt: float32 [1, 2048, 48], P(None, 'fsdp')
- grad_w_attn_out: float32 [1, 2048, 1024], P(None, 'fsdp')
- grad_w_ssm_out: float32 [1, 2048, 3072], P(None, 'fsdp')
- grad_w_gate: float32 [1, 2048, 4096], P(None, 'fsdp')
- grad_w_up: float32 [1, 2048, 4096], P(None, 'fsdp')
- grad_w_down: float32 [1, 2048, 4096], P(None, 'fsdp')
- grad_norm_gains: float32 [1, 2, 2048], replicated
- grad_dt_bias: float32 [1, 48], replicated
- grad_a_log: float32 [1, 48], replicated
- grad_skip_scale: float32 [1, 48], replicated
Inputs may be any that keep to these rules, and one draw needn't show every extreme that they name: `dt_bias`: offsets lie between -ln(1024) - 4.5 and -ln(1024) - 0.5.
All inputs are finite; a program needn't handle non-finite values.
Results may differ from a plain program's by a relative error of at most 0.03.
Values may be sent and summed in bfloat16 or wider, within the bound.
No kernel may reach another device: no remote copies, remote signals or barrier semaphores. Data moves between devices by JAX's collectives and lax.ppermute only.
A program may use at most 704 MiB of HBM per device.

v0:
```python
import math

import jax
import jax.numpy as jnp
from jax import lax
from jax.sharding import PartitionSpec as P

FF = 4096
QUERY_HEADS = 8
KEY_VALUE_HEADS = 2
HEAD_SIZE = 128
MIXER_HEADS = 48
MIXER_HEAD_SIZE = 64
STATE_SIZE = 256
LAYERS = 1


EPSILON = 1e-05
THETA = 10000.0
EXACT_PRECISION = lax.Precision.HIGHEST


def entering(value, axis, combine, identity):
    devices, place = (lax.axis_size(axis), lax.axis_index(axis))
    everything = jax.tree.map(
        lambda part, kind: lax.all_gather(part.astype(kind), axis),
        value,
        (jnp.bfloat16, jnp.bfloat16),
    )
    start = jax.tree.map(
        lambda part, zero: jnp.broadcast_to(jnp.asarray(zero, part.dtype), part.shape),
        value,
        identity,
    )

    def hop(k, before):
        reached = k < place
        new = combine(
            before, jax.tree.map(lambda part, own: part[k].astype(own.dtype), everything, value)
        )
        return jax.tree.map(lambda a, b: jnp.where(reached, a, b), new, before)

    return lax.fori_loop(0, devices, hop, start)


def prefix(value, axis, join, neutral):
    count = lax.axis_size(axis)
    place = lax.axis_index(axis)
    ahead = count - 1 - place
    gathered = jax.tree.map(
        lambda a, kind: lax.all_gather(a.astype(kind), axis),
        value,
        jax.tree.map(lambda a: jnp.bfloat16 if a.dtype == jnp.float32 else a.dtype, value),
    )
    state = jax.tree.map(lambda a, e: jnp.zeros_like(a) + jnp.asarray(e, a.dtype), value, neutral)

    def one(hop, state):
        source = count - 1 - hop
        return join(
            state,
            jax.tree.map(
                lambda a, own: lax.dynamic_index_in_dim(a, source, 0, False).astype(own.dtype),
                gathered,
                value,
            ),
        )

    return lax.fori_loop(0, ahead, one, state)


def rotary_embed(vectors, token_positions):
    half_dim = vectors.shape[-1] // 2
    frequency = THETA ** (-jnp.arange(half_dim, dtype=jnp.float32) / half_dim)
    angles = token_positions[:, None] * frequency[None, :]
    cosine = jnp.cos(angles)[:, None, :]
    sine_part = jnp.sin(angles)[:, None, :]
    first_half = vectors[..., :half_dim]
    second_half = vectors[..., half_dim:]
    return jnp.concatenate(
        [
            first_half * cosine - second_half * sine_part,
            second_half * cosine + first_half * sine_part,
        ],
        axis=-1,
    )


def rms_scale(vectors, gain_row):
    return (
        vectors
        * lax.rsqrt(jnp.mean(vectors * vectors, axis=-1, keepdims=True) + EPSILON)
        * gain_row
    )


def decay_terms(dt_raw, dt_offset, log_rate):
    step_size = jax.nn.softplus(dt_raw + dt_offset)
    level = jnp.cumsum(step_size * -jnp.exp(log_rate), axis=1)
    return (step_size, level)


def within_block(inputs, b_rows, c_rows, step_size, level):
    length_here = inputs.shape[1]
    order = jnp.arange(length_here)
    causal = (order[:, None] >= order[None, :])[None, None]
    level_head = jnp.swapaxes(level, 1, 2)
    gap_level = jnp.where(causal, level_head[:, :, :, None] - level_head[:, :, None, :], 0.0)
    fading = jnp.where(causal, jnp.exp(gap_level), 0.0)
    pairing = jnp.einsum("btn,bsn->bts", c_rows, b_rows, precision=EXACT_PRECISION)
    mixing = fading * pairing[:, None] * jnp.swapaxes(step_size, 1, 2)[:, :, None, :]
    output = jnp.einsum("bhts,bshp->bthp", mixing, inputs, precision=EXACT_PRECISION)
    weight_tail = jnp.exp(level[:, -1:, :] - level) * step_size
    fresh_state = jnp.einsum(
        "bsh,bshp,bsn->bhpn", weight_tail, inputs, b_rows, precision=EXACT_PRECISION
    )
    return (output, fresh_state, jnp.exp(level[:, -1, :]))


def from_state(c_rows, level, start_state):
    return jnp.exp(level)[..., None] * jnp.einsum(
        "btn,bhpn->bthp", c_rows, start_state, precision=EXACT_PRECISION
    )


def split_mixed(mixed_cols):
    shape_extents = [
        QUERY_HEADS * HEAD_SIZE,
        KEY_VALUE_HEADS * HEAD_SIZE,
        KEY_VALUE_HEADS * HEAD_SIZE,
        MIXER_HEADS * MIXER_HEAD_SIZE,
        MIXER_HEADS * MIXER_HEAD_SIZE,
        STATE_SIZE,
        STATE_SIZE,
    ]
    split_pieces = []
    offset = 0
    for extent in shape_extents:
        split_pieces.append(mixed_cols[..., offset : offset + extent])
        offset = offset + extent
    return split_pieces


def chain_forward(earlier, later):
    return (earlier[0] * later[0], later[0][:, :, None, None] * earlier[1] + later[1])


def chain_backward(earlier, later):
    return (earlier[0] * later[0], later[1] + later[0][:, :, None, None] * earlier[1])


def contract(left_rows, first_weight, second_weight):
    zero_first = jnp.zeros((left_rows.shape[0], first_weight.shape[1]), jnp.float32)
    zero_second = jnp.zeros((left_rows.shape[0], second_weight.shape[1]), jnp.float32)

    def absorb(totals, split_pieces, first_row):
        return (
            jnp.dot(left_rows, split_pieces[0], preferred_element_type=jnp.float32),
            jnp.dot(left_rows, split_pieces[1], preferred_element_type=jnp.float32),
        )

    return absorb(
        (zero_first, zero_second),
        (
            lax.all_gather(first_weight, "fsdp", axis=0, tiled=True),
            lax.all_gather(second_weight, "fsdp", axis=0, tiled=True),
        ),
        jnp.int32(0),
    )


def expand(first_left, second_left, first_weight, second_weight):
    model_width = first_weight.shape[0] * lax.axis_size("fsdp")
    empty_rows = jnp.zeros((first_left.shape[0], model_width), jnp.float32)

    def absorb(total_rows, split_pieces, first_row):
        part_rows = lax.dot_general(
            first_left,
            split_pieces[0],
            (((1,), (1,)), ((), ())),
            preferred_element_type=jnp.float32,
        )
        part_rows = part_rows + lax.dot_general(
            second_left,
            split_pieces[1],
            (((1,), (1,)), ((), ())),
            preferred_element_type=jnp.float32,
        )
        return part_rows

    return absorb(
        empty_rows,
        (
            lax.all_gather(first_weight, "fsdp", axis=0, tiled=True),
            lax.all_gather(second_weight, "fsdp", axis=0, tiled=True),
        ),
        jnp.int32(0),
    )


def weight_grads(pairs):
    widths = [right_rows.shape[1] for left_rows, right_rows in pairs]
    blocks = []
    for left_rows, right_rows in pairs:
        blocks.append(
            lax.dot_general(
                left_rows, right_rows, (((0,), (0,)), ((), ())), preferred_element_type=jnp.float32
            )
        )
    result = lax.psum_scatter(
        jnp.concatenate(blocks, axis=1).astype(jnp.bfloat16),
        "fsdp",
        scatter_dimension=0,
        tiled=True,
    ).astype(jnp.float32)
    split_pieces = []
    offset = 0
    for width in widths:
        split_pieces.append(result[:, offset : offset + width])
        offset = offset + width
    return tuple(split_pieces)


def attend_forward(query_rows, rows_of_key, rows_of_value, token_positions):
    sequence_count, sequence_piece = (query_rows.shape[0], query_rows.shape[1])
    group_extent = QUERY_HEADS // KEY_VALUE_HEADS
    query_grouped = query_rows.reshape(
        sequence_count, sequence_piece, KEY_VALUE_HEADS, group_extent, HEAD_SIZE
    )
    score_scale = 1.0 / math.sqrt(HEAD_SIZE)
    reshape_rows = (sequence_count, KEY_VALUE_HEADS, group_extent, sequence_piece)
    initial = (
        jnp.full(reshape_rows, -1e30, jnp.float32),
        jnp.zeros(reshape_rows, jnp.float32),
        jnp.zeros(reshape_rows + (HEAD_SIZE,), jnp.float32),
    )

    def absorb(carry_state, split_pieces, first_key):
        running_max, running_sum, running_out = carry_state
        key_total_count = split_pieces[0].shape[1]
        heads_of_key = split_pieces[0].reshape(
            sequence_count, key_total_count, KEY_VALUE_HEADS, HEAD_SIZE
        )
        heads_of_value = split_pieces[1].reshape(
            sequence_count, key_total_count, KEY_VALUE_HEADS, HEAD_SIZE
        )
        unscaled_scores = jnp.einsum(
            "bqgrd,bkgd->bgrqk", query_grouped, heads_of_key, preferred_element_type=jnp.float32
        )
        key_place = jnp.arange(key_total_count).astype(jnp.float32)
        visible = key_place[None, :] <= token_positions[:, None]
        logits = jnp.where(visible, unscaled_scores * score_scale, -1e30)
        new_max = jnp.maximum(running_max, jnp.max(logits, axis=-1))
        weight_set = jnp.exp(logits - new_max[..., None])
        running_sum = jnp.sum(weight_set, axis=-1)
        running_out = jnp.einsum(
            "bgrqk,bkgd->bgrqd",
            weight_set.astype(jnp.bfloat16),
            heads_of_value,
            preferred_element_type=jnp.float32,
        )
        return (new_max, running_sum, running_out)

    running_max, running_sum, running_out = absorb(
        initial,
        (
            lax.all_gather(rows_of_key, "ctx", axis=1, tiled=True),
            lax.all_gather(rows_of_value, "ctx", axis=1, tiled=True),
        ),
        jnp.int32(0),
    )
    attended = running_out / running_sum[..., None]
    log_total = running_max + jnp.log(running_sum)
    attended = jnp.transpose(attended, (0, 3, 1, 2, 4)).reshape(
        sequence_count, sequence_piece, QUERY_HEADS * HEAD_SIZE
    )
    return (attended, log_total)


def attend_backward(
    query_rows,
    rows_of_key,
    rows_of_value,
    attended_complete,
    log_total,
    gradient_output_rows,
    token_positions,
):
    sequence_count, sequence_piece = (query_rows.shape[0], query_rows.shape[1])
    group_extent = QUERY_HEADS // KEY_VALUE_HEADS
    query_grouped = query_rows.reshape(
        sequence_count, sequence_piece, KEY_VALUE_HEADS, group_extent, HEAD_SIZE
    )
    gradient_grouped = gradient_output_rows.reshape(
        sequence_count, sequence_piece, KEY_VALUE_HEADS, group_extent, HEAD_SIZE
    )
    score_scale = 1.0 / math.sqrt(HEAD_SIZE)
    delta_rows = jnp.sum(
        gradient_grouped.astype(jnp.float32)
        * attended_complete.reshape(
            sequence_count, sequence_piece, KEY_VALUE_HEADS, group_extent, HEAD_SIZE
        ),
        axis=-1,
    )
    delta_rows = jnp.transpose(delta_rows, (0, 2, 3, 1))
    complete_length = sequence_piece * lax.axis_size("ctx")
    initial = (
        jnp.zeros(
            (sequence_count, sequence_piece, KEY_VALUE_HEADS, group_extent, HEAD_SIZE), jnp.float32
        ),
        jnp.zeros((sequence_count, complete_length, KEY_VALUE_HEADS * HEAD_SIZE), jnp.float32),
        jnp.zeros((sequence_count, complete_length, KEY_VALUE_HEADS * HEAD_SIZE), jnp.float32),
    )

    def absorb(carry_state, split_pieces, first_key):
        key_total_count = split_pieces[0].shape[1]
        heads_of_key = split_pieces[0].reshape(
            sequence_count, key_total_count, KEY_VALUE_HEADS, HEAD_SIZE
        )
        heads_of_value = split_pieces[1].reshape(
            sequence_count, key_total_count, KEY_VALUE_HEADS, HEAD_SIZE
        )
        unscaled_scores = jnp.einsum(
            "bqgrd,bkgd->bgrqk", query_grouped, heads_of_key, preferred_element_type=jnp.float32
        )
        key_place = jnp.arange(key_total_count).astype(jnp.float32)
        visible = key_place[None, :] <= token_positions[:, None]
        probs = jnp.exp(
            jnp.where(visible, unscaled_scores * score_scale - log_total[..., None], -1e30)
        )
        grad_probs = jnp.einsum(
            "bqgrd,bkgd->bgrqk",
            gradient_grouped,
            heads_of_value,
            preferred_element_type=jnp.float32,
        )
        grad_scores = (probs * (grad_probs - delta_rows[..., None]) * score_scale).astype(
            jnp.bfloat16
        )
        grad_query = jnp.einsum(
            "bgrqk,bkgd->bqgrd", grad_scores, heads_of_key, preferred_element_type=jnp.float32
        )
        key_part = jnp.einsum(
            "bgrqk,bqgrd->bkgd", grad_scores, query_grouped, preferred_element_type=jnp.float32
        ).reshape(sequence_count, key_total_count, KEY_VALUE_HEADS * HEAD_SIZE)
        value_part = jnp.einsum(
            "bgrqk,bqgrd->bkgd",
            probs.astype(jnp.bfloat16),
            gradient_grouped,
            preferred_element_type=jnp.float32,
        ).reshape(sequence_count, key_total_count, KEY_VALUE_HEADS * HEAD_SIZE)
        return (grad_query, key_part, value_part)

    grad_query, gradient_key, gradient_value = absorb(
        initial,
        (
            lax.all_gather(rows_of_key, "ctx", axis=1, tiled=True),
            lax.all_gather(rows_of_value, "ctx", axis=1, tiled=True),
        ),
        jnp.int32(0),
    )
    gradient_key, gradient_value = (
        lax.psum_scatter(
            gradient_key.astype(jnp.bfloat16), "ctx", scatter_dimension=1, tiled=True
        ).astype(jnp.float32),
        lax.psum_scatter(
            gradient_value.astype(jnp.bfloat16), "ctx", scatter_dimension=1, tiled=True
        ).astype(jnp.float32),
    )
    return (
        grad_query.reshape(sequence_count, sequence_piece, QUERY_HEADS, HEAD_SIZE),
        gradient_key,
        gradient_value,
    )


def ssm_views(mixed_cols, dt_raw, sequence_count, sequence_piece):
    q_part, key_piece, value_piece, z_part, x_part, b_part, c_part = split_mixed(mixed_cols)
    ssm_in = x_part.reshape(sequence_count, sequence_piece, MIXER_HEADS, MIXER_HEAD_SIZE)
    b_rows = b_part.reshape(sequence_count, sequence_piece, STATE_SIZE)
    c_rows = c_part.reshape(sequence_count, sequence_piece, STATE_SIZE)
    z_rows = z_part.reshape(sequence_count, sequence_piece, MIXER_HEADS, MIXER_HEAD_SIZE)
    dt_rows = dt_raw.reshape(sequence_count, sequence_piece, MIXER_HEADS)
    return (ssm_in, b_rows, c_rows, z_rows, dt_rows)


def layer_forward(state, weight_set, token_positions, sequence_count, sequence_piece):
    (
        w_mix,
        w_dt,
        w_attn_out,
        w_ssm_out,
        w_gate,
        w_up,
        w_down,
        gain_pair,
        dt_bias,
        a_log,
        skip_scale,
    ) = weight_set
    token_count = state.shape[0]
    normed = rms_scale(state, gain_pair[0]).astype(jnp.bfloat16)
    mixed_cols, dt_raw = contract(normed, w_mix, w_dt)
    q_part, key_piece, value_piece, z_part, x_part, b_part, c_part = split_mixed(mixed_cols)
    query_rows = rotary_embed(
        q_part.reshape(sequence_count, sequence_piece, QUERY_HEADS, HEAD_SIZE), token_positions
    ).astype(jnp.bfloat16)
    rows_of_key = (
        rotary_embed(
            key_piece.reshape(sequence_count, sequence_piece, KEY_VALUE_HEADS, HEAD_SIZE),
            token_positions,
        )
        .astype(jnp.bfloat16)
        .reshape(sequence_count, sequence_piece, KEY_VALUE_HEADS * HEAD_SIZE)
    )
    rows_of_value = value_piece.astype(jnp.bfloat16).reshape(
        sequence_count, sequence_piece, KEY_VALUE_HEADS * HEAD_SIZE
    )
    attended_complete, log_total = attend_forward(
        query_rows, rows_of_key, rows_of_value, token_positions
    )
    attended = attended_complete.astype(jnp.bfloat16).reshape(token_count, QUERY_HEADS * HEAD_SIZE)
    ssm_in, b_rows, c_rows, z_rows, dt_rows = ssm_views(
        mixed_cols, dt_raw, sequence_count, sequence_piece
    )
    step_size, level = decay_terms(dt_rows, dt_bias, a_log)
    inside, fresh_state, block_decay = within_block(ssm_in, b_rows, c_rows, step_size, level)
    identity = (jnp.ones_like(block_decay), jnp.zeros_like(fresh_state))
    start_state = entering((block_decay, fresh_state), "ctx", chain_forward, identity)[1]
    full_y = inside + from_state(c_rows, level, start_state) + skip_scale[:, None] * ssm_in
    gated_rows = (
        (full_y * jax.nn.silu(z_rows))
        .reshape(token_count, MIXER_HEADS * MIXER_HEAD_SIZE)
        .astype(jnp.bfloat16)
    )
    branch = expand(attended, gated_rows, w_attn_out, w_ssm_out)
    middle = state + branch
    normed_ffn = rms_scale(middle, gain_pair[1]).astype(jnp.bfloat16)
    gate_rows, up_rows = contract(normed_ffn, w_gate, w_up)
    activated = (jax.nn.silu(gate_rows) * up_rows).astype(jnp.bfloat16)
    half_ff = FF // 2
    ffn_out = expand(
        activated[:, :half_ff], activated[:, half_ff:], w_down[:, :half_ff], w_down[:, half_ff:]
    )
    saved = (
        state,
        normed,
        mixed_cols,
        dt_raw,
        query_rows,
        rows_of_key,
        rows_of_value,
        attended_complete,
        log_total,
        attended,
        block_decay,
        start_state,
        full_y,
        gated_rows,
        middle,
        normed_ffn,
        gate_rows,
        up_rows,
        activated,
    )
    return (middle + ffn_out, saved)


def layer_backward(grad_state, weight_set, saved, token_positions, sequence_count, sequence_piece):
    (
        w_mix,
        w_dt,
        w_attn_out,
        w_ssm_out,
        w_gate,
        w_up,
        w_down,
        gain_pair,
        dt_bias,
        a_log,
        skip_scale,
    ) = weight_set
    (
        state,
        normed,
        mixed_cols,
        dt_raw,
        query_rows,
        rows_of_key,
        rows_of_value,
        attended_complete,
        log_total,
        attended,
        block_decay,
        start_state,
        full_y,
        gated_rows,
        middle,
        normed_ffn,
        gate_rows,
        up_rows,
        activated,
    ) = saved
    token_count = grad_state.shape[0]
    half_ff = FF // 2
    grad_ffn = grad_state.astype(jnp.bfloat16)
    grad_first, grad_second = contract(grad_ffn, w_down[:, :half_ff], w_down[:, half_ff:])
    grad_act = jnp.concatenate([grad_first, grad_second], axis=1)
    _, swiglu_pull = jax.vjp(
        lambda gate_in, up_in: jax.nn.silu(gate_in) * up_in, gate_rows, up_rows
    )
    grad_gate, grad_up = swiglu_pull(grad_act)
    grad_gate = grad_gate.astype(jnp.bfloat16)
    grad_up = grad_up.astype(jnp.bfloat16)
    grad_normed_ffn = expand(grad_gate, grad_up, w_gate, w_up)
    _, ffn_norm_pull = jax.vjp(rms_scale, middle, gain_pair[1])
    grad_middle_norm, grad_gain_ffn = ffn_norm_pull(grad_normed_ffn)
    grad_middle = grad_state + grad_middle_norm
    grad_branch = grad_middle.astype(jnp.bfloat16)
    grad_attended, grad_gated = contract(grad_branch, w_attn_out, w_ssm_out)
    gradient_output_rows = grad_attended.astype(jnp.bfloat16).reshape(
        sequence_count, sequence_piece, QUERY_HEADS * HEAD_SIZE
    )
    grad_query, gradient_key, gradient_value = attend_backward(
        query_rows,
        rows_of_key,
        rows_of_value,
        attended_complete,
        log_total,
        gradient_output_rows,
        token_positions,
    )
    grad_q_part = rotary_embed(grad_query, -token_positions).reshape(
        token_count, QUERY_HEADS * HEAD_SIZE
    )
    gradient_key_piece = rotary_embed(
        gradient_key.reshape(sequence_count, sequence_piece, KEY_VALUE_HEADS, HEAD_SIZE),
        -token_positions,
    ).reshape(token_count, KEY_VALUE_HEADS * HEAD_SIZE)
    gradient_value_piece = gradient_value.reshape(token_count, KEY_VALUE_HEADS * HEAD_SIZE)
    ssm_in, b_rows, c_rows, z_rows, dt_rows = ssm_views(
        mixed_cols, dt_raw, sequence_count, sequence_piece
    )
    _, gate_pull = jax.vjp(lambda y_in, z_in: y_in * jax.nn.silu(z_in), full_y, z_rows)
    grad_full, grad_z = gate_pull(
        grad_gated.reshape(sequence_count, sequence_piece, MIXER_HEADS, MIXER_HEAD_SIZE)
    )
    grad_skip = jnp.sum(grad_full * ssm_in, axis=(0, 1, 3))
    step_size, level = decay_terms(dt_rows, dt_bias, a_log)
    from_later = jnp.einsum(
        "bth,bthp,btn->bhpn", jnp.exp(level), grad_full, c_rows, precision=EXACT_PRECISION
    )
    identity = (jnp.ones_like(block_decay), jnp.zeros_like(from_later))
    grad_end = prefix((block_decay, from_later), "ctx", chain_backward, identity)[1]
    grad_decay = jnp.sum(grad_end * start_state, axis=(2, 3))

    def local_ssm(inputs, b_in, c_in, dt_in, offset_in, rate_in):
        steps_in, level_in = decay_terms(dt_in, offset_in, rate_in)
        inside, fresh_state, decay_out = within_block(inputs, b_in, c_in, steps_in, level_in)
        return (inside + from_state(c_in, level_in, start_state), fresh_state, decay_out)

    _, ssm_pull = jax.vjp(local_ssm, ssm_in, b_rows, c_rows, dt_rows, dt_bias, a_log)
    grad_x, grad_b, grad_c, grad_dt, grad_bias, grad_rate = ssm_pull(
        (grad_full, grad_end, grad_decay)
    )
    grad_x = grad_x + skip_scale[:, None] * grad_full
    grad_mixed = jnp.concatenate(
        [
            grad_q_part,
            gradient_key_piece,
            gradient_value_piece,
            grad_z.reshape(token_count, MIXER_HEADS * MIXER_HEAD_SIZE),
            grad_x.reshape(token_count, MIXER_HEADS * MIXER_HEAD_SIZE),
            grad_b.reshape(token_count, STATE_SIZE),
            grad_c.reshape(token_count, STATE_SIZE),
        ],
        axis=1,
    ).astype(jnp.bfloat16)
    grad_dt_rows = grad_dt.reshape(token_count, MIXER_HEADS).astype(jnp.bfloat16)
    grad_normed = expand(grad_mixed, grad_dt_rows, w_mix, w_dt)
    matrices = weight_grads(
        (
            (normed, grad_mixed),
            (normed, grad_dt_rows),
            (grad_branch, attended),
            (grad_branch, gated_rows),
            (normed_ffn, grad_gate),
            (normed_ffn, grad_up),
            (grad_ffn, activated),
        )
    )
    _, mix_norm_pull = jax.vjp(rms_scale, state, gain_pair[0])
    grad_state_norm, grad_gain_mix = mix_norm_pull(grad_normed)
    grad_input = grad_middle + grad_state_norm
    gain_part = jnp.stack([grad_gain_mix, grad_gain_ffn])
    head_part = jnp.stack([grad_bias, grad_rate, grad_skip])
    return (grad_input, matrices, gain_part, head_part)


def per_device(
    hidden_in,
    w_mix,
    w_dt,
    w_attn_out,
    w_ssm_out,
    w_gate,
    w_up,
    w_down,
    norm_gains,
    dt_bias,
    a_log,
    skip_scale,
    cotangent,
):
    sequence_count, sequence_piece, model_width = hidden_in.shape
    token_count = sequence_count * sequence_piece
    ctx_place = lax.axis_index("ctx")
    token_positions = (ctx_place * sequence_piece + jnp.arange(sequence_piece)).astype(jnp.float32)
    state = hidden_in.astype(jnp.float32).reshape(token_count, model_width)
    layer_no = 0
    weight_set = (
        w_mix[layer_no],
        w_dt[layer_no],
        w_attn_out[layer_no],
        w_ssm_out[layer_no],
        w_gate[layer_no],
        w_up[layer_no],
        w_down[layer_no],
        norm_gains[layer_no],
        dt_bias[layer_no],
        a_log[layer_no],
        skip_scale[layer_no],
    )
    layer_weights = [weight_set]
    state, saved = layer_forward(state, weight_set, token_positions, sequence_count, sequence_piece)
    saved_layers = [saved]
    hidden_out = state.astype(jnp.bfloat16).reshape(sequence_count, sequence_piece, model_width)
    grad_state = cotangent.astype(jnp.float32).reshape(token_count, model_width)
    matrix_layers = [None] * LAYERS
    gain_layers = [None] * LAYERS
    head_layers = [None] * LAYERS
    for layer_no in reversed(range(LAYERS)):
        grad_state, matrices, gain_part, head_part = layer_backward(
            grad_state,
            layer_weights[layer_no],
            saved_layers[layer_no],
            token_positions,
            sequence_count,
            sequence_piece,
        )
        matrix_layers[layer_no] = matrices
        gain_layers[layer_no] = gain_part
        head_layers[layer_no] = head_part
    stacked = [jnp.stack([matrix_layers[0][member]]) for member in range(7)]
    gain_grads = jnp.stack(gain_layers)
    head_grads = jnp.stack(head_layers)
    small_part = lax.psum((gain_grads, head_grads), "fsdp")
    summed = (
        lax.psum(stacked[0].astype(jnp.bfloat16), "ctx").astype(jnp.float32),
        lax.psum(stacked[1].astype(jnp.bfloat16), "ctx").astype(jnp.float32),
        lax.psum(stacked[2].astype(jnp.bfloat16), "ctx").astype(jnp.float32),
        lax.psum(stacked[3].astype(jnp.bfloat16), "ctx").astype(jnp.float32),
        lax.psum(stacked[4].astype(jnp.bfloat16), "ctx").astype(jnp.float32),
        lax.psum(stacked[5].astype(jnp.bfloat16), "ctx").astype(jnp.float32),
        lax.psum(stacked[6].astype(jnp.bfloat16), "ctx").astype(jnp.float32),
        lax.psum(small_part[0].astype(jnp.bfloat16), "ctx").astype(jnp.float32),
        lax.psum(small_part[1].astype(jnp.bfloat16), "ctx").astype(jnp.float32),
    )
    matrix_sums = summed[:7]
    small_sums = summed[7:]
    grad_hidden = grad_state.reshape(sequence_count, sequence_piece, model_width)
    head_sums = small_sums[1]
    return (
        hidden_out,
        grad_hidden,
        matrix_sums[0],
        matrix_sums[1],
        matrix_sums[2],
        matrix_sums[3],
        matrix_sums[4],
        matrix_sums[5],
        matrix_sums[6],
        small_sums[0],
        head_sums[:, 0],
        head_sums[:, 1],
        head_sums[:, 2],
    )


def solution(mesh):
    placed = (
        P("fsdp", "ctx", None),
        P(None, "fsdp", None),
        P(None, "fsdp", None),
        P(None, "fsdp", None),
        P(None, "fsdp", None),
        P(None, "fsdp", None),
        P(None, "fsdp", None),
        P(None, "fsdp", None),
        P(),
        P(),
        P(),
        P(),
        P("fsdp", "ctx", None),
    )
    return jax.shard_map(
        per_device,
        mesh=mesh,
        in_specs=placed,
        out_specs=(
            P("fsdp", "ctx", None),
            P("fsdp", "ctx", None),
            P(None, "fsdp", None),
            P(None, "fsdp", None),
            P(None, "fsdp", None),
            P(None, "fsdp", None),
            P(None, "fsdp", None),
            P(None, "fsdp", None),
            P(None, "fsdp", None),
            P(),
            P(),
            P(),
            P(),
        ),
        check_vma=False,
    )
```

profile of v0, /device:TPU:0, one launch (start us, length us, event | category | flops | bytes accessed | tf_op | source)
XLA Modules:
  0.0 2807.9 jit_solution(1037408022694052871)
XLA Ops:
  11.1 11.0 all-gather.3
  26.1 147.4 %all-gather.23.cloned.1.call-done = bf16[1,2048,8192]{2,1,0:T(8,128)(2,1)} async-done(((bf16[1,256,8192]{2,1,0:T(8,128)(2,1)}), bf16[1,2048,8192]{2,1,0:T(8,128)(2,1)}) %all-gather.23.cloned.1.call-update) | async-done | bytes 33554448 | tf_op jit(solution)/shard_map/all_gather | solution.py:164
  173.5 17.8 fusion.3
  191.3 6.3 fusion.242
  220.0 11.0 all_gather.63
  233.2 7.4 fusion.182
  240.6 46.7 %all-gather.21.cloned.1.call-done = bf16[2048,2048]{1,0:T(8,128)(2,1)} async-done(((bf16[256,2048]{1,0:T(8,128)(2,1)}), bf16[2048,2048]{1,0:T(8,128)(2,1)}) %all-gather.21.cloned.1.call-update) | async-done | bytes 8388624 | tf_op jit(solution)/shard_map/all_gather | solution.py:194
  287.2 7.4 fusion.180
  299.8 24.1 all-gather.1
  335.4 23.9 all_gather.59
  370.5 50.8 %all-gather.27.cloned.1.call-done = bf16[192,64,256]{2,1,0:T(8,128)(2,1)} async-done(((bf16[48,64,256]{2,1,0:T(8,128)(2,1)}), bf16[192,64,256]{2,1,0:T(8,128)(2,1)}) %all-gather.27.cloned.1.call-update) | async-done | bytes 6291472 | tf_op jit(solution)/shard_map/all_gather | solution.py:26
  421.3 15.2 while.29
  442.4 17.4 multiply_convert_fusion.2
  459.8 33.7 %all-gather.29.cloned.1.call-done = bf16[1,2048,3072]{2,1,0:T(8,128)(2,1)} async-done(((bf16[1,256,3072]{2,1,0:T(8,128)(2,1)}), bf16[1,2048,3072]{2,1,0:T(8,128)(2,1)}) %all-gather.29.cloned.1.call-update) | async-done | bytes 12582928 | tf_op jit(solution)/shard_map/all_gather | solution.py:194
  493.5 9.9 fusion.15
  503.4 28.6 %all-gather.25.cloned.1.call-done = bf16[1,2048,1024]{2,1,0:T(8,128)(2,1)} async-done(((bf16[1,256,1024]{2,1,0:T(8,128)(2,1)}), bf16[1,2048,1024]{2,1,0:T(8,128)(2,1)}) %all-gather.25.cloned.1.call-update) | async-done | bytes 4194320 | tf_op jit(solution)/shard_map/all_gather | solution.py:193
  539.4 84.4 %all-gather.33.cloned.1.call-done = bf16[1,2048,4096]{2,1,0:T(8,128)(2,1)} async-done(((bf16[1,256,4096]{2,1,0:T(8,128)(2,1)}), bf16[1,2048,4096]{2,1,0:T(8,128)(2,1)}) %all-gather.33.cloned.1.call-update) | async-done | bytes 16777232 | tf_op jit(solution)/shard_map/all_gather | solution.py:165
  623.8 12.6 fusion.7
  636.4 79.2 %all-gather.31.cloned.1.call-done = bf16[1,2048,4096]{2,1,0:T(8,128)(2,1)} async-done(((bf16[1,256,4096]{2,1,0:T(8,128)(2,1)}), bf16[1,2048,4096]{2,1,0:T(8,128)(2,1)}) %all-gather.31.cloned.1.call-update) | async-done | bytes 16777232 | tf_op jit(solution)/shard_map/all_gather | solution.py:164
  715.6 17.5 fusion.49
  733.1 12.2 fusion.5
  745.3 14.4 multiply_reduce_fusion.5
  772.5 6.7 fusion.52
  783.6 14.7 multiply_reduce_fusion.2
  801.9 6.7 fusion.136
  808.9 5.2 multiply_reduce_fusion.4
  814.8 7.1 fusion.121
  822.0 23.3 fusion.31
  859.7 5.8 fusion.143
  872.3 6.4 convolution_convert_fusion.3
  878.7 8.6 convolution_convert_fusion.2
  887.4 9.9 convolution_convert_fusion.1
  897.3 9.9 convert_bitcast_fusion
  913.1 32.5 %all-gather.35.cloned.1.call-done = bf16[192,64,256]{2,1,0:T(8,128)(2,1)} async-done(((bf16[48,64,256]{2,1,0:T(8,128)(2,1)}), bf16[192,64,256]{2,1,0:T(8,128)(2,1)}) %all-gather.35.cloned.1.call-update) | async-done | bytes 6291472 | tf_op jit(solution)/shard_map/all_gather | solution.py:51
  946.0 7.8 while.28
  956.7 5.9 fusion.71
  974.1 17.2 fusion.68
  1002.6 5.8 fusion.168
  1010.6 16.8 convolution_convert_fusion
  1027.4 181.0 %concatenate.46 = bf16[2048,24624]{1,0:T(8,128)(2,1)} concatenate(bf16[2048,8192]{1,0:T(8,128)(2,1)} %convolution_convert_fusion, bf16[2048,48]{1,0:T(8,128)(2,1)S(1)} %copy-done.32, bf16[2048,1024]{1,0:T(8,128)(2,1)} %convolution_convert_fusion.4, bf16[2048,3072]{1,0:T(8,128)(2,1)} %convolution_convert_fusion.3, bf16[2048,4096]{1,0:T(8,128)(2,1)} %convolution_convert_fusion.2, ...), dimensions={1} | concatenate | bytes 201719808 | tf_op jit(solution)/shard_map/concatenate | solution.py:210
  1210.3 1121.0 %all-reduce.9.cloned.1.call-done = bf16[2048,24624]{1,0:T(8,128)(2,1)} async-done(((bf16[2048,24624]{1,0:T(8,128)(2,1)}), bf16[2048,24624]{1,0:T(8,128)(2,1)}) %all-reduce.9.cloned.1.call-update) | async-done | bytes 100859920
  2341.5 9.5 dynamic-slice_bitcast_fusion.1
  2351.8 6.2 fusion.176
  2358.1 6.9 fusion.106
  2365.0 17.3 fusion.1
  2386.1 25.3 all-reduce.3
  2417.4 25.3 all-reduce.4
  2444.6 338.7 %all-reduce.11.cloned.1.call-done = (bf16[1,256,8192]{2,1,0:T(8,128)(2,1)}, bf16[1,256,1024]{2,1,0:T(8,128)(2,1)}, bf16[1,256,3072]{2,1,0:T(8,128)(2,1)}, bf16[1...) async-done(((bf16[1,256,8192]{2,1,0:T(8,128)(2,1)}, bf16[1,256,1024]{2,1,0:T(8,128)(2,1)}, bf16[1,256,3072]{2,1,0:T(8,128)(2,1)}, ...) | async-done | bytes 12582928 | tf_op jit(solution)/shard_map/psum | solution.py:658
  (343 shorter events, 213.7 us)
Async XLA Ops:
  7.2 166.3 %all-gather.23.cloned.1.call-start = ((), (), s32[]{:S(2)}) async-start(), calls=%async_computation.6 | async-start | bytes 37748736 | tf_op jit(solution)/shard_map/all_gather | solution.py:164
  7.9 225.2 %all-gather.19.cloned.1.call-start = ((), (), s32[]{:S(2)}) async-start(), calls=%async_computation.2 | async-start | bytes 9437184 | tf_op jit(solution)/shard_map/all_gather | solution.py:193
  8.8 13.3 copy-start.11
  8.8 13.6 copy-start.83
  8.8 13.7 copy-start.69
  8.8 14.1 copy-start.81
  10.3 277.0 %all-gather.21.cloned.1.call-start = ((), (), s32[]{:S(2)}) async-start(), calls=%async_computation.3 | async-start | bytes 9437184 | tf_op jit(solution)/shard_map/all_gather | solution.py:194
  11.0 410.3 %all-gather.27.cloned.1.call-start = ((), (), s32[]{:S(2)}) async-start(), calls=%async_computation.8 | async-start | bytes 7864320 | tf_op jit(solution)/shard_map/all_gather | solution.py:26
  22.4 168.9 %copy-start.78 = (f32[48]{0:T(128)}, f32[48]{0:T(128)S(1)}, u32[]{:S(2)}) copy-start(f32[48]{0:T(128)S(1)} %negate_bitcast_fusion) | copy-start | bytes 580
  22.4 168.8 %copy-start.63 = (f32[256]{0:T(256)}, f32[256]{0:T(256)S(1)}, u32[]{:S(2)}) copy-start(f32[256]{0:T(256)S(1)} %fusion.220) | copy-start | bytes 3076
  22.5 168.8 %copy-start.47 = (f32[1,1,2048]{2,1,0:T(1,128)}, f32[1,1,2048]{2,1,0:T(1,128)S(1)}, u32[]{:S(2)}) copy-start(f32[1,1,2048]{2,1,0:T(1,128)S(1)} %get-tuple-element.418) | copy-start | bytes 24580
  22.5 737.2 %copy-start.61 = (f32[1,1,2048]{2,1,0:T(1,128)}, f32[1,1,2048]{2,1,0:T(1,128)S(1)}, u32[]{:S(2)}) copy-start(f32[1,1,2048]{2,1,0:T(1,128)S(1)} %get-tuple-element.417) | copy-start | bytes 24580
  23.4 167.9 %copy-start.28 = (f32[256,48]{1,0:T(8,128)}, f32[256,48]{1,0:T(8,128)S(1)}, u32[]{:S(2)}) copy-start(f32[256,48]{1,0:T(8,128)S(1)} %convolution_add_fusion.3) | copy-start | bytes 147460
  25.2 166.1 %copy-start.76 = (f32[48]{0:T(128)}, f32[48]{0:T(128)S(1)}, u32[]{:S(2)}) copy-start(f32[48]{0:T(128)S(1)} %get-tuple-element.415) | copy-start | bytes 580
  26.0 174.0 %copy-start.53 = (f32[256,48]{0,1:T(8,128)}, f32[256,48]{0,1:T(8,128)S(1)}, u32[]{:S(2)}) copy-start(f32[256,48]{0,1:T(8,128)S(1)} %copy.259) | copy-start | bytes 147460
  204.9 288.6 %all-gather.29.cloned.1.call-start = ((), (), s32[]{:S(2)}) async-start(), calls=%async_computation.9 | async-start | bytes 14155776 | tf_op jit(solution)/shard_map/all_gather | solution.py:194
  205.5 326.5 %all-gather.25.cloned.1.call-start = ((), (), s32[]{:S(2)}) async-start(), calls=%async_computation.7 | async-start | bytes 4718592 | tf_op jit(solution)/shard_map/all_gather | solution.py:193
  206.1 417.7 %all-gather.33.cloned.1.call-start = ((), (), s32[]{:S(2)}) async-start(), calls=%async_computation.11 | async-start | bytes 18874368 | tf_op jit(solution)/shard_map/all_gather | solution.py:165
  206.8 508.8 %all-gather.31.cloned.1.call-start = ((), (), s32[]{:S(2)}) async-start(), calls=%async_computation.10 | async-start | bytes 18874368 | tf_op jit(solution)/shard_map/all_gather | solution.py:164
  207.6 699.7 %reduce-scatter.3.cloned.1.call-start = ((), (), s32[]{:S(2)}) async-start(), calls=%async_computation.4 | async-start | bytes 655360 | tf_op jit(solution)/shard_map/reduce_scatter | solution.py:362
  216.4 15.2 copy-start.58
  240.6 55.7 %slice-start = ((f32[256,8192]{1,0:T(8,128)}), f32[256,256]{1,0:T(8,128)S(1)}, s32[]{:S(2)}) async-start(f32[256,8192]{1,0:T(8,128)} %fusion.3), calls=%async_computation.15 | async-start | bytes 524288 | tf_op jit(solution)/shard_map/slice | solution.py:138
  331.8 27.6 copy-start.24
  421.3 21.1 copy-start.60
  421.3 21.1 copy-start.65
  436.5 423.1 %copy-start = (f32[1,48,64,256]{3,2,1,0:T(8,128)}, f32[1,48,64,256]{3,2,1,0:T(8,128)S(1)}, u32[]{:S(2)}) copy-start(f32[1,48,64,256]{3,2,1,0:T(8,128)S(1)} %get-tuple-element.191) | copy-start | bytes 9437188
  536.9 222.8 %copy-start.67 = (f32[256]{0:T(256)}, f32[256]{0:T(256)S(1)}, u32[]{:S(2)}) copy-start(f32[256]{0:T(256)S(1)} %fusion.221) | copy-start | bytes 3076
  772.5 8.7 copy-start.21
  772.5 8.7 copy-start.22
  783.5 125.3 %reduce-scatter.5.cloned.1.call-start = ((), (), s32[]{:S(2)}) async-start(), calls=%async_computation.5 | async-start | bytes 655360 | tf_op jit(solution)/shard_map/reduce_scatter | solution.py:365
  808.7 137.0 %all-gather.35.cloned.1.call-start = ((), (), s32[]{:S(2)}) async-start(), calls=%async_computation.12 | async-start | bytes 7864320 | tf_op jit(solution)/shard_map/all_gather | solution.py:51
  822.0 1509.3 %all-reduce.9.cloned.1.call-start = ((), (), s32[]{:S(2)}) async-start(), calls=%async_computation.13 | async-start | bytes 202375168
  845.4 11.9 copy-start.41
  859.7 9.2 copy-start.30
  887.4 9.9 copy-start.19
  974.1 21.4 copy-start.48
  974.1 21.4 copy-start.64
  994.9 7.7 copy-start.44
  994.9 7.7 copy-start.54
  1010.6 16.8 copy-start.32
  1208.4 1574.9 %all-reduce.11.cloned.1.call-start = ((), (), s32[]{:S(2)}) async-start(), calls=%async_computation.14 | async-start | bytes 25165824 | tf_op jit(solution)/shard_map/psum | solution.py:658
  2365.0 17.4 copy-start.12
  2365.0 17.4 copy-start.46
  2365.0 17.4 copy-start.56
  2382.4 29.0 %copy-start.74 = (f32[256]{0:T(256)S(1)}, f32[256]{0:T(256)}, u32[]{:S(2)}) copy-start(f32[256]{0:T(256)} %copy-done.73) | copy-start | bytes 3076
  2382.4 29.0 %copy-start.62 = (f32[1,1,2048]{2,1,0:T(1,128)S(1)}, f32[1,1,2048]{2,1,0:T(1,128)}, u32[]{:S(2)}) copy-start(f32[1,1,2048]{2,1,0:T(1,128)} %copy-done.61) | copy-start | bytes 24580
  2382.4 29.0 %copy-start.68 = (f32[256]{0:T(256)S(1)}, f32[256]{0:T(256)}, u32[]{:S(2)}) copy-start(f32[256]{0:T(256)} %copy-done.67) | copy-start | bytes 3076
  2382.4 29.0 %copy-start.72 = (f32[256]{0:T(256)S(1)}, f32[256]{0:T(256)}, u32[]{:S(2)}) copy-start(f32[256]{0:T(256)} %copy-done.71) | copy-start | bytes 3076
  (52 other events, 206.4 us)
Sparse Core Ops, SparseCore 0:
  9.9 163.5 all-gather.22
  175.9 54.3 all-gather.18
  232.8 54.3 all-gather.20
  289.2 132.0 all-gather.26
  423.0 70.4 all-gather.28
  495.3 36.7 all-gather.24
  533.9 89.8 all-gather.32
  625.7 89.8 all-gather.30
  783.7 21.6 reduce-scatter.2
  808.8 21.6 reduce-scatter.4
  832.0 113.5 all-gather.34
  1208.5 1122.6 all-reduce.8
  2351.1 432.1 all-reduce.10
where the time goes:
time: 2820 us; the launch traced here: 2810 us
  waiting for transfers between devices  1970 us (70%)
  matrix products  338 us (12%)
  local copies, waits for them, and re-layouts  284 us (10%)
  blocking collectives  121 us (4%)
  other arithmetic  81.7 us (3%)
    unnamed x14, waiting for transfers between devices  1120 us
    psum x1, waiting for transfers between devices, per_device(): lax.psum(stacked[0].astype(jnp.bfloat16), 'ctx').astype(jnp.float32)  339 us
    all_gather x2, waiting for transfers between devices, contract(): lax.all_gather(first_weight, 'fsdp', axis=0, tiled=True)  227 us
    concatenate x1, local copies, waits for them, and re-layouts, weight_grads(): jnp.concatenate(blocks, axis=1).astype(jnp.bfloat16)  181 us
    all_gather x1, waiting for transfers between devices, contract(): lax.all_gather(second_weight, 'fsdp', axis=0, tiled=True)  84.4 us
    all_gather x2, waiting for transfers between devices, expand(): lax.all_gather(second_weight, 'fsdp', axis=0, tiled=True)  80.4 us
    dot_general x3, matrix products, within_block(): jnp.einsum('bhts,bshp->bthp', mixing, inputs, precision=EXACT_PRECISION)  57.9 us
    dot_general x7, matrix products, weight_grads(): lax.dot_general(left_rows, right_rows, (((0,), (0,)), ((), ())), preferre...  57.4 us
  transfers between devices with their start and end apart: 13, of which 10 were waited for; matrix products, arithmetic and copies ran while one was open for 12% of the time, Pallas kernels for 0%

commit v1 on v0

v1 whole, which is shorter than its diff:
```python
import math

import jax
import jax.numpy as jnp
from jax import lax
from jax.sharding import PartitionSpec as P

QUERY_HEADS = 8
KEY_VALUE_HEADS = 2
HEAD_SIZE = 128
MIXER_HEADS = 48
MIXER_HEAD_SIZE = 64
STATE_SIZE = 256
BLOCK = 256
LANES = 128

EPSILON = 1e-05
THETA = 10000.0
SCALE = 1.0 / math.sqrt(HEAD_SIZE)
BF16 = jnp.bfloat16
F32 = jnp.float32


def shift_ctx(value, hop):
    count = lax.axis_size("ctx")
    return lax.ppermute(value, "ctx", [(i, (i + hop) % count) for i in range(count)])


def swap_pair(value):
    count = lax.axis_size("ctx")
    return lax.ppermute(value, "ctx", [(i, i ^ 1) for i in range(count)])


def arrivals(value):
    return [shift_ctx(value, hop) for hop in range(1, lax.axis_size("ctx"))]


def gather_ctx(value):
    count, place = lax.axis_size("ctx"), lax.axis_index("ctx")
    rows = value.shape[0]
    parts = arrivals(value)
    out = jnp.zeros((count * rows,) + value.shape[1:], value.dtype)
    out = lax.dynamic_update_slice_in_dim(out, value, place * rows, 0)
    for hop in range(1, count):
        source = (place + count - hop) % count
        out = lax.dynamic_update_slice_in_dim(out, parts[hop - 1], source * rows, 0)
    return out


def scatter_sum_ctx(value):
    count, place = lax.axis_size("ctx"), lax.axis_index("ctx")
    rows = value.shape[0] // count
    total = lax.dynamic_slice_in_dim(value, place * rows, rows, 0)
    for hop in range(1, count):
        target = (place + hop) % count
        block = lax.dynamic_slice_in_dim(value, target * rows, rows, 0).astype(BF16)
        total = total + shift_ctx(block, hop).astype(F32)
    return total


def gather_rows(value):
    return lax.all_gather(value, "fsdp", axis=0, tiled=True)


def scatter_rows(value):
    return lax.psum_scatter(value, "fsdp", scatter_dimension=0, tiled=True)


def dot(left, right, left_dim, right_dim):
    return lax.dot_general(
        left, right, (((left_dim,), (right_dim,)), ((), ())), preferred_element_type=F32
    )


def rope(vectors, cosine, sine):
    half = vectors.shape[-1] // 2
    a, b = vectors[..., :half], vectors[..., half:]
    return jnp.concatenate([a * cosine - b * sine, b * cosine + a * sine], axis=-1)


def inverse_rms(rows):
    return lax.rsqrt(jnp.mean(rows * rows, axis=-1, keepdims=True) + EPSILON)


def rms_pull(rows, inverse, gain, grad):
    scaled = grad * gain
    return inverse * (scaled - rows * inverse * inverse * jnp.mean(rows * scaled, -1, keepdims=True))


def decay_terms(dt_raw, dt_offset, log_rate):
    step_size = jax.nn.softplus(dt_raw + dt_offset)
    level = jnp.cumsum(step_size * -jnp.exp(log_rate), axis=1)
    return (step_size, level)


def ssm(inputs, b_rows, c_rows, dt_raw, dt_offset, log_rate):
    tokens, heads, size = inputs.shape
    blocks = tokens // BLOCK
    x = inputs.reshape(blocks, BLOCK, heads, size)
    b_rows = b_rows.reshape(blocks, BLOCK, STATE_SIZE)
    c_rows = c_rows.reshape(blocks, BLOCK, STATE_SIZE)
    step_size, level = decay_terms(dt_raw.reshape(blocks, BLOCK, heads), dt_offset, log_rate)
    order = jnp.arange(BLOCK)
    causal = (order[:, None] >= order[None, :])[None, None]
    by_head = jnp.swapaxes(level, 1, 2)
    gap = jnp.where(causal, by_head[:, :, :, None] - by_head[:, :, None, :], 0.0)
    fading = jnp.where(causal, jnp.exp(gap), 0.0)
    pairing = jnp.einsum("btn,bsn->bts", c_rows, b_rows)
    mixing = fading * pairing[:, None] * jnp.swapaxes(step_size, 1, 2)[:, :, None, :]
    inside = jnp.einsum("bhts,bshp->bthp", mixing, x)
    tail = jnp.exp(level[:, -1:, :] - level) * step_size
    fresh = jnp.einsum("bshp,bsn->bhpn", tail[..., None] * x, b_rows)
    decay = jnp.exp(level[:, -1, :])
    state = jnp.zeros(fresh.shape[1:], F32)
    states = []
    for k in range(blocks):
        states.append(state)
        state = decay[k][:, None, None] * state + fresh[k]
    entered = jnp.stack(states)
    outer = jnp.exp(level)[..., None] * jnp.einsum("btn,bhpn->bthp", c_rows, entered)
    return (inside + outer).reshape(tokens, heads, size)


def attention(queries, keys, values):
    tokens = keys.shape[0]
    raw = jnp.einsum("hqd,kd->hqk", queries, keys, preferred_element_type=F32)
    order = jnp.arange(tokens)
    visible = order[:, None] >= order[None, :]
    logits = jnp.where(visible, raw * SCALE, -1e30)
    top = jnp.max(logits, axis=-1, keepdims=True)
    weights = jnp.exp(logits - top)
    total = jnp.sum(weights, axis=-1, keepdims=True)
    out = jnp.einsum("hqk,kd->hqd", weights.astype(BF16), values, preferred_element_type=F32)
    return out / total, top + jnp.log(total)


def attention_pull(queries, keys, values, out, log_total, grad_out):
    tokens = keys.shape[0]
    delta = jnp.sum(grad_out.astype(F32) * out, axis=-1, keepdims=True)
    raw = jnp.einsum("hqd,kd->hqk", queries, keys, preferred_element_type=F32)
    order = jnp.arange(tokens)
    visible = order[:, None] >= order[None, :]
    probs = jnp.exp(jnp.where(visible, raw * SCALE - log_total, -1e30))
    grad_probs = jnp.einsum("hqd,kd->hqk", grad_out, values, preferred_element_type=F32)
    grad_raw = (probs * (grad_probs - delta) * SCALE).astype(BF16)
    grad_queries = jnp.einsum("hqk,kd->hqd", grad_raw, keys, preferred_element_type=F32)
    grad_keys = jnp.einsum("hqk,hqd->kd", grad_raw, queries, preferred_element_type=F32)
    grad_values = jnp.einsum(
        "hqk,hqd->kd", probs.astype(BF16), grad_out, preferred_element_type=F32
    )
    return grad_queries, grad_keys, grad_values


def place_columns(out, block, start):
    return lax.dynamic_update_slice(out, block, (0, start))


def per_device(
    hidden_in,
    w_mix,
    w_dt,
    w_attn_out,
    w_ssm_out,
    w_gate,
    w_up,
    w_down,
    norm_gains,
    dt_bias,
    a_log,
    skip_scale,
    cotangent,
):
    w_mix, w_dt, w_attn_out, w_ssm_out = w_mix[0], w_dt[0], w_attn_out[0], w_ssm_out[0]
    w_gate, w_up, w_down = w_gate[0], w_up[0], w_down[0]
    gain_mix, gain_ffn = norm_gains[0, 0], norm_gains[0, 1]
    count, place = lax.axis_size("ctx"), lax.axis_index("ctx")
    piece, width = hidden_in.shape[1], hidden_in.shape[2]
    tokens = piece * count
    rows = w_mix.shape[0]
    hidden_units = w_gate.shape[1]
    q_heads = QUERY_HEADS // count
    group = QUERY_HEADS // KEY_VALUE_HEADS
    kv_head = (place * q_heads) // group
    heads = MIXER_HEADS // count
    q_wide, z_wide = q_heads * HEAD_SIZE, heads * MIXER_HEAD_SIZE
    key_at = QUERY_HEADS * HEAD_SIZE
    value_at = key_at + KEY_VALUE_HEADS * HEAD_SIZE
    z_at = value_at + KEY_VALUE_HEADS * HEAD_SIZE
    x_at = z_at + MIXER_HEADS * MIXER_HEAD_SIZE
    b_at = x_at + MIXER_HEADS * MIXER_HEAD_SIZE

    def columns(weight, start, size):
        return lax.dynamic_slice(weight, (0, start), (weight.shape[0], size))

    mix_own = jnp.concatenate(
        [
            columns(w_mix, place * q_wide, q_wide),
            columns(w_mix, key_at + kv_head * HEAD_SIZE, HEAD_SIZE),
            columns(w_mix, value_at + kv_head * HEAD_SIZE, HEAD_SIZE),
            columns(w_mix, z_at + place * z_wide, z_wide),
            columns(w_mix, x_at + place * z_wide, z_wide),
            w_mix[:, b_at:],
            jnp.pad(columns(w_dt, place * heads, heads), ((0, 0), (0, LANES - heads))),
            columns(w_attn_out, place * q_wide, q_wide),
            columns(w_ssm_out, place * z_wide, z_wide),
        ],
        axis=1,
    )
    mix_wide = mix_own.shape[1] - q_wide - z_wide
    half = place % 2
    half_units = hidden_units // 2
    ffn_own = jnp.concatenate(
        [columns(w, half * half_units, half_units) for w in (w_gate, w_up, w_down)], axis=1
    )
    mixer_weights = gather_rows(mix_own)
    w_in, w_out = mixer_weights[:, :mix_wide], mixer_weights[:, mix_wide:]
    ffn_weights = gather_rows(ffn_own)
    w_gate_half = ffn_weights[:, :half_units]
    w_up_half = ffn_weights[:, half_units : 2 * half_units]
    w_down_half = ffn_weights[:, 2 * half_units :]

    hidden_own = hidden_in.reshape(piece, width)
    hidden = gather_ctx(hidden_own).astype(F32)
    cot_own = cotangent.reshape(piece, width)
    cot_pair = jnp.concatenate([cot_own, swap_pair(cot_own)], axis=0)

    inverse_in = inverse_rms(hidden)
    scaled_in = hidden * inverse_in
    normed = (scaled_in * gain_mix).astype(BF16)
    mixed = dot(normed, w_in, 1, 0)
    cuts = [q_wide, HEAD_SIZE, HEAD_SIZE, z_wide, z_wide, STATE_SIZE, STATE_SIZE, LANES]
    pieces, at = [], 0
    for cut in cuts:
        pieces.append(mixed[:, at : at + cut])
        at += cut
    q_part, k_part, v_part, z_part, x_part, b_part, c_part, dt_part = pieces
    dt_part = dt_part[:, :heads]
    positions = jnp.arange(tokens, dtype=F32)
    frequency = THETA ** (-jnp.arange(HEAD_SIZE // 2, dtype=F32) / (HEAD_SIZE // 2))
    angles = positions[:, None] * frequency[None, :]
    cosine, sine = jnp.cos(angles), jnp.sin(angles)
    by_head = jnp.swapaxes(q_part.reshape(tokens, q_heads, HEAD_SIZE), 0, 1)
    queries = rope(by_head, cosine, sine).astype(BF16)
    keys = rope(k_part, cosine, sine).astype(BF16)
    values = v_part.astype(BF16)
    attended_full, log_total = attention(queries, keys, values)
    attended = jnp.swapaxes(attended_full, 0, 1).reshape(tokens, q_wide).astype(BF16)

    own_bias = lax.dynamic_slice_in_dim(dt_bias[0], place * heads, heads)
    own_rate = lax.dynamic_slice_in_dim(a_log[0], place * heads, heads)
    own_skip = lax.dynamic_slice_in_dim(skip_scale[0], place * heads, heads)
    x_heads = x_part.reshape(tokens, heads, MIXER_HEAD_SIZE)
    z_heads = z_part.reshape(tokens, heads, MIXER_HEAD_SIZE)
    ssm_y, ssm_pull = jax.vjp(ssm, x_heads, b_part, c_part, dt_part, own_bias, own_rate)
    full_y = ssm_y + own_skip[:, None] * x_heads
    gated = (full_y * jax.nn.silu(z_heads)).reshape(tokens, z_wide).astype(BF16)
    branch_in = jnp.concatenate([attended, gated], axis=1)
    branch = scatter_sum_ctx(dot(branch_in, w_out, 1, 1))
    middle = hidden_own.astype(F32) + branch

    inverse_ffn = inverse_rms(middle)
    normed_ffn = (middle * inverse_ffn * gain_ffn).astype(BF16)
    normed_pair = jnp.concatenate([normed_ffn, swap_pair(normed_ffn)], axis=0)
    gate = dot(normed_pair, w_gate_half, 1, 0)
    up = dot(normed_pair, w_up_half, 1, 0)
    sigmoid = jax.nn.sigmoid(gate)
    silu = gate * sigmoid
    activated = (silu * up).astype(BF16)
    grad_act = dot(cot_pair, w_down_half, 1, 0)
    grad_gate = (grad_act * up * (sigmoid * (1.0 + gate * (1.0 - sigmoid)))).astype(BF16)
    grad_up = (grad_act * silu).astype(BF16)
    grad_normed_pair = dot(grad_gate, w_gate_half, 1, 1) + dot(grad_up, w_up_half, 1, 1)
    grad_normed_ffn = grad_normed_pair[:piece] + swap_pair(
        grad_normed_pair[piece:].astype(BF16)
    ).astype(F32)
    out_pair = dot(activated, w_down_half, 1, 1)
    ffn_out = out_pair[:piece] + swap_pair(out_pair[piece:].astype(BF16)).astype(F32)
    hidden_out = (middle + ffn_out).astype(BF16)
    grad_w_ffn = scatter_rows(
        jnp.concatenate(
            [
                dot(normed_pair, grad_gate, 0, 0),
                dot(normed_pair, grad_up, 0, 0),
                dot(cot_pair, activated, 0, 0),
            ],
            axis=1,
        ).astype(BF16)
    )

    grad_middle = cot_own.astype(F32) + rms_pull(middle, inverse_ffn, gain_ffn, grad_normed_ffn)
    grad_gain_ffn = jnp.sum(grad_normed_ffn * middle * inverse_ffn, axis=0)
    grad_branch = gather_ctx(grad_middle.astype(BF16))
    grad_joint = dot(grad_branch, w_out, 1, 0)
    grad_attended = jnp.swapaxes(
        grad_joint[:, :q_wide].astype(BF16).reshape(tokens, q_heads, HEAD_SIZE), 0, 1
    )
    grad_w_out = scatter_rows(dot(grad_branch, branch_in, 0, 0).astype(BF16))

    grad_queries, grad_keys, grad_values = attention_pull(
        queries, keys, values, attended_full, log_total, grad_attended
    )
    grad_q = jnp.swapaxes(rope(grad_queries, cosine, -sine), 0, 1).reshape(tokens, q_wide)
    grad_k = rope(grad_keys, cosine, -sine)
    grad_gated = grad_joint[:, q_wide:].reshape(tokens, heads, MIXER_HEAD_SIZE)
    z_sigmoid = jax.nn.sigmoid(z_heads)
    grad_y = grad_gated * z_heads * z_sigmoid
    grad_z = grad_gated * full_y * (z_sigmoid * (1.0 + z_heads * (1.0 - z_sigmoid)))
    grad_skip = jnp.sum(grad_y * x_heads, axis=(0, 2))
    grad_x, grad_b, grad_c, grad_dt, grad_bias, grad_rate = ssm_pull(grad_y)
    grad_x = grad_x + own_skip[:, None] * grad_y
    grad_mixed = jnp.concatenate(
        [
            grad_q,
            grad_k,
            grad_values,
            grad_z.reshape(tokens, z_wide),
            grad_x.reshape(tokens, z_wide),
            grad_b,
            grad_c,
            jnp.pad(grad_dt, ((0, 0), (0, LANES - heads))),
        ],
        axis=1,
    ).astype(BF16)
    grad_w_in = scatter_rows(dot(normed, grad_mixed, 0, 0).astype(BF16))
    grad_normed_part = dot(grad_mixed, w_in, 1, 1)
    grad_gain_mix = jnp.sum(grad_normed_part * scaled_in, axis=0)
    grad_normed = scatter_sum_ctx(grad_normed_part)
    hidden_f32 = hidden_own.astype(F32)
    grad_hidden = grad_middle + rms_pull(
        hidden_f32, inverse_rms(hidden_f32), gain_mix, grad_normed
    )

    head_part = jnp.zeros((3, MIXER_HEADS), F32)
    head_part = lax.dynamic_update_slice(
        head_part, jnp.stack([grad_bias, grad_rate, grad_skip]), (0, place * heads)
    )
    gain_sums, head_sums = lax.psum(
        (jnp.stack([grad_gain_mix, grad_gain_ffn]), head_part), ("fsdp", "ctx")
    )

    mixer_grad = jnp.concatenate([grad_w_in, grad_w_out], axis=1)
    blocks = [mixer_grad] + arrivals(mixer_grad)
    out_mix = jnp.zeros((rows, b_at), F32)
    out_attn = jnp.zeros((rows, QUERY_HEADS * HEAD_SIZE), F32)
    out_ssm = jnp.zeros((rows, MIXER_HEADS * MIXER_HEAD_SIZE), F32)
    out_dt = jnp.zeros((rows, MIXER_HEADS), F32)
    tail = jnp.zeros((rows, 2 * STATE_SIZE), F32)
    key_value = jnp.zeros((rows, 2 * KEY_VALUE_HEADS * HEAD_SIZE), F32)
    bounds = [0]
    for cut in cuts + [q_wide, z_wide]:
        bounds.append(bounds[-1] + cut)
    for hop in range(count):
        source = (place + count - hop) % count
        wide = blocks[hop].astype(F32)
        part = [wide[:, bounds[i] : bounds[i + 1]] for i in range(len(bounds) - 1)]
        out_mix = place_columns(out_mix, part[0], source * q_wide)
        out_mix = place_columns(out_mix, part[3], z_at + source * z_wide)
        out_mix = place_columns(out_mix, part[4], x_at + source * z_wide)
        out_dt = place_columns(out_dt, part[7][:, :heads], source * heads)
        out_attn = place_columns(out_attn, part[8], source * q_wide)
        out_ssm = place_columns(out_ssm, part[9], source * z_wide)
        tail = tail + jnp.concatenate([part[5], part[6]], axis=1)
        which = (source * q_heads) // group
        spread = jnp.concatenate(
            [jnp.where(which == h, part[1], 0.0) for h in range(KEY_VALUE_HEADS)]
            + [jnp.where(which == h, part[2], 0.0) for h in range(KEY_VALUE_HEADS)],
            axis=1,
        )
        key_value = key_value + spread
    out_mix = lax.dynamic_update_slice(out_mix, key_value, (0, key_at))
    out_mix = jnp.concatenate([out_mix, tail], axis=1)

    members = count // 2
    member = place // 2
    chunk = rows // members
    total = lax.dynamic_slice_in_dim(grad_w_ffn, member * chunk, chunk, 0).astype(F32)
    for hop in range(1, members):
        target = (member + hop) % members
        block = lax.dynamic_slice_in_dim(grad_w_ffn, target * chunk, chunk, 0)
        total = total + shift_ctx(block, 2 * hop).astype(F32)
    total = total.astype(BF16)
    blocks = [total] + arrivals(total)
    outs = [jnp.zeros((rows, hidden_units), F32) for _ in range(3)]
    for hop in range(count):
        source = (place + count - hop) % count
        wide = blocks[hop].astype(F32)
        for i in range(3):
            outs[i] = lax.dynamic_update_slice(
                outs[i],
                wide[:, i * half_units : (i + 1) * half_units],
                ((source // 2) * chunk, (source % 2) * half_units),
            )
    return (
        hidden_out.reshape(hidden_in.shape),
        grad_hidden.reshape(hidden_in.shape),
        out_mix[None],
        out_dt[None],
        out_attn[None],
        out_ssm[None],
        outs[0][None],
        outs[1][None],
        outs[2][None],
        gain_sums[None],
        head_sums[0][None],
        head_sums[1][None],
        head_sums[2][None],
    )


def solution(mesh):
    split, rows = P("fsdp", "ctx", None), P(None, "fsdp", None)
    return jax.shard_map(
        per_device,
        mesh=mesh,
        in_specs=(split,) + (rows,) * 7 + (P(),) * 4 + (split,),
        out_specs=(split, split) + (rows,) * 7 + (P(),) * 4,
        check_vma=False,
    )
```

time: 2820 us -> 1270 us (0.45)
  the two profiles are of different devices: /device:TPU:0 before, /device:TPU:24 now
where the time goes in v1:
time: 1270 us; the launch traced here: 1260 us
  waiting for transfers between devices  554 us (44%)
  matrix products  207 us (16%)
  local copies, waits for them, and re-layouts  178 us (14%)
  other arithmetic  113 us (9%)
  blocking collectives  109 us (9%)
  starting transfers between devices  83 us (7%)
  between operations  16 us (1%)
    ppermute x19, waiting for transfers between devices, shift_ctx(): lax.ppermute(value, 'ctx', [(i, (i + hop) % count) for i in range(count)])  505 us
    dot_general x15, matrix products, dot(): lax.dot_general(left, right, (((left_dim,), (right_dim,)), ((), ())), pre...  158 us
    psum x1, blocking collectives, per_device(): lax.psum((jnp.stack([grad_gain_mix, grad_gain_ffn]), head_part), ('fsdp',...  109 us
    ppermute x19, starting transfers between devices, shift_ctx(): lax.ppermute(value, 'ctx', [(i, (i + hop) % count) for i in range(count)])  58 us
    ppermute x4, waiting for transfers between devices, swap_pair(): return lax.ppermute(value, 'ctx', [(i, i ^ 1) for i in range(count)])  48.9 us
    unnamed x264, local copies, waits for them, and re-layouts  46 us
    another operation x12, other arithmetic  25.6 us
  transfers between devices with their start and end apart: 28, of which 14 were waited for; matrix products, arithmetic and copies ran while one was open for 21% of the time, Pallas kernels for 0%

profile of v1, /device:TPU:24, one launch (start us, length us, event | category | flops | bytes accessed | tf_op | source)
XLA Modules:
  0.0 1260.4 jit_solution(12970010764111664722)
XLA Ops:
  33.6 17.6 %collective-permute-done = bf16[256,2048]{1,0:T(8,128)(2,1)} collective-permute-done((bf16[256,2048]{1,0:T(8,128)(2,1)S(1)}, bf16[256,2048]{1,0:T(8,128)(2,1)}, u32[]{:S(2)}, u32[]{:S(2)}) %collective-permute-start) | collective-permute-done | bytes 1048608 | tf_op jit(solution)/shard_map/ppermute | solution.py:26
  53.5 64.5 %collective-permute-done.1 = bf16[256,2048]{1,0:T(8,128)(2,1)S(1)} collective-permute-done((bf16[256,2048]{1,0:T(8,128)(2,1)S(1)}, bf16[256,2048]{1,0:T(8,128)(2,1)S(1)}, u32[]{:S(2)}, u32[]{:S(2)}) %collective-permute-start.1) | collective-permute-done | bytes 1048608 | tf_op jit(solution)/shard_map/ppermute | solution.py:26
  120.1 3.8 fusion.15
  124.0 18.8 %fusion.11 = f32[1024,2688]{1,0:T(8,128)} fusion(bf16[2048,3712]{1,0:T(8,128)(2,1)} %all-gather.3.cloned.1.call-done, bf16[1024,2048]{1,0:T(8,128)(2,1)} %constant_dynamic-update-slice_fusion.18, f32[2048]{0:T(1024)S(1)} %bitcast.352, f32[1024]{0:T(1024)S(1)} %add_rsqrt_fusion), kind=kOutput, calls=%fused_computation.17 | convolution fusion | flops 11282677760 | bytes 26226688 | tf_op jit(solution)/shard_map/dot_general | solution.py:70
  164.3 4.1 bitcast_add_fusion.1
  177.4 3.9 subtract_convert_fusion.3
  187.7 4.2 fusion.113
  194.0 3.8 multiply_convert_fusion.5
  197.8 7.0 fusion.54
  209.8 23.6 %collective-permute-done.5 = bf16[256,2048]{1,0:T(8,128)(2,1)S(1)} collective-permute-done((bf16[256,2048]{1,0:T(8,128)(2,1)S(1)}, bf16[256,2048]{1,0:T(8,128)(2,1)S(1)}, u32[]{:S(2)}, u32[]{:S(2)}) %collective-permute-start.5) | collective-permute-done | bytes 1048608 | tf_op jit(solution)/shard_map/ppermute | solution.py:26
  233.4 43.0 %collective-permute-done.4 = bf16[256,2048]{1,0:T(8,128)(2,1)S(1)} collective-permute-done((bf16[256,2048]{1,0:T(8,128)(2,1)S(1)}, bf16[256,2048]{1,0:T(8,128)(2,1)S(1)}, u32[]{:S(2)}, u32[]{:S(2)}) %collective-permute-start.4) | collective-permute-done | bytes 1048608 | tf_op jit(solution)/shard_map/ppermute | solution.py:26
  278.6 22.0 %collective-permute-start.6 = (bf16[256,2048]{1,0:T(8,128)(2,1)}, bf16[256,2048]{1,0:T(8,128)(2,1)}, u32[]{:S(2)}, u32[]{:S(2)}) collective-permute-start(bf16[256,2048]{1,0:T(8,128)(2,1)} %multiply_convert_fusion.6), channel_id=1, source_target_pairs={{0,1},{1,0},{2,3},{3,2},{4,5},{5,4},{6,7},{7,6},{8,9},{9,8},{10,11... | collective-permute-start | bytes 3145736 | tf_op jit(solution)/shard_map/ppermute | solution.py:31
  300.6 10.5 fusion.16
  311.1 12.3 collective-permute-done.6
  323.4 8.1 fusion.22
  331.5 10.3 multiply_convert_fusion.2
  341.9 9.1 fusion.20
  351.0 7.0 fusion.56
  360.0 7.1 fusion.18
  367.6 16.7 %collective-permute-done.9 = bf16[256,2048]{1,0:T(8,128)(2,1)S(1)} collective-permute-done((bf16[256,2048]{1,0:T(8,128)(2,1)S(1)}, bf16[256,2048]{1,0:T(8,128)(2,1)S(1)}, u32[]{:S(2)}, u32[]{:S(2)}) %collective-permute-start.9) | collective-permute-done | bytes 1048608 | tf_op jit(solution)/shard_map/ppermute | solution.py:31
  384.3 19.9 %collective-permute-done.7 = bf16[256,2048]{1,0:T(8,128)(2,1)S(1)} collective-permute-done((bf16[256,2048]{1,0:T(8,128)(2,1)S(1)}, bf16[256,2048]{1,0:T(8,128)(2,1)S(1)}, u32[]{:S(2)}, u32[]{:S(2)}) %collective-permute-start.7) | collective-permute-done | bytes 1048608 | tf_op jit(solution)/shard_map/ppermute | solution.py:31
  412.9 22.1 %collective-permute-done.10 = bf16[256,2048]{1,0:T(8,128)(2,1)S(1)} collective-permute-done((bf16[256,2048]{1,0:T(8,128)(2,1)S(1)}, bf16[256,2048]{1,0:T(8,128)(2,1)S(1)}, u32[]{:S(2)}, u32[]{:S(2)}) %collective-permute-start.10) | collective-permute-done | bytes 1048608 | tf_op jit(solution)/shard_map/ppermute | solution.py:26
  435.1 65.4 %collective-permute-done.11 = bf16[256,2048]{1,0:T(8,128)(2,1)S(1)} collective-permute-done((bf16[256,2048]{1,0:T(8,128)(2,1)S(1)}, bf16[256,2048]{1,0:T(8,128)(2,1)S(1)}, u32[]{:S(2)}, u32[]{:S(2)}) %collective-permute-start.11) | collective-permute-done | bytes 1048608 | tf_op jit(solution)/shard_map/ppermute | solution.py:26
  500.9 8.2 fusion.52
  509.4 4.5 multiply_convert_fusion
  523.9 7.0 multiply_reduce_fusion.2
  553.3 12.1 fusion.29
  565.4 4.5 bitcast_add_fusion
  584.9 9.9 reduce-window.16
  599.1 8.7 concatenate.73
  607.8 18.5 %convolution_convert_fusion = bf16[2048,2688]{1,0:T(8,128)(2,1)} fusion(bf16[1024,2688]{1,0:T(8,128)(2,1)} %concatenate.73, bf16[1024,2048]{1,0:T(8,128)(2,1)} %constant_dynamic-update-slice_fusion.18, f32[2048]{0:T(1024)S(1)} %bitcast.353, f32[1024]{0:T(1024)S(1)} %copy-done.104), kind=kOutput, calls=%fused_computation.10 | convolution fusion | flops 11288182784 | bytes 20721664 | tf_op jit(solution)/shard_map/dot_general | solution.py:70
  627.9 8.3 convolution_convert_fusion.4
  637.7 10.8 convolution_convert_fusion.1
  648.5 8.8 convolution_convert_fusion.2
  657.3 8.5 convolution_convert_fusion.3
  665.8 18.6 %pad_maximum_fusion = bf16[2048,6144]{0,1:T(8,128)(2,1)} fusion(bf16[2048,2048]{0,1:T(8,128)(2,1)} %convolution_convert_fusion.1, bf16[2048,2048]{0,1:T(8,128)(2,1)} %convolution_convert_fusion.2, bf16[2048,2048]{0,1:T(8,128)(2,1)} %convolution_convert_fusion.3), kind=kLoop, calls=%fused_computation | loop fusion | flops 75497472 | bytes 50331648 | tf_op jit(solution)/shard_map/concatenate | solution.py:280
  684.5 17.3 %fusion.14 = (f32[2048]{0:T(1024)S(1)}, f32[1024,2048]{1,0:T(8,128)S(1)}) fusion(bf16[1024,2048]{1,0:T(8,128)(2,1)} %constant_dynamic-update-slice_fusion.18, f32[1024]{0:T(1024)S(1)} %copy-done.104, bf16[1024,2688]{1,0:T(8,128)(2,1)} %concatenate.73, bf16[2048,3712]{1,0:T(8,128)(2,1)} %all-gather.3.cloned.1.call-done), kind=kOutput, calls=%fused_computation.20 | convolution fusion | flops 11282675712 | bytes 29110272 | tf_op jit(solution)/shard_map/dot_general | solution.py:70
  711.4 108.9 %all-reduce.10 = (f32[1,2,2048]{2,1,0:T(2,128)}, f32[3,48]{1,0:T(4,128)S(1)}) all-reduce(f32[1,2,2048]{2,1,0:T(2,128)S(1)} %maximum_bitcast_fusion.5, f32[3,48]{1,0:T(4,128)S(1)} %dynamic_update_slice.207), channel_id=1, replica_groups=mesh['fsdp'=8,'ctx'=4] {'fsdp','ctx'}, use_global_device_ids=true, to_apply=%region_27.28 | all-reduce | flops 4240 | bytes 33920 | tf_op jit(solution)/shard_map/psum | solution.py:337
  820.9 3.9 fusion.74
  833.6 5.5 fusion.80
  841.5 4.1 broadcast_in_dim.199
  851.5 24.3 %collective-permute-done.18 = bf16[256,3712]{1,0:T(8,128)(2,1)} collective-permute-done((bf16[256,3712]{1,0:T(8,128)(2,1)}, bf16[256,3712]{1,0:T(8,128)(2,1)}, u32[]{:S(2)}, u32[]{:S(2)}) %collective-permute-start.18) | collective-permute-done | bytes 1900576 | tf_op jit(solution)/shard_map/ppermute | solution.py:26
  877.7 78.6 %collective-permute-done.17 = bf16[256,3712]{1,0:T(8,128)(2,1)} collective-permute-done((bf16[256,3712]{1,0:T(8,128)(2,1)}, bf16[256,3712]{1,0:T(8,128)(2,1)}, u32[]{:S(2)}, u32[]{:S(2)}) %collective-permute-start.17) | collective-permute-done | bytes 1900576 | tf_op jit(solution)/shard_map/ppermute | solution.py:26
  974.4 36.5 %collective-permute-start.19 = (bf16[128,6144]{0,1:T(8,128)(2,1)S(1)}, bf16[128,6144]{0,1:T(8,128)(2,1)}, u32[]{:S(2)}, u32[]{:S(2)}) collective-permute-start(bf16[128,6144]{0,1:T(8,128)(2,1)S(1)} %constant_dynamic-slice_fusion), channel_id=1, source_target_pairs={{0,2},{1,3},{2,0},{3,1},{4,6},{5,7},{6,4},{7,5},{8,10},{9,11},{10,... | collective-permute-start | bytes 4718600 | tf_op jit(solution)/shard_map/ppermute | solution.py:26
  1015.7 7.5 maximum_bitcast_fusion
  1023.2 55.6 %collective-permute-done.19 = bf16[128,6144]{0,1:T(8,128)(2,1)} collective-permute-done((bf16[128,6144]{0,1:T(8,128)(2,1)S(1)}, bf16[128,6144]{0,1:T(8,128)(2,1)}, u32[]{:S(2)}, u32[]{:S(2)}) %collective-permute-start.19) | collective-permute-done | bytes 1572896 | tf_op jit(solution)/shard_map/ppermute | solution.py:26
  1106.5 14.0 %collective-permute-done.20 = bf16[128,6144]{0,1:T(8,128)(2,1)} collective-permute-done((bf16[128,6144]{0,1:T(8,128)(2,1)}, bf16[128,6144]{0,1:T(8,128)(2,1)}, u32[]{:S(2)}, u32[]{:S(2)}) %collective-permute-start.20) | collective-permute-done | bytes 1572896 | tf_op jit(solution)/shard_map/ppermute | solution.py:26
  1123.6 95.9 %collective-permute-done.21 = bf16[128,6144]{0,1:T(8,128)(2,1)} collective-permute-done((bf16[128,6144]{0,1:T(8,128)(2,1)}, bf16[128,6144]{0,1:T(8,128)(2,1)}, u32[]{:S(2)}, u32[]{:S(2)}) %collective-permute-start.21) | collective-permute-done | bytes 1572896 | tf_op jit(solution)/shard_map/ppermute | solution.py:26
  (509 shorter events, 258.5 us)
Async XLA Ops:
  7.2 14.9 %copy-start = (bf16[1,256,4096]{2,1,0:T(8,128)(2,1)S(1)}, bf16[1,256,4096]{2,1,0:T(8,128)(2,1)}, u32[]{:S(2)}) copy-start(bf16[1,256,4096]{2,1,0:T(8,128)(2,1)} %param.18) | copy-start | bytes 6291460
  7.2 116.7 %all-gather.3.cloned.1.call-start = ((), (), s32[]{:S(2)}) async-start(), calls=%async_computation.3 | async-start | bytes 17104896 | tf_op jit(solution)/shard_map/all_gather | solution.py:62
  22.0 278.7 %all-gather.5.cloned.1.call-start = ((), (), s32[]{:S(2)}) async-start(), calls=%async_computation.4 | async-start | bytes 28311552 | tf_op jit(solution)/shard_map/all_gather | solution.py:62
  25.7 799.1 %reduce-scatter.4.cloned.1.call-start = ((), (), s32[]{:S(2)}) async-start(), calls=%async_computation.5 | async-start | bytes 12386304 | tf_op jit(solution)/shard_map/reduce_scatter | solution.py:66
  25.8 25.4 %collective-permute-start = (bf16[256,2048]{1,0:T(8,128)(2,1)S(1)}, bf16[256,2048]{1,0:T(8,128)(2,1)}, u32[]{:S(2)}, u32[]{:S(2)}) collective-permute-start(bf16[256,2048]{1,0:T(8,128)(2,1)S(1)} %bitcast.318), channel_id=1, source_target_pairs={{0,1},{1,2},{2,3},{3,0},{4,5},{5,6},{6,7},{7,4},{8,9},{9,10},{10,1... | collective-permute-start | bytes 3145736 | tf_op jit(solution)/shard_map/ppermute | solution.py:26
  25.8 92.2 %collective-permute-start.1 = (bf16[256,2048]{1,0:T(8,128)(2,1)S(1)}, bf16[256,2048]{1,0:T(8,128)(2,1)S(1)}, u32[]{:S(2)}, u32[]{:S(2)}) collective-permute-start(bf16[256,2048]{1,0:T(8,128)(2,1)S(1)} %bitcast.319), channel_id=1, source_target_pairs={{0,2},{1,3},{2,0},{3,1},{4,6},{5,7},{6,4},{7,5},{8,10},{9,11},{10,... | collective-permute-start | bytes 3145736 | tf_op jit(solution)/shard_map/ppermute | solution.py:26
  27.7 91.3 %collective-permute-start.2 = (bf16[256,2048]{1,0:T(8,128)(2,1)S(1)}, bf16[256,2048]{1,0:T(8,128)(2,1)S(1)}, u32[]{:S(2)}, u32[]{:S(2)}) collective-permute-start(bf16[256,2048]{1,0:T(8,128)(2,1)S(1)} %bitcast.320), channel_id=1, source_target_pairs={{0,3},{1,0},{2,1},{3,2},{4,7},{5,4},{6,5},{7,6},{8,11},{9,8},{10,9... | collective-permute-start | bytes 3145736 | tf_op jit(solution)/shard_map/ppermute | solution.py:26
  28.2 95.7 %copy-start.84 = (f32[1,1,2048]{2,1,0:T(1,128)}, f32[1,1,2048]{2,1,0:T(1,128)S(1)}, u32[]{:S(2)}) copy-start(f32[1,1,2048]{2,1,0:T(1,128)S(1)} %get-tuple-element.99) | copy-start | bytes 24580
  28.3 129.4 %copy-start.93 = (f32[12]{0:T(128)}, f32[12]{0:T(128)S(1)}, u32[]{:S(2)}) copy-start(f32[12]{0:T(128)S(1)} %get-tuple-element.117) | copy-start | bytes 148
  28.3 134.0 %copy-start.89 = (pred[256,256]{1,0:T(8,128)(4,1)}, pred[256,256]{1,0:T(8,128)(4,1)S(1)}, u32[]{:S(2)}) copy-start(pred[256,256]{1,0:T(8,128)(4,1)S(1)} %iota_compare_fusion.1) | copy-start | bytes 196612
  28.4 149.0 %copy-start.109 = (f32[64]{0:T(128)}, f32[64]{0:T(128)S(1)}, u32[]{:S(2)}) copy-start(f32[64]{0:T(128)S(1)} %multiply_power_fusion) | copy-start | bytes 772
  29.7 124.4 %copy-start.105 = (f32[12]{0:T(128)}, f32[12]{0:T(128)S(1)}, u32[]{:S(2)}) copy-start(f32[12]{0:T(128)S(1)} %negate_bitcast_fusion) | copy-start | bytes 148
  29.9 131.2 %copy-start.116 = (bf16[4]{0:T(256)(128)(2,1)}, bf16[4]{0:T(256)(128)(2,1)S(1)}, u32[]{:S(2)}) copy-start(bf16[4]{0:T(256)(128)(2,1)S(1)} %pad.80.clone) | copy-start | bytes 28
  123.9 18.9 %copy-start.103 = (f32[1024]{0:T(1024)}, f32[1024]{0:T(1024)S(1)}, u32[]{:S(2)}) copy-start(f32[1024]{0:T(1024)S(1)} %add_rsqrt_fusion) | copy-start | bytes 12292
  175.3 18.8 %copy-start.6 = (f32[1024,768]{1,0:T(8,128)}, f32[1024,768]{1,0:T(8,128)S(1)}, u32[]{:S(2)}) copy-start(f32[1024,768]{1,0:T(8,128)S(1)} %copy.308) | copy-start | bytes 9437188
  204.8 71.6 %copy-start.10 = (bf16[1,256,2048]{2,1,0:T(8,128)(2,1)S(1)}, bf16[1,256,2048]{2,1,0:T(8,128)(2,1)}, u32[]{:S(2)}) copy-start(bf16[1,256,2048]{2,1,0:T(8,128)(2,1)} %param.13) | copy-start | bytes 3145732
  205.3 28.0 %collective-permute-start.5 = (bf16[256,2048]{1,0:T(8,128)(2,1)S(1)}, bf16[256,2048]{1,0:T(8,128)(2,1)S(1)}, u32[]{:S(2)}, u32[]{:S(2)}) collective-permute-start(bf16[256,2048]{1,0:T(8,128)(2,1)S(1)} %get-tuple-element.56), channel_id=1, source_target_pairs={{0,3},{1,0},{2,1},{3,2},{4,7},{5,4},{6,5},{7,6},{8,11},{9,8},{10,9... | collective-permute-start | bytes 3145736 | tf_op jit(solution)/shard_map/ppermute | solution.py:26
  205.4 71.0 %collective-permute-start.4 = (bf16[256,2048]{1,0:T(8,128)(2,1)S(1)}, bf16[256,2048]{1,0:T(8,128)(2,1)S(1)}, u32[]{:S(2)}, u32[]{:S(2)}) collective-permute-start(bf16[256,2048]{1,0:T(8,128)(2,1)S(1)} %get-tuple-element.57), channel_id=1, source_target_pairs={{0,2},{1,3},{2,0},{3,1},{4,6},{5,7},{6,4},{7,5},{8,10},{9,11},{10,... | collective-permute-start | bytes 3145736 | tf_op jit(solution)/shard_map/ppermute | solution.py:26
  205.9 70.6 %collective-permute-start.3 = (bf16[256,2048]{1,0:T(8,128)(2,1)S(1)}, bf16[256,2048]{1,0:T(8,128)(2,1)S(1)}, u32[]{:S(2)}, u32[]{:S(2)}) collective-permute-start(bf16[256,2048]{1,0:T(8,128)(2,1)S(1)} %get-tuple-element.55), channel_id=1, source_target_pairs={{0,1},{1,2},{2,3},{3,0},{4,5},{5,6},{6,7},{7,4},{8,9},{9,10},{10,1... | collective-permute-start | bytes 3145736 | tf_op jit(solution)/shard_map/ppermute | solution.py:26
  209.2 91.4 %collective-permute-start.8 = (bf16[256,2048]{1,0:T(8,128)(2,1)S(1)}, bf16[256,2048]{1,0:T(8,128)(2,1)}, u32[]{:S(2)}, u32[]{:S(2)}) collective-permute-start(bf16[256,2048]{1,0:T(8,128)(2,1)S(1)} %bitcast.339), channel_id=1, source_target_pairs={{0,1},{1,0},{2,3},{3,2},{4,5},{5,4},{6,7},{7,6},{8,9},{9,8},{10,11... | collective-permute-start | bytes 3145736 | tf_op jit(solution)/shard_map/ppermute | solution.py:31
  278.6 44.8 %collective-permute-start.6 = (bf16[256,2048]{1,0:T(8,128)(2,1)}, bf16[256,2048]{1,0:T(8,128)(2,1)}, u32[]{:S(2)}, u32[]{:S(2)}) collective-permute-start(bf16[256,2048]{1,0:T(8,128)(2,1)} %multiply_convert_fusion.6), channel_id=1, source_target_pairs={{0,1},{1,0},{2,3},{3,2},{4,5},{5,4},{6,7},{7,6},{8,9},{9,8},{10,11... | collective-permute-start | bytes 3145736 | tf_op jit(solution)/shard_map/ppermute | solution.py:31
  300.6 22.8 %copy-start.115 = (bf16[2048,6144]{1,0:T(8,128)(2,1)S(1)}, bf16[2048,6144]{1,0:T(8,128)(2,1)}, u32[]{:S(2)}) copy-start(bf16[2048,6144]{1,0:T(8,128)(2,1)} %all-gather.5.cloned.1.call-done) | copy-start | bytes 75497472
  341.9 18.1 %copy-start.122 = (bf16[512,2048]{1,0:T(8,128)(2,1)}, bf16[512,2048]{1,0:T(8,128)(2,1)S(1)}, u32[]{:S(2)}) copy-start(bf16[512,2048]{1,0:T(8,128)(2,1)S(1)} %get-tuple-element.54) | copy-start | bytes 6291460
  358.2 26.2 %collective-permute-start.9 = (bf16[256,2048]{1,0:T(8,128)(2,1)S(1)}, bf16[256,2048]{1,0:T(8,128)(2,1)S(1)}, u32[]{:S(2)}, u32[]{:S(2)}) collective-permute-start(bf16[256,2048]{1,0:T(8,128)(2,1)S(1)} %slice.603), channel_id=1, source_target_pairs={{0,1},{1,0},{2,3},{3,2},{4,5},{5,4},{6,7},{7,6},{8,9},{9,8},{10,11... | collective-permute-start | bytes 3145736 | tf_op jit(solution)/shard_map/ppermute | solution.py:31
  367.3 37.0 %collective-permute-start.7 = (bf16[256,2048]{1,0:T(8,128)(2,1)S(1)}, bf16[256,2048]{1,0:T(8,128)(2,1)S(1)}, u32[]{:S(2)}, u32[]{:S(2)}) collective-permute-start(bf16[256,2048]{1,0:T(8,128)(2,1)S(1)} %slice.604), channel_id=1, source_target_pairs={{0,1},{1,0},{2,3},{3,2},{4,5},{5,4},{6,7},{7,6},{8,9},{9,8},{10,11... | collective-permute-start | bytes 3145736 | tf_op jit(solution)/shard_map/ppermute | solution.py:31
  409.9 25.1 %collective-permute-start.10 = (bf16[256,2048]{1,0:T(8,128)(2,1)S(1)}, bf16[256,2048]{1,0:T(8,128)(2,1)S(1)}, u32[]{:S(2)}, u32[]{:S(2)}) collective-permute-start(bf16[256,2048]{1,0:T(8,128)(2,1)S(1)} %get-tuple-element.37), channel_id=1, source_target_pairs={{0,1},{1,2},{2,3},{3,0},{4,5},{5,6},{6,7},{7,4},{8,9},{9,10},{10,1... | collective-permute-start | bytes 3145736 | tf_op jit(solution)/shard_map/ppermute | solution.py:26
  411.4 89.2 %collective-permute-start.11 = (bf16[256,2048]{1,0:T(8,128)(2,1)S(1)}, bf16[256,2048]{1,0:T(8,128)(2,1)S(1)}, u32[]{:S(2)}, u32[]{:S(2)}) collective-permute-start(bf16[256,2048]{1,0:T(8,128)(2,1)S(1)} %get-tuple-element.37), channel_id=1, source_target_pairs={{0,2},{1,3},{2,0},{3,1},{4,6},{5,7},{6,4},{7,5},{8,10},{9,11},{10,... | collective-permute-start | bytes 3145736 | tf_op jit(solution)/shard_map/ppermute | solution.py:26
  412.9 87.9 %collective-permute-start.12 = (bf16[256,2048]{1,0:T(8,128)(2,1)S(1)}, bf16[256,2048]{1,0:T(8,128)(2,1)S(1)}, u32[]{:S(2)}, u32[]{:S(2)}) collective-permute-start(bf16[256,2048]{1,0:T(8,128)(2,1)S(1)} %get-tuple-element.37), channel_id=1, source_target_pairs={{0,3},{1,0},{2,1},{3,2},{4,7},{5,4},{6,5},{7,6},{8,11},{9,8},{10,9... | collective-permute-start | bytes 3145736 | tf_op jit(solution)/shard_map/ppermute | solution.py:26
  581.7 13.5 %copy-start.106 = (f32[12]{0:T(128)S(1)}, f32[12]{0:T(128)}, u32[]{:S(2)}) copy-start(f32[12]{0:T(128)} %copy-done.105) | copy-start | bytes 148
  581.7 15.4 %copy-start.22 = (f32[2,1024,128]{2,1,0:T(8,128)S(1)}, f32[2,1024,128]{2,1,0:T(8,128)}, u32[]{:S(2)}) copy-start(f32[2,1024,128]{2,1,0:T(8,128)} %fusion.143) | copy-start | bytes 3145732
  581.7 15.4 %copy-start.30 = (f32[1024,64]{1,0:T(8,128)S(1)}, f32[1024,64]{1,0:T(8,128)}, u32[]{:S(2)}) copy-start(f32[1024,64]{1,0:T(8,128)} %copy-done.29) | copy-start | bytes 786436
  584.9 14.2 %copy-start.26 = (bf16[1024,768]{1,0:T(8,128)(2,1)S(1)}, bf16[1024,768]{1,0:T(8,128)(2,1)}, u32[]{:S(2)}) copy-start(bf16[1024,768]{1,0:T(8,128)(2,1)} %add_convert_fusion.1) | copy-start | bytes 4718596
  626.4 201.1 %reduce-scatter.6.cloned.1.call-start = ((), (), s32[]{:S(2)}) async-start(), calls=%async_computation.6 | async-start | bytes 4718592 | tf_op jit(solution)/shard_map/reduce_scatter | solution.py:66
  636.2 336.6 %reduce-scatter.8.cloned.1.call-start = ((), (), s32[]{:S(2)}) async-start(), calls=%async_computation.7 | async-start | bytes 28311552 | tf_op jit(solution)/shard_map/reduce_scatter | solution.py:66
  701.8 119.1 %copy-start.11 = (bf16[1,256,2048]{2,1,0:T(8,128)(2,1)S(1)}, bf16[1,256,2048]{2,1,0:T(8,128)(2,1)}, u32[]{:S(2)}) copy-start(bf16[1,256,2048]{2,1,0:T(8,128)(2,1)} %param.13) | copy-start | bytes 3145732
  706.9 113.9 %collective-permute-start.15 = (bf16[256,2048]{1,0:T(8,128)(2,1)}, bf16[256,2048]{1,0:T(8,128)(2,1)}, u32[]{:S(2)}, u32[]{:S(2)}) collective-permute-start(bf16[256,2048]{1,0:T(8,128)(2,1)} %get-tuple-element.50), channel_id=1, source_target_pairs={{0,3},{1,0},{2,1},{3,2},{4,7},{5,4},{6,5},{7,6},{8,11},{9,8},{10,9... | collective-permute-start | bytes 3145736 | tf_op jit(solution)/shard_map/ppermute | solution.py:26
  707.0 113.9 %collective-permute-start.14 = (bf16[256,2048]{1,0:T(8,128)(2,1)}, bf16[256,2048]{1,0:T(8,128)(2,1)}, u32[]{:S(2)}, u32[]{:S(2)}) collective-permute-start(bf16[256,2048]{1,0:T(8,128)(2,1)} %get-tuple-element.51), channel_id=1, source_target_pairs={{0,2},{1,3},{2,0},{3,1},{4,6},{5,7},{6,4},{7,5},{8,10},{9,11},{10,... | collective-permute-start | bytes 3145736 | tf_op jit(solution)/shard_map/ppermute | solution.py:26
  707.5 113.3 %collective-permute-start.13 = (bf16[256,2048]{1,0:T(8,128)(2,1)}, bf16[256,2048]{1,0:T(8,128)(2,1)}, u32[]{:S(2)}, u32[]{:S(2)}) collective-permute-start(bf16[256,2048]{1,0:T(8,128)(2,1)} %get-tuple-element.49), channel_id=1, source_target_pairs={{0,1},{1,2},{2,3},{3,0},{4,5},{5,6},{6,7},{7,4},{8,9},{9,10},{10,1... | collective-permute-start | bytes 3145736 | tf_op jit(solution)/shard_map/ppermute | solution.py:26
  829.4 46.5 %collective-permute-start.18 = (bf16[256,3712]{1,0:T(8,128)(2,1)}, bf16[256,3712]{1,0:T(8,128)(2,1)}, u32[]{:S(2)}, u32[]{:S(2)}) collective-permute-start(bf16[256,3712]{1,0:T(8,128)(2,1)} %constant_dynamic-update-slice_fusion), channel_id=1, source_target_pairs={{0,3},{1,0},{2,1},{3,2},{4,7},{5,4},{6,5},{7,6},{8,11},{9,8},{10,9... | collective-permute-start | bytes 5701640 | tf_op jit(solution)/shard_map/ppermute | solution.py:26
  829.4 127.0 %collective-permute-start.17 = (bf16[256,3712]{1,0:T(8,128)(2,1)}, bf16[256,3712]{1,0:T(8,128)(2,1)}, u32[]{:S(2)}, u32[]{:S(2)}) collective-permute-start(bf16[256,3712]{1,0:T(8,128)(2,1)} %constant_dynamic-update-slice_fusion), channel_id=1, source_target_pairs={{0,2},{1,3},{2,0},{3,1},{4,6},{5,7},{6,4},{7,5},{8,10},{9,11},{10,... | collective-permute-start | bytes 5701640 | tf_op jit(solution)/shard_map/ppermute | solution.py:26
  831.2 126.9 %collective-permute-start.16 = (bf16[256,3712]{1,0:T(8,128)(2,1)}, bf16[256,3712]{1,0:T(8,128)(2,1)}, u32[]{:S(2)}, u32[]{:S(2)}) collective-permute-start(bf16[256,3712]{1,0:T(8,128)(2,1)} %constant_dynamic-update-slice_fusion), channel_id=1, source_target_pairs={{0,1},{1,2},{2,3},{3,0},{4,5},{5,6},{6,7},{7,4},{8,9},{9,10},{10,1... | collective-permute-start | bytes 5701640 | tf_op jit(solution)/shard_map/ppermute | solution.py:26
  877.7 92.3 %copy-start.15 = (f32[256,3712]{1,0:T(8,128)}, f32[256,3712]{1,0:T(8,128)S(1)}, u32[]{:S(2)}) copy-start(f32[256,3712]{1,0:T(8,128)S(1)} %convert_element_type.181) | copy-start | bytes 11403268
  958.1 13.8 %copy-start.18 = (f32[256,3712]{1,0:T(8,128)}, f32[256,3712]{1,0:T(8,128)S(1)}, u32[]{:S(2)}) copy-start(f32[256,3712]{1,0:T(8,128)S(1)} %convert_element_type.180) | copy-start | bytes 11403268
  974.4 104.4 %collective-permute-start.19 = (bf16[128,6144]{0,1:T(8,128)(2,1)S(1)}, bf16[128,6144]{0,1:T(8,128)(2,1)}, u32[]{:S(2)}, u32[]{:S(2)}) collective-permute-start(bf16[128,6144]{0,1:T(8,128)(2,1)S(1)} %constant_dynamic-slice_fusion), channel_id=1, source_target_pairs={{0,2},{1,3},{2,0},{3,1},{4,6},{5,7},{6,4},{7,5},{8,10},{9,11},{10,... | collective-permute-start | bytes 4718600 | tf_op jit(solution)/shard_map/ppermute | solution.py:26
  1015.7 63.1 %copy-start.46 = (bf16[256,6144]{0,1:T(8,128)(2,1)S(1)}, bf16[256,6144]{0,1:T(8,128)(2,1)}, u32[]{:S(2)}) copy-start(bf16[256,6144]{0,1:T(8,128)(2,1)} %reduce-scatter.8.cloned.1.call-done) | copy-start | bytes 9437188
  1081.8 38.7 %collective-permute-start.20 = (bf16[128,6144]{0,1:T(8,128)(2,1)}, bf16[128,6144]{0,1:T(8,128)(2,1)}, u32[]{:S(2)}, u32[]{:S(2)}) collective-permute-start(bf16[128,6144]{0,1:T(8,128)(2,1)} %get-tuple-element.31), channel_id=1, source_target_pairs={{0,1},{1,2},{2,3},{3,0},{4,5},{5,6},{6,7},{7,4},{8,9},{9,10},{10,1... | collective-permute-start | bytes 4718600 | tf_op jit(solution)/shard_map/ppermute | solution.py:26
  1092.6 127.0 %collective-permute-start.21 = (bf16[128,6144]{0,1:T(8,128)(2,1)}, bf16[128,6144]{0,1:T(8,128)(2,1)}, u32[]{:S(2)}, u32[]{:S(2)}) collective-permute-start(bf16[128,6144]{0,1:T(8,128)(2,1)} %get-tuple-element.31), channel_id=1, source_target_pairs={{0,2},{1,3},{2,0},{3,1},{4,6},{5,7},{6,4},{7,5},{8,10},{9,11},{10,... | collective-permute-start | bytes 4718600 | tf_op jit(solution)/shard_map/ppermute | solution.py:26
  1092.6 131.9 %collective-permute-start.22 = (bf16[128,6144]{0,1:T(8,128)(2,1)}, bf16[128,6144]{0,1:T(8,128)(2,1)}, u32[]{:S(2)}, u32[]{:S(2)}) collective-permute-start(bf16[128,6144]{0,1:T(8,128)(2,1)} %get-tuple-element.31), channel_id=1, source_target_pairs={{0,3},{1,0},{2,1},{3,2},{4,7},{5,4},{6,5},{7,6},{8,11},{9,8},{10,9... | collective-permute-start | bytes 4718600 | tf_op jit(solution)/shard_map/ppermute | solution.py:26
  (105 other events, 430.3 us)
Sparse Core Ops, SparseCore 0:
  22.1 84.1 all-gather.2
  108.8 125.3 all-gather.4
  626.5 84.7 reduce-scatter.3
  715.0 51.3 reduce-scatter.5
  770.3 157.4 reduce-scatter.7

commit v2 on v1

v2 whole, which is shorter than its diff:
```python
import functools
import math

import jax
import jax.numpy as jnp
from jax import lax
from jax.experimental import pallas as pl
from jax.experimental.pallas import tpu as pltpu
from jax.sharding import PartitionSpec as P

QUERY_HEADS = 8
KEY_VALUE_HEADS = 2
HEAD_SIZE = 128
MIXER_HEADS = 48
MIXER_HEAD_SIZE = 64
STATE_SIZE = 256
LANES = 128

EPSILON = 1e-05
THETA = 10000.0
SCALE = 1.0 / math.sqrt(HEAD_SIZE)
VMEM_LIMIT = 56 * 1024 * 1024
BF16 = jnp.bfloat16
F32 = jnp.float32


def swap_pair(value):
    count = lax.axis_size("ctx")
    return lax.ppermute(value, "ctx", [(i, i ^ 1) for i in range(count)])


def after(value, *earlier):
    return lax.optimization_barrier((value,) + earlier)[0]


class Chain:
    def __init__(self, steps):
        self.steps, self.sends, self.result = steps, next(steps), None

    def take(self, got):
        try:
            self.sends = self.steps.send(got)
        except StopIteration as stop:
            self.sends, self.result = None, stop.value


def advance(*chains, beside=()):
    sends = [send for chain in chains for send in chain.sends]
    values = lax.optimization_barrier(tuple(value for value, _ in sends))
    got = tuple(lax.ppermute(v, "ctx", pairs) for v, (_, pairs) in zip(values, sends))
    if beside:
        sealed = lax.optimization_barrier(got + tuple(beside))
        got, beside = sealed[: len(got)], sealed[len(got) :]
    for chain in chains:
        count = len(chain.sends)
        chain.take(got[:count])
        got = got[count:]
    return beside


def finish(steps):
    chain = Chain(steps)
    while chain.sends is not None:
        advance(chain)
    return chain.result


def line_gather(value):
    count = lax.axis_size("ctx")
    up = down = value
    ups, downs = [], []
    for hop in range(1, count):
        up, down = yield [
            (up, [(i, i + 1) for i in range(hop - 1, count - 1)]),
            (down, [(i + 1, i) for i in range(count - hop)]),
        ]
        ups.append(up)
        downs.append(down)
    return ups, downs


def in_hops(value, ups, downs):
    count, place = lax.axis_size("ctx"), lax.axis_index("ctx")
    return [value] + [
        jnp.where(place >= hop, ups[hop - 1], downs[count - hop - 1]) for hop in range(1, count)
    ]


def gather_ctx(value):
    return in_hops(value, *finish(line_gather(value)))


def line_sum(parts):
    count = len(parts)
    up = down = 0.0
    for hop in range(1, count):
        up, down = yield [
            ((parts[hop] + up).astype(BF16), [(i, i + 1) for i in range(hop)]),
            (
                (parts[count - hop] + down).astype(BF16),
                [(i, i - 1) for i in range(count - hop, count)],
            ),
        ]
        up, down = up.astype(F32), down.astype(F32)
    return parts[0] + up + down


def parity_sum(grad):
    count = lax.axis_size("ctx")
    members, member = count // 2, lax.axis_index("ctx") // 2
    chunk = grad.shape[0] // members
    got = yield [
        (
            lax.dynamic_slice_in_dim(grad, ((member + hop) % members) * chunk, chunk, 0),
            [(i, (i + 2 * hop) % count) for i in range(count)],
        )
        for hop in range(1, members)
    ]
    total = lax.dynamic_slice_in_dim(grad, member * chunk, chunk, 0).astype(F32)
    for block in got:
        total = total + block.astype(F32)
    return total.astype(BF16)


def parity_gather(grad):
    total = yield from parity_sum(grad)
    ups, downs = yield from line_gather(total)
    return total, ups, downs


def gather_rows(value):
    return lax.all_gather(value, "fsdp", axis=0, tiled=True)


def scatter_rows(value):
    return lax.psum_scatter(value, "fsdp", scatter_dimension=0, tiled=True)


def dot(left, right, left_dim, right_dim):
    return lax.dot_general(
        left, right, (((left_dim,), (right_dim,)), ((), ())), preferred_element_type=F32
    )


def inverse_rms(rows):
    return lax.rsqrt(jnp.mean(rows * rows, axis=-1, keepdims=True) + EPSILON)


def rms_pull(rows, inverse, gain, grad):
    scaled = grad * gain
    return inverse * (scaled - rows * inverse * inverse * jnp.mean(rows * scaled, -1, keepdims=True))


def lanes_split(value, terms):
    parts = []
    for _ in range(terms):
        part = value.astype(BF16)
        parts.append(part)
        value = value - part.astype(F32)
    return parts


def near_exact(left, right, dims, terms, split_right):
    total = None
    for part in lanes_split(right if split_right else left, terms):
        pair = (left, part) if split_right else (part, right)
        one = lax.dot_general(*pair, (dims, ((), ())), preferred_element_type=F32)
        total = one if total is None else total + one
    return total


def mul(left, right, left_dim, right_dim):
    return lax.dot_general(
        left, right, (((left_dim,), (right_dim,)), ((), ())), preferred_element_type=F32
    )


def turn(vectors, cosine, sine):
    return vectors * cosine + pltpu.roll(vectors, HEAD_SIZE // 2, 1) * sine


def softplus(value):
    return jnp.maximum(value, 0.0) + jnp.log1p(jnp.exp(-jnp.abs(value)))


def block_terms(mixed, cuts, tri, params, spread):
    size = mixed.shape[0]
    dt_in = mixed[:, cuts["dt"] : cuts["dt"] + LANES] + params[0:1, :]
    step = softplus(dt_in)
    rate = params[1:2, :]
    level = near_exact(tri, step * rate, ((1,), (0,)), 3, True)
    last = level[size - 1 : size, :]
    enter = jnp.exp(level)
    leave = jnp.exp(last - level)
    wide = near_exact(
        jnp.concatenate([enter, step, leave * step], axis=0), spread, ((1,), (0,)), 2, False
    )
    return dict(
        dt_in=dt_in,
        step=step,
        rate=rate,
        level=level,
        last=last,
        leave=leave,
        enter_wide=wide[:size],
        step_wide=wide[size : 2 * size],
        tail_wide=wide[2 * size :],
    )


def fading_of(level, level_t, head, causal):
    gap = level[:, head : head + 1] - level_t[head : head + 1, :]
    return jnp.exp(jnp.where(causal, gap, -1e30))


def square_causal(size):
    row = lax.broadcasted_iota(jnp.int32, (size, size), 0)
    col = lax.broadcasted_iota(jnp.int32, (size, size), 1)
    return row >= col


def stacked_heads(value, at, count):
    return jnp.concatenate(
        [value[:, at + h * HEAD_SIZE : at + (h + 1) * HEAD_SIZE] for h in range(count)], axis=0
    )


def unstacked(value, count):
    size = value.shape[0] // count
    return jnp.concatenate([value[h * size : (h + 1) * size] for h in range(count)], axis=1)


def visible_keys(q_heads, size, block):
    shape = (q_heads * size, (block + 1) * size)
    row = lax.broadcasted_iota(jnp.int32, shape, 0)
    col = lax.broadcasted_iota(jnp.int32, shape, 1)
    return (row % size) + block * size >= col


def mixer_forward_kernel(
    cuts,
    q_heads,
    heads,
    blocks,
    place_ref,
    mixed_ref,
    cos_ref,
    sin_ref,
    tri_ref,
    params_ref,
    spread_ref,
    skip_ref,
    out_ref,
    state_ref,
    keys_ref,
    values_ref,
    carry,
):
    block = pl.program_id(0)
    size = mixed_ref.shape[0]
    q_wide, z_wide = q_heads * HEAD_SIZE, heads * MIXER_HEAD_SIZE

    @pl.when(block == 0)
    def _():
        carry[...] = jnp.zeros_like(carry)

    mixed = mixed_ref
    cosine, sine = cos_ref[...], sin_ref[...]
    here = pl.ds(pl.multiple_of(block * size, size), size)
    keys_ref[here, :] = turn(
        mixed[:, cuts["k"] : cuts["k"] + HEAD_SIZE], cosine, sine
    ).astype(BF16)
    values_ref[here, :] = mixed[:, cuts["v"] : cuts["v"] + HEAD_SIZE].astype(BF16)
    queries = jnp.concatenate(
        [
            turn(mixed[:, h * HEAD_SIZE : (h + 1) * HEAD_SIZE], cosine, sine)
            for h in range(q_heads)
        ],
        axis=0,
    ).astype(BF16)

    for at in range(blocks):

        @pl.when(block == at)
        def _(at=at):
            span = (at + 1) * size
            raw = mul(queries, keys_ref[:span, :], 1, 1) * SCALE
            logits = jnp.where(visible_keys(q_heads, size, at), raw, -1e30)
            weights = jnp.exp(logits - jnp.max(logits, axis=-1, keepdims=True))
            total = jnp.sum(weights, axis=-1, keepdims=True)
            attended = mul(weights.astype(BF16), values_ref[:span, :], 1, 0) / total
            out_ref[:, :q_wide] = unstacked(attended, q_heads).astype(BF16)

    terms = block_terms(mixed, cuts, tri_ref[...], params_ref, spread_ref[...])
    x = mixed[:, cuts["x"] : cuts["x"] + z_wide]
    b_rows = mixed[:, cuts["b"] : cuts["b"] + STATE_SIZE].astype(BF16)
    c_rows = mixed[:, cuts["c"] : cuts["c"] + STATE_SIZE].astype(BF16)
    causal = square_causal(size)
    pairing = mul(c_rows, b_rows, 1, 1)
    level = terms["level"]
    level_t = level.T
    x_step = (x * terms["step_wide"]).astype(BF16)
    first = lax.broadcasted_iota(jnp.int32, (size, LANES), 1) < MIXER_HEAD_SIZE
    inside = []
    for pair in range(heads // 2):
        both = x_step[:, pair * LANES : (pair + 1) * LANES]
        sides = []
        for head in (2 * pair, 2 * pair + 1):
            mixing = (fading_of(level, level_t, head, causal) * pairing).astype(BF16)
            sides.append(mul(mixing, both, 1, 0))
        inside.append(jnp.where(first, sides[0], sides[1]))
    state = carry[...]
    state_ref[0] = state
    full = (
        jnp.concatenate(inside, axis=1)
        + terms["enter_wide"] * mul(c_rows, state.astype(BF16), 1, 0)
        + skip_ref[...] * x
    )
    z = mixed[:, cuts["z"] : cuts["z"] + z_wide]
    out_ref[:, q_wide:] = (full * z * jax.nn.sigmoid(z)).astype(BF16)
    fresh = mul(b_rows, (x * terms["tail_wide"]).astype(BF16), 0, 0)
    carry[...] = terms["enter_wide"][size - 1 : size, :] * state + fresh


def mixer_backward_kernel(
    cuts,
    q_heads,
    heads,
    blocks,
    place_ref,
    mixed_ref,
    joint_ref,
    state_ref,
    keys_ref,
    values_ref,
    cos_ref,
    sin_ref,
    tri_ref,
    params_ref,
    spread_ref,
    skip_ref,
    out_ref,
    head_ref,
    grad_keys,
    grad_values,
    carry,
):
    block = blocks - 1 - pl.program_id(0)
    size = mixed_ref.shape[0]
    q_wide, z_wide = q_heads * HEAD_SIZE, heads * MIXER_HEAD_SIZE

    @pl.when(block == blocks - 1)
    def _():
        carry[...] = jnp.zeros_like(carry)
        grad_keys[...] = jnp.zeros_like(grad_keys)
        grad_values[...] = jnp.zeros_like(grad_values)
        head_ref[...] = jnp.zeros_like(head_ref)

    mixed, joint = mixed_ref, joint_ref
    cosine, sine = cos_ref[...], sin_ref[...]
    queries = jnp.concatenate(
        [
            turn(mixed[:, h * HEAD_SIZE : (h + 1) * HEAD_SIZE], cosine, sine)
            for h in range(q_heads)
        ],
        axis=0,
    ).astype(BF16)
    grad_out = stacked_heads(joint, 0, q_heads).astype(BF16)

    for at in range(blocks):

        @pl.when(block == at)
        def _(at=at):
            span = (at + 1) * size
            keys, values = keys_ref[:span, :], values_ref[:span, :]
            raw = mul(queries, keys, 1, 1) * SCALE
            logits = jnp.where(visible_keys(q_heads, size, at), raw, -1e30)
            weights = jnp.exp(logits - jnp.max(logits, axis=-1, keepdims=True))
            probs = weights / jnp.sum(weights, axis=-1, keepdims=True)
            grad_probs = mul(grad_out, values, 1, 1)
            delta = jnp.sum(probs * grad_probs, axis=-1, keepdims=True)
            grad_raw = (probs * (grad_probs - delta) * SCALE).astype(BF16)
            grad_queries = mul(grad_raw, keys, 1, 0)
            for h in range(q_heads):
                out_ref[:, h * HEAD_SIZE : (h + 1) * HEAD_SIZE] = turn(
                    grad_queries[h * size : (h + 1) * size], cosine, -sine
                ).astype(BF16)
            grad_keys[:span, :] += mul(grad_raw, queries, 0, 0)
            grad_values[:span, :] += mul(probs.astype(BF16), grad_out, 0, 0)

    here = pl.ds(pl.multiple_of(block * size, size), size)
    out_ref[:, cuts["k"] : cuts["k"] + HEAD_SIZE] = turn(
        grad_keys[here, :], cosine, -sine
    ).astype(BF16)
    out_ref[:, cuts["v"] : cuts["v"] + HEAD_SIZE] = grad_values[here, :].astype(BF16)

    tri, spread = tri_ref[...], spread_ref[...]
    terms = block_terms(mixed, cuts, tri, params_ref, spread)
    x = mixed[:, cuts["x"] : cuts["x"] + z_wide]
    z = mixed[:, cuts["z"] : cuts["z"] + z_wide]
    b_rows = mixed[:, cuts["b"] : cuts["b"] + STATE_SIZE].astype(BF16)
    c_rows = mixed[:, cuts["c"] : cuts["c"] + STATE_SIZE].astype(BF16)
    skip = skip_ref[...]
    causal = square_causal(size)
    pairing = mul(c_rows, b_rows, 1, 1)
    level = terms["level"]
    level_t = level.T
    enter_wide, step_wide, tail_wide = (
        terms["enter_wide"],
        terms["step_wide"],
        terms["tail_wide"],
    )
    x_step = (x * step_wide).astype(BF16)
    grad_gated = joint[:, q_wide:]
    sigmoid = jax.nn.sigmoid(z)
    grad_y = grad_gated * z * sigmoid
    grad_y16 = grad_y.astype(BF16)
    first = lax.broadcasted_iota(jnp.int32, (size, LANES), 1) < MIXER_HEAD_SIZE
    inside, grad_x_step = [], []
    grad_pairing = jnp.zeros((size, size), F32)
    none = jnp.zeros((size, LANES), BF16)
    for pair in range(heads // 2):
        lanes = slice(pair * LANES, (pair + 1) * LANES)
        both, grad_both = x_step[:, lanes], grad_y16[:, lanes]
        ys, xs = [], []
        for side, head in enumerate((2 * pair, 2 * pair + 1)):
            fading = fading_of(level, level_t, head, causal)
            mixing = (fading * pairing).astype(BF16)
            ys.append(mul(mixing, both, 1, 0))
            xs.append(mul(mixing, grad_both, 0, 0))
            alone = jnp.where(first == (side == 0), grad_both, none)
            grad_pairing = grad_pairing + fading * mul(alone, both, 1, 1)
        inside.append(jnp.where(first, ys[0], ys[1]))
        grad_x_step.append(jnp.where(first, xs[0], xs[1]))
    inside = jnp.concatenate(inside, axis=1)
    grad_x_step = jnp.concatenate(grad_x_step, axis=1)
    state = state_ref[0]
    state16 = state.astype(BF16)
    adjoint = carry[...]
    adjoint16 = adjoint.astype(BF16)
    outer = enter_wide * mul(c_rows, state16, 1, 0)
    full = inside + outer + skip * x
    grad_z = grad_gated * full * (sigmoid * (1.0 + z * (1.0 - sigmoid)))
    out_ref[:, cuts["z"] : cuts["z"] + z_wide] = grad_z.astype(BF16)
    entered = (enter_wide * grad_y).astype(BF16)
    pairing16 = grad_pairing.astype(BF16)
    grad_c = mul(entered, state16, 1, 1) + mul(pairing16, b_rows, 1, 0)
    grad_b = mul((x * tail_wide).astype(BF16), adjoint16, 1, 1) + mul(pairing16, c_rows, 0, 0)
    out_ref[:, cuts["b"] : cuts["b"] + STATE_SIZE] = grad_b.astype(BF16)
    out_ref[:, cuts["c"] : cuts["c"] + STATE_SIZE] = grad_c.astype(BF16)
    pushed = mul(b_rows, adjoint16, 1, 0)
    grad_x = step_wide * grad_x_step + tail_wide * pushed + skip * grad_y
    out_ref[:, cuts["x"] : cuts["x"] + z_wide] = grad_x.astype(BF16)

    def by_head(value):
        return near_exact(value, spread, ((1,), (1,)), 2, False)

    row_part = by_head(grad_y16.astype(F32) * inside + grad_y * outer)
    col_part = by_head(x_step.astype(F32) * grad_x_step)
    step_part = by_head(x * grad_x_step)
    tail_part = by_head(x * pushed)
    sums = jnp.concatenate(
        [
            jnp.sum(state * adjoint, axis=0, keepdims=True),
            jnp.sum(grad_y * x, axis=0, keepdims=True),
            jnp.zeros((6, z_wide), F32),
        ],
        axis=0,
    )
    sums = by_head(sums)
    step, leave, last = terms["step"], terms["leave"], terms["last"]
    moved = leave * step * tail_part
    grad_level = row_part - col_part - moved
    at_last = jnp.sum(moved, axis=0, keepdims=True) + jnp.exp(last) * sums[0:1, :]
    row = lax.broadcasted_iota(jnp.int32, (size, LANES), 0)
    grad_level = grad_level + jnp.where(row == size - 1, at_last, 0.0)
    grad_log = near_exact(tri, grad_level, ((0,), (0,)), 3, True)
    grad_step = step_part + leave * tail_part + grad_log * terms["rate"]
    grad_dt = grad_step * jax.nn.sigmoid(terms["dt_in"])
    lane = lax.broadcasted_iota(jnp.int32, (size, LANES), 1)
    grad_dt = jnp.where(lane < heads, grad_dt, 0.0)
    out_ref[:, cuts["dt"] : cuts["dt"] + LANES] = grad_dt.astype(BF16)
    head_ref[...] += jnp.concatenate(
        [
            jnp.sum(grad_dt, axis=0, keepdims=True),
            jnp.sum(grad_log * step, axis=0, keepdims=True) * terms["rate"],
            sums[1:2, :],
            jnp.zeros((5, LANES), F32),
        ],
        axis=0,
    )
    carry[...] = enter_wide[size - 1 : size, :] * adjoint + mul(c_rows, entered, 0, 0)


def mixer_tables(tokens, size, heads, bias, log_rate, skip):
    half = HEAD_SIZE // 2
    positions = jnp.arange(tokens, dtype=F32)
    frequency = THETA ** (-jnp.arange(half, dtype=F32) / half)
    angles = positions[:, None] * frequency[None, :]
    cosine, sine = jnp.cos(angles), jnp.sin(angles)
    order = jnp.arange(size)
    tri = (order[:, None] >= order[None, :]).astype(BF16)
    z_wide = heads * MIXER_HEAD_SIZE
    owner = jnp.arange(z_wide) // MIXER_HEAD_SIZE
    spread = (jnp.arange(LANES)[:, None] == owner[None, :]).astype(BF16)
    params = jnp.zeros((8, LANES), F32)
    params = params.at[0, :heads].set(bias).at[1, :heads].set(-jnp.exp(log_rate))
    return (
        jnp.concatenate([cosine, cosine], axis=1),
        jnp.concatenate([-sine, sine], axis=1),
        tri,
        params,
        spread,
        jnp.repeat(skip, MIXER_HEAD_SIZE)[None, :],
    )


def whole(shape):
    return pl.BlockSpec(shape, lambda i, place: (0,) * len(shape))


def mixer_forward(place, mixed, tables, cuts, q_heads, heads, blocks):
    tokens, wide = mixed.shape
    size = tokens // blocks
    cosine, sine, tri, params, spread, skip = tables
    z_wide = heads * MIXER_HEAD_SIZE
    out_wide = q_heads * HEAD_SIZE + z_wide

    def by_hop(width):
        return pl.BlockSpec(
            (size, width), lambda i, place: (lax.rem(place[0] - i + blocks, blocks), 0)
        )

    in_order = pl.BlockSpec((size, HEAD_SIZE), lambda i, place: (i, 0))
    return pl.pallas_call(
        functools.partial(mixer_forward_kernel, cuts, q_heads, heads, blocks),
        grid_spec=pltpu.PrefetchScalarGridSpec(
            num_scalar_prefetch=1,
            grid=(blocks,),
            in_specs=[
                by_hop(wide),
                in_order,
                in_order,
                whole(tri.shape),
                whole(params.shape),
                whole(spread.shape),
                whole(skip.shape),
            ],
            out_specs=[
                by_hop(out_wide),
                pl.BlockSpec((1, STATE_SIZE, z_wide), lambda i, place: (i, 0, 0)),
                whole((tokens, HEAD_SIZE)),
                whole((tokens, HEAD_SIZE)),
            ],
            scratch_shapes=[pltpu.VMEM((STATE_SIZE, z_wide), F32)],
        ),
        out_shape=[
            jax.ShapeDtypeStruct((tokens, out_wide), BF16),
            jax.ShapeDtypeStruct((blocks, STATE_SIZE, z_wide), F32),
            jax.ShapeDtypeStruct((tokens, HEAD_SIZE), BF16),
            jax.ShapeDtypeStruct((tokens, HEAD_SIZE), BF16),
        ],
        compiler_params=pltpu.CompilerParams(vmem_limit_bytes=VMEM_LIMIT),
        cost_estimate=pl.CostEstimate(
            flops=8_000_000_000, bytes_accessed=20_000_000, transcendentals=0
        ),
        name="mixer_forward",
    )(place, mixed, cosine, sine, tri, params, spread, skip)


def mixer_backward(place, mixed, joint, states, keys, values, tables, cuts, q_heads, heads, blocks):
    tokens, wide = mixed.shape
    size = tokens // blocks
    cosine, sine, tri, params, spread, skip = tables
    z_wide = heads * MIXER_HEAD_SIZE

    def by_hop(width):
        return pl.BlockSpec(
            (size, width), lambda i, place: (lax.rem(place[0] + i + 1, blocks), 0)
        )

    in_order = pl.BlockSpec((size, HEAD_SIZE), lambda i, place: (blocks - 1 - i, 0))
    return pl.pallas_call(
        functools.partial(mixer_backward_kernel, cuts, q_heads, heads, blocks),
        grid_spec=pltpu.PrefetchScalarGridSpec(
            num_scalar_prefetch=1,
            grid=(blocks,),
            in_specs=[
                by_hop(wide),
                by_hop(joint.shape[1]),
                pl.BlockSpec((1, STATE_SIZE, z_wide), lambda i, place: (blocks - 1 - i, 0, 0)),
                whole(keys.shape),
                whole(values.shape),
                in_order,
                in_order,
                whole(tri.shape),
                whole(params.shape),
                whole(spread.shape),
                whole(skip.shape),
            ],
            out_specs=[by_hop(wide), whole((8, LANES))],
            scratch_shapes=[
                pltpu.VMEM((tokens, HEAD_SIZE), F32),
                pltpu.VMEM((tokens, HEAD_SIZE), F32),
                pltpu.VMEM((STATE_SIZE, z_wide), F32),
            ],
        ),
        out_shape=[
            jax.ShapeDtypeStruct((tokens, wide), BF16),
            jax.ShapeDtypeStruct((8, LANES), F32),
        ],
        compiler_params=pltpu.CompilerParams(vmem_limit_bytes=VMEM_LIMIT),
        cost_estimate=pl.CostEstimate(
            flops=20_000_000_000, bytes_accessed=30_000_000, transcendentals=0
        ),
        name="mixer_backward",
    )(place, mixed, joint, states, keys, values, cosine, sine, tri, params, spread, skip)


def pack_kernel(cuts, starts_ref, *refs):
    sources = refs[: max(c[0] for out in cuts for c in out) + 1]
    outs = refs[len(sources) : len(sources) + len(cuts)]
    semaphores = refs[-1]
    copies, at = [], 0
    for out, ref in zip(cuts, outs):
        column = 0
        for source, wide in out:
            start = pl.multiple_of(starts_ref[at], LANES)
            copies.append(
                pltpu.make_async_copy(
                    sources[source].at[:, pl.ds(start, wide)],
                    ref.at[:, pl.ds(column, wide)],
                    semaphores.at[at],
                )
            )
            column += wide
            at += 1
    for copy in copies:
        copy.start()
    for copy in copies:
        copy.wait()


def pack_columns(sources, cuts):
    starts = jnp.stack([start for out in cuts for _, start, _ in out]).astype(jnp.int32)
    rows = sources[0].shape[0]
    anywhere = pl.BlockSpec(memory_space=pl.ANY)
    return pl.pallas_call(
        functools.partial(pack_kernel, [[(s, w) for s, _, w in out] for out in cuts]),
        grid_spec=pltpu.PrefetchScalarGridSpec(
            num_scalar_prefetch=1,
            grid=(1,),
            in_specs=[anywhere] * len(sources),
            out_specs=[
                pl.BlockSpec((rows, sum(w for _, _, w in out)), lambda i, starts: (0, 0))
                for out in cuts
            ],
            scratch_shapes=[pltpu.SemaphoreType.DMA((starts.shape[0],))],
        ),
        out_shape=[
            jax.ShapeDtypeStruct((rows, sum(w for _, _, w in out)), BF16) for out in cuts
        ],
        compiler_params=pltpu.CompilerParams(vmem_limit_bytes=VMEM_LIMIT),
        cost_estimate=pl.CostEstimate(
            flops=0, bytes_accessed=20_000_000, transcendentals=0
        ),
        name="pack_columns",
    )(starts, *sources)


def dense_cost(flops, *arrays):
    return pl.CostEstimate(
        flops=flops,
        bytes_accessed=sum(math.prod(a.shape) * a.dtype.itemsize for a in arrays),
        transcendentals=0,
    )


def mixer_in_kernel(count, place_ref, gain_ref, w_ref, *refs):
    parts = refs[: 2 * count - 1]
    out_ref, normed_ref, scaled_ref = refs[2 * count - 1 :]
    size = parts[0].shape[0]

    @pl.when(pl.program_id(0) == 0)
    def _():
        for hop in range(count):
            if hop == 0:
                rows = parts[0][...].astype(F32)
            else:
                rows = jnp.where(
                    place_ref[0] >= hop,
                    parts[hop][...].astype(F32),
                    parts[2 * count - 1 - hop][...].astype(F32),
                )
            scaled = rows * lax.rsqrt(jnp.mean(rows * rows, axis=-1, keepdims=True) + EPSILON)
            scaled_ref[hop * size : (hop + 1) * size, :] = scaled.astype(BF16)
            normed_ref[hop * size : (hop + 1) * size, :] = (scaled * gain_ref[...]).astype(BF16)

    out_ref[...] = mul(normed_ref[...], w_ref[...], 1, 0)


def mixer_in(place, own, ups, downs, gain, weight, wide):
    size, depth = own.shape
    count = len(ups) + 1
    tokens = size * count
    tile = max(t for t in range(LANES, 1025, LANES) if wide % t == 0)

    def fixed(shape):
        return pl.BlockSpec(shape, lambda j, place: (0, 0))

    outs = [
        jax.ShapeDtypeStruct((tokens, wide), F32),
        jax.ShapeDtypeStruct((tokens, depth), BF16),
        jax.ShapeDtypeStruct((tokens, depth), BF16),
    ]
    return pl.pallas_call(
        functools.partial(mixer_in_kernel, count),
        grid_spec=pltpu.PrefetchScalarGridSpec(
            num_scalar_prefetch=1,
            grid=(wide // tile,),
            in_specs=[
                fixed((1, depth)),
                pl.BlockSpec((depth, tile), lambda j, place: (0, j)),
            ]
            + [fixed((size, depth))] * (2 * count - 1),
            out_specs=[
                pl.BlockSpec((tokens, tile), lambda j, place: (0, j)),
                fixed((tokens, depth)),
                fixed((tokens, depth)),
            ],
        ),
        out_shape=outs,
        compiler_params=pltpu.CompilerParams(vmem_limit_bytes=VMEM_LIMIT),
        cost_estimate=dense_cost(2 * tokens * depth * wide, weight, *outs),
        name="mixer_in",
    )(place, gain, weight, own, *ups, *downs)


def ffn_kernel(x_ref, act_grad_ref, gate_ref, up_ref, activated_ref, grad_gate_ref, grad_up_ref):
    rows = x_ref[...]
    gate = mul(rows, gate_ref[...], 1, 0)
    up = mul(rows, up_ref[...], 1, 0)
    grad = act_grad_ref[...]
    sigmoid = jax.nn.sigmoid(gate)
    silu = gate * sigmoid
    activated_ref[...] = (silu * up).astype(BF16)
    grad_gate_ref[...] = (grad * up * (sigmoid * (1.0 + gate * (1.0 - sigmoid)))).astype(BF16)
    grad_up_ref[...] = (grad * silu).astype(BF16)


def ffn_inner(x, act_grad, weights):
    tokens, depth = x.shape
    units = act_grad.shape[1]
    tile = 256
    tiles = units // tile
    out = jax.ShapeDtypeStruct((tokens, units), BF16)
    by_unit = pl.BlockSpec((tokens, tile), lambda j: (0, j))
    return pl.pallas_call(
        ffn_kernel,
        grid=(tiles,),
        in_specs=[
            pl.BlockSpec((tokens, depth), lambda j: (0, 0)),
            by_unit,
            pl.BlockSpec((depth, tile), lambda j: (0, tiles + j)),
            pl.BlockSpec((depth, tile), lambda j: (0, 2 * tiles + j)),
        ],
        out_specs=[by_unit] * 3,
        out_shape=[out] * 3,
        compiler_params=pltpu.CompilerParams(vmem_limit_bytes=VMEM_LIMIT),
        cost_estimate=dense_cost(4 * tokens * depth * units, weights, out, out, out),
        name="ffn_inner",
    )(x, act_grad, weights, weights)


def ffn_back_kernel(grad_gate_ref, grad_up_ref, gate_ref, up_ref, own_ref, other_ref):
    total = mul(grad_gate_ref[...], gate_ref[...], 1, 1) + mul(grad_up_ref[...], up_ref[...], 1, 1)
    half = total.shape[0] // 2
    own_ref[...] = total[:half]
    other_ref[...] = total[half:].astype(BF16)


def ffn_back(grad_gate, grad_up, weights):
    tokens, units = grad_gate.shape
    depth = weights.shape[0]
    tile = 256
    whole_rows = pl.BlockSpec((tokens, units), lambda j: (0, 0))
    half = pl.BlockSpec((tokens // 2, tile), lambda j: (0, j))
    return pl.pallas_call(
        ffn_back_kernel,
        grid=(depth // tile,),
        in_specs=[
            whole_rows,
            whole_rows,
            pl.BlockSpec((tile, units), lambda j: (j, 1)),
            pl.BlockSpec((tile, units), lambda j: (j, 2)),
        ],
        out_specs=[half, half],
        out_shape=[
            jax.ShapeDtypeStruct((tokens // 2, depth), F32),
            jax.ShapeDtypeStruct((tokens // 2, depth), BF16),
        ],
        compiler_params=pltpu.CompilerParams(vmem_limit_bytes=VMEM_LIMIT),
        cost_estimate=dense_cost(4 * tokens * depth * units, weights),
        name="ffn_back",
    )(grad_gate, grad_up, weights, weights)


def outer_kernel(pairs, rider_at, *refs):
    out_ref = refs[-1]
    at = 0
    for left, right, start, wide in pairs:
        value = mul(refs[left][...], refs[right][:, start : start + wide], 0, 0)
        out_ref[:, at : at + wide] = value.astype(BF16)
        at += wide
    if rider_at is not None:
        riders = refs[-2][...]
        rows = riders.shape[0]
        for k in range(out_ref.shape[0] // rows):
            block = out_ref[k * rows : (k + 1) * rows, rider_at : rider_at + LANES]
            out_ref[k * rows : (k + 1) * rows, rider_at : rider_at + LANES] = block + riders


def weight_grads(pairs, riders=None, rider_at=None):
    operands = []

    def position(array):
        for i, held in enumerate(operands):
            if held is array:
                return i
        operands.append(array)
        return len(operands) - 1

    lefts = [position(left) for left, _, _, _ in pairs]
    n_left = len(operands)
    rights = [position(right) for _, right, _, _ in pairs]
    plan = [(l, r, p[2], p[3]) for l, r, p in zip(lefts, rights, pairs)]
    tokens, depth = operands[0].shape
    wide = sum(p[3] for p in pairs)
    tile = 256
    operands += [] if riders is None else [riders]
    specs = [pl.BlockSpec((a.shape[0], tile), lambda j: (0, j)) for a in operands[:n_left]] + [
        pl.BlockSpec(a.shape, lambda j: (0, 0)) for a in operands[n_left:]
    ]
    out = jax.ShapeDtypeStruct((depth, wide), BF16)
    return pl.pallas_call(
        functools.partial(outer_kernel, plan, rider_at),
        grid=(depth // tile,),
        in_specs=specs,
        out_specs=pl.BlockSpec((tile, wide), lambda j: (j, 0)),
        out_shape=out,
        compiler_params=pltpu.CompilerParams(vmem_limit_bytes=VMEM_LIMIT),
        cost_estimate=dense_cost(2 * tokens * depth * wide, out, *operands),
        name="weight_grads",
    )(*operands)


def unpack_kernel(cuts, out_at, q_heads, heads, gain_columns, count, place_ref, *refs):
    parts = refs[: 2 * count - 1]
    mix_ref, attn_ref, ssm_ref, extra_ref = refs[2 * count - 1 :]
    place = place_ref[0]
    q_wide, z_wide = q_heads * HEAD_SIZE, heads * MIXER_HEAD_SIZE
    group = QUERY_HEADS // KEY_VALUE_HEADS
    key_at = QUERY_HEADS * HEAD_SIZE
    kv_wide = KEY_VALUE_HEADS * HEAD_SIZE
    z_at = key_at + 2 * kv_wide
    x_at = z_at + MIXER_HEADS * MIXER_HEAD_SIZE
    b_at = x_at + MIXER_HEADS * MIXER_HEAD_SIZE
    step = mix_ref.shape[0]
    lane = lax.broadcasted_iota(jnp.int32, (step, LANES), 1)
    head_lane = heads + gain_columns
    head_at = MIXER_HEADS + gain_columns
    shared = jnp.zeros((step, 2 * STATE_SIZE), F32)
    extra = jnp.zeros((step, LANES), F32)
    mix_ref[:, key_at : key_at + 2 * kv_wide] = jnp.zeros((step, 2 * kv_wide), F32)

    for hop in range(count):
        source = lax.rem(place - hop + count, count)

        def of(start, wide, hop=hop):
            if hop == 0:
                return parts[0][:, start : start + wide].astype(F32)
            up = parts[hop][:, start : start + wide].astype(F32)
            down = parts[2 * count - 1 - hop][:, start : start + wide].astype(F32)
            return jnp.where(place >= hop, up, down)

        def put(ref, start, value):
            ref[:, pl.ds(pl.multiple_of(start, LANES), value.shape[1])] = value

        put(mix_ref, source * q_wide, of(cuts["q"], q_wide))
        put(mix_ref, z_at + source * z_wide, of(cuts["z"], z_wide))
        put(mix_ref, x_at + source * z_wide, of(cuts["x"], z_wide))
        put(attn_ref, source * q_wide, of(out_at, q_wide))
        put(ssm_ref, source * z_wide, of(out_at + q_wide, z_wide))
        shared = shared + of(cuts["b"], 2 * STATE_SIZE)
        which = lax.div(source * q_heads, group)
        for name, base in (("k", key_at), ("v", key_at + kv_wide)):
            at = pl.ds(pl.multiple_of(base + which * HEAD_SIZE, LANES), HEAD_SIZE)
            mix_ref[:, at] += of(cuts[name], HEAD_SIZE)
        small = of(cuts["dt"], LANES)
        own = jnp.where(lane < heads, small, 0.0)
        gains = jnp.where((lane >= heads) & (lane < head_lane), small, 0.0)
        column = jnp.where(lane == head_lane, small, 0.0)
        extra = (
            extra
            + pltpu.roll(own, source * heads, 1)
            + pltpu.roll(gains, MIXER_HEADS - heads, 1)
            + pltpu.roll(column, head_at - head_lane + source, 1)
        )
    mix_ref[:, b_at:] = shared
    extra_ref[...] = extra


def unpack_mixer(place, own, ups, downs, cuts, out_at, q_heads, heads, gain_columns):
    rows, wide = own.shape
    count = len(ups) + 1
    step = min(rows, 64)
    widths = (
        QUERY_HEADS * HEAD_SIZE
        + 2 * KEY_VALUE_HEADS * HEAD_SIZE
        + 2 * MIXER_HEADS * MIXER_HEAD_SIZE
        + 2 * STATE_SIZE,
        QUERY_HEADS * HEAD_SIZE,
        MIXER_HEADS * MIXER_HEAD_SIZE,
        LANES,
    )

    def spec(columns):
        return pl.BlockSpec((step, columns), lambda i, place: (i, 0))

    return pl.pallas_call(
        functools.partial(unpack_kernel, cuts, out_at, q_heads, heads, gain_columns, count),
        grid_spec=pltpu.PrefetchScalarGridSpec(
            num_scalar_prefetch=1,
            grid=(rows // step,),
            in_specs=[spec(wide)] * (2 * count - 1),
            out_specs=[spec(w) for w in widths],
        ),
        out_shape=[jax.ShapeDtypeStruct((rows, w), F32) for w in widths],
        compiler_params=pltpu.CompilerParams(vmem_limit_bytes=VMEM_LIMIT),
        cost_estimate=pl.CostEstimate(
            flops=100_000_000, bytes_accessed=26_000_000, transcendentals=0
        ),
        name="unpack_mixer",
    )(place, own, *ups, *downs)


def per_device(
    hidden_in,
    w_mix,
    w_dt,
    w_attn_out,
    w_ssm_out,
    w_gate,
    w_up,
    w_down,
    norm_gains,
    dt_bias,
    a_log,
    skip_scale,
    cotangent,
):
    w_mix, w_dt, w_attn_out, w_ssm_out = w_mix[0], w_dt[0], w_attn_out[0], w_ssm_out[0]
    w_gate, w_up, w_down = w_gate[0], w_up[0], w_down[0]
    gain_mix, gain_ffn = norm_gains[0, 0], norm_gains[0, 1]
    count, place = lax.axis_size("ctx"), lax.axis_index("ctx")
    piece, width = hidden_in.shape[1], hidden_in.shape[2]
    tokens = piece * count
    rows = w_mix.shape[0]
    hidden_units = w_gate.shape[1]
    q_heads = QUERY_HEADS // count
    group = QUERY_HEADS // KEY_VALUE_HEADS
    kv_head = (place * q_heads) // group
    heads = MIXER_HEADS // count
    q_wide, z_wide = q_heads * HEAD_SIZE, heads * MIXER_HEAD_SIZE
    key_at = QUERY_HEADS * HEAD_SIZE
    value_at = key_at + KEY_VALUE_HEADS * HEAD_SIZE
    z_at = value_at + KEY_VALUE_HEADS * HEAD_SIZE
    x_at = z_at + MIXER_HEADS * MIXER_HEAD_SIZE
    b_at = x_at + MIXER_HEADS * MIXER_HEAD_SIZE
    names = ("q", "k", "v", "z", "x", "b", "c", "dt")
    sizes = (q_wide, HEAD_SIZE, HEAD_SIZE, z_wide, z_wide, STATE_SIZE, STATE_SIZE, LANES)
    cuts, mix_wide = {}, 0
    for name, size in zip(names, sizes):
        cuts[name] = mix_wide
        mix_wide += size

    half = place % 2
    half_units = hidden_units // 2
    own_dt = lax.dynamic_slice(w_dt, (0, place * heads), (rows, heads))
    own_dt = jnp.pad(own_dt, ((0, 0), (0, LANES - heads)))
    here = jnp.reshape(place, (1,)).astype(jnp.int32)
    mix_starts = (
        (place * q_wide, q_wide),
        (key_at + kv_head * HEAD_SIZE, HEAD_SIZE),
        (value_at + kv_head * HEAD_SIZE, HEAD_SIZE),
        (z_at + place * z_wide, z_wide),
        (x_at + place * z_wide, z_wide),
        (b_at + 0 * place, 2 * STATE_SIZE),
    )
    from_half = (half * half_units, half_units)
    mixer_own, ffn_own = pack_columns(
        (w_mix, own_dt, w_attn_out, w_ssm_out, w_gate, w_up, w_down),
        (
            [(0,) + cut for cut in mix_starts]
            + [(1, 0 * place, LANES), (2, place * q_wide, q_wide), (3, place * z_wide, z_wide)],
            [(6,) + from_half, (4,) + from_half, (5,) + from_half],
        ),
    )
    w_mixer = gather_rows(mixer_own)
    w_in, w_out = w_mixer[:, :mix_wide], w_mixer[:, mix_wide:]
    w_ffn = gather_rows(ffn_own)
    w_down_half = w_ffn[:, :half_units]

    blocks = tokens // piece

    hidden_own = hidden_in.reshape(piece, width)
    hidden_ups, hidden_downs = finish(line_gather(hidden_own))
    mixed, normed, scaled_in = mixer_in(
        here, hidden_own, hidden_ups, hidden_downs, gain_mix[None, :], w_mixer, mix_wide
    )
    own = [lax.dynamic_slice_in_dim(p[0], place * heads, heads) for p in (dt_bias, a_log, skip_scale)]
    tables = mixer_tables(tokens, piece, heads, *own)
    branch_in, states, keys, values = mixer_forward(
        here, mixed, tables, cuts, q_heads, heads, blocks
    )
    cot_own = cotangent.reshape(piece, width)
    cot_swap = swap_pair(after(cot_own, *hidden_ups))
    branch_in, cot_swap = lax.optimization_barrier((branch_in, cot_swap))
    cot_pair = jnp.concatenate([cot_own, cot_swap], axis=0)
    branch = finish(
        line_sum([dot(branch_in[s * piece : (s + 1) * piece], w_out, 1, 1) for s in range(count)])
    )
    middle = hidden_own.astype(F32) + branch
    grad_act = dot(cot_pair, w_down_half, 1, 0)

    inverse_ffn = inverse_rms(middle)
    normed_ffn = (middle * inverse_ffn * gain_ffn).astype(BF16)
    normed_swap, grad_act = lax.optimization_barrier((swap_pair(normed_ffn), grad_act))
    normed_pair = jnp.concatenate([normed_ffn, normed_swap], axis=0)
    activated, grad_gate, grad_up = ffn_inner(normed_pair, grad_act, w_ffn)
    grad_normed_own, grad_normed_other = ffn_back(grad_gate, grad_up, w_ffn)
    grad_swap = swap_pair(grad_normed_other)
    activated, grad_gate, grad_up = lax.optimization_barrier(
        (activated, grad_gate, grad_up, grad_normed_other)
    )[:3]
    quarter = half_units // 2
    grad_w_first = weight_grads(
        ((normed_pair, grad_gate, 0, half_units), (normed_pair, grad_up, 0, quarter))
    )
    grad_w_second = weight_grads(
        (
            (normed_pair, grad_up, quarter, quarter),
            (cot_pair, after(activated, grad_w_first), 0, half_units),
        )
    )
    grad_swap, grad_w_second = lax.optimization_barrier((grad_swap, grad_w_second))
    grad_w_first = scatter_rows(grad_w_first)
    grad_normed_ffn = grad_normed_own + grad_swap.astype(F32)

    grad_middle = cot_own.astype(F32) + rms_pull(middle, inverse_ffn, gain_ffn, grad_normed_ffn)
    grad_gain_ffn = jnp.sum(grad_normed_ffn * middle * inverse_ffn, axis=0)
    branch_own = grad_middle.astype(BF16)
    activated = after(activated, branch_own)
    out_pair = dot(activated, w_down_half, 1, 1)
    grad_branch = jnp.concatenate(gather_ctx(branch_own), axis=0)
    grad_joint = dot(grad_branch, w_out, 1, 0)
    out_swap = swap_pair(after(out_pair[piece:].astype(BF16), grad_branch))
    grad_w_second = scatter_rows(after(grad_w_second, grad_w_first, grad_branch))
    first = Chain(parity_gather(grad_w_first))

    grad_mixed, head_part = mixer_backward(
        here, mixed, grad_joint, states, keys, values, tables, cuts, q_heads, heads, blocks
    )
    grad_mixed, head_part, out_swap = advance(first, beside=(grad_mixed, head_part, out_swap))
    ffn_out = out_pair[:piece] + out_swap.astype(F32)
    hidden_out = (middle + ffn_out).astype(BF16)
    grad_normed_part = dot(grad_mixed, w_in, 1, 1)
    grad_gain_mix = jnp.sum(grad_normed_part * scaled_in, axis=0)
    grad_normed_part, grad_gain_mix = advance(first, beside=(grad_normed_part, grad_gain_mix))

    gain_columns = 2 * width // rows
    riders = jnp.concatenate(
        [
            jnp.zeros((rows, heads), F32),
            jnp.stack([grad_gain_mix, grad_gain_ffn]).reshape(rows, gain_columns),
            jnp.pad(head_part[:3, :heads].reshape(3 * heads), (0, rows - 3 * heads))[:, None],
            jnp.zeros((rows, LANES - heads - gain_columns - 1), F32),
        ],
        axis=1,
    )
    grad_w_mixer = weight_grads(
        ((normed, grad_mixed, 0, mix_wide), (grad_branch, branch_in, 0, q_wide + z_wide)),
        riders.astype(BF16),
        cuts["dt"],
    )
    normed_sum = Chain(
        line_sum([grad_normed_part[s * piece : (s + 1) * piece] for s in range(count)])
    )
    (grad_w_mixer,) = advance(first, normed_sum, beside=(grad_w_mixer,))
    grad_w_mixer = scatter_rows(after(grad_w_mixer, grad_w_second))
    second = Chain(parity_gather(grad_w_second))
    chains = [first, normed_sum, second]
    while normed_sum.sends is not None:
        advance(*[chain for chain in chains if chain.sends is not None])
    mixer = Chain(line_gather(grad_w_mixer))
    chains = [first, second, mixer]
    while mixer.sends is not None:
        advance(*[chain for chain in chains if chain.sends is not None])
    while second.sends is not None:
        advance(*[chain for chain in chains if chain.sends is not None])
    grad_normed = normed_sum.result
    hidden_f32 = hidden_own.astype(F32)
    grad_hidden = grad_middle + rms_pull(
        hidden_f32, inverse_rms(hidden_f32), gain_mix, grad_normed
    )

    chunk = rows // (count // 2)

    outs = [jnp.zeros((rows, hidden_units), F32) for _ in range(3)]
    first, second = in_hops(*first.result), in_hops(*second.result)
    for hop in range(count):
        source = (place + count - hop) % count
        row, column = (source // 2) * chunk, (source % 2) * half_units
        for i, block, start, size, offset in (
            (0, first, 0, half_units, 0),
            (1, first, half_units, quarter, 0),
            (1, second, 0, quarter, quarter),
            (2, second, quarter, half_units, 0),
        ):
            outs[i] = lax.dynamic_update_slice(
                outs[i],
                block[hop][:, start : start + size].astype(F32),
                (row, column + offset),
            )
    out_gate, out_up, out_down = outs

    out_mix, out_attn, out_ssm, extra = unpack_mixer(
        here, grad_w_mixer, *mixer.result, cuts, mix_wide, q_heads, heads, gain_columns
    )
    head_at = MIXER_HEADS + gain_columns
    gain_sums = extra[:, MIXER_HEADS:head_at].reshape(norm_gains.shape)
    head_sums = extra[: 3 * heads, head_at : head_at + count].reshape(3, heads, count)
    head_sums = jnp.swapaxes(head_sums, 1, 2).reshape(3, MIXER_HEADS)

    return (
        hidden_out.reshape(hidden_in.shape),
        grad_hidden.reshape(hidden_in.shape),
        out_mix[None],
        extra[None, :, :MIXER_HEADS],
        out_attn[None],
        out_ssm[None],
        out_gate[None],
        out_up[None],
        out_down[None],
        gain_sums,
        head_sums[0][None],
        head_sums[1][None],
        head_sums[2][None],
    )


def solution(mesh):
    split, rows = P("fsdp", "ctx", None), P(None, "fsdp", None)
    return jax.shard_map(
        per_device,
        mesh=mesh,
        in_specs=(split,) + (rows,) * 7 + (P(),) * 4 + (split,),
        out_specs=(split, split) + (rows,) * 7 + (P(),) * 4,
        check_vma=False,
    )
```

time: 1270 us -> 852 us (0.67)
  the two profiles are of different devices: /device:TPU:24 before, /device:TPU:0 now
where the time goes in v2:
time: 852 us; the launch traced here: 844 us
  waiting for transfers between devices  383 us (45%)
  Pallas kernels  171 us (20%)
  starting transfers between devices  119 us (14%)
  matrix products  63.9 us (8%)
  other arithmetic  63.7 us (7%)
  local copies, waits for them, and re-layouts  27.9 us (3%)
  between operations  15.4 us (2%)
    ppermute x44, waiting for transfers between devices, advance(): lax.ppermute(v, 'ctx', pairs)  352 us
    ppermute x44, starting transfers between devices, advance(): lax.ppermute(v, 'ctx', pairs)  111 us
    dot_general x8, matrix products, dot(): lax.dot_general(left, right, (((left_dim,), (right_dim,)), ((), ())), pre...  63.9 us
    pallas_call x3, Pallas kernels, weight_grads(): pl.pallas_call(functools.partial(outer_kernel, plan, rider_at), grid=(dep...  49.3 us
    pallas_call x1, Pallas kernels, mixer_backward(): pl.pallas_call(functools.partial(mixer_backward_kernel, cuts, q_heads, he...  32.1 us
    pallas_call x1, Pallas kernels, mixer_in(): pl.pallas_call(functools.partial(mixer_in_kernel, count), grid_spec=pltpu...  24.8 us
    pallas_call x1, Pallas kernels, mixer_forward(): pl.pallas_call(functools.partial(mixer_forward_kernel, cuts, q_heads, hea...  17 us
  transfers between devices with their start and end apart: 53, of which 23 were waited for; matrix products, arithmetic and copies ran while one was open for 16% of the time, Pallas kernels for 13%

profile of v2, /device:TPU:0, one launch (start us, length us, event | category | flops | bytes accessed | tf_op | source)
XLA Modules:
  0.0 843.5 jit_solution(13545139784310678372)
XLA Ops:
  9.3 5.6 pack_columns.1
  16.1 5.9 collective-permute-start
  23.3 20.1 %collective-permute-done.refs_1_ = bf16[256,2048]{1,0:T(8,128)(2,1)} collective-permute-done((bf16[256,2048]{1,0:T(8,128)(2,1)S(1)}, bf16[256,2048]{1,0:T(8,128)(2,1)}, u32[]{:S(2)}, u32[]{:S(2)}) %collective-permute-start) | collective-permute-done | bytes 1048608 | tf_op jit(solution)/shard_map/ppermute | solution.py:50
  43.5 5.2 collective-permute-done.1.refs_4_
  53.4 24.2 %collective-permute-done.3.refs_5_ = bf16[256,2048]{1,0:T(8,128)(2,1)} collective-permute-done((bf16[256,2048]{1,0:T(8,128)(2,1)}, bf16[256,2048]{1,0:T(8,128)(2,1)}, u32[]{:S(2)}, u32[]{:S(2)}) %collective-permute-start.3) | collective-permute-done | bytes 1048608 | tf_op jit(solution)/shard_map/ppermute | solution.py:50
  88.9 17.8 %collective-permute-done.5.refs_6_ = bf16[256,2048]{1,0:T(8,128)(2,1)} collective-permute-done((bf16[256,2048]{1,0:T(8,128)(2,1)}, bf16[256,2048]{1,0:T(8,128)(2,1)}, u32[]{:S(2)}, u32[]{:S(2)}) %collective-permute-start.5) | collective-permute-done | bytes 1048608 | tf_op jit(solution)/shard_map/ppermute | solution.py:50
  106.7 24.8 %mixer_in.1 = (f32[1024,2688]{1,0:T(8,128)}, bf16[1024,2048]{1,0:T(8,128)(2,1)}, bf16[1024,2048]{1,0:T(8,128)(2,1)}) custom-call(s32[1]{0:T(128)} %bitcast.1.place_ref, f32[1,2048]{1,0:T(1,128)} %get-tuple-element.263.gain_ref, bf16[2048,3712]{1,0:T(8,128)(2,1)} %all-gather.3.cloned.1.call-done.w_ref, bf16[256,2048]{1,0:T(8,128)(2,1)} %bitcast.125, ...), custom_call_target="tpu_custom_call" | custom-call | flops 11274289152 | bytes 34603008 | tf_op jit(solution)/shard_map/mixer_in/pallas_call | solution.py:716
  131.5 17.0 %mixer_forward.1 = (bf16[1024,1024]{1,0:T(8,128)(2,1)}, f32[4,256,768]{2,1,0:T(8,128)}, bf16[1024,128]{1,0:T(8,128)(2,1)}, bf16[1024,128]{1,0:T(8,128)(2,1)}) custom-call(s32[1]{0:T(128)} %bitcast.1.place_ref, f32[1024,2688]{1,0:T(8,128)} %get-tuple-element.135.mixed_ref, f32[1024,128]{1,0:T(8,128)} %get-tuple-element.274.cos_ref, ...), custom_call_target="tpu_custom_call" | custom-call | flops 8000000000 | bytes 20000000 | tf_op jit(solution)/shard_map/mixer_forward/pallas_call | solution.py:535
  149.6 3.8 fusion.46
  159.0 18.3 %collective-permute-done.7 = bf16[256,2048]{1,0:T(8,128)(2,1)S(1)} collective-permute-done((bf16[256,2048]{1,0:T(8,128)(2,1)S(1)}, bf16[256,2048]{1,0:T(8,128)(2,1)S(1)}, u32[]{:S(2)}, u32[]{:S(2)}) %collective-permute-start.7) | collective-permute-done | bytes 1048608 | tf_op jit(solution)/shard_map/ppermute | solution.py:50
  177.3 3.6 add_convert_fusion.6
  180.9 4.5 collective-permute-start.9
  186.1 16.8 %collective-permute-done.9 = bf16[256,2048]{1,0:T(8,128)(2,1)S(1)} collective-permute-done((bf16[256,2048]{1,0:T(8,128)(2,1)S(1)}, bf16[256,2048]{1,0:T(8,128)(2,1)S(1)}, u32[]{:S(2)}, u32[]{:S(2)}) %collective-permute-start.9) | collective-permute-done | bytes 1048608 | tf_op jit(solution)/shard_map/ppermute | solution.py:50
  204.9 11.5 %collective-permute-start.11 = (bf16[256,2048]{1,0:T(8,128)(2,1)S(1)}, bf16[256,2048]{1,0:T(8,128)(2,1)S(1)}, u32[]{:S(2)}, u32[]{:S(2)}) collective-permute-start(bf16[256,2048]{1,0:T(8,128)(2,1)S(1)} %add_convert_fusion.5), channel_id=1, source_target_pairs={{0,1},{1,2},{2,3},{4,5},{5,6},{6,7},{8,9},{9,10},{10,11},{12,13},{... | collective-permute-start | bytes 3145736 | tf_op jit(solution)/shard_map/ppermute | solution.py:50
  216.4 19.6 %collective-permute-done.12 = bf16[256,2048]{1,0:T(8,128)(2,1)S(1)} collective-permute-done((bf16[256,2048]{1,0:T(8,128)(2,1)S(1)}, bf16[256,2048]{1,0:T(8,128)(2,1)S(1)}, u32[]{:S(2)}, u32[]{:S(2)}) %collective-permute-start.12) | collective-permute-done | bytes 1048608 | tf_op jit(solution)/shard_map/ppermute | solution.py:50
  237.2 4.0 multiply_reduce_fusion.3
  244.9 10.2 %fusion.4.act_grad_ref = f32[512,2048]{1,0:T(8,128)} fusion(bf16[2048,6144]{1,0:T(8,128)(2,1)} %all-gather.5.cloned.1.call-done.gate_ref.up_ref, bf16[256,2048]{1,0:T(8,128)(2,1)} %copy-done.34, bf16[256,2048]{1,0:T(8,128)(2,1)S(1)} %bitcast.130), kind=kOutput, calls=%fused_computation.5 | convolution fusion | flops 4299161600 | bytes 14680064 | tf_op jit(solution)/shard_map/dot_general | solution.py:140
  255.1 10.8 %collective-permute-done.13 = bf16[256,2048]{1,0:T(8,128)(2,1)} collective-permute-done((bf16[256,2048]{1,0:T(8,128)(2,1)}, bf16[256,2048]{1,0:T(8,128)(2,1)}, u32[]{:S(2)}, u32[]{:S(2)}) %collective-permute-start.13) | collective-permute-done | bytes 1048608 | tf_op jit(solution)/shard_map/ppermute | solution.py:29
  269.0 17.0 %ffn_inner.1 = (bf16[512,2048]{1,0:T(8,128)(2,1)}, bf16[512,2048]{1,0:T(8,128)(2,1)}, bf16[512,2048]{1,0:T(8,128)(2,1)}) custom-call(bf16[512,2048]{1,0:T(8,128)(2,1)} %pad_maximum_fusion.2.x_ref.refs_0_, f32[512,2048]{1,0:T(8,128)} %fusion.4.act_grad_ref, bf16[2048,6144]{1,0:T(8,128)(2,1)} %all-gather.5.cloned.1.call-done.gate_ref.up_ref, ...), custom_call_target="tpu_custom_call" | custom-call | flops 8589934592 | bytes 31457280 | tf_op jit(solution)/shard_map/ffn_inner/pallas_call | solution.py:758
  286.0 15.1 %ffn_back.1 = (f32[256,2048]{1,0:T(8,128)}, bf16[256,2048]{1,0:T(8,128)(2,1)}) custom-call(bf16[512,2048]{1,0:T(8,128)(2,1)} %get-tuple-element.156.grad_gate_ref.refs_1_, bf16[512,2048]{1,0:T(8,128)(2,1)} %get-tuple-element.155.grad_up_ref.refs_2_, bf16[2048,6144]{1,0:T(8,128)(2,1)} %all-gather.5.cloned.1.call-done.gate_ref.up_ref, ...), custom_call_target="tpu_custom_call" | custom-call | flops 8589934592 | bytes 25165824 | tf_op jit(solution)/shard_map/ffn_back/pallas_call | solution.py:788
  301.1 12.2 %weight_grads.3 = bf16[2048,3072]{1,0:T(8,128)(2,1)} custom-call(bf16[512,2048]{1,0:T(8,128)(2,1)} %pad_maximum_fusion.2.x_ref.refs_0_, bf16[512,2048]{1,0:T(8,128)(2,1)} %get-tuple-element.156.grad_gate_ref.refs_1_, bf16[512,2048]{1,0:T(8,128)(2,1)} %get-tuple-element.155.grad_up_ref.refs_2_), custom_call_target="tpu_custom_call" | custom-call | flops 6442450944 | bytes 18874368 | tf_op jit(solution)/shard_map/weight_grads/pallas_call | solution.py:845
  318.0 14.0 %weight_grads.4 = bf16[2048,3072]{1,0:T(8,128)(2,1)} custom-call(bf16[512,2048]{1,0:T(8,128)(2,1)} %pad_maximum_fusion.2.x_ref.refs_0_, bf16[512,2048]{1,0:T(8,128)(2,1)} %pad_maximum_fusion.1.refs_1_, bf16[512,2048]{1,0:T(8,128)(2,1)} %get-tuple-element.155.grad_up_ref.refs_2_, bf16[512,2048]{1,0:T(8,128)(2,1)} %get-tuple-element.159.refs_3_), custom_call_target="tpu_custom_call" | custom-call | flops 6442450944 | bytes 20971520 | tf_op jit(solution)/shard_map/weight_grads/pallas_call | solution.py:845
  346.3 16.9 %collective-permute-done.16 = bf16[256,2048]{1,0:T(8,128)(2,1)S(1)} collective-permute-done((bf16[256,2048]{1,0:T(8,128)(2,1)S(1)}, bf16[256,2048]{1,0:T(8,128)(2,1)S(1)}, u32[]{:S(2)}, u32[]{:S(2)}) %collective-permute-start.16) | collective-permute-done | bytes 1048608 | tf_op jit(solution)/shard_map/ppermute | solution.py:50
  363.3 4.2 collective-permute-done.17
  370.4 22.2 %collective-permute-done.19 = bf16[256,2048]{1,0:T(8,128)(2,1)} collective-permute-done((bf16[256,2048]{1,0:T(8,128)(2,1)S(1)}, bf16[256,2048]{1,0:T(8,128)(2,1)}, u32[]{:S(2)}, u32[]{:S(2)}) %collective-permute-start.19) | collective-permute-done | bytes 1048608 | tf_op jit(solution)/shard_map/ppermute | solution.py:50
  397.3 18.3 %collective-permute-done.20 = bf16[256,2048]{1,0:T(8,128)(2,1)S(1)} collective-permute-done((bf16[256,2048]{1,0:T(8,128)(2,1)}, bf16[256,2048]{1,0:T(8,128)(2,1)S(1)}, u32[]{:S(2)}, u32[]{:S(2)}) %collective-permute-start.20) | collective-permute-done | bytes 1048608 | tf_op jit(solution)/shard_map/ppermute | solution.py:50
  419.3 8.4 fusion.2
  428.0 11.3 %fusion.7.joint_ref = f32[1024,1024]{1,0:T(8,128)} fusion(bf16[2048,3712]{1,0:T(8,128)(2,1)} %all-gather.3.cloned.1.call-done.w_ref, bf16[256,2048]{1,0:T(8,128)(2,1)S(1)} %copy-done.14, bf16[256,2048]{1,0:T(8,128)(2,1)S(1)} %copy-done.12, bf16[256,2048]{1,0:T(8,128)(2,1)S(1)} %copy-done.16, bf16[256,2048]{1,0:T(8,128)(2,1)S(1)} %copy-done.10), kind=kOutput, calls=%fused_computation.14 | convolution fusion | flops 4311744512 | bytes 12582912 | tf_op jit(solution)/shard_map/dot_general | solution.py:140
  439.4 32.1 %mixer_backward.1 = (bf16[1024,2688]{1,0:T(8,128)(2,1)}, f32[8,128]{1,0:T(8,128)}) custom-call(s32[1]{0:T(128)} %bitcast.1.place_ref, f32[1024,2688]{1,0:T(8,128)} %get-tuple-element.135.mixed_ref, f32[1024,1024]{1,0:T(8,128)} %fusion.7.joint_ref, f32[4,256,768]{2,1,0:T(8,128)} %get-tuple-element.166.state_ref, ...), custom_call_target="tpu_custom_call" | custom-call | flops 20000000000 | bytes 30000000 | tf_op jit(solution)/shard_map/mixer_backward/pallas_call | solution.py:583
  476.6 19.1 %fusion = f32[1024,2048]{1,0:T(8,128)} fusion(bf16[1024,2688]{1,0:T(8,128)(2,1)} %get-tuple-element.176.refs_2_, bf16[2048,3712]{1,0:T(8,128)(2,1)} %all-gather.3.cloned.1.call-done.w_ref), kind=kOutput, calls=%fused_computation | convolution fusion | flops 11274289152 | bytes 24903680 | tf_op jit(solution)/shard_map/dot_general | solution.py:140
  495.9 5.7 multiply_reduce_fusion
  501.6 3.9 fusion.43
  508.3 9.5 %collective-permute-start.27 = (bf16[256,2048]{1,0:T(8,128)(2,1)}, bf16[256,2048]{1,0:T(8,128)(2,1)}, u32[]{:S(2)}, u32[]{:S(2)}) collective-permute-start(bf16[256,2048]{1,0:T(8,128)(2,1)} %get-tuple-element.183), channel_id=1, source_target_pairs={{0,1},{4,5},{8,9},{12,13},{16,17},{20,21},{24,25},{28,29}} | collective-permute-start | bytes 3145736 | tf_op jit(solution)/shard_map/ppermute | solution.py:50
  520.4 23.1 %weight_grads.5 = bf16[2048,3712]{1,0:T(8,128)(2,1)} custom-call(bf16[1024,2048]{1,0:T(8,128)(2,1)} %get-tuple-element.185.refs_0_, bf16[1024,2048]{1,0:T(8,128)(2,1)} %pad_maximum_fusion.refs_1_, bf16[1024,2688]{1,0:T(8,128)(2,1)} %get-tuple-element.176.refs_2_, bf16[1024,1024]{1,0:T(8,128)(2,1)} %get-tuple-element.138.refs_3_, ...), custom_call_target="tpu_custom_call" | custom-call | flops 15569256448 | bytes 31260672 | tf_op jit(solution)/shard_map/weight_grads/pallas_call | solution.py:845
  547.8 4.0 add_convert_fusion.2
  559.2 6.0 collective-permute-start.29
  566.0 7.1 collective-permute-done.44
  573.2 13.6 %collective-permute-done.31 = bf16[128,3072]{1,0:T(8,128)(2,1)S(1)} collective-permute-done((bf16[128,3072]{1,0:T(8,128)(2,1)S(1)}, bf16[128,3072]{1,0:T(8,128)(2,1)S(1)}, u32[]{:S(2)}, u32[]{:S(2)}) %collective-permute-start.31) | collective-permute-done | bytes 786464 | tf_op jit(solution)/shard_map/ppermute | solution.py:50
  593.3 18.5 %collective-permute-start.34 = (bf16[128,3072]{1,0:T(8,128)(2,1)S(1)}, bf16[128,3072]{1,0:T(8,128)(2,1)S(1)}, u32[]{:S(2)}, u32[]{:S(2)}) collective-permute-start(bf16[128,3072]{1,0:T(8,128)(2,1)S(1)} %add_convert_fusion.8), channel_id=1, source_target_pairs={{0,1},{1,2},{2,3},{4,5},{5,6},{6,7},{8,9},{9,10},{10,11},{12,13},{... | collective-permute-start | bytes 2359304 | tf_op jit(solution)/shard_map/ppermute | solution.py:50
  616.7 6.1 collective-permute-start.32
  622.8 7.0 collective-permute-done.34
  634.4 15.4 %reduce-scatter.8.cloned.1.call-done.refs_0_ = bf16[256,3712]{1,0:T(8,128)(2,1)} async-done(((bf16[2048,3712]{1,0:T(8,128)(2,1)}), bf16[256,3712]{1,0:T(8,128)(2,1)}) %reduce-scatter.8.cloned.1.call-update) | async-done | bytes 1900560 | tf_op jit(solution)/shard_map/reduce_scatter | solution.py:136
  663.8 51.5 %collective-permute-done.38 = bf16[128,3072]{1,0:T(8,128)(2,1)S(1)} collective-permute-done((bf16[128,3072]{1,0:T(8,128)(2,1)}, bf16[128,3072]{1,0:T(8,128)(2,1)S(1)}, u32[]{:S(2)}, u32[]{:S(2)}) %collective-permute-start.38) | collective-permute-done | bytes 786464 | tf_op jit(solution)/shard_map/ppermute | solution.py:50
  716.7 4.6 fusion.22
  724.2 13.6 %collective-permute-done.46 = bf16[128,3072]{1,0:T(8,128)(2,1)S(1)} collective-permute-done((bf16[128,3072]{1,0:T(8,128)(2,1)S(1)}, bf16[128,3072]{1,0:T(8,128)(2,1)S(1)}, u32[]{:S(2)}, u32[]{:S(2)}) %collective-permute-start.46) | collective-permute-done | bytes 786464 | tf_op jit(solution)/shard_map/ppermute | solution.py:50
  741.6 34.5 %collective-permute-done.41.refs_5_ = bf16[256,3712]{1,0:T(8,128)(2,1)S(1)} collective-permute-done((bf16[256,3712]{1,0:T(8,128)(2,1)S(1)}, bf16[256,3712]{1,0:T(8,128)(2,1)S(1)}, u32[]{:S(2)}, u32[]{:S(2)}) %collective-permute-start.41) | collective-permute-done | bytes 1900576 | tf_op jit(solution)/shard_map/ppermute | solution.py:50
  783.1 36.7 %collective-permute-done.43.refs_6_ = bf16[256,3712]{1,0:T(8,128)(2,1)S(1)} collective-permute-done((bf16[256,3712]{1,0:T(8,128)(2,1)S(1)}, bf16[256,3712]{1,0:T(8,128)(2,1)S(1)}, u32[]{:S(2)}, u32[]{:S(2)}) %collective-permute-start.43) | collective-permute-done | bytes 1900576 | tf_op jit(solution)/shard_map/ppermute | solution.py:50
  821.1 9.6 %unpack_mixer.1 = (f32[256,8192]{1,0:T(8,128)}, f32[256,1024]{1,0:T(8,128)}, f32[256,3072]{1,0:T(8,128)}, f32[256,128]{1,0:T(8,128)}) custom-call(s32[1]{0:T(128)} %bitcast.1.place_ref, bf16[256,3712]{1,0:T(8,128)(2,1)} %reduce-scatter.8.cloned.1.call-done.refs_0_, bf16[256,3712]{1,0:T(8,128)(2,1)} %copy-done.20, bf16[256,3712]{1,0:T(8,128)(2,1)} %copy-done.22, ...), custom_call_target="tpu_custom_call" | custom-call | flops 100000000 | bytes 26000000 | tf_op jit(solution)/shard_map/unpack_mixer/pallas_call | solution.py:930
  (273 shorter events, 143.3 us)
Async XLA Ops:
  7.2 99.5 %all-gather.3.cloned.1.call-start = ((), (), s32[]{:S(2)}) async-start(), calls=%async_computation.3 | async-start | bytes 17104896 | tf_op jit(solution)/shard_map/all_gather | solution.py:132
  15.0 229.9 %all-gather.5.cloned.1.call-start = ((), (), s32[]{:S(2)}) async-start(), calls=%async_computation.4 | async-start | bytes 28311552 | tf_op jit(solution)/shard_map/all_gather | solution.py:132
  15.7 403.3 %reduce-scatter.4.cloned.1.call-start = ((), (), s32[]{:S(2)}) async-start(), calls=%async_computation.5 | async-start | bytes 14155776 | tf_op jit(solution)/shard_map/reduce_scatter | solution.py:136
  16.1 27.3 %collective-permute-start = (bf16[256,2048]{1,0:T(8,128)(2,1)S(1)}, bf16[256,2048]{1,0:T(8,128)(2,1)}, u32[]{:S(2)}, u32[]{:S(2)}) collective-permute-start(bf16[256,2048]{1,0:T(8,128)(2,1)S(1)} %bitcast.126), channel_id=1, source_target_pairs={{0,1},{1,2},{2,3},{4,5},{5,6},{6,7},{8,9},{9,10},{10,11},{12,13},{... | collective-permute-start | bytes 3145736 | tf_op jit(solution)/shard_map/ppermute | solution.py:50
  22.0 26.6 %collective-permute-start.1 = (bf16[256,2048]{1,0:T(8,128)(2,1)S(1)}, bf16[256,2048]{1,0:T(8,128)(2,1)}, u32[]{:S(2)}, u32[]{:S(2)}) collective-permute-start(bf16[256,2048]{1,0:T(8,128)(2,1)S(1)} %bitcast.127), channel_id=1, source_target_pairs={{1,0},{2,1},{3,2},{5,4},{6,5},{7,6},{9,8},{10,9},{11,10},{13,12},{... | collective-permute-start | bytes 3145736 | tf_op jit(solution)/shard_map/ppermute | solution.py:50
  50.3 27.3 %collective-permute-start.3 = (bf16[256,2048]{1,0:T(8,128)(2,1)}, bf16[256,2048]{1,0:T(8,128)(2,1)}, u32[]{:S(2)}, u32[]{:S(2)}) collective-permute-start(bf16[256,2048]{1,0:T(8,128)(2,1)} %collective-permute-done.1.refs_4_), channel_id=1, source_target_pairs={{1,0},{2,1},{5,4},{6,5},{9,8},{10,9},{13,12},{14,13},{17,16},{18,1... | collective-permute-start | bytes 3145736 | tf_op jit(solution)/shard_map/ppermute | solution.py:50
  77.7 6.7 collective-permute-start.4
  78.4 28.3 %collective-permute-start.5 = (bf16[256,2048]{1,0:T(8,128)(2,1)}, bf16[256,2048]{1,0:T(8,128)(2,1)}, u32[]{:S(2)}, u32[]{:S(2)}) collective-permute-start(bf16[256,2048]{1,0:T(8,128)(2,1)} %collective-permute-done.3.refs_5_), channel_id=1, source_target_pairs={{1,0},{5,4},{9,8},{13,12},{17,16},{21,20},{25,24},{29,28}} | collective-permute-start | bytes 3145736 | tf_op jit(solution)/shard_map/ppermute | solution.py:50
  85.3 63.3 %collective-permute-start.6 = (bf16[256,2048]{1,0:T(8,128)(2,1)S(1)}, bf16[256,2048]{1,0:T(8,128)(2,1)S(1)}, u32[]{:S(2)}, u32[]{:S(2)}) collective-permute-start(bf16[256,2048]{1,0:T(8,128)(2,1)S(1)} %bitcast.129), channel_id=1, source_target_pairs={{0,1},{1,0},{2,3},{3,2},{4,5},{5,4},{6,7},{7,6},{8,9},{9,8},{10,11... | collective-permute-start | bytes 3145736 | tf_op jit(solution)/shard_map/ppermute | solution.py:29
  157.6 19.7 %collective-permute-start.7 = (bf16[256,2048]{1,0:T(8,128)(2,1)S(1)}, bf16[256,2048]{1,0:T(8,128)(2,1)S(1)}, u32[]{:S(2)}, u32[]{:S(2)}) collective-permute-start(bf16[256,2048]{1,0:T(8,128)(2,1)S(1)} %get-tuple-element.139), channel_id=1, source_target_pairs={{0,1},{4,5},{8,9},{12,13},{16,17},{20,21},{24,25},{28,29}} | collective-permute-start | bytes 3145736 | tf_op jit(solution)/shard_map/ppermute | solution.py:50
  180.9 22.0 %collective-permute-start.9 = (bf16[256,2048]{1,0:T(8,128)(2,1)S(1)}, bf16[256,2048]{1,0:T(8,128)(2,1)S(1)}, u32[]{:S(2)}, u32[]{:S(2)}) collective-permute-start(bf16[256,2048]{1,0:T(8,128)(2,1)S(1)} %get-tuple-element.141), channel_id=1, source_target_pairs={{0,1},{1,2},{4,5},{5,6},{8,9},{9,10},{12,13},{13,14},{16,17},{17,1... | collective-permute-start | bytes 3145736 | tf_op jit(solution)/shard_map/ppermute | solution.py:50
  185.4 17.8 %collective-permute-start.10 = (bf16[256,2048]{1,0:T(8,128)(2,1)S(1)}, bf16[256,2048]{1,0:T(8,128)(2,1)S(1)}, u32[]{:S(2)}, u32[]{:S(2)}) collective-permute-start(bf16[256,2048]{1,0:T(8,128)(2,1)S(1)} %get-tuple-element.142), channel_id=1, source_target_pairs={{2,1},{3,2},{6,5},{7,6},{10,9},{11,10},{14,13},{15,14},{18,17},{19... | collective-permute-start | bytes 3145736 | tf_op jit(solution)/shard_map/ppermute | solution.py:50
  203.6 32.4 %collective-permute-start.12 = (bf16[256,2048]{1,0:T(8,128)(2,1)S(1)}, bf16[256,2048]{1,0:T(8,128)(2,1)S(1)}, u32[]{:S(2)}, u32[]{:S(2)}) collective-permute-start(bf16[256,2048]{1,0:T(8,128)(2,1)S(1)} %add_convert_fusion.4), channel_id=1, source_target_pairs={{1,0},{2,1},{3,2},{5,4},{6,5},{7,6},{9,8},{10,9},{11,10},{13,12},{... | collective-permute-start | bytes 3145736 | tf_op jit(solution)/shard_map/ppermute | solution.py:50
  204.9 32.3 %collective-permute-start.11 = (bf16[256,2048]{1,0:T(8,128)(2,1)S(1)}, bf16[256,2048]{1,0:T(8,128)(2,1)S(1)}, u32[]{:S(2)}, u32[]{:S(2)}) collective-permute-start(bf16[256,2048]{1,0:T(8,128)(2,1)S(1)} %add_convert_fusion.5), channel_id=1, source_target_pairs={{0,1},{1,2},{2,3},{4,5},{5,6},{6,7},{8,9},{9,10},{10,11},{12,13},{... | collective-permute-start | bytes 3145736 | tf_op jit(solution)/shard_map/ppermute | solution.py:50
  242.4 23.5 %collective-permute-start.13 = (bf16[256,2048]{1,0:T(8,128)(2,1)}, bf16[256,2048]{1,0:T(8,128)(2,1)}, u32[]{:S(2)}, u32[]{:S(2)}) collective-permute-start(bf16[256,2048]{1,0:T(8,128)(2,1)} %multiply_convert_fusion), channel_id=1, source_target_pairs={{0,1},{1,0},{2,3},{3,2},{4,5},{5,4},{6,7},{7,6},{8,9},{9,8},{10,11... | collective-permute-start | bytes 3145736 | tf_op jit(solution)/shard_map/ppermute | solution.py:29
  313.3 230.2 %reduce-scatter.6.cloned.1.call-start = ((), (), s32[]{:S(2)}) async-start(), calls=%async_computation.6 | async-start | bytes 14155776 | tf_op jit(solution)/shard_map/reduce_scatter | solution.py:136
  313.4 22.2 %collective-permute-start.14 = (bf16[256,2048]{1,0:T(8,128)(2,1)}, bf16[256,2048]{1,0:T(8,128)(2,1)}, u32[]{:S(2)}, u32[]{:S(2)}) collective-permute-start(bf16[256,2048]{1,0:T(8,128)(2,1)} %get-tuple-element.152), channel_id=1, source_target_pairs={{0,1},{1,0},{2,3},{3,2},{4,5},{5,4},{6,7},{7,6},{8,9},{9,8},{10,11... | collective-permute-start | bytes 3145736 | tf_op jit(solution)/shard_map/ppermute | solution.py:29
  341.6 21.7 %collective-permute-start.16 = (bf16[256,2048]{1,0:T(8,128)(2,1)S(1)}, bf16[256,2048]{1,0:T(8,128)(2,1)S(1)}, u32[]{:S(2)}, u32[]{:S(2)}) collective-permute-start(bf16[256,2048]{1,0:T(8,128)(2,1)S(1)} %get-tuple-element.161), channel_id=1, source_target_pairs={{0,1},{1,2},{2,3},{4,5},{5,6},{6,7},{8,9},{9,10},{10,11},{12,13},{... | collective-permute-start | bytes 3145736 | tf_op jit(solution)/shard_map/ppermute | solution.py:50
  345.0 22.4 %collective-permute-start.17 = (bf16[256,2048]{1,0:T(8,128)(2,1)S(1)}, bf16[256,2048]{1,0:T(8,128)(2,1)S(1)}, u32[]{:S(2)}, u32[]{:S(2)}) collective-permute-start(bf16[256,2048]{1,0:T(8,128)(2,1)S(1)} %get-tuple-element.161), channel_id=1, source_target_pairs={{1,0},{2,1},{3,2},{5,4},{6,5},{7,6},{9,8},{10,9},{11,10},{13,12},{... | collective-permute-start | bytes 3145736 | tf_op jit(solution)/shard_map/ppermute | solution.py:50
  369.1 23.5 %collective-permute-start.19 = (bf16[256,2048]{1,0:T(8,128)(2,1)S(1)}, bf16[256,2048]{1,0:T(8,128)(2,1)}, u32[]{:S(2)}, u32[]{:S(2)}) collective-permute-start(bf16[256,2048]{1,0:T(8,128)(2,1)S(1)} %collective-permute-done.17), channel_id=1, source_target_pairs={{1,0},{2,1},{5,4},{6,5},{9,8},{10,9},{13,12},{14,13},{17,16},{18,1... | collective-permute-start | bytes 3145736 | tf_op jit(solution)/shard_map/ppermute | solution.py:50
  394.3 21.3 %collective-permute-start.20 = (bf16[256,2048]{1,0:T(8,128)(2,1)}, bf16[256,2048]{1,0:T(8,128)(2,1)S(1)}, u32[]{:S(2)}, u32[]{:S(2)}) collective-permute-start(bf16[256,2048]{1,0:T(8,128)(2,1)} %collective-permute-done.19), channel_id=1, source_target_pairs={{1,0},{5,4},{9,8},{13,12},{17,16},{21,20},{25,24},{29,28}} | collective-permute-start | bytes 3145736 | tf_op jit(solution)/shard_map/ppermute | solution.py:50
  419.1 230.6 %reduce-scatter.8.cloned.1.call-start = ((), (), s32[]{:S(2)}) async-start(), calls=%async_computation.7 | async-start | bytes 17104896 | tf_op jit(solution)/shard_map/reduce_scatter | solution.py:136
  427.9 43.6 %collective-permute-start.22 = (bf16[256,2048]{1,0:T(8,128)(2,1)S(1)}, bf16[256,2048]{1,0:T(8,128)(2,1)S(1)}, u32[]{:S(2)}, u32[]{:S(2)}) collective-permute-start(bf16[256,2048]{1,0:T(8,128)(2,1)S(1)} %slice.321), channel_id=1, source_target_pairs={{0,1},{1,0},{2,3},{3,2},{4,5},{5,4},{6,7},{7,6},{8,9},{9,8},{10,11... | collective-permute-start | bytes 3145736 | tf_op jit(solution)/shard_map/ppermute | solution.py:29
  439.3 32.2 %collective-permute-start.15 = (bf16[128,3072]{1,0:T(8,128)(2,1)S(1)}, bf16[128,3072]{1,0:T(8,128)(2,1)S(1)}, u32[]{:S(2)}, u32[]{:S(2)}) collective-permute-start(bf16[128,3072]{1,0:T(8,128)(2,1)S(1)} %constant_dynamic-slice_fusion.1), channel_id=1, source_target_pairs={{0,2},{1,3},{2,0},{3,1},{4,6},{5,7},{6,4},{7,5},{8,10},{9,11},{10,... | collective-permute-start | bytes 2359304 | tf_op jit(solution)/shard_map/ppermute | solution.py:50
  471.8 29.8 %collective-permute-start.23 = (bf16[128,3072]{1,0:T(8,128)(2,1)S(1)}, bf16[128,3072]{1,0:T(8,128)(2,1)}, u32[]{:S(2)}, u32[]{:S(2)}) collective-permute-start(bf16[128,3072]{1,0:T(8,128)(2,1)S(1)} %add_convert_fusion.9), channel_id=1, source_target_pairs={{0,1},{1,2},{2,3},{4,5},{5,6},{6,7},{8,9},{9,10},{10,11},{12,13},{... | collective-permute-start | bytes 2359304 | tf_op jit(solution)/shard_map/ppermute | solution.py:50
  475.3 26.3 %collective-permute-start.24 = (bf16[128,3072]{1,0:T(8,128)(2,1)S(1)}, bf16[128,3072]{1,0:T(8,128)(2,1)}, u32[]{:S(2)}, u32[]{:S(2)}) collective-permute-start(bf16[128,3072]{1,0:T(8,128)(2,1)S(1)} %add_convert_fusion.9), channel_id=1, source_target_pairs={{1,0},{2,1},{3,2},{5,4},{6,5},{7,6},{9,8},{10,9},{11,10},{13,12},{... | collective-permute-start | bytes 2359304 | tf_op jit(solution)/shard_map/ppermute | solution.py:50
  505.5 38.0 %collective-permute-start.25 = (bf16[128,3072]{1,0:T(8,128)(2,1)}, bf16[128,3072]{1,0:T(8,128)(2,1)}, u32[]{:S(2)}, u32[]{:S(2)}) collective-permute-start(bf16[128,3072]{1,0:T(8,128)(2,1)} %collective-permute-done.23), channel_id=1, source_target_pairs={{1,2},{2,3},{5,6},{6,7},{9,10},{10,11},{13,14},{14,15},{17,18},{18... | collective-permute-start | bytes 2359304 | tf_op jit(solution)/shard_map/ppermute | solution.py:50
  507.0 36.5 %collective-permute-start.26 = (bf16[128,3072]{1,0:T(8,128)(2,1)}, bf16[128,3072]{1,0:T(8,128)(2,1)}, u32[]{:S(2)}, u32[]{:S(2)}) collective-permute-start(bf16[128,3072]{1,0:T(8,128)(2,1)} %collective-permute-done.24), channel_id=1, source_target_pairs={{1,0},{2,1},{5,4},{6,5},{9,8},{10,9},{13,12},{14,13},{17,16},{18,1... | collective-permute-start | bytes 2359304 | tf_op jit(solution)/shard_map/ppermute | solution.py:50
  508.3 35.2 %collective-permute-start.27 = (bf16[256,2048]{1,0:T(8,128)(2,1)}, bf16[256,2048]{1,0:T(8,128)(2,1)}, u32[]{:S(2)}, u32[]{:S(2)}) collective-permute-start(bf16[256,2048]{1,0:T(8,128)(2,1)} %get-tuple-element.183), channel_id=1, source_target_pairs={{0,1},{4,5},{8,9},{12,13},{16,17},{20,21},{24,25},{28,29}} | collective-permute-start | bytes 3145736 | tf_op jit(solution)/shard_map/ppermute | solution.py:50
  517.8 25.7 %collective-permute-start.28 = (bf16[256,2048]{1,0:T(8,128)(2,1)}, bf16[256,2048]{1,0:T(8,128)(2,1)}, u32[]{:S(2)}, u32[]{:S(2)}) collective-permute-start(bf16[256,2048]{1,0:T(8,128)(2,1)} %get-tuple-element.184), channel_id=1, source_target_pairs={{3,2},{7,6},{11,10},{15,14},{19,18},{23,22},{27,26},{31,30}} | collective-permute-start | bytes 3145736 | tf_op jit(solution)/shard_map/ppermute | solution.py:50
  551.9 21.2 %collective-permute-start.44 = (bf16[128,3072]{1,0:T(8,128)(2,1)}, bf16[128,3072]{1,0:T(8,128)(2,1)S(1)}, u32[]{:S(2)}, u32[]{:S(2)}) collective-permute-start(bf16[128,3072]{1,0:T(8,128)(2,1)} %collective-permute-done.26), channel_id=1, source_target_pairs={{1,0},{5,4},{9,8},{13,12},{17,16},{21,20},{25,24},{29,28}} | collective-permute-start | bytes 2359304 | tf_op jit(solution)/shard_map/ppermute | solution.py:50
  556.9 29.9 %collective-permute-start.31 = (bf16[128,3072]{1,0:T(8,128)(2,1)S(1)}, bf16[128,3072]{1,0:T(8,128)(2,1)S(1)}, u32[]{:S(2)}, u32[]{:S(2)}) collective-permute-start(bf16[128,3072]{1,0:T(8,128)(2,1)S(1)} %constant_dynamic-slice_fusion), channel_id=1, source_target_pairs={{0,2},{1,3},{2,0},{3,1},{4,6},{5,7},{6,4},{7,5},{8,10},{9,11},{10,... | collective-permute-start | bytes 2359304 | tf_op jit(solution)/shard_map/ppermute | solution.py:50
  558.5 32.2 %collective-permute-start.30 = (bf16[256,2048]{1,0:T(8,128)(2,1)S(1)}, bf16[256,2048]{1,0:T(8,128)(2,1)S(1)}, u32[]{:S(2)}, u32[]{:S(2)}) collective-permute-start(bf16[256,2048]{1,0:T(8,128)(2,1)S(1)} %get-tuple-element.195), channel_id=1, source_target_pairs={{2,1},{3,2},{6,5},{7,6},{10,9},{11,10},{14,13},{15,14},{18,17},{19... | collective-permute-start | bytes 3145736 | tf_op jit(solution)/shard_map/ppermute | solution.py:50
  559.2 31.5 %collective-permute-start.29 = (bf16[256,2048]{1,0:T(8,128)(2,1)S(1)}, bf16[256,2048]{1,0:T(8,128)(2,1)S(1)}, u32[]{:S(2)}, u32[]{:S(2)}) collective-permute-start(bf16[256,2048]{1,0:T(8,128)(2,1)S(1)} %get-tuple-element.194), channel_id=1, source_target_pairs={{0,1},{1,2},{4,5},{5,6},{8,9},{9,10},{12,13},{13,14},{16,17},{17,1... | collective-permute-start | bytes 3145736 | tf_op jit(solution)/shard_map/ppermute | solution.py:50
  565.3 48.8 %collective-permute-start.45 = (bf16[128,3072]{1,0:T(8,128)(2,1)}, bf16[128,3072]{1,0:T(8,128)(2,1)S(1)}, u32[]{:S(2)}, u32[]{:S(2)}) collective-permute-start(bf16[128,3072]{1,0:T(8,128)(2,1)} %collective-permute-done.25), channel_id=1, source_target_pairs={{2,3},{6,7},{10,11},{14,15},{18,19},{22,23},{26,27},{30,31}} | collective-permute-start | bytes 2359304 | tf_op jit(solution)/shard_map/ppermute | solution.py:50
  593.3 36.5 %collective-permute-start.34 = (bf16[128,3072]{1,0:T(8,128)(2,1)S(1)}, bf16[128,3072]{1,0:T(8,128)(2,1)S(1)}, u32[]{:S(2)}, u32[]{:S(2)}) collective-permute-start(bf16[128,3072]{1,0:T(8,128)(2,1)S(1)} %add_convert_fusion.8), channel_id=1, source_target_pairs={{0,1},{1,2},{2,3},{4,5},{5,6},{6,7},{8,9},{9,10},{10,11},{12,13},{... | collective-permute-start | bytes 2359304 | tf_op jit(solution)/shard_map/ppermute | solution.py:50
  611.9 22.5 %collective-permute-start.35 = (bf16[128,3072]{1,0:T(8,128)(2,1)S(1)}, bf16[128,3072]{1,0:T(8,128)(2,1)}, u32[]{:S(2)}, u32[]{:S(2)}) collective-permute-start(bf16[128,3072]{1,0:T(8,128)(2,1)S(1)} %add_convert_fusion.8), channel_id=1, source_target_pairs={{1,0},{2,1},{3,2},{5,4},{6,5},{7,6},{9,8},{10,9},{11,10},{13,12},{... | collective-permute-start | bytes 2359304 | tf_op jit(solution)/shard_map/ppermute | solution.py:50
  615.4 44.1 %collective-permute-start.33 = (bf16[256,2048]{1,0:T(8,128)(2,1)}, bf16[256,2048]{1,0:T(8,128)(2,1)}, u32[]{:S(2)}, u32[]{:S(2)}) collective-permute-start(bf16[256,2048]{1,0:T(8,128)(2,1)} %get-tuple-element.198), channel_id=1, source_target_pairs={{1,0},{2,1},{3,2},{5,4},{6,5},{7,6},{9,8},{10,9},{11,10},{13,12},{... | collective-permute-start | bytes 3145736 | tf_op jit(solution)/shard_map/ppermute | solution.py:50
  616.7 44.1 %collective-permute-start.32 = (bf16[256,2048]{1,0:T(8,128)(2,1)}, bf16[256,2048]{1,0:T(8,128)(2,1)}, u32[]{:S(2)}, u32[]{:S(2)}) collective-permute-start(bf16[256,2048]{1,0:T(8,128)(2,1)} %get-tuple-element.197), channel_id=1, source_target_pairs={{0,1},{1,2},{2,3},{4,5},{5,6},{6,7},{8,9},{9,10},{10,11},{12,13},{... | collective-permute-start | bytes 3145736 | tf_op jit(solution)/shard_map/ppermute | solution.py:50
  649.7 65.6 %collective-permute-start.36 = (bf16[256,3712]{1,0:T(8,128)(2,1)}, bf16[256,3712]{1,0:T(8,128)(2,1)S(1)}, u32[]{:S(2)}, u32[]{:S(2)}) collective-permute-start(bf16[256,3712]{1,0:T(8,128)(2,1)} %reduce-scatter.8.cloned.1.call-done.refs_0_), channel_id=1, source_target_pairs={{0,1},{1,2},{2,3},{4,5},{5,6},{6,7},{8,9},{9,10},{10,11},{12,13},{... | collective-permute-start | bytes 5701640 | tf_op jit(solution)/shard_map/ppermute | solution.py:50
  653.3 62.0 %collective-permute-start.39 = (bf16[256,3712]{1,0:T(8,128)(2,1)}, bf16[256,3712]{1,0:T(8,128)(2,1)S(1)}, u32[]{:S(2)}, u32[]{:S(2)}) collective-permute-start(bf16[256,3712]{1,0:T(8,128)(2,1)} %reduce-scatter.8.cloned.1.call-done.refs_0_), channel_id=1, source_target_pairs={{1,0},{2,1},{3,2},{5,4},{6,5},{7,6},{9,8},{10,9},{11,10},{13,12},{... | collective-permute-start | bytes 5701640 | tf_op jit(solution)/shard_map/ppermute | solution.py:50
  659.5 55.9 %collective-permute-start.38 = (bf16[128,3072]{1,0:T(8,128)(2,1)}, bf16[128,3072]{1,0:T(8,128)(2,1)S(1)}, u32[]{:S(2)}, u32[]{:S(2)}) collective-permute-start(bf16[128,3072]{1,0:T(8,128)(2,1)} %collective-permute-done.35), channel_id=1, source_target_pairs={{1,0},{2,1},{5,4},{6,5},{9,8},{10,9},{13,12},{14,13},{17,16},{18,1... | collective-permute-start | bytes 2359304 | tf_op jit(solution)/shard_map/ppermute | solution.py:50
  715.4 22.4 %collective-permute-start.46 = (bf16[128,3072]{1,0:T(8,128)(2,1)S(1)}, bf16[128,3072]{1,0:T(8,128)(2,1)S(1)}, u32[]{:S(2)}, u32[]{:S(2)}) collective-permute-start(bf16[128,3072]{1,0:T(8,128)(2,1)S(1)} %collective-permute-done.38), channel_id=1, source_target_pairs={{1,0},{5,4},{9,8},{13,12},{17,16},{21,20},{25,24},{29,28}} | collective-permute-start | bytes 2359304 | tf_op jit(solution)/shard_map/ppermute | solution.py:50
  721.4 20.2 %collective-permute-start.40 = (bf16[256,3712]{1,0:T(8,128)(2,1)S(1)}, bf16[256,3712]{1,0:T(8,128)(2,1)S(1)}, u32[]{:S(2)}, u32[]{:S(2)}) collective-permute-start(bf16[256,3712]{1,0:T(8,128)(2,1)S(1)} %collective-permute-done.36.refs_1_), channel_id=1, source_target_pairs={{1,2},{2,3},{5,6},{6,7},{9,10},{10,11},{13,14},{14,15},{17,18},{18... | collective-permute-start | bytes 5701640 | tf_op jit(solution)/shard_map/ppermute | solution.py:50
  722.2 53.9 %collective-permute-start.41 = (bf16[256,3712]{1,0:T(8,128)(2,1)S(1)}, bf16[256,3712]{1,0:T(8,128)(2,1)S(1)}, u32[]{:S(2)}, u32[]{:S(2)}) collective-permute-start(bf16[256,3712]{1,0:T(8,128)(2,1)S(1)} %collective-permute-done.39.refs_4_), channel_id=1, source_target_pairs={{1,0},{2,1},{5,4},{6,5},{9,8},{10,9},{13,12},{14,13},{17,16},{18,1... | collective-permute-start | bytes 5701640 | tf_op jit(solution)/shard_map/ppermute | solution.py:50
  723.5 16.9 %collective-permute-start.47 = (bf16[128,3072]{1,0:T(8,128)(2,1)S(1)}, bf16[128,3072]{1,0:T(8,128)(2,1)S(1)}, u32[]{:S(2)}, u32[]{:S(2)}) collective-permute-start(bf16[128,3072]{1,0:T(8,128)(2,1)S(1)} %collective-permute-done.37), channel_id=1, source_target_pairs={{2,3},{6,7},{10,11},{14,15},{18,19},{22,23},{26,27},{30,31}} | collective-permute-start | bytes 2359304 | tf_op jit(solution)/shard_map/ppermute | solution.py:50
  776.1 7.0 collective-permute-start.42
  776.9 42.9 %collective-permute-start.43 = (bf16[256,3712]{1,0:T(8,128)(2,1)S(1)}, bf16[256,3712]{1,0:T(8,128)(2,1)S(1)}, u32[]{:S(2)}, u32[]{:S(2)}) collective-permute-start(bf16[256,3712]{1,0:T(8,128)(2,1)S(1)} %collective-permute-done.41.refs_5_), channel_id=1, source_target_pairs={{1,0},{5,4},{9,8},{13,12},{17,16},{21,20},{25,24},{29,28}} | collective-permute-start | bytes 5701640 | tf_op jit(solution)/shard_map/ppermute | solution.py:50
  (53 other events, 947.4 us)
Sparse Core Ops, SparseCore 0:
  15.1 85.9 all-gather.2
  103.5 125.3 all-gather.4
  313.5 91.5 reduce-scatter.3
  419.2 89.5 reduce-scatter.5
  543.7 105.9 reduce-scatter.7

commit v3 on v2

--- a/solution.py
+++ b/solution.py
@@ -44,18 +44,31 @@
             self.sends, self.result = None, stop.value
 
 
+class Flight:
+    def __init__(self, *chains):
+        self.chains = chains
+        sends = [send for chain in chains for send in chain.sends]
+        self.values = lax.optimization_barrier(tuple(value for value, _ in sends))
+        self.got = tuple(
+            lax.ppermute(v, "ctx", pairs) for v, (_, pairs) in zip(self.values, sends)
+        )
+
+    def land(self, beside=()):
+        sealed = lax.optimization_barrier(self.got + tuple(beside))
+        got = sealed[: len(self.got)]
+        for chain in self.chains:
+            count = len(chain.sends)
+            chain.take(got[:count])
+            got = got[count:]
+        return sealed[len(self.got) :]
+
+
 def advance(*chains, beside=()):
-    sends = [send for chain in chains for send in chain.sends]
-    values = lax.optimization_barrier(tuple(value for value, _ in sends))
-    got = tuple(lax.ppermute(v, "ctx", pairs) for v, (_, pairs) in zip(values, sends))
-    if beside:
-        sealed = lax.optimization_barrier(got + tuple(beside))
-        got, beside = sealed[: len(got)], sealed[len(got) :]
-    for chain in chains:
-        count = len(chain.sends)
-        chain.take(got[:count])
-        got = got[count:]
-    return beside
+    return Flight(*chains).land(beside)
+
+
+def live(*chains):
+    return [chain for chain in chains if chain.sends is not None]
 
 
 def finish(steps):
@@ -736,8 +749,23 @@
     )(place, gain, weight, own, *ups, *downs)
 
 
-def ffn_kernel(x_ref, act_grad_ref, gate_ref, up_ref, activated_ref, grad_gate_ref, grad_up_ref):
-    rows = x_ref[...]
+def ffn_kernel(
+    own_ref,
+    other_ref,
+    act_grad_ref,
+    gate_ref,
+    up_ref,
+    activated_ref,
+    grad_gate_ref,
+    grad_up_ref,
+    rows_ref,
+):
+    @pl.when(pl.program_id(0) == 0)
+    def _():
+        rows_ref[: own_ref.shape[0], :] = own_ref[...]
+        rows_ref[own_ref.shape[0] :, :] = other_ref[...]
+
+    rows = rows_ref[...]
     gate = mul(rows, gate_ref[...], 1, 0)
     up = mul(rows, up_ref[...], 1, 0)
     grad = act_grad_ref[...]
@@ -748,8 +776,8 @@
     grad_up_ref[...] = (grad * silu).astype(BF16)
 
 
-def ffn_inner(x, act_grad, weights):
-    tokens, depth = x.shape
+def ffn_inner(own, other, act_grad, weights):
+    tokens, depth = 2 * own.shape[0], own.shape[1]
     units = act_grad.shape[1]
     tile = 256
     tiles = units // tile
@@ -759,50 +787,131 @@
         ffn_kernel,
         grid=(tiles,),
         in_specs=[
-            pl.BlockSpec((tokens, depth), lambda j: (0, 0)),
+            pl.BlockSpec(own.shape, lambda j: (0, 0)),
+            pl.BlockSpec(own.shape, lambda j: (0, 0)),
             by_unit,
             pl.BlockSpec((depth, tile), lambda j: (0, tiles + j)),
             pl.BlockSpec((depth, tile), lambda j: (0, 2 * tiles + j)),
         ],
-        out_specs=[by_unit] * 3,
-        out_shape=[out] * 3,
+        out_specs=[by_unit] * 3 + [pl.BlockSpec((tokens, depth), lambda j: (0, 0))],
+        out_shape=[out] * 3 + [jax.ShapeDtypeStruct((tokens, depth), BF16)],
         compiler_params=pltpu.CompilerParams(vmem_limit_bytes=VMEM_LIMIT),
         cost_estimate=dense_cost(4 * tokens * depth * units, weights, out, out, out),
         name="ffn_inner",
-    )(x, act_grad, weights, weights)
-
-
-def ffn_back_kernel(grad_gate_ref, grad_up_ref, gate_ref, up_ref, own_ref, other_ref):
-    total = mul(grad_gate_ref[...], gate_ref[...], 1, 1) + mul(grad_up_ref[...], up_ref[...], 1, 1)
+    )(own, other, act_grad, weights, weights)
+
+
+def ffn_back_kernel(count, *refs):
+    own_ref, other_ref = refs[-2:]
+    total = mul(refs[0][...], refs[count][...], 1, 1)
+    for i in range(1, count):
+        total = total + mul(refs[i][...], refs[count + i][...], 1, 1)
     half = total.shape[0] // 2
     own_ref[...] = total[:half]
     other_ref[...] = total[half:].astype(BF16)
 
 
-def ffn_back(grad_gate, grad_up, weights):
-    tokens, units = grad_gate.shape
+def ffn_back(grads, weights, columns):
+    tokens, units = grads[0].shape
     depth = weights.shape[0]
     tile = 256
-    whole_rows = pl.BlockSpec((tokens, units), lambda j: (0, 0))
     half = pl.BlockSpec((tokens // 2, tile), lambda j: (0, j))
     return pl.pallas_call(
-        ffn_back_kernel,
+        functools.partial(ffn_back_kernel, len(grads)),
         grid=(depth // tile,),
-        in_specs=[
-            whole_rows,
-            whole_rows,
-            pl.BlockSpec((tile, units), lambda j: (j, 1)),
-            pl.BlockSpec((tile, units), lambda j: (j, 2)),
-        ],
+        in_specs=[pl.BlockSpec((tokens, units), lambda j: (0, 0)) for _ in grads]
+        + [pl.BlockSpec((tile, units), lambda j, c=c: (j, c)) for c in columns],
         out_specs=[half, half],
         out_shape=[
             jax.ShapeDtypeStruct((tokens // 2, depth), F32),
             jax.ShapeDtypeStruct((tokens // 2, depth), BF16),
         ],
         compiler_params=pltpu.CompilerParams(vmem_limit_bytes=VMEM_LIMIT),
-        cost_estimate=dense_cost(4 * tokens * depth * units, weights),
+        cost_estimate=dense_cost(2 * len(grads) * tokens * depth * units, weights),
         name="ffn_back",
-    )(grad_gate, grad_up, weights, weights)
+    )(*grads, *[weights for _ in columns])
+
+
+def joint_kernel(count, place_ref, w_ref, *refs):
+    parts = refs[: 2 * count - 1]
+    out_ref, rows_ref = refs[2 * count - 1 :]
+    size = parts[0].shape[0]
+
+    @pl.when(pl.program_id(0) == 0)
+    def _():
+        rows_ref[:size, :] = parts[0][...]
+        for hop in range(1, count):
+            rows_ref[hop * size : (hop + 1) * size, :] = jnp.where(
+                place_ref[0] >= hop,
+                parts[hop][...].astype(F32),
+                parts[2 * count - 1 - hop][...].astype(F32),
+            ).astype(BF16)
+
+    out_ref[...] = mul(rows_ref[...], w_ref[...], 1, 0)
+
+
+def joint(place, own, ups, downs, weight):
+    size, depth = own.shape
+    count = len(ups) + 1
+    tokens, wide = size * count, weight.shape[1]
+    tile = min(wide, 512)
+
+    def fixed(shape):
+        return pl.BlockSpec(shape, lambda j, place: (0, 0))
+
+    outs = [
+        jax.ShapeDtypeStruct((tokens, wide), F32),
+        jax.ShapeDtypeStruct((tokens, depth), BF16),
+    ]
+    return pl.pallas_call(
+        functools.partial(joint_kernel, count),
+        grid_spec=pltpu.PrefetchScalarGridSpec(
+            num_scalar_prefetch=1,
+            grid=(wide // tile,),
+            in_specs=[pl.BlockSpec((depth, tile), lambda j, place: (0, j))]
+            + [fixed((size, depth))] * (2 * count - 1),
+            out_specs=[
+                pl.BlockSpec((tokens, tile), lambda j, place: (0, j)),
+                fixed((tokens, depth)),
+            ],
+        ),
+        out_shape=outs,
+        compiler_params=pltpu.CompilerParams(vmem_limit_bytes=VMEM_LIMIT),
+        cost_estimate=dense_cost(2 * tokens * depth * wide, weight, *outs),
+        name="joint",
+    )(place, weight, own, *ups, *downs)
+
+
+def mixer_out_kernel(grad_ref, w_ref, scaled_ref, gain_ref, own_ref, *other_refs):
+    total = mul(grad_ref[...], w_ref[:, : grad_ref.shape[1]], 1, 1)
+    size = own_ref.shape[0]
+    own_ref[...] = total[:size]
+    for hop, ref in enumerate(other_refs, 1):
+        ref[...] = total[hop * size : (hop + 1) * size].astype(BF16)
+    sums = jnp.sum(total * scaled_ref[...].astype(F32), axis=0, keepdims=True)
+    gain_ref[...] = jnp.broadcast_to(sums, gain_ref.shape)
+
+
+def mixer_out(grad, weights, scaled, size):
+    tokens, wide = grad.shape
+    depth = weights.shape[0]
+    tile = 256
+    outs = [jax.ShapeDtypeStruct((8, depth), F32), jax.ShapeDtypeStruct((size, depth), F32)]
+    outs += [jax.ShapeDtypeStruct((size, depth), BF16)] * (tokens // size - 1)
+    return pl.pallas_call(
+        mixer_out_kernel,
+        grid=(depth // tile,),
+        in_specs=[
+            pl.BlockSpec((tokens, wide), lambda j: (0, 0)),
+            pl.BlockSpec((tile, weights.shape[1]), lambda j: (j, 0)),
+            pl.BlockSpec((tokens, tile), lambda j: (0, j)),
+        ],
+        out_specs=[pl.BlockSpec((o.shape[0], tile), lambda j: (0, j)) for o in outs],
+        out_shape=outs,
+        compiler_params=pltpu.CompilerParams(vmem_limit_bytes=VMEM_LIMIT),
+        cost_estimate=dense_cost(2 * tokens * depth * wide, grad, weights, scaled, *outs),
+        name="mixer_out",
+    )(grad, weights, scaled)
 
 
 def outer_kernel(pairs, rider_at, *refs):
@@ -854,9 +963,10 @@
     )(*operands)
 
 
-def unpack_kernel(cuts, out_at, q_heads, heads, gain_columns, count, place_ref, *refs):
-    parts = refs[: 2 * count - 1]
-    mix_ref, attn_ref, ssm_ref, extra_ref = refs[2 * count - 1 :]
+def unpack_kernel(places, q_heads, heads, gain_columns, count, place_ref, *refs):
+    arrays = 2 * count - 1
+    groups = [refs[i : i + arrays] for i in range(0, len(refs) - 4, arrays)]
+    mix_ref, attn_ref, ssm_ref, extra_ref = refs[-4:]
     place = place_ref[0]
     q_wide, z_wide = q_heads * HEAD_SIZE, heads * MIXER_HEAD_SIZE
     group = QUERY_HEADS // KEY_VALUE_HEADS
@@ -876,7 +986,9 @@
     for hop in range(count):
         source = lax.rem(place - hop + count, count)
 
-        def of(start, wide, hop=hop):
+        def of(name, hop=hop):
+            group, start, wide = places[name]
+            parts = groups[group]
             if hop == 0:
                 return parts[0][:, start : start + wide].astype(F32)
             up = parts[hop][:, start : start + wide].astype(F32)
@@ -886,17 +998,17 @@
         def put(ref, start, value):
             ref[:, pl.ds(pl.multiple_of(start, LANES), value.shape[1])] = value
 
-        put(mix_ref, source * q_wide, of(cuts["q"], q_wide))
-        put(mix_ref, z_at + source * z_wide, of(cuts["z"], z_wide))
-        put(mix_ref, x_at + source * z_wide, of(cuts["x"], z_wide))
-        put(attn_ref, source * q_wide, of(out_at, q_wide))
-        put(ssm_ref, source * z_wide, of(out_at + q_wide, z_wide))
-        shared = shared + of(cuts["b"], 2 * STATE_SIZE)
+        put(mix_ref, source * q_wide, of("q"))
+        put(mix_ref, z_at + source * z_wide, of("z"))
+        put(mix_ref, x_at + source * z_wide, of("x"))
+        put(attn_ref, source * q_wide, of("attn"))
+        put(ssm_ref, source * z_wide, of("ssm"))
+        shared = shared + of("bc")
         which = lax.div(source * q_heads, group)
         for name, base in (("k", key_at), ("v", key_at + kv_wide)):
             at = pl.ds(pl.multiple_of(base + which * HEAD_SIZE, LANES), HEAD_SIZE)
-            mix_ref[:, at] += of(cuts[name], HEAD_SIZE)
-        small = of(cuts["dt"], LANES)
+            mix_ref[:, at] += of(name)
+        small = of("dt")
         own = jnp.where(lane < heads, small, 0.0)
         gains = jnp.where((lane >= heads) & (lane < head_lane), small, 0.0)
         column = jnp.where(lane == head_lane, small, 0.0)
@@ -910,9 +1022,9 @@
     extra_ref[...] = extra
 
 
-def unpack_mixer(place, own, ups, downs, cuts, out_at, q_heads, heads, gain_columns):
-    rows, wide = own.shape
-    count = len(ups) + 1
+def unpack_mixer(place, groups, places, q_heads, heads, gain_columns):
+    count = len(groups[0][1]) + 1
+    rows = groups[0][0].shape[0]
     step = min(rows, 64)
     widths = (
         QUERY_HEADS * HEAD_SIZE
@@ -923,16 +1035,17 @@
         MIXER_HEADS * MIXER_HEAD_SIZE,
         LANES,
     )
+    operands = [part for own, ups, downs in groups for part in (own, *ups, *downs)]
 
     def spec(columns):
         return pl.BlockSpec((step, columns), lambda i, place: (i, 0))
 
     return pl.pallas_call(
-        functools.partial(unpack_kernel, cuts, out_at, q_heads, heads, gain_columns, count),
+        functools.partial(unpack_kernel, places, q_heads, heads, gain_columns, count),
         grid_spec=pltpu.PrefetchScalarGridSpec(
             num_scalar_prefetch=1,
             grid=(rows // step,),
-            in_specs=[spec(wide)] * (2 * count - 1),
+            in_specs=[spec(o.shape[1]) for o in operands],
             out_specs=[spec(w) for w in widths],
         ),
         out_shape=[jax.ShapeDtypeStruct((rows, w), F32) for w in widths],
@@ -941,7 +1054,61 @@
             flops=100_000_000, bytes_accessed=26_000_000, transcendentals=0
         ),
         name="unpack_mixer",
-    )(place, own, *ups, *downs)
+    )(place, *operands)
+
+
+def unpack_ffn_kernel(count, place_ref, *refs):
+    arrays = 2 * count - 1
+    groups = (refs[:arrays], refs[arrays : 2 * arrays])
+    outs = refs[2 * arrays :]
+    place = place_ref[0]
+    chunk = groups[0][0].shape[0]
+    half = outs[0].shape[1] // 2
+    quarter = half // 2
+    pieces = (
+        (0, 0, 0, half, 0),
+        (1, 0, half, quarter, 0),
+        (1, 1, 0, quarter, quarter),
+        (2, 1, quarter, half, 0),
+    )
+    for hop in range(count):
+        source = lax.rem(place - hop + count, count)
+        row = pl.multiple_of(lax.div(source, 2) * chunk, chunk)
+        side = lax.rem(source, 2) * half
+        for out, group, start, wide, offset in pieces:
+            parts = groups[group]
+            value = parts[0][:, start : start + wide] if hop == 0 else None
+            if hop:
+                up = parts[hop][:, start : start + wide]
+                down = parts[arrays - hop][:, start : start + wide]
+                value = jnp.where(place >= hop, up.astype(F32), down.astype(F32))
+            column = pl.multiple_of(side + offset, LANES)
+            outs[out][pl.ds(row, chunk), pl.ds(column, wide)] = value.astype(F32)
+
+
+def unpack_ffn(place, groups, units):
+    count = len(groups[0][1]) + 1
+    rows = groups[0][0].shape[0] * (count // 2)
+    operands = [part for own, ups, downs in groups for part in (own, *ups, *downs)]
+
+    def fixed(shape):
+        return pl.BlockSpec(shape, lambda i, place: (0, 0))
+
+    return pl.pallas_call(
+        functools.partial(unpack_ffn_kernel, count),
+        grid_spec=pltpu.PrefetchScalarGridSpec(
+            num_scalar_prefetch=1,
+            grid=(1,),
+            in_specs=[fixed(o.shape) for o in operands],
+            out_specs=[fixed((rows, units))] * 3,
+        ),
+        out_shape=[jax.ShapeDtypeStruct((rows, units), F32)] * 3,
+        compiler_params=pltpu.CompilerParams(vmem_limit_bytes=VMEM_LIMIT),
+        cost_estimate=pl.CostEstimate(
+            flops=100_000_000, bytes_accessed=22_000_000, transcendentals=0
+        ),
+        name="unpack_ffn",
+    )(place, *operands)
 
 
 def per_device(
@@ -998,17 +1165,18 @@
         (b_at + 0 * place, 2 * STATE_SIZE),
     )
     from_half = (half * half_units, half_units)
-    mixer_own, ffn_own = pack_columns(
-        (w_mix, own_dt, w_attn_out, w_ssm_out, w_gate, w_up, w_down),
+    (mixer_own,) = pack_columns(
+        (w_mix, own_dt, w_attn_out, w_ssm_out),
         (
             [(0,) + cut for cut in mix_starts]
             + [(1, 0 * place, LANES), (2, place * q_wide, q_wide), (3, place * z_wide, z_wide)],
-            [(6,) + from_half, (4,) + from_half, (5,) + from_half],
         ),
     )
-    w_mixer = gather_rows(mixer_own)
-    w_in, w_out = w_mixer[:, :mix_wide], w_mixer[:, mix_wide:]
-    w_ffn = gather_rows(ffn_own)
+    (ffn_own,) = pack_columns(
+        (w_gate, w_up, w_down), ([(2,) + from_half, (0,) + from_half, (1,) + from_half],)
+    )
+    w_mixer, w_ffn = gather_rows(mixer_own), gather_rows(ffn_own)
+    w_out = w_mixer[:, mix_wide:]
     w_down_half = w_ffn[:, :half_units]
 
     blocks = tokens // piece
@@ -1024,21 +1192,41 @@
         here, mixed, tables, cuts, q_heads, heads, blocks
     )
     cot_own = cotangent.reshape(piece, width)
-    cot_swap = swap_pair(after(cot_own, *hidden_ups))
+    cot_swap = swap_pair(after(cot_own, mixed))
     branch_in, cot_swap = lax.optimization_barrier((branch_in, cot_swap))
     cot_pair = jnp.concatenate([cot_own, cot_swap], axis=0)
-    branch = finish(
-        line_sum([dot(branch_in[s * piece : (s + 1) * piece], w_out, 1, 1) for s in range(count)])
-    )
+    halves = []
+    for half_rows in (w_out[: width // 2], w_out[width // 2 :]):
+        terms = [None] * count
+
+        def branch_term(rows_in, hop, half_rows=half_rows):
+            return dot(rows_in[hop * piece : (hop + 1) * piece], half_rows, 1, 1)
+
+        for hop in (1, count - 1):
+            terms[hop] = branch_term(branch_in, hop)
+        branch_line = Chain(line_sum(terms))
+        flight = Flight(branch_line)
+        late_in = after(branch_in, *flight.values)
+        for hop in range(count):
+            if terms[hop] is None:
+                terms[hop] = branch_term(late_in, hop)
+        halves.append((branch_line, flight))
+    for branch_line, flight in halves:
+        flight.land()
+    for branch_line, _ in halves:
+        while live(branch_line):
+            advance(branch_line)
+    branch = jnp.concatenate([branch_line.result for branch_line, _ in halves], axis=1)
     middle = hidden_own.astype(F32) + branch
     grad_act = dot(cot_pair, w_down_half, 1, 0)
 
     inverse_ffn = inverse_rms(middle)
     normed_ffn = (middle * inverse_ffn * gain_ffn).astype(BF16)
     normed_swap, grad_act = lax.optimization_barrier((swap_pair(normed_ffn), grad_act))
-    normed_pair = jnp.concatenate([normed_ffn, normed_swap], axis=0)
-    activated, grad_gate, grad_up = ffn_inner(normed_pair, grad_act, w_ffn)
-    grad_normed_own, grad_normed_other = ffn_back(grad_gate, grad_up, w_ffn)
+    activated, grad_gate, grad_up, normed_pair = ffn_inner(
+        normed_ffn, normed_swap, grad_act, w_ffn
+    )
+    grad_normed_own, grad_normed_other = ffn_back((grad_gate, grad_up), w_ffn, (1, 2))
     grad_swap = swap_pair(grad_normed_other)
     activated, grad_gate, grad_up = lax.optimization_barrier(
         (activated, grad_gate, grad_up, grad_normed_other)
@@ -1047,42 +1235,40 @@
     grad_w_first = weight_grads(
         ((normed_pair, grad_gate, 0, half_units), (normed_pair, grad_up, 0, quarter))
     )
-    grad_w_second = weight_grads(
-        (
-            (normed_pair, grad_up, quarter, quarter),
-            (cot_pair, after(activated, grad_w_first), 0, half_units),
-        )
-    )
-    grad_swap, grad_w_second = lax.optimization_barrier((grad_swap, grad_w_second))
+    grad_swap, grad_w_first = lax.optimization_barrier((grad_swap, grad_w_first))
     grad_w_first = scatter_rows(grad_w_first)
     grad_normed_ffn = grad_normed_own + grad_swap.astype(F32)
 
     grad_middle = cot_own.astype(F32) + rms_pull(middle, inverse_ffn, gain_ffn, grad_normed_ffn)
     grad_gain_ffn = jnp.sum(grad_normed_ffn * middle * inverse_ffn, axis=0)
     branch_own = grad_middle.astype(BF16)
-    activated = after(activated, branch_own)
-    out_pair = dot(activated, w_down_half, 1, 1)
-    grad_branch = jnp.concatenate(gather_ctx(branch_own), axis=0)
-    grad_joint = dot(grad_branch, w_out, 1, 0)
-    out_swap = swap_pair(after(out_pair[piece:].astype(BF16), grad_branch))
-    grad_w_second = scatter_rows(after(grad_w_second, grad_w_first, grad_branch))
+    branch_line = Chain(line_gather(branch_own))
+    late_activated, late_up = lax.optimization_barrier((activated, grad_up, branch_own))[:2]
+    grad_w_second = weight_grads(
+        ((normed_pair, late_up, quarter, quarter), (cot_pair, late_activated, 0, half_units))
+    )
+    (grad_w_second,) = advance(branch_line, beside=(grad_w_second,))
+    out_half, out_other = ffn_back((after(activated, grad_w_second),), w_ffn, (0,))
+    out_half, out_other = advance(branch_line, beside=(out_half, out_other))
+    while branch_line.sends is not None:
+        advance(branch_line)
+    grad_joint, grad_branch = joint(here, branch_own, *branch_line.result, w_out)
+    out_swap = swap_pair(after(out_other, *branch_line.result[0]))
     first = Chain(parity_gather(grad_w_first))
+    grad_w_second = scatter_rows(after(grad_w_second, grad_w_first, grad_joint))
 
     grad_mixed, head_part = mixer_backward(
         here, mixed, grad_joint, states, keys, values, tables, cuts, q_heads, heads, blocks
     )
     grad_mixed, head_part, out_swap = advance(first, beside=(grad_mixed, head_part, out_swap))
-    ffn_out = out_pair[:piece] + out_swap.astype(F32)
-    hidden_out = (middle + ffn_out).astype(BF16)
-    grad_normed_part = dot(grad_mixed, w_in, 1, 1)
-    grad_gain_mix = jnp.sum(grad_normed_part * scaled_in, axis=0)
-    grad_normed_part, grad_gain_mix = advance(first, beside=(grad_normed_part, grad_gain_mix))
+    gain_rows, *dn_parts = mixer_out(grad_mixed, w_mixer, scaled_in, piece)
+    gain_rows, *dn_parts = advance(first, beside=(gain_rows, *dn_parts))
 
     gain_columns = 2 * width // rows
     riders = jnp.concatenate(
         [
             jnp.zeros((rows, heads), F32),
-            jnp.stack([grad_gain_mix, grad_gain_ffn]).reshape(rows, gain_columns),
+            jnp.stack([gain_rows[0], grad_gain_ffn]).reshape(rows, gain_columns),
             jnp.pad(head_part[:3, :heads].reshape(3 * heads), (0, rows - 3 * heads))[:, None],
             jnp.zeros((rows, LANES - heads - gain_columns - 1), F32),
         ],
@@ -1093,49 +1279,41 @@
         riders.astype(BF16),
         cuts["dt"],
     )
-    normed_sum = Chain(
-        line_sum([grad_normed_part[s * piece : (s + 1) * piece] for s in range(count)])
-    )
+    normed_sum = Chain(line_sum(dn_parts))
     (grad_w_mixer,) = advance(first, normed_sum, beside=(grad_w_mixer,))
     grad_w_mixer = scatter_rows(after(grad_w_mixer, grad_w_second))
     second = Chain(parity_gather(grad_w_second))
-    chains = [first, normed_sum, second]
-    while normed_sum.sends is not None:
-        advance(*[chain for chain in chains if chain.sends is not None])
-    mixer = Chain(line_gather(grad_w_mixer))
-    chains = [first, second, mixer]
-    while mixer.sends is not None:
-        advance(*[chain for chain in chains if chain.sends is not None])
-    while second.sends is not None:
-        advance(*[chain for chain in chains if chain.sends is not None])
-    grad_normed = normed_sum.result
+    advance(*live(second, first))
+    while live(normed_sum):
+        advance(*live(second, first, normed_sum))
+    mixer = Chain(line_gather(after(grad_w_mixer, normed_sum.result)))
+    while live(second, first):
+        advance(*live(mixer, second, first))
+
+    sealed = lax.optimization_barrier(
+        (first.result, second.result, tuple(value for value, _ in mixer.sends))
+    )
+    outs = tuple(unpack_ffn(here, sealed[:2], hidden_units))
+    outs = advance(*live(mixer), beside=outs)
+    sealed = lax.optimization_barrier(
+        (normed_sum.result, out_swap, tuple(value for value, _ in mixer.sends))
+    )
+    hidden_out = (middle + (out_half + sealed[1].astype(F32))).astype(BF16)
     hidden_f32 = hidden_own.astype(F32)
     grad_hidden = grad_middle + rms_pull(
-        hidden_f32, inverse_rms(hidden_f32), gain_mix, grad_normed
-    )
-
-    chunk = rows // (count // 2)
-
-    outs = [jnp.zeros((rows, hidden_units), F32) for _ in range(3)]
-    first, second = in_hops(*first.result), in_hops(*second.result)
-    for hop in range(count):
-        source = (place + count - hop) % count
-        row, column = (source // 2) * chunk, (source % 2) * half_units
-        for i, block, start, size, offset in (
-            (0, first, 0, half_units, 0),
-            (1, first, half_units, quarter, 0),
-            (1, second, 0, quarter, quarter),
-            (2, second, quarter, half_units, 0),
-        ):
-            outs[i] = lax.dynamic_update_slice(
-                outs[i],
-                block[hop][:, start : start + size].astype(F32),
-                (row, column + offset),
-            )
+        hidden_f32, inverse_rms(hidden_f32), gain_mix, sealed[0]
+    )
+    hidden_out, grad_hidden = advance(mixer, beside=(hidden_out, grad_hidden))
+    while live(mixer):
+        advance(mixer)
     out_gate, out_up, out_down = outs
 
+    places = {name: (0, cuts[name], size) for name, size in zip(names, sizes)}
+    places["bc"] = (0, cuts["b"], 2 * STATE_SIZE)
+    places["attn"] = (0, mix_wide, q_wide)
+    places["ssm"] = (0, mix_wide + q_wide, z_wide)
     out_mix, out_attn, out_ssm, extra = unpack_mixer(
-        here, grad_w_mixer, *mixer.result, cuts, mix_wide, q_heads, heads, gain_columns
+        here, ((grad_w_mixer,) + mixer.result,), places, q_heads, heads, gain_columns
     )
     head_at = MIXER_HEADS + gain_columns
     gain_sums = extra[:, MIXER_HEADS:head_at].reshape(norm_gains.shape)

time: 852 us -> 798 us (0.937)
  Pallas kernels: 171 us -> 224 us
  other arithmetic: 63.7 us -> 27.3 us
  matrix products: 63.9 us -> 30.7 us
  waiting for transfers between devices: 383 us -> 362 us
  starting transfers between devices: 119 us -> 107 us
    pallas_call x3 -> x7, Pallas kernels: 41.6 us -> 92 us  [the longest x2 25.9 us: ffn_back(): pl.pallas_call(functools.partial(ffn_back_kernel, len(grads)), grid=(dept...]
    dot_general x8 -> x9, matrix products: 63.9 us -> 30.7 us  [dot(): lax.dot_general(left, right, (((left_dim,), (right_dim,)), ((), ())), pre...]
    ppermute x44 -> x50, waiting for transfers between devices: 352 us -> 336 us  [__init__(): lax.ppermute(v, 'ctx', pairs)]
    dynamic_update_slice x16 -> x0, other arithmetic: 14.3 us -> none  [per_device(): lax.dynamic_update_slice(outs[i], block[hop][:, start:start + size].astyp...]
    reduce_scatter x3, waiting for transfers between devices: 15.4 us -> 1.84 us  [scatter_rows(): return lax.psum_scatter(value, 'fsdp', scatter_dimension=0, tiled=True)]
    ppermute x4, waiting for transfers between devices: 14.4 us -> 24.7 us  [swap_pair(): return lax.ppermute(value, 'ctx', [(i, i ^ 1) for i in range(count)])]
    ppermute x44 -> x50, starting transfers between devices: 111 us -> 101 us  [__init__(): lax.ppermute(v, 'ctx', pairs)]
  transfers between devices with their start and end apart: 53 -> 59, of which waited for: 23 -> 25; matrix products, arithmetic and copies ran while one was open for 16% -> 9% of each run, Pallas kernels for 13% -> 23%
where the time goes in v3:
time: 798 us; the launch traced here: 791 us
  waiting for transfers between devices  362 us (45%)
  Pallas kernels  224 us (28%)
  starting transfers between devices  107 us (13%)
  matrix products  30.7 us (4%)
  other arithmetic  27.3 us (3%)
  local copies, waits for them, and re-layouts  24.1 us (3%)
  between operations  15.4 us (2%)
    ppermute x50, waiting for transfers between devices, __init__(): lax.ppermute(v, 'ctx', pairs)  336 us
    ppermute x50, starting transfers between devices, __init__(): lax.ppermute(v, 'ctx', pairs)  101 us
    pallas_call x3, Pallas kernels, weight_grads(): pl.pallas_call(functools.partial(outer_kernel, plan, rider_at), grid=(dep...  50 us
    pallas_call x1, Pallas kernels, mixer_backward(): pl.pallas_call(functools.partial(mixer_backward_kernel, cuts, q_heads, he...  32.3 us
    dot_general x9, matrix products, dot(): lax.dot_general(left, right, (((left_dim,), (right_dim,)), ((), ())), pre...  30.7 us
    pallas_call x2, Pallas kernels, ffn_back(): pl.pallas_call(functools.partial(ffn_back_kernel, len(grads)), grid=(dept...  25.9 us
    pallas_call x1, Pallas kernels, mixer_in(): pl.pallas_call(functools.partial(mixer_in_kernel, count), grid_spec=pltpu...  25.1 us
    ppermute x4, waiting for transfers between devices, swap_pair(): return lax.ppermute(value, 'ctx', [(i, i ^ 1) for i in range(count)])  24.7 us
  transfers between devices with their start and end apart: 59, of which 25 were waited for; matrix products, arithmetic and copies ran while one was open for 9% of the time, Pallas kernels for 23%

profile of v3, /device:TPU:0, one launch (start us, length us, event | category | flops | bytes accessed | tf_op | source)
XLA Modules:
  0.0 790.9 jit_solution(2148683211147542974)
XLA Ops:
  9.3 3.5 pack_columns.2
  13.5 4.2 pack_columns.3
  18.9 5.0 collective-permute-start
  25.2 21.0 %collective-permute-done.refs_1_ = bf16[256,2048]{1,0:T(8,128)(2,1)S(1)} collective-permute-done((bf16[256,2048]{1,0:T(8,128)(2,1)S(1)}, bf16[256,2048]{1,0:T(8,128)(2,1)S(1)}, u32[]{:S(2)}, u32[]{:S(2)}) %collective-permute-start) | collective-permute-done | bytes 1048608 | tf_op jit(solution)/shard_map/ppermute | solution.py:53
  46.2 4.2 collective-permute-done.1.refs_4_
  53.6 25.6 %collective-permute-done.3.refs_5_ = bf16[256,2048]{1,0:T(8,128)(2,1)} collective-permute-done((bf16[256,2048]{1,0:T(8,128)(2,1)S(1)}, bf16[256,2048]{1,0:T(8,128)(2,1)}, u32[]{:S(2)}, u32[]{:S(2)}) %collective-permute-start.3) | collective-permute-done | bytes 1048608 | tf_op jit(solution)/shard_map/ppermute | solution.py:53
  86.8 18.1 %collective-permute-done.5.refs_6_ = bf16[256,2048]{1,0:T(8,128)(2,1)} collective-permute-done((bf16[256,2048]{1,0:T(8,128)(2,1)}, bf16[256,2048]{1,0:T(8,128)(2,1)}, u32[]{:S(2)}, u32[]{:S(2)}) %collective-permute-start.5) | collective-permute-done | bytes 1048608 | tf_op jit(solution)/shard_map/ppermute | solution.py:53
  104.9 25.1 %mixer_in.1 = (f32[1024,2688]{1,0:T(8,128)}, bf16[1024,2048]{1,0:T(8,128)(2,1)}, bf16[1024,2048]{1,0:T(8,128)(2,1)}) custom-call(s32[1]{0:T(128)} %bitcast.1.place_ref, f32[1,2048]{1,0:T(1,128)} %get-tuple-element.445.gain_ref, bf16[2048,3712]{1,0:T(8,128)(2,1)} %all-gather.3.cloned.1.call-done.w_ref, bf16[256,2048]{1,0:T(8,128)(2,1)} %bitcast.42, ...), custom_call_target="tpu_custom_call" | custom-call | flops 11274289152 | bytes 34603008 | tf_op jit(solution)/shard_map/mixer_in/pallas_call | solution.py:729
  130.8 16.9 %mixer_forward.1 = (bf16[1024,1024]{1,0:T(8,128)(2,1)}, f32[4,256,768]{2,1,0:T(8,128)}, bf16[1024,128]{1,0:T(8,128)(2,1)}, bf16[1024,128]{1,0:T(8,128)(2,1)}) custom-call(s32[1]{0:T(128)} %bitcast.1.place_ref, f32[1024,2688]{1,0:T(8,128)} %get-tuple-element.231.mixed_ref, f32[1024,128]{1,0:T(8,128)} %get-tuple-element.458.cos_ref, ...), custom_call_target="tpu_custom_call" | custom-call | flops 8000000000 | bytes 20000000 | tf_op jit(solution)/shard_map/mixer_forward/pallas_call | solution.py:548
  168.9 4.2 collective-permute-start.15
  179.9 4.4 collective-permute-start.9
  185.0 5.8 collective-permute-done.15
  191.1 4.4 collective-permute-start.17
  196.9 5.2 collective-permute-done.9
  202.4 4.4 collective-permute-start.11
  213.3 7.8 collective-permute-done.11
  226.8 10.5 %fusion.act_grad_ref = f32[512,2048]{1,0:T(8,128)} fusion(bf16[2048,6144]{1,0:T(8,128)(2,1)} %all-gather.5.cloned.1.call-done.gate_ref.up_ref.refs_2_.refs_3_.refs_1_, bf16[256,2048]{1,0:T(8,128)(2,1)} %copy-done.19, bf16[256,2048]{1,0:T(8,128)(2,1)} %bitcast.46), kind=kOutput, calls=%fused_computation | convolution fusion | flops 4299161600 | bytes 14680064 | tf_op jit(solution)/shard_map/dot_general | solution.py:153
  237.3 9.7 %collective-permute-done.19.other_ref = bf16[256,2048]{1,0:T(8,128)(2,1)} collective-permute-done((bf16[256,2048]{1,0:T(8,128)(2,1)}, bf16[256,2048]{1,0:T(8,128)(2,1)}, u32[]{:S(2)}, u32[]{:S(2)}) %collective-permute-start.19) | collective-permute-done | bytes 1048608 | tf_op jit(solution)/shard_map/ppermute | solution.py:29
  247.0 17.1 %ffn_inner.1 = (bf16[512,2048]{1,0:T(8,128)(2,1)}, bf16[512,2048]{1,0:T(8,128)(2,1)}, bf16[512,2048]{1,0:T(8,128)(2,1)}, bf16[512,2048]{1,0:T(8,128)(2,1)}) custom-call(bf16[256,2048]{1,0:T(8,128)(2,1)} %multiply_convert_fusion.own_ref, bf16[256,2048]{1,0:T(8,128)(2,1)} %collective-permute-done.19.other_ref, f32[512,2048]{1,0:T(8,128)} %fusion.act_grad_ref, ...), custom_call_target="tpu_custom_call" | custom-call | flops 8589934592 | bytes 31457280 | tf_op jit(solution)/shard_map/ffn_inner/pallas_call | solution.py:786
  264.1 15.1 %ffn_back.2 = (f32[256,2048]{1,0:T(8,128)}, bf16[256,2048]{1,0:T(8,128)(2,1)}) custom-call(bf16[512,2048]{1,0:T(8,128)(2,1)} %get-tuple-element.269.refs_0_.refs_1_, bf16[512,2048]{1,0:T(8,128)(2,1)} %get-tuple-element.277.refs_1_.refs_2_, bf16[2048,6144]{1,0:T(8,128)(2,1)} %all-gather.5.cloned.1.call-done.gate_ref.up_ref.refs_2_.refs_3_.refs_1_, ...), custom_call_target="tpu_custom_call" | custom-call | flops 8589934592 | bytes 25165824 | tf_op jit(solution)/shard_map/ffn_back/pallas_call | solution.py:819
  281.0 12.3 %weight_grads.3 = bf16[2048,3072]{1,0:T(8,128)(2,1)} custom-call(bf16[512,2048]{1,0:T(8,128)(2,1)} %get-tuple-element.267.refs_0_, bf16[512,2048]{1,0:T(8,128)(2,1)} %get-tuple-element.269.refs_0_.refs_1_, bf16[512,2048]{1,0:T(8,128)(2,1)} %get-tuple-element.277.refs_1_.refs_2_), custom_call_target="tpu_custom_call" | custom-call | flops 6442450944 | bytes 18874368 | tf_op jit(solution)/shard_map/weight_grads/pallas_call | solution.py:954
  293.3 7.5 collective-permute-done.20
  303.6 4.0 fusion.46
  307.6 4.4 collective-permute-start.22
  314.8 14.5 %weight_grads.4 = bf16[2048,3072]{1,0:T(8,128)(2,1)} custom-call(bf16[512,2048]{1,0:T(8,128)(2,1)} %get-tuple-element.267.refs_0_, bf16[512,2048]{1,0:T(8,128)(2,1)} %pad_maximum_fusion.refs_1_, bf16[512,2048]{1,0:T(8,128)(2,1)} %get-tuple-element.277.refs_1_.refs_2_, bf16[512,2048]{1,0:T(8,128)(2,1)} %get-tuple-element.284.refs_3_.refs_0_), custom_call_target="tpu_custom_call" | custom-call | flops 6442450944 | bytes 20971520 | tf_op jit(solution)/shard_map/weight_grads/pallas_call | solution.py:954
  329.3 6.2 collective-permute-done.23.refs_4_
  337.5 10.7 %ffn_back.3 = (f32[256,2048]{1,0:T(8,128)}, bf16[256,2048]{1,0:T(8,128)(2,1)}) custom-call(bf16[512,2048]{1,0:T(8,128)(2,1)} %get-tuple-element.284.refs_3_.refs_0_, bf16[2048,6144]{1,0:T(8,128)(2,1)} %all-gather.5.cloned.1.call-done.gate_ref.up_ref.refs_2_.refs_3_.refs_1_), custom_call_target="tpu_custom_call" | custom-call | flops 4294967296 | bytes 25165824 | tf_op jit(solution)/shard_map/ffn_back/pallas_call | solution.py:819
  348.2 12.5 %collective-permute-done.25.refs_5_ = bf16[256,2048]{1,0:T(8,128)(2,1)S(1)} collective-permute-done((bf16[256,2048]{1,0:T(8,128)(2,1)}, bf16[256,2048]{1,0:T(8,128)(2,1)S(1)}, u32[]{:S(2)}, u32[]{:S(2)}) %collective-permute-start.25) | collective-permute-done | bytes 1048608 | tf_op jit(solution)/shard_map/ppermute | solution.py:53
  362.7 4.7 slice.136.w_ref
  367.4 14.2 %collective-permute-done.27.refs_6_ = bf16[256,2048]{1,0:T(8,128)(2,1)S(1)} collective-permute-done((bf16[256,2048]{1,0:T(8,128)(2,1)S(1)}, bf16[256,2048]{1,0:T(8,128)(2,1)S(1)}, u32[]{:S(2)}, u32[]{:S(2)}) %collective-permute-start.27) | collective-permute-done | bytes 1048608 | tf_op jit(solution)/shard_map/ppermute | solution.py:53
  382.7 10.5 %joint.1 = (f32[1024,1024]{1,0:T(8,128)}, bf16[1024,2048]{1,0:T(8,128)(2,1)}) custom-call(s32[1]{0:T(128)} %bitcast.1.place_ref, bf16[2048,1024]{1,0:T(8,128)(2,1)} %slice.136.w_ref, bf16[256,2048]{1,0:T(8,128)(2,1)} %get-tuple-element.275.refs_0_, bf16[256,2048]{1,0:T(8,128)(2,1)} %collective-permute-done.22.refs_1_, bf16[256,2048]{1,0:T(8,128)(2,1)} %copy-done.37, ...), custom_call_target="tpu_custom_call" | custom-call | flops 4294967296 | bytes 12582912 | tf_op jit(solution)/shard_map/joint/pallas_call | solution.py:866
  400.4 32.3 %mixer_backward.1 = (bf16[1024,2688]{1,0:T(8,128)(2,1)}, f32[8,128]{1,0:T(8,128)}) custom-call(s32[1]{0:T(128)} %bitcast.1.place_ref, f32[1024,2688]{1,0:T(8,128)} %get-tuple-element.231.mixed_ref, f32[1024,1024]{1,0:T(8,128)} %get-tuple-element.293.joint_ref, f32[4,256,768]{2,1,0:T(8,128)} %get-tuple-element.294.state_ref, ...), custom_call_target="tpu_custom_call" | custom-call | flops 20000000000 | bytes 30000000 | tf_op jit(solution)/shard_map/mixer_backward/pallas_call | solution.py:596
  432.7 4.5 collective-permute-done.28
  438.4 5.1 collective-permute-start.29
  445.0 19.1 %mixer_out.1 = (f32[8,2048]{1,0:T(8,128)}, f32[256,2048]{1,0:T(8,128)}, bf16[256,2048]{1,0:T(8,128)(2,1)}, bf16[256,2048]{1,0:T(8,128)(2,1)}, bf16[256,2048]{1,0:T(8,128)(2,1)}) custom-call(bf16[1024,2688]{1,0:T(8,128)(2,1)} %get-tuple-element.304.grad_ref.refs_2_, bf16[2048,3712]{1,0:T(8,128)(2,1)} %all-gather.3.cloned.1.call-done.w_ref, ...), custom_call_target="tpu_custom_call" | custom-call | flops 11274289152 | bytes 30212096 | tf_op jit(solution)/shard_map/mixer_out/pallas_call | solution.py:901
  467.0 7.0 collective-permute-start.33
  477.4 23.2 %weight_grads.5 = bf16[2048,3712]{1,0:T(8,128)(2,1)} custom-call(bf16[1024,2048]{1,0:T(8,128)(2,1)} %get-tuple-element.319.refs_0_, bf16[1024,2048]{1,0:T(8,128)(2,1)} %get-tuple-element.320.refs_1_, bf16[1024,2688]{1,0:T(8,128)(2,1)} %get-tuple-element.304.grad_ref.refs_2_, bf16[1024,1024]{1,0:T(8,128)(2,1)} %get-tuple-element.237.refs_3_, ...), custom_call_target="tpu_custom_call" | custom-call | flops 15569256448 | bytes 31260672 | tf_op jit(solution)/shard_map/weight_grads/pallas_call | solution.py:954
  506.9 30.4 %collective-permute-done.35 = bf16[128,3072]{1,0:T(8,128)(2,1)S(1)} collective-permute-done((bf16[128,3072]{1,0:T(8,128)(2,1)S(1)}, bf16[128,3072]{1,0:T(8,128)(2,1)S(1)}, u32[]{:S(2)}, u32[]{:S(2)}) %collective-permute-start.35) | collective-permute-done | bytes 786464 | tf_op jit(solution)/shard_map/ppermute | solution.py:53
  542.3 4.1 collective-permute-start.38
  547.7 30.2 %collective-permute-done.38.refs_8_ = bf16[128,3072]{1,0:T(8,128)(2,1)S(1)} collective-permute-done((bf16[128,3072]{1,0:T(8,128)(2,1)S(1)}, bf16[128,3072]{1,0:T(8,128)(2,1)S(1)}, u32[]{:S(2)}, u32[]{:S(2)}) %collective-permute-start.38) | collective-permute-done | bytes 786464 | tf_op jit(solution)/shard_map/ppermute | solution.py:53
  578.8 6.6 collective-permute-start.44
  588.7 34.8 %collective-permute-done.43.refs_12_ = bf16[128,3072]{1,0:T(8,128)(2,1)S(1)} collective-permute-done((bf16[128,3072]{1,0:T(8,128)(2,1)S(1)}, bf16[128,3072]{1,0:T(8,128)(2,1)S(1)}, u32[]{:S(2)}, u32[]{:S(2)}) %collective-permute-start.43) | collective-permute-done | bytes 786464 | tf_op jit(solution)/shard_map/ppermute | solution.py:53
  626.2 4.2 collective-permute-start.46
  633.7 53.1 %collective-permute-done.49.refs_13_ = bf16[128,3072]{1,0:T(8,128)(2,1)S(1)} collective-permute-done((bf16[128,3072]{1,0:T(8,128)(2,1)}, bf16[128,3072]{1,0:T(8,128)(2,1)S(1)}, u32[]{:S(2)}, u32[]{:S(2)}) %collective-permute-start.49) | collective-permute-done | bytes 786464 | tf_op jit(solution)/shard_map/ppermute | solution.py:53
  690.1 9.9 %unpack_ffn.1 = (f32[256,4096]{1,0:T(8,128)}, f32[256,4096]{1,0:T(8,128)}, f32[256,4096]{1,0:T(8,128)}) custom-call(s32[1]{0:T(128)} %bitcast.1.place_ref, bf16[128,3072]{1,0:T(8,128)(2,1)} %add_convert_fusion.4.refs_0_, bf16[128,3072]{1,0:T(8,128)(2,1)} %collective-permute-done.29.refs_1_, bf16[128,3072]{1,0:T(8,128)(2,1)} %collective-permute-done.31.refs_2_, ...), custom_call_target="tpu_custom_call" | custom-call | flops 100000000 | bytes 22000000 | tf_op jit(solution)/shard_map/unpack_ffn/pallas_call | solution.py:1097
  700.0 28.5 %collective-permute-done.51.refs_5_ = bf16[256,3712]{1,0:T(8,128)(2,1)} collective-permute-done((bf16[256,3712]{1,0:T(8,128)(2,1)}, bf16[256,3712]{1,0:T(8,128)(2,1)}, u32[]{:S(2)}, u32[]{:S(2)}) %collective-permute-start.51) | collective-permute-done | bytes 1900576 | tf_op jit(solution)/shard_map/ppermute | solution.py:53
  736.1 32.1 %collective-permute-done.53.refs_6_ = bf16[256,3712]{1,0:T(8,128)(2,1)} collective-permute-done((bf16[256,3712]{1,0:T(8,128)(2,1)}, bf16[256,3712]{1,0:T(8,128)(2,1)}, u32[]{:S(2)}, u32[]{:S(2)}) %collective-permute-start.53) | collective-permute-done | bytes 1900576 | tf_op jit(solution)/shard_map/ppermute | solution.py:53
  768.2 9.6 %unpack_mixer.1 = (f32[256,8192]{1,0:T(8,128)}, f32[256,1024]{1,0:T(8,128)}, f32[256,3072]{1,0:T(8,128)}, f32[256,128]{1,0:T(8,128)}) custom-call(s32[1]{0:T(128)} %bitcast.1.place_ref, bf16[256,3712]{1,0:T(8,128)(2,1)} %reduce-scatter.8.cloned.1.call-done.refs_0_, bf16[256,3712]{1,0:T(8,128)(2,1)} %collective-permute-done.46.refs_1_, ...), custom_call_target="tpu_custom_call" | custom-call | flops 100000000 | bytes 26000000 | tf_op jit(solution)/shard_map/unpack_mixer/pallas_call | solution.py:1043
  (262 shorter events, 127.3 us)
Async XLA Ops:
  7.2 97.7 %all-gather.3.cloned.1.call-start = ((), (), s32[]{:S(2)}) async-start(), calls=%async_computation.3 | async-start | bytes 17104896 | tf_op jit(solution)/shard_map/all_gather | solution.py:145
  12.9 213.9 %all-gather.5.cloned.1.call-start = ((), (), s32[]{:S(2)}) async-start(), calls=%async_computation.4 | async-start | bytes 28311552 | tf_op jit(solution)/shard_map/all_gather | solution.py:145
  17.7 377.2 %reduce-scatter.4.cloned.1.call-start = ((), (), s32[]{:S(2)}) async-start(), calls=%async_computation.5 | async-start | bytes 14155776 | tf_op jit(solution)/shard_map/reduce_scatter | solution.py:149
  18.9 27.3 %collective-permute-start = (bf16[256,2048]{1,0:T(8,128)(2,1)S(1)}, bf16[256,2048]{1,0:T(8,128)(2,1)S(1)}, u32[]{:S(2)}, u32[]{:S(2)}) collective-permute-start(bf16[256,2048]{1,0:T(8,128)(2,1)S(1)} %bitcast.43), channel_id=1, source_target_pairs={{0,1},{1,2},{2,3},{4,5},{5,6},{6,7},{8,9},{9,10},{10,11},{12,13},{... | collective-permute-start | bytes 3145736 | tf_op jit(solution)/shard_map/ppermute | solution.py:53
  23.9 26.5 %collective-permute-start.1 = (bf16[256,2048]{1,0:T(8,128)(2,1)S(1)}, bf16[256,2048]{1,0:T(8,128)(2,1)S(1)}, u32[]{:S(2)}, u32[]{:S(2)}) collective-permute-start(bf16[256,2048]{1,0:T(8,128)(2,1)S(1)} %bitcast.44), channel_id=1, source_target_pairs={{1,0},{2,1},{3,2},{5,4},{6,5},{7,6},{9,8},{10,9},{11,10},{13,12},{... | collective-permute-start | bytes 3145736 | tf_op jit(solution)/shard_map/ppermute | solution.py:53
  51.1 28.0 %collective-permute-start.3 = (bf16[256,2048]{1,0:T(8,128)(2,1)S(1)}, bf16[256,2048]{1,0:T(8,128)(2,1)}, u32[]{:S(2)}, u32[]{:S(2)}) collective-permute-start(bf16[256,2048]{1,0:T(8,128)(2,1)S(1)} %collective-permute-done.1.refs_4_), channel_id=1, source_target_pairs={{1,0},{2,1},{5,4},{6,5},{9,8},{10,9},{13,12},{14,13},{17,16},{18,1... | collective-permute-start | bytes 3145736 | tf_op jit(solution)/shard_map/ppermute | solution.py:53
  79.9 25.0 %collective-permute-start.5 = (bf16[256,2048]{1,0:T(8,128)(2,1)}, bf16[256,2048]{1,0:T(8,128)(2,1)}, u32[]{:S(2)}, u32[]{:S(2)}) collective-permute-start(bf16[256,2048]{1,0:T(8,128)(2,1)} %collective-permute-done.3.refs_5_), channel_id=1, source_target_pairs={{1,0},{5,4},{9,8},{13,12},{17,16},{21,20},{25,24},{29,28}} | collective-permute-start | bytes 3145736 | tf_op jit(solution)/shard_map/ppermute | solution.py:53
  130.0 20.7 %collective-permute-start.6 = (bf16[256,2048]{1,0:T(8,128)(2,1)S(1)}, bf16[256,2048]{1,0:T(8,128)(2,1)S(1)}, u32[]{:S(2)}, u32[]{:S(2)}) collective-permute-start(bf16[256,2048]{1,0:T(8,128)(2,1)S(1)} %bitcast.47), channel_id=1, source_target_pairs={{0,1},{1,0},{2,3},{3,2},{4,5},{5,4},{6,7},{7,6},{8,9},{9,8},{10,11... | collective-permute-start | bytes 3145736 | tf_op jit(solution)/shard_map/ppermute | solution.py:29
  163.6 16.0 %collective-permute-start.7 = (bf16[256,1024]{1,0:T(8,128)(2,1)S(1)}, bf16[256,1024]{1,0:T(8,128)(2,1)S(1)}, u32[]{:S(2)}, u32[]{:S(2)}) collective-permute-start(bf16[256,1024]{1,0:T(8,128)(2,1)S(1)} %get-tuple-element.235), channel_id=1, source_target_pairs={{0,1},{4,5},{8,9},{12,13},{16,17},{20,21},{24,25},{28,29}} | collective-permute-start | bytes 1572872 | tf_op jit(solution)/shard_map/ppermute | solution.py:53
  168.9 21.9 %collective-permute-start.15 = (bf16[256,1024]{1,0:T(8,128)(2,1)S(1)}, bf16[256,1024]{1,0:T(8,128)(2,1)S(1)}, u32[]{:S(2)}, u32[]{:S(2)}) collective-permute-start(bf16[256,1024]{1,0:T(8,128)(2,1)S(1)} %get-tuple-element.253), channel_id=1, source_target_pairs={{0,1},{1,2},{4,5},{5,6},{8,9},{9,10},{12,13},{13,14},{16,17},{17,1... | collective-permute-start | bytes 1572872 | tf_op jit(solution)/shard_map/ppermute | solution.py:53
  173.1 17.7 %collective-permute-start.16 = (bf16[256,1024]{1,0:T(8,128)(2,1)S(1)}, bf16[256,1024]{1,0:T(8,128)(2,1)S(1)}, u32[]{:S(2)}, u32[]{:S(2)}) collective-permute-start(bf16[256,1024]{1,0:T(8,128)(2,1)S(1)} %get-tuple-element.254), channel_id=1, source_target_pairs={{2,1},{3,2},{6,5},{7,6},{10,9},{11,10},{14,13},{15,14},{18,17},{19... | collective-permute-start | bytes 1572872 | tf_op jit(solution)/shard_map/ppermute | solution.py:53
  179.9 22.2 %collective-permute-start.9 = (bf16[256,1024]{1,0:T(8,128)(2,1)S(1)}, bf16[256,1024]{1,0:T(8,128)(2,1)S(1)}, u32[]{:S(2)}, u32[]{:S(2)}) collective-permute-start(bf16[256,1024]{1,0:T(8,128)(2,1)S(1)} %get-tuple-element.240), channel_id=1, source_target_pairs={{0,1},{1,2},{4,5},{5,6},{8,9},{9,10},{12,13},{13,14},{16,17},{17,1... | collective-permute-start | bytes 1572872 | tf_op jit(solution)/shard_map/ppermute | solution.py:53
  184.3 17.7 %collective-permute-start.10 = (bf16[256,1024]{1,0:T(8,128)(2,1)S(1)}, bf16[256,1024]{1,0:T(8,128)(2,1)S(1)}, u32[]{:S(2)}, u32[]{:S(2)}) collective-permute-start(bf16[256,1024]{1,0:T(8,128)(2,1)S(1)} %get-tuple-element.241), channel_id=1, source_target_pairs={{2,1},{3,2},{6,5},{7,6},{10,9},{11,10},{14,13},{15,14},{18,17},{19... | collective-permute-start | bytes 1572872 | tf_op jit(solution)/shard_map/ppermute | solution.py:53
  191.1 22.2 %collective-permute-start.17 = (bf16[256,1024]{1,0:T(8,128)(2,1)S(1)}, bf16[256,1024]{1,0:T(8,128)(2,1)S(1)}, u32[]{:S(2)}, u32[]{:S(2)}) collective-permute-start(bf16[256,1024]{1,0:T(8,128)(2,1)S(1)} %add_convert_fusion.6), channel_id=1, source_target_pairs={{0,1},{1,2},{2,3},{4,5},{5,6},{6,7},{8,9},{9,10},{10,11},{12,13},{... | collective-permute-start | bytes 1572872 | tf_op jit(solution)/shard_map/ppermute | solution.py:53
  195.6 17.7 %collective-permute-start.18 = (bf16[256,1024]{1,0:T(8,128)(2,1)S(1)}, bf16[256,1024]{1,0:T(8,128)(2,1)S(1)}, u32[]{:S(2)}, u32[]{:S(2)}) collective-permute-start(bf16[256,1024]{1,0:T(8,128)(2,1)S(1)} %add_convert_fusion.5), channel_id=1, source_target_pairs={{1,0},{2,1},{3,2},{5,4},{6,5},{7,6},{9,8},{10,9},{11,10},{13,12},{... | collective-permute-start | bytes 1572872 | tf_op jit(solution)/shard_map/ppermute | solution.py:53
  202.4 18.6 %collective-permute-start.11 = (bf16[256,1024]{1,0:T(8,128)(2,1)S(1)}, bf16[256,1024]{1,0:T(8,128)(2,1)S(1)}, u32[]{:S(2)}, u32[]{:S(2)}) collective-permute-start(bf16[256,1024]{1,0:T(8,128)(2,1)S(1)} %add_convert_fusion.10), channel_id=1, source_target_pairs={{0,1},{1,2},{2,3},{4,5},{5,6},{6,7},{8,9},{9,10},{10,11},{12,13},{... | collective-permute-start | bytes 1572872 | tf_op jit(solution)/shard_map/ppermute | solution.py:53
  206.8 14.2 %collective-permute-start.12 = (bf16[256,1024]{1,0:T(8,128)(2,1)S(1)}, bf16[256,1024]{1,0:T(8,128)(2,1)S(1)}, u32[]{:S(2)}, u32[]{:S(2)}) collective-permute-start(bf16[256,1024]{1,0:T(8,128)(2,1)S(1)} %add_convert_fusion.9), channel_id=1, source_target_pairs={{1,0},{2,1},{3,2},{5,4},{6,5},{7,6},{9,8},{10,9},{11,10},{13,12},{... | collective-permute-start | bytes 1572872 | tf_op jit(solution)/shard_map/ppermute | solution.py:53
  224.1 22.9 %collective-permute-start.19 = (bf16[256,2048]{1,0:T(8,128)(2,1)}, bf16[256,2048]{1,0:T(8,128)(2,1)}, u32[]{:S(2)}, u32[]{:S(2)}) collective-permute-start(bf16[256,2048]{1,0:T(8,128)(2,1)} %multiply_convert_fusion.own_ref), channel_id=1, source_target_pairs={{0,1},{1,0},{2,3},{3,2},{4,5},{5,4},{6,7},{7,6},{8,9},{9,8},{10,11... | collective-permute-start | bytes 3145736 | tf_op jit(solution)/shard_map/ppermute | solution.py:29
  279.3 21.5 %collective-permute-start.20 = (bf16[256,2048]{1,0:T(8,128)(2,1)}, bf16[256,2048]{1,0:T(8,128)(2,1)}, u32[]{:S(2)}, u32[]{:S(2)}) collective-permute-start(bf16[256,2048]{1,0:T(8,128)(2,1)} %get-tuple-element.266), channel_id=1, source_target_pairs={{0,1},{1,0},{2,3},{3,2},{4,5},{5,4},{6,7},{7,6},{8,9},{9,8},{10,11... | collective-permute-start | bytes 3145736 | tf_op jit(solution)/shard_map/ppermute | solution.py:29
  300.7 199.8 %reduce-scatter.6.cloned.1.call-start = ((), (), s32[]{:S(2)}) async-start(), calls=%async_computation.6 | async-start | bytes 14155776 | tf_op jit(solution)/shard_map/reduce_scatter | solution.py:149
  307.6 21.7 %collective-permute-start.22 = (bf16[256,2048]{1,0:T(8,128)(2,1)}, bf16[256,2048]{1,0:T(8,128)(2,1)}, u32[]{:S(2)}, u32[]{:S(2)}) collective-permute-start(bf16[256,2048]{1,0:T(8,128)(2,1)} %get-tuple-element.275.refs_0_), channel_id=1, source_target_pairs={{0,1},{1,2},{2,3},{4,5},{5,6},{6,7},{8,9},{9,10},{10,11},{12,13},{... | collective-permute-start | bytes 3145736 | tf_op jit(solution)/shard_map/ppermute | solution.py:53
  312.0 23.5 %collective-permute-start.23 = (bf16[256,2048]{1,0:T(8,128)(2,1)}, bf16[256,2048]{1,0:T(8,128)(2,1)}, u32[]{:S(2)}, u32[]{:S(2)}) collective-permute-start(bf16[256,2048]{1,0:T(8,128)(2,1)} %get-tuple-element.275.refs_0_), channel_id=1, source_target_pairs={{1,0},{2,1},{3,2},{5,4},{6,5},{7,6},{9,8},{10,9},{11,10},{13,12},{... | collective-permute-start | bytes 3145736 | tf_op jit(solution)/shard_map/ppermute | solution.py:53
  336.2 24.5 %collective-permute-start.25 = (bf16[256,2048]{1,0:T(8,128)(2,1)}, bf16[256,2048]{1,0:T(8,128)(2,1)S(1)}, u32[]{:S(2)}, u32[]{:S(2)}) collective-permute-start(bf16[256,2048]{1,0:T(8,128)(2,1)} %collective-permute-done.23.refs_4_), channel_id=1, source_target_pairs={{1,0},{2,1},{5,4},{6,5},{9,8},{10,9},{13,12},{14,13},{17,16},{18,1... | collective-permute-start | bytes 3145736 | tf_op jit(solution)/shard_map/ppermute | solution.py:53
  361.4 20.3 %collective-permute-start.27 = (bf16[256,2048]{1,0:T(8,128)(2,1)S(1)}, bf16[256,2048]{1,0:T(8,128)(2,1)S(1)}, u32[]{:S(2)}, u32[]{:S(2)}) collective-permute-start(bf16[256,2048]{1,0:T(8,128)(2,1)S(1)} %collective-permute-done.25.refs_5_), channel_id=1, source_target_pairs={{1,0},{5,4},{9,8},{13,12},{17,16},{21,20},{25,24},{29,28}} | collective-permute-start | bytes 3145736 | tf_op jit(solution)/shard_map/ppermute | solution.py:53
  395.0 231.2 %reduce-scatter.8.cloned.1.call-start = ((), (), s32[]{:S(2)}) async-start(), calls=%async_computation.7 | async-start | bytes 17104896 | tf_op jit(solution)/shard_map/reduce_scatter | solution.py:149
  395.2 42.0 %collective-permute-start.28 = (bf16[256,2048]{1,0:T(8,128)(2,1)}, bf16[256,2048]{1,0:T(8,128)(2,1)S(1)}, u32[]{:S(2)}, u32[]{:S(2)}) collective-permute-start(bf16[256,2048]{1,0:T(8,128)(2,1)} %get-tuple-element.300), channel_id=1, source_target_pairs={{0,1},{1,0},{2,3},{3,2},{4,5},{5,4},{6,7},{7,6},{8,9},{9,8},{10,11... | collective-permute-start | bytes 3145736 | tf_op jit(solution)/shard_map/ppermute | solution.py:29
  397.9 39.3 %collective-permute-start.21 = (bf16[128,3072]{1,0:T(8,128)(2,1)S(1)}, bf16[128,3072]{1,0:T(8,128)(2,1)S(1)}, u32[]{:S(2)}, u32[]{:S(2)}) collective-permute-start(bf16[128,3072]{1,0:T(8,128)(2,1)S(1)} %constant_dynamic-slice_fusion.1), channel_id=1, source_target_pairs={{0,2},{1,3},{2,0},{3,1},{4,6},{5,7},{6,4},{7,5},{8,10},{9,11},{10,... | collective-permute-start | bytes 2359304 | tf_op jit(solution)/shard_map/ppermute | solution.py:53
  438.4 25.7 %collective-permute-start.29 = (bf16[128,3072]{1,0:T(8,128)(2,1)}, bf16[128,3072]{1,0:T(8,128)(2,1)}, u32[]{:S(2)}, u32[]{:S(2)}) collective-permute-start(bf16[128,3072]{1,0:T(8,128)(2,1)} %add_convert_fusion.4.refs_0_), channel_id=1, source_target_pairs={{0,1},{1,2},{2,3},{4,5},{5,6},{6,7},{8,9},{9,10},{10,11},{12,13},{... | collective-permute-start | bytes 2359304 | tf_op jit(solution)/shard_map/ppermute | solution.py:53
  443.5 20.6 %collective-permute-start.30 = (bf16[128,3072]{1,0:T(8,128)(2,1)}, bf16[128,3072]{1,0:T(8,128)(2,1)}, u32[]{:S(2)}, u32[]{:S(2)}) collective-permute-start(bf16[128,3072]{1,0:T(8,128)(2,1)} %add_convert_fusion.4.refs_0_), channel_id=1, source_target_pairs={{1,0},{2,1},{3,2},{5,4},{6,5},{7,6},{9,8},{10,9},{11,10},{13,12},{... | collective-permute-start | bytes 2359304 | tf_op jit(solution)/shard_map/ppermute | solution.py:53
  464.1 36.4 %collective-permute-start.31 = (bf16[128,3072]{1,0:T(8,128)(2,1)}, bf16[128,3072]{1,0:T(8,128)(2,1)}, u32[]{:S(2)}, u32[]{:S(2)}) collective-permute-start(bf16[128,3072]{1,0:T(8,128)(2,1)} %collective-permute-done.29.refs_1_), channel_id=1, source_target_pairs={{1,2},{2,3},{5,6},{6,7},{9,10},{10,11},{13,14},{14,15},{17,18},{18... | collective-permute-start | bytes 2359304 | tf_op jit(solution)/shard_map/ppermute | solution.py:53
  465.7 34.8 %collective-permute-start.32 = (bf16[128,3072]{1,0:T(8,128)(2,1)}, bf16[128,3072]{1,0:T(8,128)(2,1)}, u32[]{:S(2)}, u32[]{:S(2)}) collective-permute-start(bf16[128,3072]{1,0:T(8,128)(2,1)} %collective-permute-done.30.refs_4_), channel_id=1, source_target_pairs={{1,0},{2,1},{5,4},{6,5},{9,8},{10,9},{13,12},{14,13},{17,16},{18,1... | collective-permute-start | bytes 2359304 | tf_op jit(solution)/shard_map/ppermute | solution.py:53
  467.0 33.6 %collective-permute-start.33 = (bf16[256,2048]{1,0:T(8,128)(2,1)}, bf16[256,2048]{1,0:T(8,128)(2,1)}, u32[]{:S(2)}, u32[]{:S(2)}) collective-permute-start(bf16[256,2048]{1,0:T(8,128)(2,1)} %get-tuple-element.317), channel_id=1, source_target_pairs={{0,1},{4,5},{8,9},{12,13},{16,17},{20,21},{24,25},{28,29}} | collective-permute-start | bytes 3145736 | tf_op jit(solution)/shard_map/ppermute | solution.py:53
  474.0 26.6 %collective-permute-start.34 = (bf16[256,2048]{1,0:T(8,128)(2,1)}, bf16[256,2048]{1,0:T(8,128)(2,1)}, u32[]{:S(2)}, u32[]{:S(2)}) collective-permute-start(bf16[256,2048]{1,0:T(8,128)(2,1)} %get-tuple-element.318), channel_id=1, source_target_pairs={{3,2},{7,6},{11,10},{15,14},{19,18},{23,22},{27,26},{31,30}} | collective-permute-start | bytes 3145736 | tf_op jit(solution)/shard_map/ppermute | solution.py:53
  501.9 35.4 %collective-permute-start.35 = (bf16[128,3072]{1,0:T(8,128)(2,1)S(1)}, bf16[128,3072]{1,0:T(8,128)(2,1)S(1)}, u32[]{:S(2)}, u32[]{:S(2)}) collective-permute-start(bf16[128,3072]{1,0:T(8,128)(2,1)S(1)} %constant_dynamic-slice_fusion), channel_id=1, source_target_pairs={{0,2},{1,3},{2,0},{3,1},{4,6},{5,7},{6,4},{7,5},{8,10},{9,11},{10,... | collective-permute-start | bytes 2359304 | tf_op jit(solution)/shard_map/ppermute | solution.py:53
  502.8 34.6 %collective-permute-start.36 = (bf16[128,3072]{1,0:T(8,128)(2,1)}, bf16[128,3072]{1,0:T(8,128)(2,1)S(1)}, u32[]{:S(2)}, u32[]{:S(2)}) collective-permute-start(bf16[128,3072]{1,0:T(8,128)(2,1)} %collective-permute-done.31.refs_2_), channel_id=1, source_target_pairs={{2,3},{6,7},{10,11},{14,15},{18,19},{22,23},{26,27},{30,31}} | collective-permute-start | bytes 2359304 | tf_op jit(solution)/shard_map/ppermute | solution.py:53
  503.5 36.1 %collective-permute-start.37 = (bf16[128,3072]{1,0:T(8,128)(2,1)}, bf16[128,3072]{1,0:T(8,128)(2,1)S(1)}, u32[]{:S(2)}, u32[]{:S(2)}) collective-permute-start(bf16[128,3072]{1,0:T(8,128)(2,1)} %collective-permute-done.32.refs_5_), channel_id=1, source_target_pairs={{1,0},{5,4},{9,8},{13,12},{17,16},{21,20},{25,24},{29,28}} | collective-permute-start | bytes 2359304 | tf_op jit(solution)/shard_map/ppermute | solution.py:53
  539.8 38.1 %collective-permute-start.40 = (bf16[256,2048]{1,0:T(8,128)(2,1)S(1)}, bf16[256,2048]{1,0:T(8,128)(2,1)S(1)}, u32[]{:S(2)}, u32[]{:S(2)}) collective-permute-start(bf16[256,2048]{1,0:T(8,128)(2,1)S(1)} %get-tuple-element.338), channel_id=1, source_target_pairs={{0,1},{1,2},{4,5},{5,6},{8,9},{9,10},{12,13},{13,14},{16,17},{17,1... | collective-permute-start | bytes 3145736 | tf_op jit(solution)/shard_map/ppermute | solution.py:53
  541.6 36.4 %collective-permute-start.41 = (bf16[256,2048]{1,0:T(8,128)(2,1)S(1)}, bf16[256,2048]{1,0:T(8,128)(2,1)S(1)}, u32[]{:S(2)}, u32[]{:S(2)}) collective-permute-start(bf16[256,2048]{1,0:T(8,128)(2,1)S(1)} %get-tuple-element.339), channel_id=1, source_target_pairs={{2,1},{3,2},{6,5},{7,6},{10,9},{11,10},{14,13},{15,14},{18,17},{19... | collective-permute-start | bytes 3145736 | tf_op jit(solution)/shard_map/ppermute | solution.py:53
  542.3 35.6 %collective-permute-start.38 = (bf16[128,3072]{1,0:T(8,128)(2,1)S(1)}, bf16[128,3072]{1,0:T(8,128)(2,1)S(1)}, u32[]{:S(2)}, u32[]{:S(2)}) collective-permute-start(bf16[128,3072]{1,0:T(8,128)(2,1)S(1)} %add_convert_fusion.3.refs_7_), channel_id=1, source_target_pairs={{0,1},{1,2},{2,3},{4,5},{5,6},{6,7},{8,9},{9,10},{10,11},{12,13},{... | collective-permute-start | bytes 2359304 | tf_op jit(solution)/shard_map/ppermute | solution.py:53
  546.4 31.5 %collective-permute-start.39 = (bf16[128,3072]{1,0:T(8,128)(2,1)S(1)}, bf16[128,3072]{1,0:T(8,128)(2,1)S(1)}, u32[]{:S(2)}, u32[]{:S(2)}) collective-permute-start(bf16[128,3072]{1,0:T(8,128)(2,1)S(1)} %add_convert_fusion.3.refs_7_), channel_id=1, source_target_pairs={{1,0},{2,1},{3,2},{5,4},{6,5},{7,6},{9,8},{10,9},{11,10},{13,12},{... | collective-permute-start | bytes 2359304 | tf_op jit(solution)/shard_map/ppermute | solution.py:53
  578.8 44.7 %collective-permute-start.44 = (bf16[256,2048]{1,0:T(8,128)(2,1)S(1)}, bf16[256,2048]{1,0:T(8,128)(2,1)S(1)}, u32[]{:S(2)}, u32[]{:S(2)}) collective-permute-start(bf16[256,2048]{1,0:T(8,128)(2,1)S(1)} %add_convert_fusion.2), channel_id=1, source_target_pairs={{0,1},{1,2},{2,3},{4,5},{5,6},{6,7},{8,9},{9,10},{10,11},{12,13},{... | collective-permute-start | bytes 3145736 | tf_op jit(solution)/shard_map/ppermute | solution.py:53
  585.4 38.2 %collective-permute-start.45 = (bf16[256,2048]{1,0:T(8,128)(2,1)S(1)}, bf16[256,2048]{1,0:T(8,128)(2,1)S(1)}, u32[]{:S(2)}, u32[]{:S(2)}) collective-permute-start(bf16[256,2048]{1,0:T(8,128)(2,1)S(1)} %add_convert_fusion.1), channel_id=1, source_target_pairs={{1,0},{2,1},{3,2},{5,4},{6,5},{7,6},{9,8},{10,9},{11,10},{13,12},{... | collective-permute-start | bytes 3145736 | tf_op jit(solution)/shard_map/ppermute | solution.py:53
  587.4 36.1 %collective-permute-start.43 = (bf16[128,3072]{1,0:T(8,128)(2,1)S(1)}, bf16[128,3072]{1,0:T(8,128)(2,1)S(1)}, u32[]{:S(2)}, u32[]{:S(2)}) collective-permute-start(bf16[128,3072]{1,0:T(8,128)(2,1)S(1)} %collective-permute-done.39.refs_11_), channel_id=1, source_target_pairs={{1,0},{2,1},{5,4},{6,5},{9,8},{10,9},{13,12},{14,13},{17,16},{18,1... | collective-permute-start | bytes 2359304 | tf_op jit(solution)/shard_map/ppermute | solution.py:53
  626.2 60.7 %collective-permute-start.46 = (bf16[256,3712]{1,0:T(8,128)(2,1)}, bf16[256,3712]{1,0:T(8,128)(2,1)}, u32[]{:S(2)}, u32[]{:S(2)}) collective-permute-start(bf16[256,3712]{1,0:T(8,128)(2,1)} %reduce-scatter.8.cloned.1.call-done.refs_0_), channel_id=1, source_target_pairs={{0,1},{1,2},{2,3},{4,5},{5,6},{6,7},{8,9},{9,10},{10,11},{12,13},{... | collective-permute-start | bytes 5701640 | tf_op jit(solution)/shard_map/ppermute | solution.py:53
  630.4 56.5 %collective-permute-start.47 = (bf16[256,3712]{1,0:T(8,128)(2,1)}, bf16[256,3712]{1,0:T(8,128)(2,1)}, u32[]{:S(2)}, u32[]{:S(2)}) collective-permute-start(bf16[256,3712]{1,0:T(8,128)(2,1)} %reduce-scatter.8.cloned.1.call-done.refs_0_), channel_id=1, source_target_pairs={{1,0},{2,1},{3,2},{5,4},{6,5},{7,6},{9,8},{10,9},{11,10},{13,12},{... | collective-permute-start | bytes 5701640 | tf_op jit(solution)/shard_map/ppermute | solution.py:53
  632.4 54.5 %collective-permute-start.49 = (bf16[128,3072]{1,0:T(8,128)(2,1)}, bf16[128,3072]{1,0:T(8,128)(2,1)S(1)}, u32[]{:S(2)}, u32[]{:S(2)}) collective-permute-start(bf16[128,3072]{1,0:T(8,128)(2,1)} %copy-done.26), channel_id=1, source_target_pairs={{1,0},{5,4},{9,8},{13,12},{17,16},{21,20},{25,24},{29,28}} | collective-permute-start | bytes 2359304 | tf_op jit(solution)/shard_map/ppermute | solution.py:53
  688.8 39.7 %collective-permute-start.51 = (bf16[256,3712]{1,0:T(8,128)(2,1)}, bf16[256,3712]{1,0:T(8,128)(2,1)}, u32[]{:S(2)}, u32[]{:S(2)}) collective-permute-start(bf16[256,3712]{1,0:T(8,128)(2,1)} %collective-permute-done.47.refs_4_), channel_id=1, source_target_pairs={{1,0},{2,1},{5,4},{6,5},{9,8},{10,9},{13,12},{14,13},{17,16},{18,1... | collective-permute-start | bytes 5701640 | tf_op jit(solution)/shard_map/ppermute | solution.py:53
  730.4 37.8 %collective-permute-start.53 = (bf16[256,3712]{1,0:T(8,128)(2,1)}, bf16[256,3712]{1,0:T(8,128)(2,1)}, u32[]{:S(2)}, u32[]{:S(2)}) collective-permute-start(bf16[256,3712]{1,0:T(8,128)(2,1)} %collective-permute-done.51.refs_5_), channel_id=1, source_target_pairs={{1,0},{5,4},{9,8},{13,12},{17,16},{21,20},{25,24},{29,28}} | collective-permute-start | bytes 5701640 | tf_op jit(solution)/shard_map/ppermute | solution.py:53
  (56 other events, 1169.3 us)
Sparse Core Ops, SparseCore 0:
  13.0 85.9 all-gather.2
  101.5 125.2 all-gather.4
  300.9 94.0 reduce-scatter.3
  398.3 92.4 reduce-scatter.5
  500.7 106.7 reduce-scatter.7

commit v4 on v3

--- a/solution.py
+++ b/solution.py
@@ -689,25 +689,42 @@
     )
 
 
+def fetch_hops(count, place, parts, target, semaphores):
+    size = parts[0].shape[0]
+
+    def copy(source, hop):
+        return pltpu.make_async_copy(
+            source, target.at[hop * size : (hop + 1) * size, :], semaphores.at[hop]
+        )
+
+    copy(parts[0], 0).start()
+    for hop in range(1, count):
+
+        @pl.when(place >= hop)
+        def _(hop=hop):
+            copy(parts[hop], hop).start()
+
+        @pl.when(place < hop)
+        def _(hop=hop):
+            copy(parts[2 * count - 1 - hop], hop).start()
+
+    for hop in range(count):
+        copy(parts[0], hop).wait()
+
+
 def mixer_in_kernel(count, place_ref, gain_ref, w_ref, *refs):
     parts = refs[: 2 * count - 1]
-    out_ref, normed_ref, scaled_ref = refs[2 * count - 1 :]
+    out_ref, normed_ref, raw, semaphores = refs[2 * count - 1 :]
     size = parts[0].shape[0]
 
     @pl.when(pl.program_id(0) == 0)
     def _():
+        fetch_hops(count, place_ref[0], parts, raw, semaphores)
         for hop in range(count):
-            if hop == 0:
-                rows = parts[0][...].astype(F32)
-            else:
-                rows = jnp.where(
-                    place_ref[0] >= hop,
-                    parts[hop][...].astype(F32),
-                    parts[2 * count - 1 - hop][...].astype(F32),
-                )
+            at = slice(hop * size, (hop + 1) * size)
+            rows = raw[at, :].astype(F32)
             scaled = rows * lax.rsqrt(jnp.mean(rows * rows, axis=-1, keepdims=True) + EPSILON)
-            scaled_ref[hop * size : (hop + 1) * size, :] = scaled.astype(BF16)
-            normed_ref[hop * size : (hop + 1) * size, :] = (scaled * gain_ref[...]).astype(BF16)
+            normed_ref[at, :] = (scaled * gain_ref[...]).astype(BF16)
 
     out_ref[...] = mul(normed_ref[...], w_ref[...], 1, 0)
 
@@ -723,7 +740,6 @@
 
     outs = [
         jax.ShapeDtypeStruct((tokens, wide), F32),
-        jax.ShapeDtypeStruct((tokens, depth), BF16),
         jax.ShapeDtypeStruct((tokens, depth), BF16),
     ]
     return pl.pallas_call(
@@ -735,11 +751,14 @@
                 fixed((1, depth)),
                 pl.BlockSpec((depth, tile), lambda j, place: (0, j)),
             ]
-            + [fixed((size, depth))] * (2 * count - 1),
+            + [pl.BlockSpec(memory_space=pl.ANY)] * (2 * count - 1),
             out_specs=[
                 pl.BlockSpec((tokens, tile), lambda j, place: (0, j)),
                 fixed((tokens, depth)),
-                fixed((tokens, depth)),
+            ],
+            scratch_shapes=[
+                pltpu.VMEM((tokens, depth), BF16),
+                pltpu.SemaphoreType.DMA((count,)),
             ],
         ),
         out_shape=outs,
@@ -834,18 +853,11 @@
 
 def joint_kernel(count, place_ref, w_ref, *refs):
     parts = refs[: 2 * count - 1]
-    out_ref, rows_ref = refs[2 * count - 1 :]
-    size = parts[0].shape[0]
+    out_ref, rows_ref, semaphores = refs[2 * count - 1 :]
 
     @pl.when(pl.program_id(0) == 0)
     def _():
-        rows_ref[:size, :] = parts[0][...]
-        for hop in range(1, count):
-            rows_ref[hop * size : (hop + 1) * size, :] = jnp.where(
-                place_ref[0] >= hop,
-                parts[hop][...].astype(F32),
-                parts[2 * count - 1 - hop][...].astype(F32),
-            ).astype(BF16)
+        fetch_hops(count, place_ref[0], parts, rows_ref, semaphores)
 
     out_ref[...] = mul(rows_ref[...], w_ref[...], 1, 0)
 
@@ -855,10 +867,6 @@
     count = len(ups) + 1
     tokens, wide = size * count, weight.shape[1]
     tile = min(wide, 512)
-
-    def fixed(shape):
-        return pl.BlockSpec(shape, lambda j, place: (0, 0))
-
     outs = [
         jax.ShapeDtypeStruct((tokens, wide), F32),
         jax.ShapeDtypeStruct((tokens, depth), BF16),
@@ -869,11 +877,12 @@
             num_scalar_prefetch=1,
             grid=(wide // tile,),
             in_specs=[pl.BlockSpec((depth, tile), lambda j, place: (0, j))]
-            + [fixed((size, depth))] * (2 * count - 1),
+            + [pl.BlockSpec(memory_space=pl.ANY)] * (2 * count - 1),
             out_specs=[
                 pl.BlockSpec((tokens, tile), lambda j, place: (0, j)),
-                fixed((tokens, depth)),
+                pl.BlockSpec((tokens, depth), lambda j, place: (0, 0)),
             ],
+            scratch_shapes=[pltpu.SemaphoreType.DMA((count,))],
         ),
         out_shape=outs,
         compiler_params=pltpu.CompilerParams(vmem_limit_bytes=VMEM_LIMIT),
@@ -882,17 +891,17 @@
     )(place, weight, own, *ups, *downs)
 
 
-def mixer_out_kernel(grad_ref, w_ref, scaled_ref, gain_ref, own_ref, *other_refs):
+def mixer_out_kernel(grad_ref, w_ref, normed_ref, gain_ref, sum_ref, own_ref, *other_refs):
     total = mul(grad_ref[...], w_ref[:, : grad_ref.shape[1]], 1, 1)
     size = own_ref.shape[0]
     own_ref[...] = total[:size]
     for hop, ref in enumerate(other_refs, 1):
         ref[...] = total[hop * size : (hop + 1) * size].astype(BF16)
-    sums = jnp.sum(total * scaled_ref[...].astype(F32), axis=0, keepdims=True)
-    gain_ref[...] = jnp.broadcast_to(sums, gain_ref.shape)
-
-
-def mixer_out(grad, weights, scaled, size):
+    sums = jnp.sum(total * normed_ref[...].astype(F32), axis=0, keepdims=True) / gain_ref[...]
+    sum_ref[...] = jnp.broadcast_to(sums, sum_ref.shape)
+
+
+def mixer_out(grad, weights, normed, gain, size):
     tokens, wide = grad.shape
     depth = weights.shape[0]
     tile = 256
@@ -905,13 +914,14 @@
             pl.BlockSpec((tokens, wide), lambda j: (0, 0)),
             pl.BlockSpec((tile, weights.shape[1]), lambda j: (j, 0)),
             pl.BlockSpec((tokens, tile), lambda j: (0, j)),
+            pl.BlockSpec((1, tile), lambda j: (0, j)),
         ],
         out_specs=[pl.BlockSpec((o.shape[0], tile), lambda j: (0, j)) for o in outs],
         out_shape=outs,
         compiler_params=pltpu.CompilerParams(vmem_limit_bytes=VMEM_LIMIT),
-        cost_estimate=dense_cost(2 * tokens * depth * wide, grad, weights, scaled, *outs),
+        cost_estimate=dense_cost(2 * tokens * depth * wide, grad, weights, normed, *outs),
         name="mixer_out",
-    )(grad, weights, scaled)
+    )(grad, weights, normed, gain)
 
 
 def outer_kernel(pairs, rider_at, *refs):
@@ -1025,7 +1035,7 @@
 def unpack_mixer(place, groups, places, q_heads, heads, gain_columns):
     count = len(groups[0][1]) + 1
     rows = groups[0][0].shape[0]
-    step = min(rows, 64)
+    step = min(rows, 128)
     widths = (
         QUERY_HEADS * HEAD_SIZE
         + 2 * KEY_VALUE_HEADS * HEAD_SIZE
@@ -1183,7 +1193,7 @@
 
     hidden_own = hidden_in.reshape(piece, width)
     hidden_ups, hidden_downs = finish(line_gather(hidden_own))
-    mixed, normed, scaled_in = mixer_in(
+    mixed, normed = mixer_in(
         here, hidden_own, hidden_ups, hidden_downs, gain_mix[None, :], w_mixer, mix_wide
     )
     own = [lax.dynamic_slice_in_dim(p[0], place * heads, heads) for p in (dt_bias, a_log, skip_scale)]
@@ -1192,10 +1202,10 @@
         here, mixed, tables, cuts, q_heads, heads, blocks
     )
     cot_own = cotangent.reshape(piece, width)
-    cot_swap = swap_pair(after(cot_own, mixed))
+    cot_swap = swap_pair(after(cot_own, hidden_ups[-1], hidden_downs[-1]))
     branch_in, cot_swap = lax.optimization_barrier((branch_in, cot_swap))
     cot_pair = jnp.concatenate([cot_own, cot_swap], axis=0)
-    halves = []
+    halves, ready = [], branch_in
     for half_rows in (w_out[: width // 2], w_out[width // 2 :]):
         terms = [None] * count
 
@@ -1203,10 +1213,10 @@
             return dot(rows_in[hop * piece : (hop + 1) * piece], half_rows, 1, 1)
 
         for hop in (1, count - 1):
-            terms[hop] = branch_term(branch_in, hop)
+            terms[hop] = branch_term(ready, hop)
         branch_line = Chain(line_sum(terms))
         flight = Flight(branch_line)
-        late_in = after(branch_in, *flight.values)
+        late_in = ready = after(branch_in, *flight.values)
         for hop in range(count):
             if terms[hop] is None:
                 terms[hop] = branch_term(late_in, hop)
@@ -1249,19 +1259,19 @@
     )
     (grad_w_second,) = advance(branch_line, beside=(grad_w_second,))
     out_half, out_other = ffn_back((after(activated, grad_w_second),), w_ffn, (0,))
+    grad_w_second = scatter_rows(grad_w_second)
     out_half, out_other = advance(branch_line, beside=(out_half, out_other))
     while branch_line.sends is not None:
         advance(branch_line)
     grad_joint, grad_branch = joint(here, branch_own, *branch_line.result, w_out)
     out_swap = swap_pair(after(out_other, *branch_line.result[0]))
     first = Chain(parity_gather(grad_w_first))
-    grad_w_second = scatter_rows(after(grad_w_second, grad_w_first, grad_joint))
 
     grad_mixed, head_part = mixer_backward(
         here, mixed, grad_joint, states, keys, values, tables, cuts, q_heads, heads, blocks
     )
     grad_mixed, head_part, out_swap = advance(first, beside=(grad_mixed, head_part, out_swap))
-    gain_rows, *dn_parts = mixer_out(grad_mixed, w_mixer, scaled_in, piece)
+    gain_rows, *dn_parts = mixer_out(grad_mixed, w_mixer, normed, gain_mix[None, :], piece)
     gain_rows, *dn_parts = advance(first, beside=(gain_rows, *dn_parts))
 
     gain_columns = 2 * width // rows

time: 798 us -> 791 us (level)
    ppermute x4, waiting for transfers between devices: 24.7 us -> 9.03 us  [swap_pair(): return lax.ppermute(value, 'ctx', [(i, i ^ 1) for i in range(count)])]
    ppermute x50, waiting for transfers between devices: 336 us -> 348 us  [__init__(): lax.ppermute(v, 'ctx', pairs)]
  transfers between devices with their start and end apart: 59 -> 59, of which waited for: 25 -> 24; matrix products, arithmetic and copies ran while one was open for 9% -> 9% of each run, Pallas kernels for 23% -> 23%
where the time goes in v4:
time: 791 us; the launch traced here: 785 us
  waiting for transfers between devices  358 us (45%)
  Pallas kernels  222 us (28%)
  starting transfers between devices  107 us (14%)
  matrix products  31 us (4%)
  other arithmetic  28.4 us (4%)
  local copies, waits for them, and re-layouts  22.8 us (3%)
  between operations  15.2 us (2%)
    ppermute x50, waiting for transfers between devices, __init__(): lax.ppermute(v, 'ctx', pairs)  348 us
    ppermute x50, starting transfers between devices, __init__(): lax.ppermute(v, 'ctx', pairs)  105 us
    pallas_call x3, Pallas kernels, weight_grads(): pl.pallas_call(functools.partial(outer_kernel, plan, rider_at), grid=(dep...  49.9 us
    pallas_call x1, Pallas kernels, mixer_backward(): pl.pallas_call(functools.partial(mixer_backward_kernel, cuts, q_heads, he...  32.2 us
    dot_general x9, matrix products, dot(): lax.dot_general(left, right, (((left_dim,), (right_dim,)), ((), ())), pre...  31 us
    pallas_call x2, Pallas kernels, ffn_back(): pl.pallas_call(functools.partial(ffn_back_kernel, len(grads)), grid=(dept...  25.9 us
    pallas_call x1, Pallas kernels, mixer_in(): pl.pallas_call(functools.partial(mixer_in_kernel, count), grid_spec=pltpu...  24.6 us
    pallas_call x1, Pallas kernels, mixer_out(): pl.pallas_call(mixer_out_kernel, grid=(depth // tile,), in_specs=[pl.Bloc...  18.5 us
  transfers between devices with their start and end apart: 59, of which 24 were waited for; matrix products, arithmetic and copies ran while one was open for 9% of the time, Pallas kernels for 23%

profile of v4, /device:TPU:0, one launch (start us, length us, event | category | flops | bytes accessed | tf_op | source)
XLA Modules:
  0.0 784.7 jit_solution(9508730563007255669)
XLA Ops:
  9.3 3.5 pack_columns.2
  13.5 4.2 pack_columns.3
  18.9 5.0 collective-permute-start
  25.2 21.0 %collective-permute-done.refs_1_ = bf16[256,2048]{1,0:T(8,128)(2,1)S(1)} collective-permute-done((bf16[256,2048]{1,0:T(8,128)(2,1)S(1)}, bf16[256,2048]{1,0:T(8,128)(2,1)S(1)}, u32[]{:S(2)}, u32[]{:S(2)}) %collective-permute-start) | collective-permute-done | bytes 1048608 | tf_op jit(solution)/shard_map/ppermute | solution.py:53
  46.2 4.2 collective-permute-done.1.refs_4_
  55.1 24.9 %collective-permute-done.3.refs_5_ = bf16[256,2048]{1,0:T(8,128)(2,1)} collective-permute-done((bf16[256,2048]{1,0:T(8,128)(2,1)S(1)}, bf16[256,2048]{1,0:T(8,128)(2,1)}, u32[]{:S(2)}, u32[]{:S(2)}) %collective-permute-start.3) | collective-permute-done | bytes 1048608 | tf_op jit(solution)/shard_map/ppermute | solution.py:53
  86.7 18.9 %collective-permute-done.5.refs_6_ = bf16[256,2048]{1,0:T(8,128)(2,1)S(1)} collective-permute-done((bf16[256,2048]{1,0:T(8,128)(2,1)}, bf16[256,2048]{1,0:T(8,128)(2,1)S(1)}, u32[]{:S(2)}, u32[]{:S(2)}) %collective-permute-start.5) | collective-permute-done | bytes 1048608 | tf_op jit(solution)/shard_map/ppermute | solution.py:53
  106.6 24.6 %mixer_in.1 = (f32[1024,2688]{1,0:T(8,128)}, bf16[1024,2048]{1,0:T(8,128)(2,1)}) custom-call(s32[1]{0:T(128)} %bitcast.1.place_ref, f32[1,2048]{1,0:T(1,128)} %get-tuple-element.441.gain_ref, bf16[2048,3712]{1,0:T(8,128)(2,1)} %all-gather.3.cloned.1.call-done.w_ref, bf16[256,2048]{1,0:T(8,128)(2,1)} %bitcast.42, bf16[256,2048]{1,0:T(8,128)(2,1)} %copy-done.31, ...), custom_call_target="tpu_custom_call" | custom-call | flops 11274289152 | bytes 30408704 | tf_op jit(solution)/shard_map/mixer_in/pallas_call | solution.py:745
  131.2 16.7 %mixer_forward.1 = (bf16[1024,1024]{1,0:T(8,128)(2,1)}, f32[4,256,768]{2,1,0:T(8,128)}, bf16[1024,128]{1,0:T(8,128)(2,1)}, bf16[1024,128]{1,0:T(8,128)(2,1)}) custom-call(s32[1]{0:T(128)} %bitcast.1.place_ref, f32[1024,2688]{1,0:T(8,128)} %get-tuple-element.229.mixed_ref, f32[1024,128]{1,0:T(8,128)} %get-tuple-element.454.cos_ref, ...), custom_call_target="tpu_custom_call" | custom-call | flops 8000000000 | bytes 20000000 | tf_op jit(solution)/shard_map/mixer_forward/pallas_call | solution.py:548
  159.2 4.0 collective-permute-start.13
  168.2 7.3 collective-permute-done.13
  175.8 4.4 collective-permute-start.15
  183.3 3.5 collective-permute-done.7
  187.0 4.4 collective-permute-start.9
  192.2 5.8 collective-permute-done.15
  198.3 4.4 collective-permute-start.17
  204.0 5.2 collective-permute-done.9
  209.5 4.4 collective-permute-start.11
  220.0 5.5 collective-permute-done.11
  231.1 10.5 %fusion.act_grad_ref = f32[512,2048]{1,0:T(8,128)} fusion(bf16[2048,6144]{1,0:T(8,128)(2,1)} %all-gather.5.cloned.1.call-done.gate_ref.up_ref.refs_2_.refs_3_.refs_1_, bf16[256,2048]{1,0:T(8,128)(2,1)} %copy-done.17, bf16[256,2048]{1,0:T(8,128)(2,1)} %bitcast.46), kind=kOutput, calls=%fused_computation | convolution fusion | flops 4299161600 | bytes 14680064 | tf_op jit(solution)/shard_map/dot_general | solution.py:153
  241.6 6.0 collective-permute-done.19.other_ref
  247.6 17.4 %ffn_inner.1 = (bf16[512,2048]{1,0:T(8,128)(2,1)}, bf16[512,2048]{1,0:T(8,128)(2,1)}, bf16[512,2048]{1,0:T(8,128)(2,1)}, bf16[512,2048]{1,0:T(8,128)(2,1)}) custom-call(bf16[256,2048]{1,0:T(8,128)(2,1)} %multiply_convert_fusion.own_ref, bf16[256,2048]{1,0:T(8,128)(2,1)} %collective-permute-done.19.other_ref, f32[512,2048]{1,0:T(8,128)} %fusion.act_grad_ref, ...), custom_call_target="tpu_custom_call" | custom-call | flops 8589934592 | bytes 31457280 | tf_op jit(solution)/shard_map/ffn_inner/pallas_call | solution.py:805
  265.0 15.1 %ffn_back.2 = (f32[256,2048]{1,0:T(8,128)}, bf16[256,2048]{1,0:T(8,128)(2,1)}) custom-call(bf16[512,2048]{1,0:T(8,128)(2,1)} %get-tuple-element.267.refs_0_.refs_1_, bf16[512,2048]{1,0:T(8,128)(2,1)} %get-tuple-element.275.refs_1_.refs_2_, bf16[2048,6144]{1,0:T(8,128)(2,1)} %all-gather.5.cloned.1.call-done.gate_ref.up_ref.refs_2_.refs_3_.refs_1_, ...), custom_call_target="tpu_custom_call" | custom-call | flops 8589934592 | bytes 25165824 | tf_op jit(solution)/shard_map/ffn_back/pallas_call | solution.py:838
  281.4 12.3 %weight_grads.3 = bf16[2048,3072]{1,0:T(8,128)(2,1)} custom-call(bf16[512,2048]{1,0:T(8,128)(2,1)} %get-tuple-element.265.refs_0_, bf16[512,2048]{1,0:T(8,128)(2,1)} %get-tuple-element.267.refs_0_.refs_1_, bf16[512,2048]{1,0:T(8,128)(2,1)} %get-tuple-element.275.refs_1_.refs_2_), custom_call_target="tpu_custom_call" | custom-call | flops 6442450944 | bytes 18874368 | tf_op jit(solution)/shard_map/weight_grads/pallas_call | solution.py:964
  299.6 4.0 fusion.46
  303.5 4.6 collective-permute-start.22
  310.9 14.5 %weight_grads.4 = bf16[2048,3072]{1,0:T(8,128)(2,1)} custom-call(bf16[512,2048]{1,0:T(8,128)(2,1)} %get-tuple-element.265.refs_0_, bf16[512,2048]{1,0:T(8,128)(2,1)} %pad_maximum_fusion.refs_1_, bf16[512,2048]{1,0:T(8,128)(2,1)} %get-tuple-element.275.refs_1_.refs_2_, bf16[512,2048]{1,0:T(8,128)(2,1)} %get-tuple-element.282.refs_3_.refs_0_), custom_call_target="tpu_custom_call" | custom-call | flops 6442450944 | bytes 20971520 | tf_op jit(solution)/shard_map/weight_grads/pallas_call | solution.py:964
  331.7 10.8 %ffn_back.3 = (f32[256,2048]{1,0:T(8,128)}, bf16[256,2048]{1,0:T(8,128)(2,1)}) custom-call(bf16[512,2048]{1,0:T(8,128)(2,1)} %get-tuple-element.282.refs_3_.refs_0_, bf16[2048,6144]{1,0:T(8,128)(2,1)} %all-gather.5.cloned.1.call-done.gate_ref.up_ref.refs_2_.refs_3_.refs_1_), custom_call_target="tpu_custom_call" | custom-call | flops 4294967296 | bytes 25165824 | tf_op jit(solution)/shard_map/ffn_back/pallas_call | solution.py:838
  342.5 11.4 %collective-permute-done.25.refs_5_ = bf16[256,2048]{1,0:T(8,128)(2,1)} collective-permute-done((bf16[256,2048]{1,0:T(8,128)(2,1)}, bf16[256,2048]{1,0:T(8,128)(2,1)}, u32[]{:S(2)}, u32[]{:S(2)}) %collective-permute-start.25) | collective-permute-done | bytes 1048608 | tf_op jit(solution)/shard_map/ppermute | solution.py:53
  357.0 4.6 slice.142.w_ref
  361.6 19.1 %collective-permute-done.27.refs_6_ = bf16[256,2048]{1,0:T(8,128)(2,1)} collective-permute-done((bf16[256,2048]{1,0:T(8,128)(2,1)}, bf16[256,2048]{1,0:T(8,128)(2,1)}, u32[]{:S(2)}, u32[]{:S(2)}) %collective-permute-start.27) | collective-permute-done | bytes 1048608 | tf_op jit(solution)/shard_map/ppermute | solution.py:53
  380.8 10.8 %joint.1 = (f32[1024,1024]{1,0:T(8,128)}, bf16[1024,2048]{1,0:T(8,128)(2,1)}) custom-call(s32[1]{0:T(128)} %bitcast.1.place_ref, bf16[2048,1024]{1,0:T(8,128)(2,1)} %slice.142.w_ref, bf16[256,2048]{1,0:T(8,128)(2,1)} %get-tuple-element.273.refs_0_, bf16[256,2048]{1,0:T(8,128)(2,1)} %collective-permute-done.22.refs_1_, ...), custom_call_target="tpu_custom_call" | custom-call | flops 4294967296 | bytes 12582912 | tf_op jit(solution)/shard_map/joint/pallas_call | solution.py:874
  394.5 32.2 %mixer_backward.1 = (bf16[1024,2688]{1,0:T(8,128)(2,1)}, f32[8,128]{1,0:T(8,128)}) custom-call(s32[1]{0:T(128)} %bitcast.1.place_ref, f32[1024,2688]{1,0:T(8,128)} %get-tuple-element.229.mixed_ref, f32[1024,1024]{1,0:T(8,128)} %get-tuple-element.291.joint_ref, f32[4,256,768]{2,1,0:T(8,128)} %get-tuple-element.292.state_ref, ...), custom_call_target="tpu_custom_call" | custom-call | flops 20000000000 | bytes 30000000 | tf_op jit(solution)/shard_map/mixer_backward/pallas_call | solution.py:596
  430.2 3.3 collective-permute-start.29
  435.0 18.5 %mixer_out.1 = (f32[8,2048]{1,0:T(8,128)}, f32[256,2048]{1,0:T(8,128)}, bf16[256,2048]{1,0:T(8,128)(2,1)}, bf16[256,2048]{1,0:T(8,128)(2,1)}, bf16[256,2048]{1,0:T(8,128)(2,1)}) custom-call(bf16[1024,2688]{1,0:T(8,128)(2,1)} %get-tuple-element.302.grad_ref.refs_2_, bf16[2048,3712]{1,0:T(8,128)(2,1)} %all-gather.3.cloned.1.call-done.w_ref, ...), custom_call_target="tpu_custom_call" | custom-call | flops 11274289152 | bytes 30212096 | tf_op jit(solution)/shard_map/mixer_out/pallas_call | solution.py:910
  457.7 7.8 collective-permute-start.33
  468.9 23.1 %weight_grads.5 = bf16[2048,3712]{1,0:T(8,128)(2,1)} custom-call(bf16[1024,2048]{1,0:T(8,128)(2,1)} %get-tuple-element.303.normed_ref.refs_0_, bf16[1024,2048]{1,0:T(8,128)(2,1)} %get-tuple-element.317.refs_1_, bf16[1024,2688]{1,0:T(8,128)(2,1)} %get-tuple-element.302.grad_ref.refs_2_, bf16[1024,1024]{1,0:T(8,128)(2,1)} %get-tuple-element.248.refs_3_, ...), custom_call_target="tpu_custom_call" | custom-call | flops 15569256448 | bytes 31260672 | tf_op jit(solution)/shard_map/weight_grads/pallas_call | solution.py:964
  498.3 31.1 %collective-permute-done.35 = bf16[128,3072]{1,0:T(8,128)(2,1)S(1)} collective-permute-done((bf16[128,3072]{1,0:T(8,128)(2,1)S(1)}, bf16[128,3072]{1,0:T(8,128)(2,1)S(1)}, u32[]{:S(2)}, u32[]{:S(2)}) %collective-permute-start.35) | collective-permute-done | bytes 786464 | tf_op jit(solution)/shard_map/ppermute | solution.py:53
  534.4 4.1 collective-permute-start.38
  539.8 30.8 %collective-permute-done.38.refs_8_ = bf16[128,3072]{1,0:T(8,128)(2,1)S(1)} collective-permute-done((bf16[128,3072]{1,0:T(8,128)(2,1)S(1)}, bf16[128,3072]{1,0:T(8,128)(2,1)S(1)}, u32[]{:S(2)}, u32[]{:S(2)}) %collective-permute-start.38) | collective-permute-done | bytes 786464 | tf_op jit(solution)/shard_map/ppermute | solution.py:53
  571.6 6.6 collective-permute-start.44
  581.6 35.1 %collective-permute-done.43.refs_12_ = bf16[128,3072]{1,0:T(8,128)(2,1)S(1)} collective-permute-done((bf16[128,3072]{1,0:T(8,128)(2,1)S(1)}, bf16[128,3072]{1,0:T(8,128)(2,1)S(1)}, u32[]{:S(2)}, u32[]{:S(2)}) %collective-permute-start.43) | collective-permute-done | bytes 786464 | tf_op jit(solution)/shard_map/ppermute | solution.py:53
  619.4 4.6 collective-permute-start.46
  627.3 53.6 %collective-permute-done.49.refs_13_ = bf16[128,3072]{1,0:T(8,128)(2,1)S(1)} collective-permute-done((bf16[128,3072]{1,0:T(8,128)(2,1)}, bf16[128,3072]{1,0:T(8,128)(2,1)S(1)}, u32[]{:S(2)}, u32[]{:S(2)}) %collective-permute-start.49) | collective-permute-done | bytes 786464 | tf_op jit(solution)/shard_map/ppermute | solution.py:53
  684.2 9.9 %unpack_ffn.1 = (f32[256,4096]{1,0:T(8,128)}, f32[256,4096]{1,0:T(8,128)}, f32[256,4096]{1,0:T(8,128)}) custom-call(s32[1]{0:T(128)} %bitcast.1.place_ref, bf16[128,3072]{1,0:T(8,128)(2,1)} %add_convert_fusion.4.refs_0_, bf16[128,3072]{1,0:T(8,128)(2,1)} %collective-permute-done.29.refs_1_, bf16[128,3072]{1,0:T(8,128)(2,1)} %collective-permute-done.31.refs_2_, ...), custom_call_target="tpu_custom_call" | custom-call | flops 100000000 | bytes 22000000 | tf_op jit(solution)/shard_map/unpack_ffn/pallas_call | solution.py:1107
  694.1 28.5 %collective-permute-done.51.refs_5_ = bf16[256,3712]{1,0:T(8,128)(2,1)} collective-permute-done((bf16[256,3712]{1,0:T(8,128)(2,1)}, bf16[256,3712]{1,0:T(8,128)(2,1)}, u32[]{:S(2)}, u32[]{:S(2)}) %collective-permute-start.51) | collective-permute-done | bytes 1900576 | tf_op jit(solution)/shard_map/ppermute | solution.py:53
  731.2 31.6 %collective-permute-done.53.refs_6_ = bf16[256,3712]{1,0:T(8,128)(2,1)} collective-permute-done((bf16[256,3712]{1,0:T(8,128)(2,1)}, bf16[256,3712]{1,0:T(8,128)(2,1)}, u32[]{:S(2)}, u32[]{:S(2)}) %collective-permute-start.53) | collective-permute-done | bytes 1900576 | tf_op jit(solution)/shard_map/ppermute | solution.py:53
  762.8 9.0 %unpack_mixer.1 = (f32[256,8192]{1,0:T(8,128)}, f32[256,1024]{1,0:T(8,128)}, f32[256,3072]{1,0:T(8,128)}, f32[256,128]{1,0:T(8,128)}) custom-call(s32[1]{0:T(128)} %bitcast.1.place_ref, bf16[256,3712]{1,0:T(8,128)(2,1)} %reduce-scatter.8.cloned.1.call-done.refs_0_, bf16[256,3712]{1,0:T(8,128)(2,1)} %collective-permute-done.46.refs_1_, ...), custom_call_target="tpu_custom_call" | custom-call | flops 100000000 | bytes 26000000 | tf_op jit(solution)/shard_map/unpack_mixer/pallas_call | solution.py:1053
  (250 shorter events, 126.8 us)
Async XLA Ops:
  7.2 99.4 %all-gather.3.cloned.1.call-start = ((), (), s32[]{:S(2)}) async-start(), calls=%async_computation.3 | async-start | bytes 17104896 | tf_op jit(solution)/shard_map/all_gather | solution.py:145
  12.9 218.2 %all-gather.5.cloned.1.call-start = ((), (), s32[]{:S(2)}) async-start(), calls=%async_computation.4 | async-start | bytes 28311552 | tf_op jit(solution)/shard_map/all_gather | solution.py:145
  17.7 373.9 %reduce-scatter.4.cloned.1.call-start = ((), (), s32[]{:S(2)}) async-start(), calls=%async_computation.5 | async-start | bytes 14155776 | tf_op jit(solution)/shard_map/reduce_scatter | solution.py:149
  18.9 27.3 %collective-permute-start = (bf16[256,2048]{1,0:T(8,128)(2,1)S(1)}, bf16[256,2048]{1,0:T(8,128)(2,1)S(1)}, u32[]{:S(2)}, u32[]{:S(2)}) collective-permute-start(bf16[256,2048]{1,0:T(8,128)(2,1)S(1)} %bitcast.43), channel_id=1, source_target_pairs={{0,1},{1,2},{2,3},{4,5},{5,6},{6,7},{8,9},{9,10},{10,11},{12,13},{... | collective-permute-start | bytes 3145736 | tf_op jit(solution)/shard_map/ppermute | solution.py:53
  23.9 26.5 %collective-permute-start.1 = (bf16[256,2048]{1,0:T(8,128)(2,1)S(1)}, bf16[256,2048]{1,0:T(8,128)(2,1)S(1)}, u32[]{:S(2)}, u32[]{:S(2)}) collective-permute-start(bf16[256,2048]{1,0:T(8,128)(2,1)S(1)} %bitcast.44), channel_id=1, source_target_pairs={{1,0},{2,1},{3,2},{5,4},{6,5},{7,6},{9,8},{10,9},{11,10},{13,12},{... | collective-permute-start | bytes 3145736 | tf_op jit(solution)/shard_map/ppermute | solution.py:53
  52.0 28.0 %collective-permute-start.3 = (bf16[256,2048]{1,0:T(8,128)(2,1)S(1)}, bf16[256,2048]{1,0:T(8,128)(2,1)}, u32[]{:S(2)}, u32[]{:S(2)}) collective-permute-start(bf16[256,2048]{1,0:T(8,128)(2,1)S(1)} %collective-permute-done.1.refs_4_), channel_id=1, source_target_pairs={{1,0},{2,1},{5,4},{6,5},{9,8},{10,9},{13,12},{14,13},{17,16},{18,1... | collective-permute-start | bytes 3145736 | tf_op jit(solution)/shard_map/ppermute | solution.py:53
  80.8 24.9 %collective-permute-start.5 = (bf16[256,2048]{1,0:T(8,128)(2,1)}, bf16[256,2048]{1,0:T(8,128)(2,1)S(1)}, u32[]{:S(2)}, u32[]{:S(2)}) collective-permute-start(bf16[256,2048]{1,0:T(8,128)(2,1)} %collective-permute-done.3.refs_5_), channel_id=1, source_target_pairs={{1,0},{5,4},{9,8},{13,12},{17,16},{21,20},{25,24},{29,28}} | collective-permute-start | bytes 3145736 | tf_op jit(solution)/shard_map/ppermute | solution.py:53
  106.6 41.3 %collective-permute-start.6 = (bf16[256,2048]{1,0:T(8,128)(2,1)S(1)}, bf16[256,2048]{1,0:T(8,128)(2,1)S(1)}, u32[]{:S(2)}, u32[]{:S(2)}) collective-permute-start(bf16[256,2048]{1,0:T(8,128)(2,1)S(1)} %bitcast.47), channel_id=1, source_target_pairs={{0,1},{1,0},{2,3},{3,2},{4,5},{5,4},{6,7},{7,6},{8,9},{9,8},{10,11... | collective-permute-start | bytes 3145736 | tf_op jit(solution)/shard_map/ppermute | solution.py:29
  159.2 16.3 %collective-permute-start.13 = (bf16[256,1024]{1,0:T(8,128)(2,1)S(1)}, bf16[256,1024]{1,0:T(8,128)(2,1)S(1)}, u32[]{:S(2)}, u32[]{:S(2)}) collective-permute-start(bf16[256,1024]{1,0:T(8,128)(2,1)S(1)} %get-tuple-element.246), channel_id=1, source_target_pairs={{0,1},{4,5},{8,9},{12,13},{16,17},{20,21},{24,25},{28,29}} | collective-permute-start | bytes 1572872 | tf_op jit(solution)/shard_map/ppermute | solution.py:53
  163.9 22.9 %collective-permute-start.7 = (bf16[256,1024]{1,0:T(8,128)(2,1)S(1)}, bf16[256,1024]{1,0:T(8,128)(2,1)S(1)}, u32[]{:S(2)}, u32[]{:S(2)}) collective-permute-start(bf16[256,1024]{1,0:T(8,128)(2,1)S(1)} %get-tuple-element.233), channel_id=1, source_target_pairs={{0,1},{4,5},{8,9},{12,13},{16,17},{20,21},{24,25},{28,29}} | collective-permute-start | bytes 1572872 | tf_op jit(solution)/shard_map/ppermute | solution.py:53
  165.2 21.5 %collective-permute-start.8 = (bf16[256,1024]{1,0:T(8,128)(2,1)S(1)}, bf16[256,1024]{1,0:T(8,128)(2,1)S(1)}, u32[]{:S(2)}, u32[]{:S(2)}) collective-permute-start(bf16[256,1024]{1,0:T(8,128)(2,1)S(1)} %get-tuple-element.234), channel_id=1, source_target_pairs={{3,2},{7,6},{11,10},{15,14},{19,18},{23,22},{27,26},{31,30}} | collective-permute-start | bytes 1572872 | tf_op jit(solution)/shard_map/ppermute | solution.py:53
  175.8 22.2 %collective-permute-start.15 = (bf16[256,1024]{1,0:T(8,128)(2,1)S(1)}, bf16[256,1024]{1,0:T(8,128)(2,1)S(1)}, u32[]{:S(2)}, u32[]{:S(2)}) collective-permute-start(bf16[256,1024]{1,0:T(8,128)(2,1)S(1)} %get-tuple-element.251), channel_id=1, source_target_pairs={{0,1},{1,2},{4,5},{5,6},{8,9},{9,10},{12,13},{13,14},{16,17},{17,1... | collective-permute-start | bytes 1572872 | tf_op jit(solution)/shard_map/ppermute | solution.py:53
  180.2 17.7 %collective-permute-start.16 = (bf16[256,1024]{1,0:T(8,128)(2,1)S(1)}, bf16[256,1024]{1,0:T(8,128)(2,1)S(1)}, u32[]{:S(2)}, u32[]{:S(2)}) collective-permute-start(bf16[256,1024]{1,0:T(8,128)(2,1)S(1)} %get-tuple-element.252), channel_id=1, source_target_pairs={{2,1},{3,2},{6,5},{7,6},{10,9},{11,10},{14,13},{15,14},{18,17},{19... | collective-permute-start | bytes 1572872 | tf_op jit(solution)/shard_map/ppermute | solution.py:53
  187.0 22.2 %collective-permute-start.9 = (bf16[256,1024]{1,0:T(8,128)(2,1)S(1)}, bf16[256,1024]{1,0:T(8,128)(2,1)S(1)}, u32[]{:S(2)}, u32[]{:S(2)}) collective-permute-start(bf16[256,1024]{1,0:T(8,128)(2,1)S(1)} %get-tuple-element.238), channel_id=1, source_target_pairs={{0,1},{1,2},{4,5},{5,6},{8,9},{9,10},{12,13},{13,14},{16,17},{17,1... | collective-permute-start | bytes 1572872 | tf_op jit(solution)/shard_map/ppermute | solution.py:53
  191.5 17.7 %collective-permute-start.10 = (bf16[256,1024]{1,0:T(8,128)(2,1)S(1)}, bf16[256,1024]{1,0:T(8,128)(2,1)S(1)}, u32[]{:S(2)}, u32[]{:S(2)}) collective-permute-start(bf16[256,1024]{1,0:T(8,128)(2,1)S(1)} %get-tuple-element.239), channel_id=1, source_target_pairs={{2,1},{3,2},{6,5},{7,6},{10,9},{11,10},{14,13},{15,14},{18,17},{19... | collective-permute-start | bytes 1572872 | tf_op jit(solution)/shard_map/ppermute | solution.py:53
  198.3 21.7 %collective-permute-start.17 = (bf16[256,1024]{1,0:T(8,128)(2,1)S(1)}, bf16[256,1024]{1,0:T(8,128)(2,1)S(1)}, u32[]{:S(2)}, u32[]{:S(2)}) collective-permute-start(bf16[256,1024]{1,0:T(8,128)(2,1)S(1)} %add_convert_fusion.6), channel_id=1, source_target_pairs={{0,1},{1,2},{2,3},{4,5},{5,6},{6,7},{8,9},{9,10},{10,11},{12,13},{... | collective-permute-start | bytes 1572872 | tf_op jit(solution)/shard_map/ppermute | solution.py:53
  202.7 17.3 %collective-permute-start.18 = (bf16[256,1024]{1,0:T(8,128)(2,1)S(1)}, bf16[256,1024]{1,0:T(8,128)(2,1)S(1)}, u32[]{:S(2)}, u32[]{:S(2)}) collective-permute-start(bf16[256,1024]{1,0:T(8,128)(2,1)S(1)} %add_convert_fusion.5), channel_id=1, source_target_pairs={{1,0},{2,1},{3,2},{5,4},{6,5},{7,6},{9,8},{10,9},{11,10},{13,12},{... | collective-permute-start | bytes 1572872 | tf_op jit(solution)/shard_map/ppermute | solution.py:53
  230.1 17.5 %collective-permute-start.19 = (bf16[256,2048]{1,0:T(8,128)(2,1)}, bf16[256,2048]{1,0:T(8,128)(2,1)}, u32[]{:S(2)}, u32[]{:S(2)}) collective-permute-start(bf16[256,2048]{1,0:T(8,128)(2,1)} %multiply_convert_fusion.own_ref), channel_id=1, source_target_pairs={{0,1},{1,0},{2,3},{3,2},{4,5},{5,4},{6,7},{7,6},{8,9},{9,8},{10,11... | collective-permute-start | bytes 3145736 | tf_op jit(solution)/shard_map/ppermute | solution.py:29
  280.1 16.6 %collective-permute-start.20 = (bf16[256,2048]{1,0:T(8,128)(2,1)}, bf16[256,2048]{1,0:T(8,128)(2,1)}, u32[]{:S(2)}, u32[]{:S(2)}) collective-permute-start(bf16[256,2048]{1,0:T(8,128)(2,1)} %get-tuple-element.264), channel_id=1, source_target_pairs={{0,1},{1,0},{2,3},{3,2},{4,5},{5,4},{6,7},{7,6},{8,9},{9,8},{10,11... | collective-permute-start | bytes 3145736 | tf_op jit(solution)/shard_map/ppermute | solution.py:29
  296.7 195.3 %reduce-scatter.6.cloned.1.call-start = ((), (), s32[]{:S(2)}) async-start(), calls=%async_computation.6 | async-start | bytes 14155776 | tf_op jit(solution)/shard_map/reduce_scatter | solution.py:149
  303.5 21.9 %collective-permute-start.22 = (bf16[256,2048]{1,0:T(8,128)(2,1)}, bf16[256,2048]{1,0:T(8,128)(2,1)}, u32[]{:S(2)}, u32[]{:S(2)}) collective-permute-start(bf16[256,2048]{1,0:T(8,128)(2,1)} %get-tuple-element.273.refs_0_), channel_id=1, source_target_pairs={{0,1},{1,2},{2,3},{4,5},{5,6},{6,7},{8,9},{9,10},{10,11},{12,13},{... | collective-permute-start | bytes 3145736 | tf_op jit(solution)/shard_map/ppermute | solution.py:53
  308.1 20.6 %collective-permute-start.23 = (bf16[256,2048]{1,0:T(8,128)(2,1)}, bf16[256,2048]{1,0:T(8,128)(2,1)}, u32[]{:S(2)}, u32[]{:S(2)}) collective-permute-start(bf16[256,2048]{1,0:T(8,128)(2,1)} %get-tuple-element.273.refs_0_), channel_id=1, source_target_pairs={{1,0},{2,1},{3,2},{5,4},{6,5},{7,6},{9,8},{10,9},{11,10},{13,12},{... | collective-permute-start | bytes 3145736 | tf_op jit(solution)/shard_map/ppermute | solution.py:53
  328.8 290.6 %reduce-scatter.8.cloned.1.call-start = ((), (), s32[]{:S(2)}) async-start(), calls=%async_computation.7 | async-start | bytes 17104896 | tf_op jit(solution)/shard_map/reduce_scatter | solution.py:149
  330.5 23.4 %collective-permute-start.25 = (bf16[256,2048]{1,0:T(8,128)(2,1)}, bf16[256,2048]{1,0:T(8,128)(2,1)}, u32[]{:S(2)}, u32[]{:S(2)}) collective-permute-start(bf16[256,2048]{1,0:T(8,128)(2,1)} %collective-permute-done.23.refs_4_), channel_id=1, source_target_pairs={{1,0},{2,1},{5,4},{6,5},{9,8},{10,9},{13,12},{14,13},{17,16},{18,1... | collective-permute-start | bytes 3145736 | tf_op jit(solution)/shard_map/ppermute | solution.py:53
  355.6 25.2 %collective-permute-start.27 = (bf16[256,2048]{1,0:T(8,128)(2,1)}, bf16[256,2048]{1,0:T(8,128)(2,1)}, u32[]{:S(2)}, u32[]{:S(2)}) collective-permute-start(bf16[256,2048]{1,0:T(8,128)(2,1)} %collective-permute-done.25.refs_5_), channel_id=1, source_target_pairs={{1,0},{5,4},{9,8},{13,12},{17,16},{21,20},{25,24},{29,28}} | collective-permute-start | bytes 3145736 | tf_op jit(solution)/shard_map/ppermute | solution.py:53
  380.8 45.8 %collective-permute-start.28 = (bf16[256,2048]{1,0:T(8,128)(2,1)}, bf16[256,2048]{1,0:T(8,128)(2,1)}, u32[]{:S(2)}, u32[]{:S(2)}) collective-permute-start(bf16[256,2048]{1,0:T(8,128)(2,1)} %get-tuple-element.298), channel_id=1, source_target_pairs={{0,1},{1,0},{2,3},{3,2},{4,5},{5,4},{6,7},{7,6},{8,9},{9,8},{10,11... | collective-permute-start | bytes 3145736 | tf_op jit(solution)/shard_map/ppermute | solution.py:29
  392.8 36.3 %collective-permute-start.21 = (bf16[128,3072]{1,0:T(8,128)(2,1)S(1)}, bf16[128,3072]{1,0:T(8,128)(2,1)S(1)}, u32[]{:S(2)}, u32[]{:S(2)}) collective-permute-start(bf16[128,3072]{1,0:T(8,128)(2,1)S(1)} %constant_dynamic-slice_fusion.1), channel_id=1, source_target_pairs={{0,2},{1,3},{2,0},{3,1},{4,6},{5,7},{6,4},{7,5},{8,10},{9,11},{10,... | collective-permute-start | bytes 2359304 | tf_op jit(solution)/shard_map/ppermute | solution.py:53
  430.2 23.3 %collective-permute-start.29 = (bf16[128,3072]{1,0:T(8,128)(2,1)}, bf16[128,3072]{1,0:T(8,128)(2,1)}, u32[]{:S(2)}, u32[]{:S(2)}) collective-permute-start(bf16[128,3072]{1,0:T(8,128)(2,1)} %add_convert_fusion.4.refs_0_), channel_id=1, source_target_pairs={{0,1},{1,2},{2,3},{4,5},{5,6},{6,7},{8,9},{9,10},{10,11},{12,13},{... | collective-permute-start | bytes 2359304 | tf_op jit(solution)/shard_map/ppermute | solution.py:53
  433.5 21.4 %collective-permute-start.30 = (bf16[128,3072]{1,0:T(8,128)(2,1)}, bf16[128,3072]{1,0:T(8,128)(2,1)}, u32[]{:S(2)}, u32[]{:S(2)}) collective-permute-start(bf16[128,3072]{1,0:T(8,128)(2,1)} %add_convert_fusion.4.refs_0_), channel_id=1, source_target_pairs={{1,0},{2,1},{3,2},{5,4},{6,5},{7,6},{9,8},{10,9},{11,10},{13,12},{... | collective-permute-start | bytes 2359304 | tf_op jit(solution)/shard_map/ppermute | solution.py:53
  454.9 37.1 %collective-permute-start.31 = (bf16[128,3072]{1,0:T(8,128)(2,1)}, bf16[128,3072]{1,0:T(8,128)(2,1)}, u32[]{:S(2)}, u32[]{:S(2)}) collective-permute-start(bf16[128,3072]{1,0:T(8,128)(2,1)} %collective-permute-done.29.refs_1_), channel_id=1, source_target_pairs={{1,2},{2,3},{5,6},{6,7},{9,10},{10,11},{13,14},{14,15},{17,18},{18... | collective-permute-start | bytes 2359304 | tf_op jit(solution)/shard_map/ppermute | solution.py:53
  456.4 35.6 %collective-permute-start.32 = (bf16[128,3072]{1,0:T(8,128)(2,1)}, bf16[128,3072]{1,0:T(8,128)(2,1)}, u32[]{:S(2)}, u32[]{:S(2)}) collective-permute-start(bf16[128,3072]{1,0:T(8,128)(2,1)} %collective-permute-done.30.refs_4_), channel_id=1, source_target_pairs={{1,0},{2,1},{5,4},{6,5},{9,8},{10,9},{13,12},{14,13},{17,16},{18,1... | collective-permute-start | bytes 2359304 | tf_op jit(solution)/shard_map/ppermute | solution.py:53
  457.7 34.3 %collective-permute-start.33 = (bf16[256,2048]{1,0:T(8,128)(2,1)}, bf16[256,2048]{1,0:T(8,128)(2,1)}, u32[]{:S(2)}, u32[]{:S(2)}) collective-permute-start(bf16[256,2048]{1,0:T(8,128)(2,1)} %get-tuple-element.315), channel_id=1, source_target_pairs={{0,1},{4,5},{8,9},{12,13},{16,17},{20,21},{24,25},{28,29}} | collective-permute-start | bytes 3145736 | tf_op jit(solution)/shard_map/ppermute | solution.py:53
  465.5 26.5 %collective-permute-start.34 = (bf16[256,2048]{1,0:T(8,128)(2,1)}, bf16[256,2048]{1,0:T(8,128)(2,1)}, u32[]{:S(2)}, u32[]{:S(2)}) collective-permute-start(bf16[256,2048]{1,0:T(8,128)(2,1)} %get-tuple-element.316), channel_id=1, source_target_pairs={{3,2},{7,6},{11,10},{15,14},{19,18},{23,22},{27,26},{31,30}} | collective-permute-start | bytes 3145736 | tf_op jit(solution)/shard_map/ppermute | solution.py:53
  493.4 36.1 %collective-permute-start.35 = (bf16[128,3072]{1,0:T(8,128)(2,1)S(1)}, bf16[128,3072]{1,0:T(8,128)(2,1)S(1)}, u32[]{:S(2)}, u32[]{:S(2)}) collective-permute-start(bf16[128,3072]{1,0:T(8,128)(2,1)S(1)} %constant_dynamic-slice_fusion), channel_id=1, source_target_pairs={{0,2},{1,3},{2,0},{3,1},{4,6},{5,7},{6,4},{7,5},{8,10},{9,11},{10,... | collective-permute-start | bytes 2359304 | tf_op jit(solution)/shard_map/ppermute | solution.py:53
  494.2 35.3 %collective-permute-start.36 = (bf16[128,3072]{1,0:T(8,128)(2,1)}, bf16[128,3072]{1,0:T(8,128)(2,1)S(1)}, u32[]{:S(2)}, u32[]{:S(2)}) collective-permute-start(bf16[128,3072]{1,0:T(8,128)(2,1)} %collective-permute-done.31.refs_2_), channel_id=1, source_target_pairs={{2,3},{6,7},{10,11},{14,15},{18,19},{22,23},{26,27},{30,31}} | collective-permute-start | bytes 2359304 | tf_op jit(solution)/shard_map/ppermute | solution.py:53
  494.9 36.8 %collective-permute-start.37 = (bf16[128,3072]{1,0:T(8,128)(2,1)}, bf16[128,3072]{1,0:T(8,128)(2,1)S(1)}, u32[]{:S(2)}, u32[]{:S(2)}) collective-permute-start(bf16[128,3072]{1,0:T(8,128)(2,1)} %collective-permute-done.32.refs_5_), channel_id=1, source_target_pairs={{1,0},{5,4},{9,8},{13,12},{17,16},{21,20},{25,24},{29,28}} | collective-permute-start | bytes 2359304 | tf_op jit(solution)/shard_map/ppermute | solution.py:53
  531.9 38.7 %collective-permute-start.40 = (bf16[256,2048]{1,0:T(8,128)(2,1)S(1)}, bf16[256,2048]{1,0:T(8,128)(2,1)S(1)}, u32[]{:S(2)}, u32[]{:S(2)}) collective-permute-start(bf16[256,2048]{1,0:T(8,128)(2,1)S(1)} %get-tuple-element.334), channel_id=1, source_target_pairs={{0,1},{1,2},{4,5},{5,6},{8,9},{9,10},{12,13},{13,14},{16,17},{17,1... | collective-permute-start | bytes 3145736 | tf_op jit(solution)/shard_map/ppermute | solution.py:53
  533.7 37.0 %collective-permute-start.41 = (bf16[256,2048]{1,0:T(8,128)(2,1)S(1)}, bf16[256,2048]{1,0:T(8,128)(2,1)S(1)}, u32[]{:S(2)}, u32[]{:S(2)}) collective-permute-start(bf16[256,2048]{1,0:T(8,128)(2,1)S(1)} %get-tuple-element.335), channel_id=1, source_target_pairs={{2,1},{3,2},{6,5},{7,6},{10,9},{11,10},{14,13},{15,14},{18,17},{19... | collective-permute-start | bytes 3145736 | tf_op jit(solution)/shard_map/ppermute | solution.py:53
  534.4 36.2 %collective-permute-start.38 = (bf16[128,3072]{1,0:T(8,128)(2,1)S(1)}, bf16[128,3072]{1,0:T(8,128)(2,1)S(1)}, u32[]{:S(2)}, u32[]{:S(2)}) collective-permute-start(bf16[128,3072]{1,0:T(8,128)(2,1)S(1)} %add_convert_fusion.3.refs_7_), channel_id=1, source_target_pairs={{0,1},{1,2},{2,3},{4,5},{5,6},{6,7},{8,9},{9,10},{10,11},{12,13},{... | collective-permute-start | bytes 2359304 | tf_op jit(solution)/shard_map/ppermute | solution.py:53
  538.5 32.1 %collective-permute-start.39 = (bf16[128,3072]{1,0:T(8,128)(2,1)S(1)}, bf16[128,3072]{1,0:T(8,128)(2,1)S(1)}, u32[]{:S(2)}, u32[]{:S(2)}) collective-permute-start(bf16[128,3072]{1,0:T(8,128)(2,1)S(1)} %add_convert_fusion.3.refs_7_), channel_id=1, source_target_pairs={{1,0},{2,1},{3,2},{5,4},{6,5},{7,6},{9,8},{10,9},{11,10},{13,12},{... | collective-permute-start | bytes 2359304 | tf_op jit(solution)/shard_map/ppermute | solution.py:53
  571.6 45.1 %collective-permute-start.44 = (bf16[256,2048]{1,0:T(8,128)(2,1)S(1)}, bf16[256,2048]{1,0:T(8,128)(2,1)S(1)}, u32[]{:S(2)}, u32[]{:S(2)}) collective-permute-start(bf16[256,2048]{1,0:T(8,128)(2,1)S(1)} %add_convert_fusion.2), channel_id=1, source_target_pairs={{0,1},{1,2},{2,3},{4,5},{5,6},{6,7},{8,9},{9,10},{10,11},{12,13},{... | collective-permute-start | bytes 3145736 | tf_op jit(solution)/shard_map/ppermute | solution.py:53
  578.2 38.5 %collective-permute-start.45 = (bf16[256,2048]{1,0:T(8,128)(2,1)S(1)}, bf16[256,2048]{1,0:T(8,128)(2,1)S(1)}, u32[]{:S(2)}, u32[]{:S(2)}) collective-permute-start(bf16[256,2048]{1,0:T(8,128)(2,1)S(1)} %add_convert_fusion.1), channel_id=1, source_target_pairs={{1,0},{2,1},{3,2},{5,4},{6,5},{7,6},{9,8},{10,9},{11,10},{13,12},{... | collective-permute-start | bytes 3145736 | tf_op jit(solution)/shard_map/ppermute | solution.py:53
  580.2 36.5 %collective-permute-start.43 = (bf16[128,3072]{1,0:T(8,128)(2,1)S(1)}, bf16[128,3072]{1,0:T(8,128)(2,1)S(1)}, u32[]{:S(2)}, u32[]{:S(2)}) collective-permute-start(bf16[128,3072]{1,0:T(8,128)(2,1)S(1)} %collective-permute-done.39.refs_11_), channel_id=1, source_target_pairs={{1,0},{2,1},{5,4},{6,5},{9,8},{10,9},{13,12},{14,13},{17,16},{18,1... | collective-permute-start | bytes 2359304 | tf_op jit(solution)/shard_map/ppermute | solution.py:53
  619.4 61.5 %collective-permute-start.46 = (bf16[256,3712]{1,0:T(8,128)(2,1)}, bf16[256,3712]{1,0:T(8,128)(2,1)}, u32[]{:S(2)}, u32[]{:S(2)}) collective-permute-start(bf16[256,3712]{1,0:T(8,128)(2,1)} %reduce-scatter.8.cloned.1.call-done.refs_0_), channel_id=1, source_target_pairs={{0,1},{1,2},{2,3},{4,5},{5,6},{6,7},{8,9},{9,10},{10,11},{12,13},{... | collective-permute-start | bytes 5701640 | tf_op jit(solution)/shard_map/ppermute | solution.py:53
  624.0 56.9 %collective-permute-start.47 = (bf16[256,3712]{1,0:T(8,128)(2,1)}, bf16[256,3712]{1,0:T(8,128)(2,1)}, u32[]{:S(2)}, u32[]{:S(2)}) collective-permute-start(bf16[256,3712]{1,0:T(8,128)(2,1)} %reduce-scatter.8.cloned.1.call-done.refs_0_), channel_id=1, source_target_pairs={{1,0},{2,1},{3,2},{5,4},{6,5},{7,6},{9,8},{10,9},{11,10},{13,12},{... | collective-permute-start | bytes 5701640 | tf_op jit(solution)/shard_map/ppermute | solution.py:53
  626.0 54.9 %collective-permute-start.49 = (bf16[128,3072]{1,0:T(8,128)(2,1)}, bf16[128,3072]{1,0:T(8,128)(2,1)S(1)}, u32[]{:S(2)}, u32[]{:S(2)}) collective-permute-start(bf16[128,3072]{1,0:T(8,128)(2,1)} %copy-done.24), channel_id=1, source_target_pairs={{1,0},{5,4},{9,8},{13,12},{17,16},{21,20},{25,24},{29,28}} | collective-permute-start | bytes 2359304 | tf_op jit(solution)/shard_map/ppermute | solution.py:53
  682.9 39.7 %collective-permute-start.51 = (bf16[256,3712]{1,0:T(8,128)(2,1)}, bf16[256,3712]{1,0:T(8,128)(2,1)}, u32[]{:S(2)}, u32[]{:S(2)}) collective-permute-start(bf16[256,3712]{1,0:T(8,128)(2,1)} %collective-permute-done.47.refs_4_), channel_id=1, source_target_pairs={{1,0},{2,1},{5,4},{6,5},{9,8},{10,9},{13,12},{14,13},{17,16},{18,1... | collective-permute-start | bytes 5701640 | tf_op jit(solution)/shard_map/ppermute | solution.py:53
  724.4 38.4 %collective-permute-start.53 = (bf16[256,3712]{1,0:T(8,128)(2,1)}, bf16[256,3712]{1,0:T(8,128)(2,1)}, u32[]{:S(2)}, u32[]{:S(2)}) collective-permute-start(bf16[256,3712]{1,0:T(8,128)(2,1)} %collective-permute-done.51.refs_5_), channel_id=1, source_target_pairs={{1,0},{5,4},{9,8},{13,12},{17,16},{21,20},{25,24},{29,28}} | collective-permute-start | bytes 5701640 | tf_op jit(solution)/shard_map/ppermute | solution.py:53
  (50 other events, 1149.4 us)
Sparse Core Ops, SparseCore 0:
  13.0 85.8 all-gather.2
  101.4 125.3 all-gather.4
  296.8 93.9 reduce-scatter.3
  394.1 92.3 reduce-scatter.5
  492.2 106.7 reduce-scatter.7

commit v5 on v4

--- a/solution.py
+++ b/solution.py
@@ -1121,6 +1121,47 @@
     )(place, *operands)
 
 
+def norm_back_kernel(grad_ref, swap_ref, rows_ref, gain_ref, base_ref, out_ref, low_ref, sum_ref):
+    grad = grad_ref[...] + swap_ref[...].astype(F32)
+    rows = rows_ref[...]
+    inverse = lax.rsqrt(jnp.mean(rows * rows, axis=-1, keepdims=True) + EPSILON)
+    unit = rows * inverse
+    scaled = grad * gain_ref[...]
+    out = base_ref[...].astype(F32) + inverse * (
+        scaled - unit * jnp.mean(unit * scaled, axis=-1, keepdims=True)
+    )
+    out_ref[...] = out
+    low_ref[...] = out.astype(BF16)
+
+    @pl.when(pl.program_id(0) == 0)
+    def _():
+        sum_ref[...] = jnp.zeros_like(sum_ref)
+
+    sum_ref[...] += jnp.broadcast_to(jnp.sum(grad * unit, axis=0, keepdims=True), sum_ref.shape)
+
+
+def norm_back(grad, swap, rows, gain, base):
+    size, depth = rows.shape
+    step = min(size, 64)
+    tile = pl.BlockSpec((step, depth), lambda i: (i, 0))
+    fixed = lambda i: (0, 0)
+    outs = [
+        jax.ShapeDtypeStruct((size, depth), F32),
+        jax.ShapeDtypeStruct((size, depth), BF16),
+        jax.ShapeDtypeStruct((8, depth), F32),
+    ]
+    return pl.pallas_call(
+        norm_back_kernel,
+        grid=(size // step,),
+        in_specs=[tile, tile, tile, pl.BlockSpec((1, depth), fixed), tile],
+        out_specs=[tile, tile, pl.BlockSpec((8, depth), fixed)],
+        out_shape=outs,
+        compiler_params=pltpu.CompilerParams(vmem_limit_bytes=VMEM_LIMIT),
+        cost_estimate=dense_cost(20 * size * depth, grad, swap, rows, *outs),
+        name="norm_back",
+    )(grad, swap, rows, gain, base)
+
+
 def per_device(
     hidden_in,
     w_mix,
@@ -1182,17 +1223,23 @@
             + [(1, 0 * place, LANES), (2, place * q_wide, q_wide), (3, place * z_wide, z_wide)],
         ),
     )
+    hidden_own = hidden_in.reshape(piece, width)
+    hidden_line = Chain(line_gather(hidden_own))
+    advance(hidden_line)
+    late_down = after(w_down, *[value for value, _ in hidden_line.sends])
     (ffn_own,) = pack_columns(
-        (w_gate, w_up, w_down), ([(2,) + from_half, (0,) + from_half, (1,) + from_half],)
-    )
+        (w_gate, w_up, late_down), ([(2,) + from_half, (0,) + from_half, (1,) + from_half],)
+    )
+    (ffn_own,) = advance(hidden_line, beside=(ffn_own,))
     w_mixer, w_ffn = gather_rows(mixer_own), gather_rows(ffn_own)
     w_out = w_mixer[:, mix_wide:]
     w_down_half = w_ffn[:, :half_units]
 
     blocks = tokens // piece
 
-    hidden_own = hidden_in.reshape(piece, width)
-    hidden_ups, hidden_downs = finish(line_gather(hidden_own))
+    while live(hidden_line):
+        advance(hidden_line)
+    hidden_ups, hidden_downs = hidden_line.result
     mixed, normed = mixer_in(
         here, hidden_own, hidden_ups, hidden_downs, gain_mix[None, :], w_mixer, mix_wide
     )
@@ -1247,11 +1294,10 @@
     )
     grad_swap, grad_w_first = lax.optimization_barrier((grad_swap, grad_w_first))
     grad_w_first = scatter_rows(grad_w_first)
-    grad_normed_ffn = grad_normed_own + grad_swap.astype(F32)
-
-    grad_middle = cot_own.astype(F32) + rms_pull(middle, inverse_ffn, gain_ffn, grad_normed_ffn)
-    grad_gain_ffn = jnp.sum(grad_normed_ffn * middle * inverse_ffn, axis=0)
-    branch_own = grad_middle.astype(BF16)
+
+    grad_middle, branch_own, gain_ffn_rows = norm_back(
+        grad_normed_own, grad_swap, middle, gain_ffn[None, :], cot_own
+    )
     branch_line = Chain(line_gather(branch_own))
     late_activated, late_up = lax.optimization_barrier((activated, grad_up, branch_own))[:2]
     grad_w_second = weight_grads(
@@ -1278,7 +1324,7 @@
     riders = jnp.concatenate(
         [
             jnp.zeros((rows, heads), F32),
-            jnp.stack([gain_rows[0], grad_gain_ffn]).reshape(rows, gain_columns),
+            jnp.stack([gain_rows[0], gain_ffn_rows[0]]).reshape(rows, gain_columns),
             jnp.pad(head_part[:3, :heads].reshape(3 * heads), (0, rows - 3 * heads))[:, None],
             jnp.zeros((rows, LANES - heads - gain_columns - 1), F32),
         ],

time: 791 us -> 789 us (level)
  other arithmetic: 28.4 us -> 18.9 us
    ppermute x50, waiting for transfers between devices: 348 us -> 335 us  [__init__(): lax.ppermute(v, 'ctx', pairs)]
  transfers between devices with their start and end apart: 59 -> 59, of which waited for: 24 -> 24; matrix products, arithmetic and copies ran while one was open for 9% -> 8% of each run, Pallas kernels for 23% -> 23%
where the time goes in v5:
time: 789 us; the launch traced here: 778 us
  waiting for transfers between devices  353 us (45%)
  Pallas kernels  227 us (29%)
  starting transfers between devices  106 us (13%)
  matrix products  30.4 us (4%)
  local copies, waits for them, and re-layouts  27.9 us (4%)
  other arithmetic  18.9 us (2%)
  between operations  15.3 us (2%)
    ppermute x50, waiting for transfers between devices, __init__(): lax.ppermute(v, 'ctx', pairs)  335 us
    ppermute x50, starting transfers between devices, __init__(): lax.ppermute(v, 'ctx', pairs)  101 us
    pallas_call x3, Pallas kernels, weight_grads(): pl.pallas_call(functools.partial(outer_kernel, plan, rider_at), grid=(dep...  50.2 us
    pallas_call x1, Pallas kernels, mixer_backward(): pl.pallas_call(functools.partial(mixer_backward_kernel, cuts, q_heads, he...  33.1 us
    dot_general x9, matrix products, dot(): lax.dot_general(left, right, (((left_dim,), (right_dim,)), ((), ())), pre...  30.4 us
    pallas_call x2, Pallas kernels, ffn_back(): pl.pallas_call(functools.partial(ffn_back_kernel, len(grads)), grid=(dept...  25.7 us
    pallas_call x1, Pallas kernels, mixer_in(): pl.pallas_call(functools.partial(mixer_in_kernel, count), grid_spec=pltpu...  22.6 us
    pallas_call x1, Pallas kernels, mixer_out(): pl.pallas_call(mixer_out_kernel, grid=(depth // tile,), in_specs=[pl.Bloc...  18.4 us
  transfers between devices with their start and end apart: 59, of which 24 were waited for; matrix products, arithmetic and copies ran while one was open for 8% of the time, Pallas kernels for 23%

profile of v5, /device:TPU:0, one launch (start us, length us, event | category | flops | bytes accessed | tf_op | source)
XLA Modules:
  0.0 778.0 jit_solution(17009789421284435345)
XLA Ops:
  9.3 3.6 pack_columns.2
  13.1 5.0 collective-permute-start
  19.4 21.1 %collective-permute-done.refs_1_ = bf16[256,2048]{1,0:T(8,128)(2,1)S(1)} collective-permute-done((bf16[256,2048]{1,0:T(8,128)(2,1)S(1)}, bf16[256,2048]{1,0:T(8,128)(2,1)S(1)}, u32[]{:S(2)}, u32[]{:S(2)}) %collective-permute-start) | collective-permute-done | bytes 1048608 | tf_op jit(solution)/shard_map/ppermute | solution.py:53
  40.4 4.2 collective-permute-done.1.refs_4_
  47.2 4.2 pack_columns.3
  51.5 22.0 %collective-permute-done.3.refs_5_ = bf16[256,2048]{1,0:T(8,128)(2,1)} collective-permute-done((bf16[256,2048]{1,0:T(8,128)(2,1)S(1)}, bf16[256,2048]{1,0:T(8,128)(2,1)}, u32[]{:S(2)}, u32[]{:S(2)}) %collective-permute-start.3) | collective-permute-done | bytes 1048608 | tf_op jit(solution)/shard_map/ppermute | solution.py:53
  82.1 19.1 %collective-permute-done.5.refs_6_ = bf16[256,2048]{1,0:T(8,128)(2,1)S(1)} collective-permute-done((bf16[256,2048]{1,0:T(8,128)(2,1)}, bf16[256,2048]{1,0:T(8,128)(2,1)S(1)}, u32[]{:S(2)}, u32[]{:S(2)}) %collective-permute-start.5) | collective-permute-done | bytes 1048608 | tf_op jit(solution)/shard_map/ppermute | solution.py:53
  102.2 22.6 %mixer_in.1 = (f32[1024,2688]{1,0:T(8,128)}, bf16[1024,2048]{1,0:T(8,128)(2,1)}) custom-call(s32[1]{0:T(128)} %bitcast.1.place_ref, f32[1,2048]{1,0:T(1,128)} %get-tuple-element.447.gain_ref, bf16[2048,3712]{1,0:T(8,128)(2,1)} %all-gather.3.cloned.1.call-done.w_ref, bf16[256,2048]{1,0:T(8,128)(2,1)} %bitcast.42, bf16[256,2048]{1,0:T(8,128)(2,1)} %copy-done.40, ...), custom_call_target="tpu_custom_call" | custom-call | flops 11274289152 | bytes 30408704 | tf_op jit(solution)/shard_map/mixer_in/pallas_call | solution.py:745
  124.8 16.5 %mixer_forward.1 = (bf16[1024,1024]{1,0:T(8,128)(2,1)}, f32[4,256,768]{2,1,0:T(8,128)}, bf16[1024,128]{1,0:T(8,128)(2,1)}, bf16[1024,128]{1,0:T(8,128)(2,1)}) custom-call(s32[1]{0:T(128)} %bitcast.1.place_ref, f32[1024,2688]{1,0:T(8,128)} %get-tuple-element.235.mixed_ref, f32[1024,128]{1,0:T(8,128)} %get-tuple-element.461.cos_ref, ...), custom_call_target="tpu_custom_call" | custom-call | flops 8000000000 | bytes 20000000 | tf_op jit(solution)/shard_map/mixer_forward/pallas_call | solution.py:548
  146.7 4.0 collective-permute-start.7
  162.9 4.4 collective-permute-start.9
  174.1 4.4 collective-permute-start.15
  179.3 5.8 collective-permute-done.9
  185.4 4.4 collective-permute-start.11
  191.1 5.2 collective-permute-done.15
  196.6 4.4 collective-permute-start.17
  207.5 7.2 collective-permute-done.17
  220.5 6.4 all-gather.5.cloned.1.call-done.gate_ref.up_ref.refs_2_.refs_3_.refs_1_
  226.9 10.5 %fusion.act_grad_ref = f32[512,2048]{1,0:T(8,128)} fusion(bf16[2048,6144]{1,0:T(8,128)(2,1)} %all-gather.5.cloned.1.call-done.gate_ref.up_ref.refs_2_.refs_3_.refs_1_, bf16[256,2048]{1,0:T(8,128)(2,1)} %copy-done.22, bf16[256,2048]{1,0:T(8,128)(2,1)} %bitcast.46), kind=kOutput, calls=%fused_computation | convolution fusion | flops 4299161600 | bytes 14680064 | tf_op jit(solution)/shard_map/dot_general | solution.py:153
  240.2 16.9 %ffn_inner.1 = (bf16[512,2048]{1,0:T(8,128)(2,1)}, bf16[512,2048]{1,0:T(8,128)(2,1)}, bf16[512,2048]{1,0:T(8,128)(2,1)}, bf16[512,2048]{1,0:T(8,128)(2,1)}) custom-call(bf16[256,2048]{1,0:T(8,128)(2,1)} %multiply_convert_fusion.own_ref, bf16[256,2048]{1,0:T(8,128)(2,1)} %collective-permute-done.19.other_ref, f32[512,2048]{1,0:T(8,128)} %fusion.act_grad_ref, ...), custom_call_target="tpu_custom_call" | custom-call | flops 8589934592 | bytes 31457280 | tf_op jit(solution)/shard_map/ffn_inner/pallas_call | solution.py:805
  257.2 15.1 %ffn_back.2 = (f32[256,2048]{1,0:T(8,128)}, bf16[256,2048]{1,0:T(8,128)(2,1)}) custom-call(bf16[512,2048]{1,0:T(8,128)(2,1)} %get-tuple-element.274.refs_0_.refs_1_, bf16[512,2048]{1,0:T(8,128)(2,1)} %get-tuple-element.283.refs_1_.refs_2_, bf16[2048,6144]{1,0:T(8,128)(2,1)} %all-gather.5.cloned.1.call-done.gate_ref.up_ref.refs_2_.refs_3_.refs_1_, ...), custom_call_target="tpu_custom_call" | custom-call | flops 8589934592 | bytes 25165824 | tf_op jit(solution)/shard_map/ffn_back/pallas_call | solution.py:838
  274.0 12.2 %weight_grads.3 = bf16[2048,3072]{1,0:T(8,128)(2,1)} custom-call(bf16[512,2048]{1,0:T(8,128)(2,1)} %get-tuple-element.272.refs_0_, bf16[512,2048]{1,0:T(8,128)(2,1)} %get-tuple-element.274.refs_0_.refs_1_, bf16[512,2048]{1,0:T(8,128)(2,1)} %get-tuple-element.283.refs_1_.refs_2_), custom_call_target="tpu_custom_call" | custom-call | flops 6442450944 | bytes 18874368 | tf_op jit(solution)/shard_map/weight_grads/pallas_call | solution.py:964
  286.2 8.8 %collective-permute-done.20.swap_ref = bf16[256,2048]{1,0:T(8,128)(2,1)S(1)} collective-permute-done((bf16[256,2048]{1,0:T(8,128)(2,1)}, bf16[256,2048]{1,0:T(8,128)(2,1)S(1)}, u32[]{:S(2)}, u32[]{:S(2)}) %collective-permute-start.20) | collective-permute-done | bytes 1048608 | tf_op jit(solution)/shard_map/ppermute | solution.py:29
  296.0 5.6 norm_back.1
  301.6 3.5 collective-permute-start.22
  307.9 14.8 %weight_grads.4 = bf16[2048,3072]{1,0:T(8,128)(2,1)} custom-call(bf16[512,2048]{1,0:T(8,128)(2,1)} %get-tuple-element.272.refs_0_, bf16[512,2048]{1,0:T(8,128)(2,1)} %pad_maximum_fusion.refs_1_, bf16[512,2048]{1,0:T(8,128)(2,1)} %get-tuple-element.283.refs_1_.refs_2_, bf16[512,2048]{1,0:T(8,128)(2,1)} %get-tuple-element.290.refs_3_.refs_0_), custom_call_target="tpu_custom_call" | custom-call | flops 6442450944 | bytes 20971520 | tf_op jit(solution)/shard_map/weight_grads/pallas_call | solution.py:964
  324.1 10.4 %collective-permute-done.23.refs_4_ = bf16[256,2048]{1,0:T(8,128)(2,1)S(1)} collective-permute-done((bf16[256,2048]{1,0:T(8,128)(2,1)}, bf16[256,2048]{1,0:T(8,128)(2,1)S(1)}, u32[]{:S(2)}, u32[]{:S(2)}) %collective-permute-start.23) | collective-permute-done | bytes 1048608 | tf_op jit(solution)/shard_map/ppermute | solution.py:53
  337.6 10.6 %ffn_back.3 = (f32[256,2048]{1,0:T(8,128)}, bf16[256,2048]{1,0:T(8,128)(2,1)}) custom-call(bf16[512,2048]{1,0:T(8,128)(2,1)} %get-tuple-element.290.refs_3_.refs_0_, bf16[2048,6144]{1,0:T(8,128)(2,1)} %all-gather.5.cloned.1.call-done.gate_ref.up_ref.refs_2_.refs_3_.refs_1_), custom_call_target="tpu_custom_call" | custom-call | flops 4294967296 | bytes 25165824 | tf_op jit(solution)/shard_map/ffn_back/pallas_call | solution.py:838
  348.2 13.9 %collective-permute-done.25.refs_5_ = bf16[256,2048]{1,0:T(8,128)(2,1)} collective-permute-done((bf16[256,2048]{1,0:T(8,128)(2,1)S(1)}, bf16[256,2048]{1,0:T(8,128)(2,1)}, u32[]{:S(2)}, u32[]{:S(2)}) %collective-permute-start.25) | collective-permute-done | bytes 1048608 | tf_op jit(solution)/shard_map/ppermute | solution.py:53
  364.3 4.9 slice.147.w_ref
  370.9 17.3 %collective-permute-done.27.refs_6_ = bf16[256,2048]{1,0:T(8,128)(2,1)} collective-permute-done((bf16[256,2048]{1,0:T(8,128)(2,1)}, bf16[256,2048]{1,0:T(8,128)(2,1)}, u32[]{:S(2)}, u32[]{:S(2)}) %collective-permute-start.27) | collective-permute-done | bytes 1048608 | tf_op jit(solution)/shard_map/ppermute | solution.py:53
  388.2 10.9 %joint.1 = (f32[1024,1024]{1,0:T(8,128)}, bf16[1024,2048]{1,0:T(8,128)(2,1)}) custom-call(s32[1]{0:T(128)} %bitcast.1.place_ref, bf16[2048,1024]{1,0:T(8,128)(2,1)} %slice.147.w_ref, bf16[256,2048]{1,0:T(8,128)(2,1)} %get-tuple-element.281.refs_0_, bf16[256,2048]{1,0:T(8,128)(2,1)} %copy-done.37, bf16[256,2048]{1,0:T(8,128)(2,1)} %collective-permute-done.24.refs_2_, ...), custom_call_target="tpu_custom_call" | custom-call | flops 4294967296 | bytes 12582912 | tf_op jit(solution)/shard_map/joint/pallas_call | solution.py:874
  400.4 33.1 %mixer_backward.1 = (bf16[1024,2688]{1,0:T(8,128)(2,1)}, f32[8,128]{1,0:T(8,128)}) custom-call(s32[1]{0:T(128)} %bitcast.1.place_ref, f32[1024,2688]{1,0:T(8,128)} %get-tuple-element.235.mixed_ref, f32[1024,1024]{1,0:T(8,128)} %get-tuple-element.299.joint_ref, f32[4,256,768]{2,1,0:T(8,128)} %get-tuple-element.300.state_ref, ...), custom_call_target="tpu_custom_call" | custom-call | flops 20000000000 | bytes 30000000 | tf_op jit(solution)/shard_map/mixer_backward/pallas_call | solution.py:596
  435.0 4.9 collective-permute-start.29
  441.2 18.4 %mixer_out.1 = (f32[8,2048]{1,0:T(8,128)}, f32[256,2048]{1,0:T(8,128)}, bf16[256,2048]{1,0:T(8,128)(2,1)}, bf16[256,2048]{1,0:T(8,128)(2,1)}, bf16[256,2048]{1,0:T(8,128)(2,1)}) custom-call(bf16[1024,2688]{1,0:T(8,128)(2,1)} %get-tuple-element.310.grad_ref.refs_2_, bf16[2048,3712]{1,0:T(8,128)(2,1)} %all-gather.3.cloned.1.call-done.w_ref, ...), custom_call_target="tpu_custom_call" | custom-call | flops 11274289152 | bytes 30212096 | tf_op jit(solution)/shard_map/mixer_out/pallas_call | solution.py:910
  463.4 7.3 collective-permute-start.33
  472.1 23.2 %weight_grads.5 = bf16[2048,3712]{1,0:T(8,128)(2,1)} custom-call(bf16[1024,2048]{1,0:T(8,128)(2,1)} %get-tuple-element.311.normed_ref.refs_0_, bf16[1024,2048]{1,0:T(8,128)(2,1)} %get-tuple-element.325.refs_1_, bf16[1024,2688]{1,0:T(8,128)(2,1)} %get-tuple-element.310.grad_ref.refs_2_, bf16[1024,1024]{1,0:T(8,128)(2,1)} %get-tuple-element.254.refs_3_, ...), custom_call_target="tpu_custom_call" | custom-call | flops 15569256448 | bytes 31260672 | tf_op jit(solution)/shard_map/weight_grads/pallas_call | solution.py:964
  505.1 22.4 %collective-permute-done.35 = bf16[128,3072]{1,0:T(8,128)(2,1)S(1)} collective-permute-done((bf16[128,3072]{1,0:T(8,128)(2,1)S(1)}, bf16[128,3072]{1,0:T(8,128)(2,1)S(1)}, u32[]{:S(2)}, u32[]{:S(2)}) %collective-permute-start.35) | collective-permute-done | bytes 786464 | tf_op jit(solution)/shard_map/ppermute | solution.py:53
  533.0 4.1 collective-permute-start.38
  538.4 29.6 %collective-permute-done.38.refs_8_ = bf16[128,3072]{1,0:T(8,128)(2,1)S(1)} collective-permute-done((bf16[128,3072]{1,0:T(8,128)(2,1)S(1)}, bf16[128,3072]{1,0:T(8,128)(2,1)S(1)}, u32[]{:S(2)}, u32[]{:S(2)}) %collective-permute-start.38) | collective-permute-done | bytes 786464 | tf_op jit(solution)/shard_map/ppermute | solution.py:53
  568.9 6.6 collective-permute-start.44
  578.9 34.2 %collective-permute-done.43.refs_12_ = bf16[128,3072]{1,0:T(8,128)(2,1)S(1)} collective-permute-done((bf16[128,3072]{1,0:T(8,128)(2,1)S(1)}, bf16[128,3072]{1,0:T(8,128)(2,1)S(1)}, u32[]{:S(2)}, u32[]{:S(2)}) %collective-permute-start.43) | collective-permute-done | bytes 786464 | tf_op jit(solution)/shard_map/ppermute | solution.py:53
  614.5 4.4 collective-permute-start.46
  622.2 53.1 %collective-permute-done.49.refs_13_ = bf16[128,3072]{1,0:T(8,128)(2,1)S(1)} collective-permute-done((bf16[128,3072]{1,0:T(8,128)(2,1)}, bf16[128,3072]{1,0:T(8,128)(2,1)S(1)}, u32[]{:S(2)}, u32[]{:S(2)}) %collective-permute-start.49) | collective-permute-done | bytes 786464 | tf_op jit(solution)/shard_map/ppermute | solution.py:53
  678.6 10.0 %unpack_ffn.1 = (f32[256,4096]{1,0:T(8,128)}, f32[256,4096]{1,0:T(8,128)}, f32[256,4096]{1,0:T(8,128)}) custom-call(s32[1]{0:T(128)} %bitcast.1.place_ref, bf16[128,3072]{1,0:T(8,128)(2,1)} %copy-done.8, bf16[128,3072]{1,0:T(8,128)(2,1)} %collective-permute-done.29.refs_1_, bf16[128,3072]{1,0:T(8,128)(2,1)} %collective-permute-done.31.refs_2_, ...), custom_call_target="tpu_custom_call" | custom-call | flops 100000000 | bytes 22000000 | tf_op jit(solution)/shard_map/unpack_ffn/pallas_call | solution.py:1107
  688.6 28.4 %collective-permute-done.51.refs_5_ = bf16[256,3712]{1,0:T(8,128)(2,1)} collective-permute-done((bf16[256,3712]{1,0:T(8,128)(2,1)}, bf16[256,3712]{1,0:T(8,128)(2,1)}, u32[]{:S(2)}, u32[]{:S(2)}) %collective-permute-start.51) | collective-permute-done | bytes 1900576 | tf_op jit(solution)/shard_map/ppermute | solution.py:53
  724.5 31.6 %collective-permute-done.53.refs_6_ = bf16[256,3712]{1,0:T(8,128)(2,1)} collective-permute-done((bf16[256,3712]{1,0:T(8,128)(2,1)}, bf16[256,3712]{1,0:T(8,128)(2,1)}, u32[]{:S(2)}, u32[]{:S(2)}) %collective-permute-start.53) | collective-permute-done | bytes 1900576 | tf_op jit(solution)/shard_map/ppermute | solution.py:53
  756.2 9.0 %unpack_mixer.1 = (f32[256,8192]{1,0:T(8,128)}, f32[256,1024]{1,0:T(8,128)}, f32[256,3072]{1,0:T(8,128)}, f32[256,128]{1,0:T(8,128)}) custom-call(s32[1]{0:T(128)} %bitcast.1.place_ref, bf16[256,3712]{1,0:T(8,128)(2,1)} %reduce-scatter.8.cloned.1.call-done.refs_0_, bf16[256,3712]{1,0:T(8,128)(2,1)} %collective-permute-done.46.refs_1_, ...), custom_call_target="tpu_custom_call" | custom-call | flops 100000000 | bytes 26000000 | tf_op jit(solution)/shard_map/unpack_mixer/pallas_call | solution.py:1053
  (270 shorter events, 122.6 us)
Async XLA Ops:
  7.2 95.0 %all-gather.3.cloned.1.call-start = ((), (), s32[]{:S(2)}) async-start(), calls=%async_computation.3 | async-start | bytes 17104896 | tf_op jit(solution)/shard_map/all_gather | solution.py:145
  13.0 213.9 %all-gather.5.cloned.1.call-start = ((), (), s32[]{:S(2)}) async-start(), calls=%async_computation.4 | async-start | bytes 28311552 | tf_op jit(solution)/shard_map/all_gather | solution.py:145
  13.1 27.4 %collective-permute-start = (bf16[256,2048]{1,0:T(8,128)(2,1)S(1)}, bf16[256,2048]{1,0:T(8,128)(2,1)S(1)}, u32[]{:S(2)}, u32[]{:S(2)}) collective-permute-start(bf16[256,2048]{1,0:T(8,128)(2,1)S(1)} %bitcast.43), channel_id=1, source_target_pairs={{0,1},{1,2},{2,3},{4,5},{5,6},{6,7},{8,9},{9,10},{10,11},{12,13},{... | collective-permute-start | bytes 3145736 | tf_op jit(solution)/shard_map/ppermute | solution.py:53
  18.1 26.5 %collective-permute-start.1 = (bf16[256,2048]{1,0:T(8,128)(2,1)S(1)}, bf16[256,2048]{1,0:T(8,128)(2,1)S(1)}, u32[]{:S(2)}, u32[]{:S(2)}) collective-permute-start(bf16[256,2048]{1,0:T(8,128)(2,1)S(1)} %bitcast.44), channel_id=1, source_target_pairs={{1,0},{2,1},{3,2},{5,4},{6,5},{7,6},{9,8},{10,9},{11,10},{13,12},{... | collective-permute-start | bytes 3145736 | tf_op jit(solution)/shard_map/ppermute | solution.py:53
  45.3 28.1 %collective-permute-start.3 = (bf16[256,2048]{1,0:T(8,128)(2,1)S(1)}, bf16[256,2048]{1,0:T(8,128)(2,1)}, u32[]{:S(2)}, u32[]{:S(2)}) collective-permute-start(bf16[256,2048]{1,0:T(8,128)(2,1)S(1)} %collective-permute-done.1.refs_4_), channel_id=1, source_target_pairs={{1,0},{2,1},{5,4},{6,5},{9,8},{10,9},{13,12},{14,13},{17,16},{18,1... | collective-permute-start | bytes 3145736 | tf_op jit(solution)/shard_map/ppermute | solution.py:53
  73.5 325.7 %reduce-scatter.4.cloned.1.call-start = ((), (), s32[]{:S(2)}) async-start(), calls=%async_computation.5 | async-start | bytes 14155776 | tf_op jit(solution)/shard_map/reduce_scatter | solution.py:149
  76.2 25.0 %collective-permute-start.5 = (bf16[256,2048]{1,0:T(8,128)(2,1)}, bf16[256,2048]{1,0:T(8,128)(2,1)S(1)}, u32[]{:S(2)}, u32[]{:S(2)}) collective-permute-start(bf16[256,2048]{1,0:T(8,128)(2,1)} %collective-permute-done.3.refs_5_), channel_id=1, source_target_pairs={{1,0},{5,4},{9,8},{13,12},{17,16},{21,20},{25,24},{29,28}} | collective-permute-start | bytes 3145736 | tf_op jit(solution)/shard_map/ppermute | solution.py:53
  102.2 39.2 %collective-permute-start.6 = (bf16[256,2048]{1,0:T(8,128)(2,1)S(1)}, bf16[256,2048]{1,0:T(8,128)(2,1)S(1)}, u32[]{:S(2)}, u32[]{:S(2)}) collective-permute-start(bf16[256,2048]{1,0:T(8,128)(2,1)S(1)} %bitcast.48), channel_id=1, source_target_pairs={{0,1},{1,0},{2,3},{3,2},{4,5},{5,4},{6,7},{7,6},{8,9},{9,8},{10,11... | collective-permute-start | bytes 3145736 | tf_op jit(solution)/shard_map/ppermute | solution.py:29
  146.7 15.9 %collective-permute-start.7 = (bf16[256,1024]{1,0:T(8,128)(2,1)S(1)}, bf16[256,1024]{1,0:T(8,128)(2,1)S(1)}, u32[]{:S(2)}, u32[]{:S(2)}) collective-permute-start(bf16[256,1024]{1,0:T(8,128)(2,1)S(1)} %get-tuple-element.239), channel_id=1, source_target_pairs={{0,1},{4,5},{8,9},{12,13},{16,17},{20,21},{24,25},{28,29}} | collective-permute-start | bytes 1572872 | tf_op jit(solution)/shard_map/ppermute | solution.py:53
  157.0 16.8 %collective-permute-start.13 = (bf16[256,1024]{1,0:T(8,128)(2,1)S(1)}, bf16[256,1024]{1,0:T(8,128)(2,1)S(1)}, u32[]{:S(2)}, u32[]{:S(2)}) collective-permute-start(bf16[256,1024]{1,0:T(8,128)(2,1)S(1)} %get-tuple-element.252), channel_id=1, source_target_pairs={{0,1},{4,5},{8,9},{12,13},{16,17},{20,21},{24,25},{28,29}} | collective-permute-start | bytes 1572872 | tf_op jit(solution)/shard_map/ppermute | solution.py:53
  162.9 22.2 %collective-permute-start.9 = (bf16[256,1024]{1,0:T(8,128)(2,1)S(1)}, bf16[256,1024]{1,0:T(8,128)(2,1)S(1)}, u32[]{:S(2)}, u32[]{:S(2)}) collective-permute-start(bf16[256,1024]{1,0:T(8,128)(2,1)S(1)} %get-tuple-element.244), channel_id=1, source_target_pairs={{0,1},{1,2},{4,5},{5,6},{8,9},{9,10},{12,13},{13,14},{16,17},{17,1... | collective-permute-start | bytes 1572872 | tf_op jit(solution)/shard_map/ppermute | solution.py:53
  167.3 17.7 %collective-permute-start.10 = (bf16[256,1024]{1,0:T(8,128)(2,1)S(1)}, bf16[256,1024]{1,0:T(8,128)(2,1)S(1)}, u32[]{:S(2)}, u32[]{:S(2)}) collective-permute-start(bf16[256,1024]{1,0:T(8,128)(2,1)S(1)} %get-tuple-element.245), channel_id=1, source_target_pairs={{2,1},{3,2},{6,5},{7,6},{10,9},{11,10},{14,13},{15,14},{18,17},{19... | collective-permute-start | bytes 1572872 | tf_op jit(solution)/shard_map/ppermute | solution.py:53
  174.1 22.2 %collective-permute-start.15 = (bf16[256,1024]{1,0:T(8,128)(2,1)S(1)}, bf16[256,1024]{1,0:T(8,128)(2,1)S(1)}, u32[]{:S(2)}, u32[]{:S(2)}) collective-permute-start(bf16[256,1024]{1,0:T(8,128)(2,1)S(1)} %get-tuple-element.257), channel_id=1, source_target_pairs={{0,1},{1,2},{4,5},{5,6},{8,9},{9,10},{12,13},{13,14},{16,17},{17,1... | collective-permute-start | bytes 1572872 | tf_op jit(solution)/shard_map/ppermute | solution.py:53
  178.6 17.7 %collective-permute-start.16 = (bf16[256,1024]{1,0:T(8,128)(2,1)S(1)}, bf16[256,1024]{1,0:T(8,128)(2,1)S(1)}, u32[]{:S(2)}, u32[]{:S(2)}) collective-permute-start(bf16[256,1024]{1,0:T(8,128)(2,1)S(1)} %get-tuple-element.258), channel_id=1, source_target_pairs={{2,1},{3,2},{6,5},{7,6},{10,9},{11,10},{14,13},{15,14},{18,17},{19... | collective-permute-start | bytes 1572872 | tf_op jit(solution)/shard_map/ppermute | solution.py:53
  185.4 22.2 %collective-permute-start.11 = (bf16[256,1024]{1,0:T(8,128)(2,1)S(1)}, bf16[256,1024]{1,0:T(8,128)(2,1)S(1)}, u32[]{:S(2)}, u32[]{:S(2)}) collective-permute-start(bf16[256,1024]{1,0:T(8,128)(2,1)S(1)} %add_convert_fusion.10), channel_id=1, source_target_pairs={{0,1},{1,2},{2,3},{4,5},{5,6},{6,7},{8,9},{9,10},{10,11},{12,13},{... | collective-permute-start | bytes 1572872 | tf_op jit(solution)/shard_map/ppermute | solution.py:53
  189.8 17.7 %collective-permute-start.12 = (bf16[256,1024]{1,0:T(8,128)(2,1)S(1)}, bf16[256,1024]{1,0:T(8,128)(2,1)S(1)}, u32[]{:S(2)}, u32[]{:S(2)}) collective-permute-start(bf16[256,1024]{1,0:T(8,128)(2,1)S(1)} %add_convert_fusion.9), channel_id=1, source_target_pairs={{1,0},{2,1},{3,2},{5,4},{6,5},{7,6},{9,8},{10,9},{11,10},{13,12},{... | collective-permute-start | bytes 1572872 | tf_op jit(solution)/shard_map/ppermute | solution.py:53
  196.6 18.1 %collective-permute-start.17 = (bf16[256,1024]{1,0:T(8,128)(2,1)S(1)}, bf16[256,1024]{1,0:T(8,128)(2,1)S(1)}, u32[]{:S(2)}, u32[]{:S(2)}) collective-permute-start(bf16[256,1024]{1,0:T(8,128)(2,1)S(1)} %add_convert_fusion.6), channel_id=1, source_target_pairs={{0,1},{1,2},{2,3},{4,5},{5,6},{6,7},{8,9},{9,10},{10,11},{12,13},{... | collective-permute-start | bytes 1572872 | tf_op jit(solution)/shard_map/ppermute | solution.py:53
  218.0 22.3 %collective-permute-start.19 = (bf16[256,2048]{1,0:T(8,128)(2,1)}, bf16[256,2048]{1,0:T(8,128)(2,1)}, u32[]{:S(2)}, u32[]{:S(2)}) collective-permute-start(bf16[256,2048]{1,0:T(8,128)(2,1)} %multiply_convert_fusion.own_ref), channel_id=1, source_target_pairs={{0,1},{1,0},{2,3},{3,2},{4,5},{5,4},{6,7},{7,6},{8,9},{9,8},{10,11... | collective-permute-start | bytes 3145736 | tf_op jit(solution)/shard_map/ppermute | solution.py:29
  272.3 22.7 %collective-permute-start.20 = (bf16[256,2048]{1,0:T(8,128)(2,1)}, bf16[256,2048]{1,0:T(8,128)(2,1)S(1)}, u32[]{:S(2)}, u32[]{:S(2)}) collective-permute-start(bf16[256,2048]{1,0:T(8,128)(2,1)} %get-tuple-element.271), channel_id=1, source_target_pairs={{0,1},{1,0},{2,3},{3,2},{4,5},{5,4},{6,7},{7,6},{8,9},{9,8},{10,11... | collective-permute-start | bytes 3145736 | tf_op jit(solution)/shard_map/ppermute | solution.py:29
  296.0 201.3 %reduce-scatter.6.cloned.1.call-start = ((), (), s32[]{:S(2)}) async-start(), calls=%async_computation.6 | async-start | bytes 14155776 | tf_op jit(solution)/shard_map/reduce_scatter | solution.py:149
  301.6 22.6 %collective-permute-start.22 = (bf16[256,2048]{1,0:T(8,128)(2,1)}, bf16[256,2048]{1,0:T(8,128)(2,1)S(1)}, u32[]{:S(2)}, u32[]{:S(2)}) collective-permute-start(bf16[256,2048]{1,0:T(8,128)(2,1)} %get-tuple-element.281.refs_0_), channel_id=1, source_target_pairs={{0,1},{1,2},{2,3},{4,5},{5,6},{6,7},{8,9},{9,10},{10,11},{12,13},{... | collective-permute-start | bytes 3145736 | tf_op jit(solution)/shard_map/ppermute | solution.py:53
  305.0 29.5 %collective-permute-start.23 = (bf16[256,2048]{1,0:T(8,128)(2,1)}, bf16[256,2048]{1,0:T(8,128)(2,1)S(1)}, u32[]{:S(2)}, u32[]{:S(2)}) collective-permute-start(bf16[256,2048]{1,0:T(8,128)(2,1)} %get-tuple-element.281.refs_0_), channel_id=1, source_target_pairs={{1,0},{2,1},{3,2},{5,4},{6,5},{7,6},{9,8},{10,9},{11,10},{13,12},{... | collective-permute-start | bytes 3145736 | tf_op jit(solution)/shard_map/ppermute | solution.py:53
  334.6 279.9 %reduce-scatter.8.cloned.1.call-start = ((), (), s32[]{:S(2)}) async-start(), calls=%async_computation.7 | async-start | bytes 17104896 | tf_op jit(solution)/shard_map/reduce_scatter | solution.py:149
  336.3 25.8 %collective-permute-start.25 = (bf16[256,2048]{1,0:T(8,128)(2,1)S(1)}, bf16[256,2048]{1,0:T(8,128)(2,1)}, u32[]{:S(2)}, u32[]{:S(2)}) collective-permute-start(bf16[256,2048]{1,0:T(8,128)(2,1)S(1)} %collective-permute-done.23.refs_4_), channel_id=1, source_target_pairs={{1,0},{2,1},{5,4},{6,5},{9,8},{10,9},{13,12},{14,13},{17,16},{18,1... | collective-permute-start | bytes 3145736 | tf_op jit(solution)/shard_map/ppermute | solution.py:53
  362.8 25.4 %collective-permute-start.27 = (bf16[256,2048]{1,0:T(8,128)(2,1)}, bf16[256,2048]{1,0:T(8,128)(2,1)}, u32[]{:S(2)}, u32[]{:S(2)}) collective-permute-start(bf16[256,2048]{1,0:T(8,128)(2,1)} %collective-permute-done.25.refs_5_), channel_id=1, source_target_pairs={{1,0},{5,4},{9,8},{13,12},{17,16},{21,20},{25,24},{29,28}} | collective-permute-start | bytes 3145736 | tf_op jit(solution)/shard_map/ppermute | solution.py:53
  388.2 45.3 %collective-permute-start.28 = (bf16[256,2048]{1,0:T(8,128)(2,1)S(1)}, bf16[256,2048]{1,0:T(8,128)(2,1)S(1)}, u32[]{:S(2)}, u32[]{:S(2)}) collective-permute-start(bf16[256,2048]{1,0:T(8,128)(2,1)S(1)} %copy-done.39), channel_id=1, source_target_pairs={{0,1},{1,0},{2,3},{3,2},{4,5},{5,4},{6,7},{7,6},{8,9},{9,8},{10,11... | collective-permute-start | bytes 3145736 | tf_op jit(solution)/shard_map/ppermute | solution.py:29
  400.3 33.3 %collective-permute-start.21 = (bf16[128,3072]{1,0:T(8,128)(2,1)S(1)}, bf16[128,3072]{1,0:T(8,128)(2,1)S(1)}, u32[]{:S(2)}, u32[]{:S(2)}) collective-permute-start(bf16[128,3072]{1,0:T(8,128)(2,1)S(1)} %constant_dynamic-slice_fusion.1), channel_id=1, source_target_pairs={{0,2},{1,3},{2,0},{3,1},{4,6},{5,7},{6,4},{7,5},{8,10},{9,11},{10,... | collective-permute-start | bytes 2359304 | tf_op jit(solution)/shard_map/ppermute | solution.py:53
  435.0 24.5 %collective-permute-start.29 = (bf16[128,3072]{1,0:T(8,128)(2,1)S(1)}, bf16[128,3072]{1,0:T(8,128)(2,1)}, u32[]{:S(2)}, u32[]{:S(2)}) collective-permute-start(bf16[128,3072]{1,0:T(8,128)(2,1)S(1)} %add_convert_fusion.4.refs_0_), channel_id=1, source_target_pairs={{0,1},{1,2},{2,3},{4,5},{5,6},{6,7},{8,9},{9,10},{10,11},{12,13},{... | collective-permute-start | bytes 2359304 | tf_op jit(solution)/shard_map/ppermute | solution.py:53
  439.9 19.7 %collective-permute-start.30 = (bf16[128,3072]{1,0:T(8,128)(2,1)S(1)}, bf16[128,3072]{1,0:T(8,128)(2,1)}, u32[]{:S(2)}, u32[]{:S(2)}) collective-permute-start(bf16[128,3072]{1,0:T(8,128)(2,1)S(1)} %add_convert_fusion.4.refs_0_), channel_id=1, source_target_pairs={{1,0},{2,1},{3,2},{5,4},{6,5},{7,6},{9,8},{10,9},{11,10},{13,12},{... | collective-permute-start | bytes 2359304 | tf_op jit(solution)/shard_map/ppermute | solution.py:53
  460.5 34.8 %collective-permute-start.31 = (bf16[128,3072]{1,0:T(8,128)(2,1)}, bf16[128,3072]{1,0:T(8,128)(2,1)}, u32[]{:S(2)}, u32[]{:S(2)}) collective-permute-start(bf16[128,3072]{1,0:T(8,128)(2,1)} %collective-permute-done.29.refs_1_), channel_id=1, source_target_pairs={{1,2},{2,3},{5,6},{6,7},{9,10},{10,11},{13,14},{14,15},{17,18},{18... | collective-permute-start | bytes 2359304 | tf_op jit(solution)/shard_map/ppermute | solution.py:53
  462.1 33.3 %collective-permute-start.32 = (bf16[128,3072]{1,0:T(8,128)(2,1)}, bf16[128,3072]{1,0:T(8,128)(2,1)}, u32[]{:S(2)}, u32[]{:S(2)}) collective-permute-start(bf16[128,3072]{1,0:T(8,128)(2,1)} %collective-permute-done.30.refs_4_), channel_id=1, source_target_pairs={{1,0},{2,1},{5,4},{6,5},{9,8},{10,9},{13,12},{14,13},{17,16},{18,1... | collective-permute-start | bytes 2359304 | tf_op jit(solution)/shard_map/ppermute | solution.py:53
  463.4 32.0 %collective-permute-start.33 = (bf16[256,2048]{1,0:T(8,128)(2,1)}, bf16[256,2048]{1,0:T(8,128)(2,1)S(1)}, u32[]{:S(2)}, u32[]{:S(2)}) collective-permute-start(bf16[256,2048]{1,0:T(8,128)(2,1)} %get-tuple-element.323), channel_id=1, source_target_pairs={{0,1},{4,5},{8,9},{12,13},{16,17},{20,21},{24,25},{28,29}} | collective-permute-start | bytes 3145736 | tf_op jit(solution)/shard_map/ppermute | solution.py:53
  470.6 24.7 %collective-permute-start.34 = (bf16[256,2048]{1,0:T(8,128)(2,1)}, bf16[256,2048]{1,0:T(8,128)(2,1)S(1)}, u32[]{:S(2)}, u32[]{:S(2)}) collective-permute-start(bf16[256,2048]{1,0:T(8,128)(2,1)} %get-tuple-element.324), channel_id=1, source_target_pairs={{3,2},{7,6},{11,10},{15,14},{19,18},{23,22},{27,26},{31,30}} | collective-permute-start | bytes 3145736 | tf_op jit(solution)/shard_map/ppermute | solution.py:53
  498.8 28.8 %collective-permute-start.35 = (bf16[128,3072]{1,0:T(8,128)(2,1)S(1)}, bf16[128,3072]{1,0:T(8,128)(2,1)S(1)}, u32[]{:S(2)}, u32[]{:S(2)}) collective-permute-start(bf16[128,3072]{1,0:T(8,128)(2,1)S(1)} %constant_dynamic-slice_fusion), channel_id=1, source_target_pairs={{0,2},{1,3},{2,0},{3,1},{4,6},{5,7},{6,4},{7,5},{8,10},{9,11},{10,... | collective-permute-start | bytes 2359304 | tf_op jit(solution)/shard_map/ppermute | solution.py:53
  500.4 27.2 %collective-permute-start.36 = (bf16[128,3072]{1,0:T(8,128)(2,1)}, bf16[128,3072]{1,0:T(8,128)(2,1)S(1)}, u32[]{:S(2)}, u32[]{:S(2)}) collective-permute-start(bf16[128,3072]{1,0:T(8,128)(2,1)} %collective-permute-done.31.refs_2_), channel_id=1, source_target_pairs={{2,3},{6,7},{10,11},{14,15},{18,19},{22,23},{26,27},{30,31}} | collective-permute-start | bytes 2359304 | tf_op jit(solution)/shard_map/ppermute | solution.py:53
  501.1 29.1 %collective-permute-start.37 = (bf16[128,3072]{1,0:T(8,128)(2,1)}, bf16[128,3072]{1,0:T(8,128)(2,1)S(1)}, u32[]{:S(2)}, u32[]{:S(2)}) collective-permute-start(bf16[128,3072]{1,0:T(8,128)(2,1)} %collective-permute-done.32.refs_5_), channel_id=1, source_target_pairs={{1,0},{5,4},{9,8},{13,12},{17,16},{21,20},{25,24},{29,28}} | collective-permute-start | bytes 2359304 | tf_op jit(solution)/shard_map/ppermute | solution.py:53
  530.4 37.7 %collective-permute-start.40 = (bf16[256,2048]{1,0:T(8,128)(2,1)S(1)}, bf16[256,2048]{1,0:T(8,128)(2,1)S(1)}, u32[]{:S(2)}, u32[]{:S(2)}) collective-permute-start(bf16[256,2048]{1,0:T(8,128)(2,1)S(1)} %get-tuple-element.343), channel_id=1, source_target_pairs={{0,1},{1,2},{4,5},{5,6},{8,9},{9,10},{12,13},{13,14},{16,17},{17,1... | collective-permute-start | bytes 3145736 | tf_op jit(solution)/shard_map/ppermute | solution.py:53
  532.3 35.8 %collective-permute-start.41 = (bf16[256,2048]{1,0:T(8,128)(2,1)S(1)}, bf16[256,2048]{1,0:T(8,128)(2,1)S(1)}, u32[]{:S(2)}, u32[]{:S(2)}) collective-permute-start(bf16[256,2048]{1,0:T(8,128)(2,1)S(1)} %get-tuple-element.344), channel_id=1, source_target_pairs={{2,1},{3,2},{6,5},{7,6},{10,9},{11,10},{14,13},{15,14},{18,17},{19... | collective-permute-start | bytes 3145736 | tf_op jit(solution)/shard_map/ppermute | solution.py:53
  533.0 35.0 %collective-permute-start.38 = (bf16[128,3072]{1,0:T(8,128)(2,1)S(1)}, bf16[128,3072]{1,0:T(8,128)(2,1)S(1)}, u32[]{:S(2)}, u32[]{:S(2)}) collective-permute-start(bf16[128,3072]{1,0:T(8,128)(2,1)S(1)} %add_convert_fusion.3.refs_7_), channel_id=1, source_target_pairs={{0,1},{1,2},{2,3},{4,5},{5,6},{6,7},{8,9},{9,10},{10,11},{12,13},{... | collective-permute-start | bytes 2359304 | tf_op jit(solution)/shard_map/ppermute | solution.py:53
  537.1 30.9 %collective-permute-start.39 = (bf16[128,3072]{1,0:T(8,128)(2,1)S(1)}, bf16[128,3072]{1,0:T(8,128)(2,1)S(1)}, u32[]{:S(2)}, u32[]{:S(2)}) collective-permute-start(bf16[128,3072]{1,0:T(8,128)(2,1)S(1)} %add_convert_fusion.3.refs_7_), channel_id=1, source_target_pairs={{1,0},{2,1},{3,2},{5,4},{6,5},{7,6},{9,8},{10,9},{11,10},{13,12},{... | collective-permute-start | bytes 2359304 | tf_op jit(solution)/shard_map/ppermute | solution.py:53
  568.9 44.2 %collective-permute-start.44 = (bf16[256,2048]{1,0:T(8,128)(2,1)S(1)}, bf16[256,2048]{1,0:T(8,128)(2,1)S(1)}, u32[]{:S(2)}, u32[]{:S(2)}) collective-permute-start(bf16[256,2048]{1,0:T(8,128)(2,1)S(1)} %add_convert_fusion.2), channel_id=1, source_target_pairs={{0,1},{1,2},{2,3},{4,5},{5,6},{6,7},{8,9},{9,10},{10,11},{12,13},{... | collective-permute-start | bytes 3145736 | tf_op jit(solution)/shard_map/ppermute | solution.py:53
  575.5 38.5 %collective-permute-start.45 = (bf16[256,2048]{1,0:T(8,128)(2,1)S(1)}, bf16[256,2048]{1,0:T(8,128)(2,1)S(1)}, u32[]{:S(2)}, u32[]{:S(2)}) collective-permute-start(bf16[256,2048]{1,0:T(8,128)(2,1)S(1)} %add_convert_fusion.1), channel_id=1, source_target_pairs={{1,0},{2,1},{3,2},{5,4},{6,5},{7,6},{9,8},{10,9},{11,10},{13,12},{... | collective-permute-start | bytes 3145736 | tf_op jit(solution)/shard_map/ppermute | solution.py:53
  577.5 35.6 %collective-permute-start.43 = (bf16[128,3072]{1,0:T(8,128)(2,1)S(1)}, bf16[128,3072]{1,0:T(8,128)(2,1)S(1)}, u32[]{:S(2)}, u32[]{:S(2)}) collective-permute-start(bf16[128,3072]{1,0:T(8,128)(2,1)S(1)} %collective-permute-done.39.refs_11_), channel_id=1, source_target_pairs={{1,0},{2,1},{5,4},{6,5},{9,8},{10,9},{13,12},{14,13},{17,16},{18,1... | collective-permute-start | bytes 2359304 | tf_op jit(solution)/shard_map/ppermute | solution.py:53
  614.5 60.8 %collective-permute-start.46 = (bf16[256,3712]{1,0:T(8,128)(2,1)}, bf16[256,3712]{1,0:T(8,128)(2,1)}, u32[]{:S(2)}, u32[]{:S(2)}) collective-permute-start(bf16[256,3712]{1,0:T(8,128)(2,1)} %reduce-scatter.8.cloned.1.call-done.refs_0_), channel_id=1, source_target_pairs={{0,1},{1,2},{2,3},{4,5},{5,6},{6,7},{8,9},{9,10},{10,11},{12,13},{... | collective-permute-start | bytes 5701640 | tf_op jit(solution)/shard_map/ppermute | solution.py:53
  618.8 56.5 %collective-permute-start.47 = (bf16[256,3712]{1,0:T(8,128)(2,1)}, bf16[256,3712]{1,0:T(8,128)(2,1)}, u32[]{:S(2)}, u32[]{:S(2)}) collective-permute-start(bf16[256,3712]{1,0:T(8,128)(2,1)} %reduce-scatter.8.cloned.1.call-done.refs_0_), channel_id=1, source_target_pairs={{1,0},{2,1},{3,2},{5,4},{6,5},{7,6},{9,8},{10,9},{11,10},{13,12},{... | collective-permute-start | bytes 5701640 | tf_op jit(solution)/shard_map/ppermute | solution.py:53
  620.8 54.5 %collective-permute-start.49 = (bf16[128,3072]{1,0:T(8,128)(2,1)}, bf16[128,3072]{1,0:T(8,128)(2,1)S(1)}, u32[]{:S(2)}, u32[]{:S(2)}) collective-permute-start(bf16[128,3072]{1,0:T(8,128)(2,1)} %copy-done.30), channel_id=1, source_target_pairs={{1,0},{5,4},{9,8},{13,12},{17,16},{21,20},{25,24},{29,28}} | collective-permute-start | bytes 2359304 | tf_op jit(solution)/shard_map/ppermute | solution.py:53
  677.3 39.7 %collective-permute-start.51 = (bf16[256,3712]{1,0:T(8,128)(2,1)}, bf16[256,3712]{1,0:T(8,128)(2,1)}, u32[]{:S(2)}, u32[]{:S(2)}) collective-permute-start(bf16[256,3712]{1,0:T(8,128)(2,1)} %collective-permute-done.47.refs_4_), channel_id=1, source_target_pairs={{1,0},{2,1},{5,4},{6,5},{9,8},{10,9},{13,12},{14,13},{17,16},{18,1... | collective-permute-start | bytes 5701640 | tf_op jit(solution)/shard_map/ppermute | solution.py:53
  718.9 37.3 %collective-permute-start.53 = (bf16[256,3712]{1,0:T(8,128)(2,1)}, bf16[256,3712]{1,0:T(8,128)(2,1)}, u32[]{:S(2)}, u32[]{:S(2)}) collective-permute-start(bf16[256,3712]{1,0:T(8,128)(2,1)} %collective-permute-done.51.refs_5_), channel_id=1, source_target_pairs={{1,0},{5,4},{9,8},{13,12},{17,16},{21,20},{25,24},{29,28}} | collective-permute-start | bytes 5701640 | tf_op jit(solution)/shard_map/ppermute | solution.py:53
  (61 other events, 1005.3 us)
Sparse Core Ops, SparseCore 0:
  13.1 85.8 all-gather.2
  101.5 125.3 all-gather.4
  295.1 96.7 reduce-scatter.3
  395.3 92.3 reduce-scatter.5
  497.4 106.7 reduce-scatter.7

commit v6 on v5

--- a/solution.py
+++ b/solution.py
@@ -389,7 +389,7 @@
             raw = mul(queries, keys, 1, 1) * SCALE
             logits = jnp.where(visible_keys(q_heads, size, at), raw, -1e30)
             weights = jnp.exp(logits - jnp.max(logits, axis=-1, keepdims=True))
-            probs = weights / jnp.sum(weights, axis=-1, keepdims=True)
+            probs = weights * (1.0 / jnp.sum(weights, axis=-1, keepdims=True))
             grad_probs = mul(grad_out, values, 1, 1)
             delta = jnp.sum(probs * grad_probs, axis=-1, keepdims=True)
             grad_raw = (probs * (grad_probs - delta) * SCALE).astype(BF16)

time: 789 us -> 789 us (level)
  no operation moved by 1% of the time
where the time goes in v6:
time: 789 us; the launch traced here: 778 us
  waiting for transfers between devices  353 us (45%)
  Pallas kernels  227 us (29%)
  starting transfers between devices  106 us (13%)
  matrix products  30.4 us (4%)
  local copies, waits for them, and re-layouts  27.9 us (4%)
  other arithmetic  18.9 us (2%)
  between operations  15.3 us (2%)
    ppermute x50, waiting for transfers between devices, __init__(): lax.ppermute(v, 'ctx', pairs)  335 us
    ppermute x50, starting transfers between devices, __init__(): lax.ppermute(v, 'ctx', pairs)  101 us
    pallas_call x3, Pallas kernels, weight_grads(): pl.pallas_call(functools.partial(outer_kernel, plan, rider_at), grid=(dep...  50.2 us
    pallas_call x1, Pallas kernels, mixer_backward(): pl.pallas_call(functools.partial(mixer_backward_kernel, cuts, q_heads, he...  33.1 us
    dot_general x9, matrix products, dot(): lax.dot_general(left, right, (((left_dim,), (right_dim,)), ((), ())), pre...  30.4 us
    pallas_call x2, Pallas kernels, ffn_back(): pl.pallas_call(functools.partial(ffn_back_kernel, len(grads)), grid=(dept...  25.7 us
    pallas_call x1, Pallas kernels, mixer_in(): pl.pallas_call(functools.partial(mixer_in_kernel, count), grid_spec=pltpu...  22.6 us
    pallas_call x1, Pallas kernels, mixer_out(): pl.pallas_call(mixer_out_kernel, grid=(depth // tile,), in_specs=[pl.Bloc...  18.4 us
  transfers between devices with their start and end apart: 59, of which 24 were waited for; matrix products, arithmetic and copies ran while one was open for 8% of the time, Pallas kernels for 23%

profile of v6, /device:TPU:0, one launch (start us, length us, event | category | flops | bytes accessed | tf_op | source)
XLA Modules:
  0.0 778.0 jit_solution(17009789421284435345)
XLA Ops:
  9.3 3.6 pack_columns.2
  13.1 5.0 collective-permute-start
  19.4 21.1 %collective-permute-done.refs_1_ = bf16[256,2048]{1,0:T(8,128)(2,1)S(1)} collective-permute-done((bf16[256,2048]{1,0:T(8,128)(2,1)S(1)}, bf16[256,2048]{1,0:T(8,128)(2,1)S(1)}, u32[]{:S(2)}, u32[]{:S(2)}) %collective-permute-start) | collective-permute-done | bytes 1048608 | tf_op jit(solution)/shard_map/ppermute | solution.py:53
  40.4 4.2 collective-permute-done.1.refs_4_
  47.2 4.2 pack_columns.3
  51.5 22.0 %collective-permute-done.3.refs_5_ = bf16[256,2048]{1,0:T(8,128)(2,1)} collective-permute-done((bf16[256,2048]{1,0:T(8,128)(2,1)S(1)}, bf16[256,2048]{1,0:T(8,128)(2,1)}, u32[]{:S(2)}, u32[]{:S(2)}) %collective-permute-start.3) | collective-permute-done | bytes 1048608 | tf_op jit(solution)/shard_map/ppermute | solution.py:53
  82.1 19.1 %collective-permute-done.5.refs_6_ = bf16[256,2048]{1,0:T(8,128)(2,1)S(1)} collective-permute-done((bf16[256,2048]{1,0:T(8,128)(2,1)}, bf16[256,2048]{1,0:T(8,128)(2,1)S(1)}, u32[]{:S(2)}, u32[]{:S(2)}) %collective-permute-start.5) | collective-permute-done | bytes 1048608 | tf_op jit(solution)/shard_map/ppermute | solution.py:53
  102.2 22.6 %mixer_in.1 = (f32[1024,2688]{1,0:T(8,128)}, bf16[1024,2048]{1,0:T(8,128)(2,1)}) custom-call(s32[1]{0:T(128)} %bitcast.1.place_ref, f32[1,2048]{1,0:T(1,128)} %get-tuple-element.447.gain_ref, bf16[2048,3712]{1,0:T(8,128)(2,1)} %all-gather.3.cloned.1.call-done.w_ref, bf16[256,2048]{1,0:T(8,128)(2,1)} %bitcast.42, bf16[256,2048]{1,0:T(8,128)(2,1)} %copy-done.40, ...), custom_call_target="tpu_custom_call" | custom-call | flops 11274289152 | bytes 30408704 | tf_op jit(solution)/shard_map/mixer_in/pallas_call | solution.py:745
  124.8 16.5 %mixer_forward.1 = (bf16[1024,1024]{1,0:T(8,128)(2,1)}, f32[4,256,768]{2,1,0:T(8,128)}, bf16[1024,128]{1,0:T(8,128)(2,1)}, bf16[1024,128]{1,0:T(8,128)(2,1)}) custom-call(s32[1]{0:T(128)} %bitcast.1.place_ref, f32[1024,2688]{1,0:T(8,128)} %get-tuple-element.235.mixed_ref, f32[1024,128]{1,0:T(8,128)} %get-tuple-element.461.cos_ref, ...), custom_call_target="tpu_custom_call" | custom-call | flops 8000000000 | bytes 20000000 | tf_op jit(solution)/shard_map/mixer_forward/pallas_call | solution.py:548
  146.7 4.0 collective-permute-start.7
  162.9 4.4 collective-permute-start.9
  174.1 4.4 collective-permute-start.15
  179.3 5.8 collective-permute-done.9
  185.4 4.4 collective-permute-start.11
  191.1 5.2 collective-permute-done.15
  196.6 4.4 collective-permute-start.17
  207.5 7.2 collective-permute-done.17
  220.5 6.4 all-gather.5.cloned.1.call-done.gate_ref.up_ref.refs_2_.refs_3_.refs_1_
  226.9 10.5 %fusion.act_grad_ref = f32[512,2048]{1,0:T(8,128)} fusion(bf16[2048,6144]{1,0:T(8,128)(2,1)} %all-gather.5.cloned.1.call-done.gate_ref.up_ref.refs_2_.refs_3_.refs_1_, bf16[256,2048]{1,0:T(8,128)(2,1)} %copy-done.22, bf16[256,2048]{1,0:T(8,128)(2,1)} %bitcast.46), kind=kOutput, calls=%fused_computation | convolution fusion | flops 4299161600 | bytes 14680064 | tf_op jit(solution)/shard_map/dot_general | solution.py:153
  240.2 16.9 %ffn_inner.1 = (bf16[512,2048]{1,0:T(8,128)(2,1)}, bf16[512,2048]{1,0:T(8,128)(2,1)}, bf16[512,2048]{1,0:T(8,128)(2,1)}, bf16[512,2048]{1,0:T(8,128)(2,1)}) custom-call(bf16[256,2048]{1,0:T(8,128)(2,1)} %multiply_convert_fusion.own_ref, bf16[256,2048]{1,0:T(8,128)(2,1)} %collective-permute-done.19.other_ref, f32[512,2048]{1,0:T(8,128)} %fusion.act_grad_ref, ...), custom_call_target="tpu_custom_call" | custom-call | flops 8589934592 | bytes 31457280 | tf_op jit(solution)/shard_map/ffn_inner/pallas_call | solution.py:805
  257.2 15.1 %ffn_back.2 = (f32[256,2048]{1,0:T(8,128)}, bf16[256,2048]{1,0:T(8,128)(2,1)}) custom-call(bf16[512,2048]{1,0:T(8,128)(2,1)} %get-tuple-element.274.refs_0_.refs_1_, bf16[512,2048]{1,0:T(8,128)(2,1)} %get-tuple-element.283.refs_1_.refs_2_, bf16[2048,6144]{1,0:T(8,128)(2,1)} %all-gather.5.cloned.1.call-done.gate_ref.up_ref.refs_2_.refs_3_.refs_1_, ...), custom_call_target="tpu_custom_call" | custom-call | flops 8589934592 | bytes 25165824 | tf_op jit(solution)/shard_map/ffn_back/pallas_call | solution.py:838
  274.0 12.2 %weight_grads.3 = bf16[2048,3072]{1,0:T(8,128)(2,1)} custom-call(bf16[512,2048]{1,0:T(8,128)(2,1)} %get-tuple-element.272.refs_0_, bf16[512,2048]{1,0:T(8,128)(2,1)} %get-tuple-element.274.refs_0_.refs_1_, bf16[512,2048]{1,0:T(8,128)(2,1)} %get-tuple-element.283.refs_1_.refs_2_), custom_call_target="tpu_custom_call" | custom-call | flops 6442450944 | bytes 18874368 | tf_op jit(solution)/shard_map/weight_grads/pallas_call | solution.py:964
  286.2 8.8 %collective-permute-done.20.swap_ref = bf16[256,2048]{1,0:T(8,128)(2,1)S(1)} collective-permute-done((bf16[256,2048]{1,0:T(8,128)(2,1)}, bf16[256,2048]{1,0:T(8,128)(2,1)S(1)}, u32[]{:S(2)}, u32[]{:S(2)}) %collective-permute-start.20) | collective-permute-done | bytes 1048608 | tf_op jit(solution)/shard_map/ppermute | solution.py:29
  296.0 5.6 norm_back.1
  301.6 3.5 collective-permute-start.22
  307.9 14.8 %weight_grads.4 = bf16[2048,3072]{1,0:T(8,128)(2,1)} custom-call(bf16[512,2048]{1,0:T(8,128)(2,1)} %get-tuple-element.272.refs_0_, bf16[512,2048]{1,0:T(8,128)(2,1)} %pad_maximum_fusion.refs_1_, bf16[512,2048]{1,0:T(8,128)(2,1)} %get-tuple-element.283.refs_1_.refs_2_, bf16[512,2048]{1,0:T(8,128)(2,1)} %get-tuple-element.290.refs_3_.refs_0_), custom_call_target="tpu_custom_call" | custom-call | flops 6442450944 | bytes 20971520 | tf_op jit(solution)/shard_map/weight_grads/pallas_call | solution.py:964
  324.1 10.4 %collective-permute-done.23.refs_4_ = bf16[256,2048]{1,0:T(8,128)(2,1)S(1)} collective-permute-done((bf16[256,2048]{1,0:T(8,128)(2,1)}, bf16[256,2048]{1,0:T(8,128)(2,1)S(1)}, u32[]{:S(2)}, u32[]{:S(2)}) %collective-permute-start.23) | collective-permute-done | bytes 1048608 | tf_op jit(solution)/shard_map/ppermute | solution.py:53
  337.6 10.6 %ffn_back.3 = (f32[256,2048]{1,0:T(8,128)}, bf16[256,2048]{1,0:T(8,128)(2,1)}) custom-call(bf16[512,2048]{1,0:T(8,128)(2,1)} %get-tuple-element.290.refs_3_.refs_0_, bf16[2048,6144]{1,0:T(8,128)(2,1)} %all-gather.5.cloned.1.call-done.gate_ref.up_ref.refs_2_.refs_3_.refs_1_), custom_call_target="tpu_custom_call" | custom-call | flops 4294967296 | bytes 25165824 | tf_op jit(solution)/shard_map/ffn_back/pallas_call | solution.py:838
  348.2 13.9 %collective-permute-done.25.refs_5_ = bf16[256,2048]{1,0:T(8,128)(2,1)} collective-permute-done((bf16[256,2048]{1,0:T(8,128)(2,1)S(1)}, bf16[256,2048]{1,0:T(8,128)(2,1)}, u32[]{:S(2)}, u32[]{:S(2)}) %collective-permute-start.25) | collective-permute-done | bytes 1048608 | tf_op jit(solution)/shard_map/ppermute | solution.py:53
  364.3 4.9 slice.147.w_ref
  370.9 17.3 %collective-permute-done.27.refs_6_ = bf16[256,2048]{1,0:T(8,128)(2,1)} collective-permute-done((bf16[256,2048]{1,0:T(8,128)(2,1)}, bf16[256,2048]{1,0:T(8,128)(2,1)}, u32[]{:S(2)}, u32[]{:S(2)}) %collective-permute-start.27) | collective-permute-done | bytes 1048608 | tf_op jit(solution)/shard_map/ppermute | solution.py:53
  388.2 10.9 %joint.1 = (f32[1024,1024]{1,0:T(8,128)}, bf16[1024,2048]{1,0:T(8,128)(2,1)}) custom-call(s32[1]{0:T(128)} %bitcast.1.place_ref, bf16[2048,1024]{1,0:T(8,128)(2,1)} %slice.147.w_ref, bf16[256,2048]{1,0:T(8,128)(2,1)} %get-tuple-element.281.refs_0_, bf16[256,2048]{1,0:T(8,128)(2,1)} %copy-done.37, bf16[256,2048]{1,0:T(8,128)(2,1)} %collective-permute-done.24.refs_2_, ...), custom_call_target="tpu_custom_call" | custom-call | flops 4294967296 | bytes 12582912 | tf_op jit(solution)/shard_map/joint/pallas_call | solution.py:874
  400.4 33.1 %mixer_backward.1 = (bf16[1024,2688]{1,0:T(8,128)(2,1)}, f32[8,128]{1,0:T(8,128)}) custom-call(s32[1]{0:T(128)} %bitcast.1.place_ref, f32[1024,2688]{1,0:T(8,128)} %get-tuple-element.235.mixed_ref, f32[1024,1024]{1,0:T(8,128)} %get-tuple-element.299.joint_ref, f32[4,256,768]{2,1,0:T(8,128)} %get-tuple-element.300.state_ref, ...), custom_call_target="tpu_custom_call" | custom-call | flops 20000000000 | bytes 30000000 | tf_op jit(solution)/shard_map/mixer_backward/pallas_call | solution.py:596
  435.0 4.9 collective-permute-start.29
  441.2 18.4 %mixer_out.1 = (f32[8,2048]{1,0:T(8,128)}, f32[256,2048]{1,0:T(8,128)}, bf16[256,2048]{1,0:T(8,128)(2,1)}, bf16[256,2048]{1,0:T(8,128)(2,1)}, bf16[256,2048]{1,0:T(8,128)(2,1)}) custom-call(bf16[1024,2688]{1,0:T(8,128)(2,1)} %get-tuple-element.310.grad_ref.refs_2_, bf16[2048,3712]{1,0:T(8,128)(2,1)} %all-gather.3.cloned.1.call-done.w_ref, ...), custom_call_target="tpu_custom_call" | custom-call | flops 11274289152 | bytes 30212096 | tf_op jit(solution)/shard_map/mixer_out/pallas_call | solution.py:910
  463.4 7.3 collective-permute-start.33
  472.1 23.2 %weight_grads.5 = bf16[2048,3712]{1,0:T(8,128)(2,1)} custom-call(bf16[1024,2048]{1,0:T(8,128)(2,1)} %get-tuple-element.311.normed_ref.refs_0_, bf16[1024,2048]{1,0:T(8,128)(2,1)} %get-tuple-element.325.refs_1_, bf16[1024,2688]{1,0:T(8,128)(2,1)} %get-tuple-element.310.grad_ref.refs_2_, bf16[1024,1024]{1,0:T(8,128)(2,1)} %get-tuple-element.254.refs_3_, ...), custom_call_target="tpu_custom_call" | custom-call | flops 15569256448 | bytes 31260672 | tf_op jit(solution)/shard_map/weight_grads/pallas_call | solution.py:964
  505.1 22.4 %collective-permute-done.35 = bf16[128,3072]{1,0:T(8,128)(2,1)S(1)} collective-permute-done((bf16[128,3072]{1,0:T(8,128)(2,1)S(1)}, bf16[128,3072]{1,0:T(8,128)(2,1)S(1)}, u32[]{:S(2)}, u32[]{:S(2)}) %collective-permute-start.35) | collective-permute-done | bytes 786464 | tf_op jit(solution)/shard_map/ppermute | solution.py:53
  533.0 4.1 collective-permute-start.38
  538.4 29.6 %collective-permute-done.38.refs_8_ = bf16[128,3072]{1,0:T(8,128)(2,1)S(1)} collective-permute-done((bf16[128,3072]{1,0:T(8,128)(2,1)S(1)}, bf16[128,3072]{1,0:T(8,128)(2,1)S(1)}, u32[]{:S(2)}, u32[]{:S(2)}) %collective-permute-start.38) | collective-permute-done | bytes 786464 | tf_op jit(solution)/shard_map/ppermute | solution.py:53
  568.9 6.6 collective-permute-start.44
  578.9 34.2 %collective-permute-done.43.refs_12_ = bf16[128,3072]{1,0:T(8,128)(2,1)S(1)} collective-permute-done((bf16[128,3072]{1,0:T(8,128)(2,1)S(1)}, bf16[128,3072]{1,0:T(8,128)(2,1)S(1)}, u32[]{:S(2)}, u32[]{:S(2)}) %collective-permute-start.43) | collective-permute-done | bytes 786464 | tf_op jit(solution)/shard_map/ppermute | solution.py:53
  614.5 4.4 collective-permute-start.46
  622.2 53.1 %collective-permute-done.49.refs_13_ = bf16[128,3072]{1,0:T(8,128)(2,1)S(1)} collective-permute-done((bf16[128,3072]{1,0:T(8,128)(2,1)}, bf16[128,3072]{1,0:T(8,128)(2,1)S(1)}, u32[]{:S(2)}, u32[]{:S(2)}) %collective-permute-start.49) | collective-permute-done | bytes 786464 | tf_op jit(solution)/shard_map/ppermute | solution.py:53
  678.6 10.0 %unpack_ffn.1 = (f32[256,4096]{1,0:T(8,128)}, f32[256,4096]{1,0:T(8,128)}, f32[256,4096]{1,0:T(8,128)}) custom-call(s32[1]{0:T(128)} %bitcast.1.place_ref, bf16[128,3072]{1,0:T(8,128)(2,1)} %copy-done.8, bf16[128,3072]{1,0:T(8,128)(2,1)} %collective-permute-done.29.refs_1_, bf16[128,3072]{1,0:T(8,128)(2,1)} %collective-permute-done.31.refs_2_, ...), custom_call_target="tpu_custom_call" | custom-call | flops 100000000 | bytes 22000000 | tf_op jit(solution)/shard_map/unpack_ffn/pallas_call | solution.py:1107
  688.6 28.4 %collective-permute-done.51.refs_5_ = bf16[256,3712]{1,0:T(8,128)(2,1)} collective-permute-done((bf16[256,3712]{1,0:T(8,128)(2,1)}, bf16[256,3712]{1,0:T(8,128)(2,1)}, u32[]{:S(2)}, u32[]{:S(2)}) %collective-permute-start.51) | collective-permute-done | bytes 1900576 | tf_op jit(solution)/shard_map/ppermute | solution.py:53
  724.5 31.6 %collective-permute-done.53.refs_6_ = bf16[256,3712]{1,0:T(8,128)(2,1)} collective-permute-done((bf16[256,3712]{1,0:T(8,128)(2,1)}, bf16[256,3712]{1,0:T(8,128)(2,1)}, u32[]{:S(2)}, u32[]{:S(2)}) %collective-permute-start.53) | collective-permute-done | bytes 1900576 | tf_op jit(solution)/shard_map/ppermute | solution.py:53
  756.2 9.0 %unpack_mixer.1 = (f32[256,8192]{1,0:T(8,128)}, f32[256,1024]{1,0:T(8,128)}, f32[256,3072]{1,0:T(8,128)}, f32[256,128]{1,0:T(8,128)}) custom-call(s32[1]{0:T(128)} %bitcast.1.place_ref, bf16[256,3712]{1,0:T(8,128)(2,1)} %reduce-scatter.8.cloned.1.call-done.refs_0_, bf16[256,3712]{1,0:T(8,128)(2,1)} %collective-permute-done.46.refs_1_, ...), custom_call_target="tpu_custom_call" | custom-call | flops 100000000 | bytes 26000000 | tf_op jit(solution)/shard_map/unpack_mixer/pallas_call | solution.py:1053
  (270 shorter events, 122.6 us)
Async XLA Ops:
  7.2 95.0 %all-gather.3.cloned.1.call-start = ((), (), s32[]{:S(2)}) async-start(), calls=%async_computation.3 | async-start | bytes 17104896 | tf_op jit(solution)/shard_map/all_gather | solution.py:145
  13.0 213.9 %all-gather.5.cloned.1.call-start = ((), (), s32[]{:S(2)}) async-start(), calls=%async_computation.4 | async-start | bytes 28311552 | tf_op jit(solution)/shard_map/all_gather | solution.py:145
  13.1 27.4 %collective-permute-start = (bf16[256,2048]{1,0:T(8,128)(2,1)S(1)}, bf16[256,2048]{1,0:T(8,128)(2,1)S(1)}, u32[]{:S(2)}, u32[]{:S(2)}) collective-permute-start(bf16[256,2048]{1,0:T(8,128)(2,1)S(1)} %bitcast.43), channel_id=1, source_target_pairs={{0,1},{1,2},{2,3},{4,5},{5,6},{6,7},{8,9},{9,10},{10,11},{12,13},{... | collective-permute-start | bytes 3145736 | tf_op jit(solution)/shard_map/ppermute | solution.py:53
  18.1 26.5 %collective-permute-start.1 = (bf16[256,2048]{1,0:T(8,128)(2,1)S(1)}, bf16[256,2048]{1,0:T(8,128)(2,1)S(1)}, u32[]{:S(2)}, u32[]{:S(2)}) collective-permute-start(bf16[256,2048]{1,0:T(8,128)(2,1)S(1)} %bitcast.44), channel_id=1, source_target_pairs={{1,0},{2,1},{3,2},{5,4},{6,5},{7,6},{9,8},{10,9},{11,10},{13,12},{... | collective-permute-start | bytes 3145736 | tf_op jit(solution)/shard_map/ppermute | solution.py:53
  45.3 28.1 %collective-permute-start.3 = (bf16[256,2048]{1,0:T(8,128)(2,1)S(1)}, bf16[256,2048]{1,0:T(8,128)(2,1)}, u32[]{:S(2)}, u32[]{:S(2)}) collective-permute-start(bf16[256,2048]{1,0:T(8,128)(2,1)S(1)} %collective-permute-done.1.refs_4_), channel_id=1, source_target_pairs={{1,0},{2,1},{5,4},{6,5},{9,8},{10,9},{13,12},{14,13},{17,16},{18,1... | collective-permute-start | bytes 3145736 | tf_op jit(solution)/shard_map/ppermute | solution.py:53
  73.5 325.7 %reduce-scatter.4.cloned.1.call-start = ((), (), s32[]{:S(2)}) async-start(), calls=%async_computation.5 | async-start | bytes 14155776 | tf_op jit(solution)/shard_map/reduce_scatter | solution.py:149
  76.2 25.0 %collective-permute-start.5 = (bf16[256,2048]{1,0:T(8,128)(2,1)}, bf16[256,2048]{1,0:T(8,128)(2,1)S(1)}, u32[]{:S(2)}, u32[]{:S(2)}) collective-permute-start(bf16[256,2048]{1,0:T(8,128)(2,1)} %collective-permute-done.3.refs_5_), channel_id=1, source_target_pairs={{1,0},{5,4},{9,8},{13,12},{17,16},{21,20},{25,24},{29,28}} | collective-permute-start | bytes 3145736 | tf_op jit(solution)/shard_map/ppermute | solution.py:53
  102.2 39.2 %collective-permute-start.6 = (bf16[256,2048]{1,0:T(8,128)(2,1)S(1)}, bf16[256,2048]{1,0:T(8,128)(2,1)S(1)}, u32[]{:S(2)}, u32[]{:S(2)}) collective-permute-start(bf16[256,2048]{1,0:T(8,128)(2,1)S(1)} %bitcast.48), channel_id=1, source_target_pairs={{0,1},{1,0},{2,3},{3,2},{4,5},{5,4},{6,7},{7,6},{8,9},{9,8},{10,11... | collective-permute-start | bytes 3145736 | tf_op jit(solution)/shard_map/ppermute | solution.py:29
  146.7 15.9 %collective-permute-start.7 = (bf16[256,1024]{1,0:T(8,128)(2,1)S(1)}, bf16[256,1024]{1,0:T(8,128)(2,1)S(1)}, u32[]{:S(2)}, u32[]{:S(2)}) collective-permute-start(bf16[256,1024]{1,0:T(8,128)(2,1)S(1)} %get-tuple-element.239), channel_id=1, source_target_pairs={{0,1},{4,5},{8,9},{12,13},{16,17},{20,21},{24,25},{28,29}} | collective-permute-start | bytes 1572872 | tf_op jit(solution)/shard_map/ppermute | solution.py:53
  157.0 16.8 %collective-permute-start.13 = (bf16[256,1024]{1,0:T(8,128)(2,1)S(1)}, bf16[256,1024]{1,0:T(8,128)(2,1)S(1)}, u32[]{:S(2)}, u32[]{:S(2)}) collective-permute-start(bf16[256,1024]{1,0:T(8,128)(2,1)S(1)} %get-tuple-element.252), channel_id=1, source_target_pairs={{0,1},{4,5},{8,9},{12,13},{16,17},{20,21},{24,25},{28,29}} | collective-permute-start | bytes 1572872 | tf_op jit(solution)/shard_map/ppermute | solution.py:53
  162.9 22.2 %collective-permute-start.9 = (bf16[256,1024]{1,0:T(8,128)(2,1)S(1)}, bf16[256,1024]{1,0:T(8,128)(2,1)S(1)}, u32[]{:S(2)}, u32[]{:S(2)}) collective-permute-start(bf16[256,1024]{1,0:T(8,128)(2,1)S(1)} %get-tuple-element.244), channel_id=1, source_target_pairs={{0,1},{1,2},{4,5},{5,6},{8,9},{9,10},{12,13},{13,14},{16,17},{17,1... | collective-permute-start | bytes 1572872 | tf_op jit(solution)/shard_map/ppermute | solution.py:53
  167.3 17.7 %collective-permute-start.10 = (bf16[256,1024]{1,0:T(8,128)(2,1)S(1)}, bf16[256,1024]{1,0:T(8,128)(2,1)S(1)}, u32[]{:S(2)}, u32[]{:S(2)}) collective-permute-start(bf16[256,1024]{1,0:T(8,128)(2,1)S(1)} %get-tuple-element.245), channel_id=1, source_target_pairs={{2,1},{3,2},{6,5},{7,6},{10,9},{11,10},{14,13},{15,14},{18,17},{19... | collective-permute-start | bytes 1572872 | tf_op jit(solution)/shard_map/ppermute | solution.py:53
  174.1 22.2 %collective-permute-start.15 = (bf16[256,1024]{1,0:T(8,128)(2,1)S(1)}, bf16[256,1024]{1,0:T(8,128)(2,1)S(1)}, u32[]{:S(2)}, u32[]{:S(2)}) collective-permute-start(bf16[256,1024]{1,0:T(8,128)(2,1)S(1)} %get-tuple-element.257), channel_id=1, source_target_pairs={{0,1},{1,2},{4,5},{5,6},{8,9},{9,10},{12,13},{13,14},{16,17},{17,1... | collective-permute-start | bytes 1572872 | tf_op jit(solution)/shard_map/ppermute | solution.py:53
  178.6 17.7 %collective-permute-start.16 = (bf16[256,1024]{1,0:T(8,128)(2,1)S(1)}, bf16[256,1024]{1,0:T(8,128)(2,1)S(1)}, u32[]{:S(2)}, u32[]{:S(2)}) collective-permute-start(bf16[256,1024]{1,0:T(8,128)(2,1)S(1)} %get-tuple-element.258), channel_id=1, source_target_pairs={{2,1},{3,2},{6,5},{7,6},{10,9},{11,10},{14,13},{15,14},{18,17},{19... | collective-permute-start | bytes 1572872 | tf_op jit(solution)/shard_map/ppermute | solution.py:53
  185.4 22.2 %collective-permute-start.11 = (bf16[256,1024]{1,0:T(8,128)(2,1)S(1)}, bf16[256,1024]{1,0:T(8,128)(2,1)S(1)}, u32[]{:S(2)}, u32[]{:S(2)}) collective-permute-start(bf16[256,1024]{1,0:T(8,128)(2,1)S(1)} %add_convert_fusion.10), channel_id=1, source_target_pairs={{0,1},{1,2},{2,3},{4,5},{5,6},{6,7},{8,9},{9,10},{10,11},{12,13},{... | collective-permute-start | bytes 1572872 | tf_op jit(solution)/shard_map/ppermute | solution.py:53
  189.8 17.7 %collective-permute-start.12 = (bf16[256,1024]{1,0:T(8,128)(2,1)S(1)}, bf16[256,1024]{1,0:T(8,128)(2,1)S(1)}, u32[]{:S(2)}, u32[]{:S(2)}) collective-permute-start(bf16[256,1024]{1,0:T(8,128)(2,1)S(1)} %add_convert_fusion.9), channel_id=1, source_target_pairs={{1,0},{2,1},{3,2},{5,4},{6,5},{7,6},{9,8},{10,9},{11,10},{13,12},{... | collective-permute-start | bytes 1572872 | tf_op jit(solution)/shard_map/ppermute | solution.py:53
  196.6 18.1 %collective-permute-start.17 = (bf16[256,1024]{1,0:T(8,128)(2,1)S(1)}, bf16[256,1024]{1,0:T(8,128)(2,1)S(1)}, u32[]{:S(2)}, u32[]{:S(2)}) collective-permute-start(bf16[256,1024]{1,0:T(8,128)(2,1)S(1)} %add_convert_fusion.6), channel_id=1, source_target_pairs={{0,1},{1,2},{2,3},{4,5},{5,6},{6,7},{8,9},{9,10},{10,11},{12,13},{... | collective-permute-start | bytes 1572872 | tf_op jit(solution)/shard_map/ppermute | solution.py:53
  218.0 22.3 %collective-permute-start.19 = (bf16[256,2048]{1,0:T(8,128)(2,1)}, bf16[256,2048]{1,0:T(8,128)(2,1)}, u32[]{:S(2)}, u32[]{:S(2)}) collective-permute-start(bf16[256,2048]{1,0:T(8,128)(2,1)} %multiply_convert_fusion.own_ref), channel_id=1, source_target_pairs={{0,1},{1,0},{2,3},{3,2},{4,5},{5,4},{6,7},{7,6},{8,9},{9,8},{10,11... | collective-permute-start | bytes 3145736 | tf_op jit(solution)/shard_map/ppermute | solution.py:29
  272.3 22.7 %collective-permute-start.20 = (bf16[256,2048]{1,0:T(8,128)(2,1)}, bf16[256,2048]{1,0:T(8,128)(2,1)S(1)}, u32[]{:S(2)}, u32[]{:S(2)}) collective-permute-start(bf16[256,2048]{1,0:T(8,128)(2,1)} %get-tuple-element.271), channel_id=1, source_target_pairs={{0,1},{1,0},{2,3},{3,2},{4,5},{5,4},{6,7},{7,6},{8,9},{9,8},{10,11... | collective-permute-start | bytes 3145736 | tf_op jit(solution)/shard_map/ppermute | solution.py:29
  296.0 201.3 %reduce-scatter.6.cloned.1.call-start = ((), (), s32[]{:S(2)}) async-start(), calls=%async_computation.6 | async-start | bytes 14155776 | tf_op jit(solution)/shard_map/reduce_scatter | solution.py:149
  301.6 22.6 %collective-permute-start.22 = (bf16[256,2048]{1,0:T(8,128)(2,1)}, bf16[256,2048]{1,0:T(8,128)(2,1)S(1)}, u32[]{:S(2)}, u32[]{:S(2)}) collective-permute-start(bf16[256,2048]{1,0:T(8,128)(2,1)} %get-tuple-element.281.refs_0_), channel_id=1, source_target_pairs={{0,1},{1,2},{2,3},{4,5},{5,6},{6,7},{8,9},{9,10},{10,11},{12,13},{... | collective-permute-start | bytes 3145736 | tf_op jit(solution)/shard_map/ppermute | solution.py:53
  305.0 29.5 %collective-permute-start.23 = (bf16[256,2048]{1,0:T(8,128)(2,1)}, bf16[256,2048]{1,0:T(8,128)(2,1)S(1)}, u32[]{:S(2)}, u32[]{:S(2)}) collective-permute-start(bf16[256,2048]{1,0:T(8,128)(2,1)} %get-tuple-element.281.refs_0_), channel_id=1, source_target_pairs={{1,0},{2,1},{3,2},{5,4},{6,5},{7,6},{9,8},{10,9},{11,10},{13,12},{... | collective-permute-start | bytes 3145736 | tf_op jit(solution)/shard_map/ppermute | solution.py:53
  334.6 279.9 %reduce-scatter.8.cloned.1.call-start = ((), (), s32[]{:S(2)}) async-start(), calls=%async_computation.7 | async-start | bytes 17104896 | tf_op jit(solution)/shard_map/reduce_scatter | solution.py:149
  336.3 25.8 %collective-permute-start.25 = (bf16[256,2048]{1,0:T(8,128)(2,1)S(1)}, bf16[256,2048]{1,0:T(8,128)(2,1)}, u32[]{:S(2)}, u32[]{:S(2)}) collective-permute-start(bf16[256,2048]{1,0:T(8,128)(2,1)S(1)} %collective-permute-done.23.refs_4_), channel_id=1, source_target_pairs={{1,0},{2,1},{5,4},{6,5},{9,8},{10,9},{13,12},{14,13},{17,16},{18,1... | collective-permute-start | bytes 3145736 | tf_op jit(solution)/shard_map/ppermute | solution.py:53
  362.8 25.4 %collective-permute-start.27 = (bf16[256,2048]{1,0:T(8,128)(2,1)}, bf16[256,2048]{1,0:T(8,128)(2,1)}, u32[]{:S(2)}, u32[]{:S(2)}) collective-permute-start(bf16[256,2048]{1,0:T(8,128)(2,1)} %collective-permute-done.25.refs_5_), channel_id=1, source_target_pairs={{1,0},{5,4},{9,8},{13,12},{17,16},{21,20},{25,24},{29,28}} | collective-permute-start | bytes 3145736 | tf_op jit(solution)/shard_map/ppermute | solution.py:53
  388.2 45.3 %collective-permute-start.28 = (bf16[256,2048]{1,0:T(8,128)(2,1)S(1)}, bf16[256,2048]{1,0:T(8,128)(2,1)S(1)}, u32[]{:S(2)}, u32[]{:S(2)}) collective-permute-start(bf16[256,2048]{1,0:T(8,128)(2,1)S(1)} %copy-done.39), channel_id=1, source_target_pairs={{0,1},{1,0},{2,3},{3,2},{4,5},{5,4},{6,7},{7,6},{8,9},{9,8},{10,11... | collective-permute-start | bytes 3145736 | tf_op jit(solution)/shard_map/ppermute | solution.py:29
  400.3 33.3 %collective-permute-start.21 = (bf16[128,3072]{1,0:T(8,128)(2,1)S(1)}, bf16[128,3072]{1,0:T(8,128)(2,1)S(1)}, u32[]{:S(2)}, u32[]{:S(2)}) collective-permute-start(bf16[128,3072]{1,0:T(8,128)(2,1)S(1)} %constant_dynamic-slice_fusion.1), channel_id=1, source_target_pairs={{0,2},{1,3},{2,0},{3,1},{4,6},{5,7},{6,4},{7,5},{8,10},{9,11},{10,... | collective-permute-start | bytes 2359304 | tf_op jit(solution)/shard_map/ppermute | solution.py:53
  435.0 24.5 %collective-permute-start.29 = (bf16[128,3072]{1,0:T(8,128)(2,1)S(1)}, bf16[128,3072]{1,0:T(8,128)(2,1)}, u32[]{:S(2)}, u32[]{:S(2)}) collective-permute-start(bf16[128,3072]{1,0:T(8,128)(2,1)S(1)} %add_convert_fusion.4.refs_0_), channel_id=1, source_target_pairs={{0,1},{1,2},{2,3},{4,5},{5,6},{6,7},{8,9},{9,10},{10,11},{12,13},{... | collective-permute-start | bytes 2359304 | tf_op jit(solution)/shard_map/ppermute | solution.py:53
  439.9 19.7 %collective-permute-start.30 = (bf16[128,3072]{1,0:T(8,128)(2,1)S(1)}, bf16[128,3072]{1,0:T(8,128)(2,1)}, u32[]{:S(2)}, u32[]{:S(2)}) collective-permute-start(bf16[128,3072]{1,0:T(8,128)(2,1)S(1)} %add_convert_fusion.4.refs_0_), channel_id=1, source_target_pairs={{1,0},{2,1},{3,2},{5,4},{6,5},{7,6},{9,8},{10,9},{11,10},{13,12},{... | collective-permute-start | bytes 2359304 | tf_op jit(solution)/shard_map/ppermute | solution.py:53
  460.5 34.8 %collective-permute-start.31 = (bf16[128,3072]{1,0:T(8,128)(2,1)}, bf16[128,3072]{1,0:T(8,128)(2,1)}, u32[]{:S(2)}, u32[]{:S(2)}) collective-permute-start(bf16[128,3072]{1,0:T(8,128)(2,1)} %collective-permute-done.29.refs_1_), channel_id=1, source_target_pairs={{1,2},{2,3},{5,6},{6,7},{9,10},{10,11},{13,14},{14,15},{17,18},{18... | collective-permute-start | bytes 2359304 | tf_op jit(solution)/shard_map/ppermute | solution.py:53
  462.1 33.3 %collective-permute-start.32 = (bf16[128,3072]{1,0:T(8,128)(2,1)}, bf16[128,3072]{1,0:T(8,128)(2,1)}, u32[]{:S(2)}, u32[]{:S(2)}) collective-permute-start(bf16[128,3072]{1,0:T(8,128)(2,1)} %collective-permute-done.30.refs_4_), channel_id=1, source_target_pairs={{1,0},{2,1},{5,4},{6,5},{9,8},{10,9},{13,12},{14,13},{17,16},{18,1... | collective-permute-start | bytes 2359304 | tf_op jit(solution)/shard_map/ppermute | solution.py:53
  463.4 32.0 %collective-permute-start.33 = (bf16[256,2048]{1,0:T(8,128)(2,1)}, bf16[256,2048]{1,0:T(8,128)(2,1)S(1)}, u32[]{:S(2)}, u32[]{:S(2)}) collective-permute-start(bf16[256,2048]{1,0:T(8,128)(2,1)} %get-tuple-element.323), channel_id=1, source_target_pairs={{0,1},{4,5},{8,9},{12,13},{16,17},{20,21},{24,25},{28,29}} | collective-permute-start | bytes 3145736 | tf_op jit(solution)/shard_map/ppermute | solution.py:53
  470.6 24.7 %collective-permute-start.34 = (bf16[256,2048]{1,0:T(8,128)(2,1)}, bf16[256,2048]{1,0:T(8,128)(2,1)S(1)}, u32[]{:S(2)}, u32[]{:S(2)}) collective-permute-start(bf16[256,2048]{1,0:T(8,128)(2,1)} %get-tuple-element.324), channel_id=1, source_target_pairs={{3,2},{7,6},{11,10},{15,14},{19,18},{23,22},{27,26},{31,30}} | collective-permute-start | bytes 3145736 | tf_op jit(solution)/shard_map/ppermute | solution.py:53
  498.8 28.8 %collective-permute-start.35 = (bf16[128,3072]{1,0:T(8,128)(2,1)S(1)}, bf16[128,3072]{1,0:T(8,128)(2,1)S(1)}, u32[]{:S(2)}, u32[]{:S(2)}) collective-permute-start(bf16[128,3072]{1,0:T(8,128)(2,1)S(1)} %constant_dynamic-slice_fusion), channel_id=1, source_target_pairs={{0,2},{1,3},{2,0},{3,1},{4,6},{5,7},{6,4},{7,5},{8,10},{9,11},{10,... | collective-permute-start | bytes 2359304 | tf_op jit(solution)/shard_map/ppermute | solution.py:53
  500.4 27.2 %collective-permute-start.36 = (bf16[128,3072]{1,0:T(8,128)(2,1)}, bf16[128,3072]{1,0:T(8,128)(2,1)S(1)}, u32[]{:S(2)}, u32[]{:S(2)}) collective-permute-start(bf16[128,3072]{1,0:T(8,128)(2,1)} %collective-permute-done.31.refs_2_), channel_id=1, source_target_pairs={{2,3},{6,7},{10,11},{14,15},{18,19},{22,23},{26,27},{30,31}} | collective-permute-start | bytes 2359304 | tf_op jit(solution)/shard_map/ppermute | solution.py:53
  501.1 29.1 %collective-permute-start.37 = (bf16[128,3072]{1,0:T(8,128)(2,1)}, bf16[128,3072]{1,0:T(8,128)(2,1)S(1)}, u32[]{:S(2)}, u32[]{:S(2)}) collective-permute-start(bf16[128,3072]{1,0:T(8,128)(2,1)} %collective-permute-done.32.refs_5_), channel_id=1, source_target_pairs={{1,0},{5,4},{9,8},{13,12},{17,16},{21,20},{25,24},{29,28}} | collective-permute-start | bytes 2359304 | tf_op jit(solution)/shard_map/ppermute | solution.py:53
  530.4 37.7 %collective-permute-start.40 = (bf16[256,2048]{1,0:T(8,128)(2,1)S(1)}, bf16[256,2048]{1,0:T(8,128)(2,1)S(1)}, u32[]{:S(2)}, u32[]{:S(2)}) collective-permute-start(bf16[256,2048]{1,0:T(8,128)(2,1)S(1)} %get-tuple-element.343), channel_id=1, source_target_pairs={{0,1},{1,2},{4,5},{5,6},{8,9},{9,10},{12,13},{13,14},{16,17},{17,1... | collective-permute-start | bytes 3145736 | tf_op jit(solution)/shard_map/ppermute | solution.py:53
  532.3 35.8 %collective-permute-start.41 = (bf16[256,2048]{1,0:T(8,128)(2,1)S(1)}, bf16[256,2048]{1,0:T(8,128)(2,1)S(1)}, u32[]{:S(2)}, u32[]{:S(2)}) collective-permute-start(bf16[256,2048]{1,0:T(8,128)(2,1)S(1)} %get-tuple-element.344), channel_id=1, source_target_pairs={{2,1},{3,2},{6,5},{7,6},{10,9},{11,10},{14,13},{15,14},{18,17},{19... | collective-permute-start | bytes 3145736 | tf_op jit(solution)/shard_map/ppermute | solution.py:53
  533.0 35.0 %collective-permute-start.38 = (bf16[128,3072]{1,0:T(8,128)(2,1)S(1)}, bf16[128,3072]{1,0:T(8,128)(2,1)S(1)}, u32[]{:S(2)}, u32[]{:S(2)}) collective-permute-start(bf16[128,3072]{1,0:T(8,128)(2,1)S(1)} %add_convert_fusion.3.refs_7_), channel_id=1, source_target_pairs={{0,1},{1,2},{2,3},{4,5},{5,6},{6,7},{8,9},{9,10},{10,11},{12,13},{... | collective-permute-start | bytes 2359304 | tf_op jit(solution)/shard_map/ppermute | solution.py:53
  537.1 30.9 %collective-permute-start.39 = (bf16[128,3072]{1,0:T(8,128)(2,1)S(1)}, bf16[128,3072]{1,0:T(8,128)(2,1)S(1)}, u32[]{:S(2)}, u32[]{:S(2)}) collective-permute-start(bf16[128,3072]{1,0:T(8,128)(2,1)S(1)} %add_convert_fusion.3.refs_7_), channel_id=1, source_target_pairs={{1,0},{2,1},{3,2},{5,4},{6,5},{7,6},{9,8},{10,9},{11,10},{13,12},{... | collective-permute-start | bytes 2359304 | tf_op jit(solution)/shard_map/ppermute | solution.py:53
  568.9 44.2 %collective-permute-start.44 = (bf16[256,2048]{1,0:T(8,128)(2,1)S(1)}, bf16[256,2048]{1,0:T(8,128)(2,1)S(1)}, u32[]{:S(2)}, u32[]{:S(2)}) collective-permute-start(bf16[256,2048]{1,0:T(8,128)(2,1)S(1)} %add_convert_fusion.2), channel_id=1, source_target_pairs={{0,1},{1,2},{2,3},{4,5},{5,6},{6,7},{8,9},{9,10},{10,11},{12,13},{... | collective-permute-start | bytes 3145736 | tf_op jit(solution)/shard_map/ppermute | solution.py:53
  575.5 38.5 %collective-permute-start.45 = (bf16[256,2048]{1,0:T(8,128)(2,1)S(1)}, bf16[256,2048]{1,0:T(8,128)(2,1)S(1)}, u32[]{:S(2)}, u32[]{:S(2)}) collective-permute-start(bf16[256,2048]{1,0:T(8,128)(2,1)S(1)} %add_convert_fusion.1), channel_id=1, source_target_pairs={{1,0},{2,1},{3,2},{5,4},{6,5},{7,6},{9,8},{10,9},{11,10},{13,12},{... | collective-permute-start | bytes 3145736 | tf_op jit(solution)/shard_map/ppermute | solution.py:53
  577.5 35.6 %collective-permute-start.43 = (bf16[128,3072]{1,0:T(8,128)(2,1)S(1)}, bf16[128,3072]{1,0:T(8,128)(2,1)S(1)}, u32[]{:S(2)}, u32[]{:S(2)}) collective-permute-start(bf16[128,3072]{1,0:T(8,128)(2,1)S(1)} %collective-permute-done.39.refs_11_), channel_id=1, source_target_pairs={{1,0},{2,1},{5,4},{6,5},{9,8},{10,9},{13,12},{14,13},{17,16},{18,1... | collective-permute-start | bytes 2359304 | tf_op jit(solution)/shard_map/ppermute | solution.py:53
  614.5 60.8 %collective-permute-start.46 = (bf16[256,3712]{1,0:T(8,128)(2,1)}, bf16[256,3712]{1,0:T(8,128)(2,1)}, u32[]{:S(2)}, u32[]{:S(2)}) collective-permute-start(bf16[256,3712]{1,0:T(8,128)(2,1)} %reduce-scatter.8.cloned.1.call-done.refs_0_), channel_id=1, source_target_pairs={{0,1},{1,2},{2,3},{4,5},{5,6},{6,7},{8,9},{9,10},{10,11},{12,13},{... | collective-permute-start | bytes 5701640 | tf_op jit(solution)/shard_map/ppermute | solution.py:53
  618.8 56.5 %collective-permute-start.47 = (bf16[256,3712]{1,0:T(8,128)(2,1)}, bf16[256,3712]{1,0:T(8,128)(2,1)}, u32[]{:S(2)}, u32[]{:S(2)}) collective-permute-start(bf16[256,3712]{1,0:T(8,128)(2,1)} %reduce-scatter.8.cloned.1.call-done.refs_0_), channel_id=1, source_target_pairs={{1,0},{2,1},{3,2},{5,4},{6,5},{7,6},{9,8},{10,9},{11,10},{13,12},{... | collective-permute-start | bytes 5701640 | tf_op jit(solution)/shard_map/ppermute | solution.py:53
  620.8 54.5 %collective-permute-start.49 = (bf16[128,3072]{1,0:T(8,128)(2,1)}, bf16[128,3072]{1,0:T(8,128)(2,1)S(1)}, u32[]{:S(2)}, u32[]{:S(2)}) collective-permute-start(bf16[128,3072]{1,0:T(8,128)(2,1)} %copy-done.30), channel_id=1, source_target_pairs={{1,0},{5,4},{9,8},{13,12},{17,16},{21,20},{25,24},{29,28}} | collective-permute-start | bytes 2359304 | tf_op jit(solution)/shard_map/ppermute | solution.py:53
  677.3 39.7 %collective-permute-start.51 = (bf16[256,3712]{1,0:T(8,128)(2,1)}, bf16[256,3712]{1,0:T(8,128)(2,1)}, u32[]{:S(2)}, u32[]{:S(2)}) collective-permute-start(bf16[256,3712]{1,0:T(8,128)(2,1)} %collective-permute-done.47.refs_4_), channel_id=1, source_target_pairs={{1,0},{2,1},{5,4},{6,5},{9,8},{10,9},{13,12},{14,13},{17,16},{18,1... | collective-permute-start | bytes 5701640 | tf_op jit(solution)/shard_map/ppermute | solution.py:53
  718.9 37.3 %collective-permute-start.53 = (bf16[256,3712]{1,0:T(8,128)(2,1)}, bf16[256,3712]{1,0:T(8,128)(2,1)}, u32[]{:S(2)}, u32[]{:S(2)}) collective-permute-start(bf16[256,3712]{1,0:T(8,128)(2,1)} %collective-permute-done.51.refs_5_), channel_id=1, source_target_pairs={{1,0},{5,4},{9,8},{13,12},{17,16},{21,20},{25,24},{29,28}} | collective-permute-start | bytes 5701640 | tf_op jit(solution)/shard_map/ppermute | solution.py:53
  (61 other events, 1005.3 us)
Sparse Core Ops, SparseCore 0:
  13.1 85.8 all-gather.2
  101.5 125.3 all-gather.4
  295.1 96.7 reduce-scatter.3
  395.3 92.3 reduce-scatter.5
  497.4 106.7 reduce-scatter.7
